TPU v7x, 32 devices: a whole 2x2x4 slice. The times are simulated.
32 devices in a mesh: section: 2 (over x), expert: 16 (over z, y, core).
Axes of the slice: x: 2, y: 2, z: 4, core: 2. Of those that a mesh axis runs over, the one named last changes fastest.
Arguments:
- tokens: bfloat16 [2048, 4096], P('expert', 'section'), may hold values from -6 to 6
- expert_ids: int32 [2048, 8], P('expert'), may hold values from 0 to 15, all different within a row; in each aligned block of 128 rows (0 to 127, 128 to 255, ...) at most 80 rows name the same one
- numerators: int32 [2048, 8], P('expert'), may hold values from 1 to 255
- gate_up_weight: bfloat16 [16, 4096, 3072], P('expert', None, 'section'), may hold values from -0.09375 to 0.09375
- down_weight: bfloat16 [16, 1536, 4096], P('expert', None, 'section'), may hold values from -0.15625 to 0.15625
Outputs:
- mixed: bfloat16 [2048, 4096], P('expert', 'section')
Inputs may be any that keep to these rules, and one draw needn't show every extreme that they name: `expert_ids`: each row names 8 different experts. Among the rows of one index of expert (aligned blocks of 128 rows) no expert is named more than 80 times, and in every draw some expert is named exactly 80 times there.
All inputs are finite; a program needn't handle non-finite values.
Results may differ from a plain program's by a relative error of at most 0.0057.
Values may be sent and summed in bfloat16 or wider, within the bound.
No kernel may reach another device: no remote copies, remote signals or barrier semaphores. Data moves between devices by JAX's collectives and lax.ppermute only.
A program may use at most 128 MiB of HBM per device.

v0:
```python
import jax
import jax.numpy as jnp
from jax import lax
from jax.sharding import PartitionSpec as P

BLOCK_UNITS = 64


denominator = 256.0


def shards(tokens, expert_ids, numerators, gate_up_weight, down_weight):
    tok_rows = tokens.shape[0]
    top_count = expert_ids.shape[1]
    experts = lax.axis_size("expert") * gate_up_weight.shape[0]
    capacity = tok_rows * top_count * 5 // (4 * experts)
    flat = expert_ids.reshape(-1)
    hits = (flat[:, None] == jnp.arange(experts, dtype=jnp.int32)[None, :]).astype(jnp.int32)
    rank = jnp.sum((jnp.cumsum(hits, axis=0) - hits) * hits, axis=1)
    slot = flat * capacity + rank
    source = jnp.arange(tok_rows * top_count, dtype=jnp.int32) // top_count
    table = jnp.full((experts * capacity,), tok_rows, jnp.int32).at[slot].set(source)
    outgoing = jnp.take(tokens, table, axis=0, mode="fill", fill_value=0)
    slices = lax.all_to_all(outgoing, "expert", split_axis=0, concat_axis=0, tiled=True)
    arrived = lax.all_gather(slices, "section", axis=1, tiled=True)
    slot_rows = arrived.shape[0]
    local_units = gate_up_weight.shape[2] // 2
    both = jnp.dot(arrived, gate_up_weight[0], preferred_element_type=jnp.float32)
    split_up = both.reshape(slot_rows, local_units // BLOCK_UNITS, 2, BLOCK_UNITS)
    gate = split_up[:, :, 0, :].reshape(slot_rows, local_units)
    up = split_up[:, :, 1, :].reshape(slot_rows, local_units)
    hidden = (jax.nn.silu(gate) * up).astype(jnp.bfloat16)
    all_hidden = lax.all_gather(hidden, "section", axis=1, tiled=True)
    result = jnp.dot(all_hidden, down_weight[0], preferred_element_type=jnp.float32).astype(
        jnp.bfloat16
    )
    returned = lax.all_to_all(result, "expert", split_axis=0, concat_axis=0, tiled=True)
    picked = jnp.take(returned, slot, axis=0).astype(jnp.float32)
    weights = numerators.reshape(-1).astype(jnp.float32) / denominator
    weighted = (picked * weights[:, None]).reshape(tok_rows, top_count, -1)
    return jnp.sum(weighted, axis=1).astype(jnp.bfloat16)


def solution(mesh):
    in_specs = (
        P("expert", "section"),
        P("expert", None),
        P("expert", None),
        P("expert", None, "section"),
        P("expert", None, "section"),
    )
    out_specs = P("expert", "section")
    return jax.shard_map(shards, mesh=mesh, in_specs=in_specs, out_specs=out_specs, check_vma=False)
```

profile of v0, /device:TPU:13, one launch (start us, length us, event | category | flops | bytes accessed | tf_op | source)
XLA Modules:
  0.0 514.7 jit_solution(1305554737030272560)
XLA Ops:
  6.5 0.8 copy.18
  7.6 0.7 broadcast_multiply_fusion
  8.3 4.5 reduce-window.6
  12.9 0.1 copy.20
  13.2 0.1 copy.24
  13.3 0.1 mul.41
  13.5 4.3 scatter_custom_fusion
  17.9 6.1 %gather_fusion = bf16[1280,2048]{1,0:T(8,128)(2,1)} fusion(bf16[128,2048]{1,0:T(8,128)(2,1)S(1)} %copy-done, s32[2048]{0:T(1024)S(1)} %pad_clamp_fusion), kind=kCustom, calls=%fused_computation | custom fusion | bytes 10490880 | tf_op jit(solution)/shard_map/jit(_take)/gather | solution.py:23
  24.0 2.9 broadcast_select_fusion
  27.0 121.2 %all_to_all.21 = bf16[16,80,2048]{2,1,0:T(8,128)(2,1)} all-to-all(bf16[16,80,2048]{2,1,0:T(8,128)(2,1)S(1)} %broadcast_select_fusion), channel_id=1, replica_groups=mesh['section'=2,'expert'=16] {'expert'}, dimensions={0} | all-to-all | bytes 10485760 | tf_op jit(solution)/shard_map/all_to_all | solution.py:24
  148.2 0.2 all-gather.5.cloned.1.call-start
  148.4 17.3 %copy.25 = bf16[1,4096,1536]{1,2,0:T(8,128)(2,1)} copy(bf16[1,4096,1536]{2,1,0:T(8,128)(2,1)} %param.8) | data formatting | bytes 25165824 | tf_op args[3]
  165.6 112.1 %all-gather.3.cloned.1.call-done = bf16[1280,4096]{1,0:T(8,128)(2,1)} async-done(((bf16[1280,2048]{1,0:T(8,128)(2,1)}), bf16[1280,4096]{1,0:T(8,128)(2,1)}) %all-gather.3.cloned.1.call-update) | async-done | bytes 10485776 | tf_op jit(solution)/shard_map/all_gather | solution.py:25
  277.8 19.9 %fusion = f32[1280,12,2,64]{0,3,2,1:T(8,128)S(1)} fusion(bf16[12,2,64,4096]{3,2,1,0:T(8,128)(2,1)} %bitcast.62, bf16[1280,4096]{1,0:T(8,128)(2,1)} %all-gather.3.cloned.1.call-done), kind=kOutput, calls=%fused_computation.3 | convolution fusion | flops 16106127360 | bytes 30932992 | tf_op jit(solution)/shard_map/dot_general | solution.py:28
  297.7 0.8 fusion.16
  298.5 2.4 fusion.3
  300.9 54.0 %all-gather.5.cloned.1.call-done = bf16[1280,1536]{0,1:T(8,128)(2,1)} async-done(((bf16[1280,768]{0,1:T(8,128)(2,1)}), bf16[1280,1536]{0,1:T(8,128)(2,1)}) %all-gather.5.cloned.1.call-update) | async-done | bytes 3932176 | tf_op jit(solution)/shard_map/all_gather | solution.py:33
  354.8 13.2 %convolution_convert_fusion = bf16[1280,2048]{1,0:T(8,128)(2,1)} fusion(bf16[1280,1536]{0,1:T(8,128)(2,1)} %all-gather.5.cloned.1.call-done, bf16[1,1536,2048]{2,1,0:T(8,128)(2,1)} %param.9), kind=kOutput, calls=%fused_computation.6 | convolution fusion | flops 8055685120 | bytes 15466496 | tf_op jit(solution)/shard_map/dot_general | solution.py:34
  368.1 6.5 %all-to-all-start.1 = ((bf16[16,80,2048]{2,1,0:T(8,128)(2,1)}), bf16[16,80,2048]{2,1,0:T(8,128)(2,1)}, u32[]{:S(2)}, u32[]{:S(2)}) async-start(bf16[16,80,2048]{2,1,0:T(8,128)(2,1)} %bitcast.63), calls=%async_computation.1 | async-start | bytes 10485760 | tf_op jit(solution)/shard_map/all_to_all | solution.py:37
  374.7 0.1 copy.23
  374.9 0.1 copy.26
  375.0 114.5 %all-to-all-done.1 = bf16[16,80,2048]{2,1,0:T(8,128)(2,1)} async-done(((bf16[16,80,2048]{2,1,0:T(8,128)(2,1)}), bf16[16,80,2048]{2,1,0:T(8,128)(2,1)}, u32[]{:S(2)}, u32[]{:S(2)}) %all-to-all-start.1) | async-done | bytes 5242912 | tf_op jit(solution)/shard_map/all_to_all | solution.py:37
  489.5 12.1 %gather_fusion.1 = bf16[1024,2048]{1,0:T(8,128)(2,1)} fusion(bf16[1280,2048]{1,0:T(8,128)(2,1)} %bitcast.15, s32[1024]{0:T(1024)S(1)} %broadcast_clamp_fusion), kind=kCustom, calls=%fused_computation.1 | custom fusion | bytes 8392704 | tf_op jit(solution)/shard_map/jit(_take)/gather | solution.py:38
  501.6 6.3 %multiply_reduce_fusion = bf16[128,2048]{1,0:T(8,128)(2,1)} fusion(bf16[1024,2048]{1,0:T(8,128)(2,1)} %gather_fusion.1, f32[128,8]{1,0:T(8,128)S(1)} %copy.26, pred[128,8]{1,0:T(8,128)(4,1)S(1)} %copy.23), kind=kLoop, calls=%fused_computation.5 | loop fusion | flops 8126464 | bytes 4723712 | tf_op jit(solution)/shard_map/reduce_sum | solution.py:41
  (31 shorter events, 0.8 us)
Async XLA Ops:
  6.5 11.4 %copy-start = (bf16[128,2048]{1,0:T(8,128)(2,1)S(1)}, bf16[128,2048]{1,0:T(8,128)(2,1)}, u32[]{:S(2)}) copy-start(bf16[128,2048]{1,0:T(8,128)(2,1)} %param.5) | copy-start | bytes 1572868
  6.5 271.2 %all-gather.3.cloned.1.call-start = ((), (), s32[]{:S(2)}) async-start(), calls=%async_computation.2 | async-start | bytes 15728640 | tf_op jit(solution)/shard_map/all_gather | solution.py:25
  148.2 206.7 %all-gather.5.cloned.1.call-start = ((), (), s32[]{:S(2)}) async-start(), calls=%async_computation.3 | async-start | bytes 5898240 | tf_op jit(solution)/shard_map/all_gather | solution.py:33
  368.1 6.6 %copy-start.2 = (s32[128,8]{0,1:T(8,128)S(1)}, s32[128,8]{0,1:T(8,128)}, u32[]{:S(2)}) copy-start(s32[128,8]{0,1:T(8,128)} %param.6) | copy-start | bytes 12292
  368.1 6.8 %copy-start.3 = (s32[128,8]{0,1:T(8,128)S(1)}, s32[128,8]{0,1:T(8,128)}, u32[]{:S(2)}) copy-start(s32[128,8]{0,1:T(8,128)} %param.7) | copy-start | bytes 12292
  368.1 121.4 %all-to-all-start.1 = ((bf16[16,80,2048]{2,1,0:T(8,128)(2,1)}), bf16[16,80,2048]{2,1,0:T(8,128)(2,1)}, u32[]{:S(2)}, u32[]{:S(2)}) async-start(bf16[16,80,2048]{2,1,0:T(8,128)(2,1)} %bitcast.63), calls=%async_computation.1 | async-start | bytes 10485760 | tf_op jit(solution)/shard_map/all_to_all | solution.py:37
  489.5 18.4 %copy-start.1 = (bf16[128,2048]{1,0:T(8,128)(2,1)S(1)}, bf16[128,2048]{1,0:T(8,128)(2,1)}, u32[]{:S(2)}) copy-start(bf16[128,2048]{1,0:T(8,128)(2,1)} %param.5) | copy-start | bytes 1572868
Sparse Core Ops, SparseCore 0:
  148.3 129.4 all-gather.2
  301.0 53.8 all-gather.4
where the time goes:
time: 515 us
  waiting for transfers between devices  281 us (55%)
  blocking collectives  121 us (23%)
  local copies, waits for them, and re-layouts  42.5 us (8%)
  matrix products  33.1 us (6%)
  other arithmetic  17 us (3%)
  between operations  13.5 us (3%)
  starting transfers between devices  6.73 us (1%)
    all_to_all x1, blocking collectives, shards(): lax.all_to_all(outgoing, 'expert', split_axis=0, concat_axis=0, tiled=True)  121 us
    all_to_all x1, waiting for transfers between devices, shards(): lax.all_to_all(result, 'expert', split_axis=0, concat_axis=0, tiled=True)  115 us
    all_gather x1, waiting for transfers between devices, shards(): arrived = lax.all_gather(slices, 'section', axis=1, tiled=True)  112 us
    all_gather x1, waiting for transfers between devices, shards(): all_hidden = lax.all_gather(hidden, 'section', axis=1, tiled=True)  54 us
    dot_general x1, matrix products, shards(): jnp.dot(arrived, gate_up_weight[0], preferred_element_type=jnp.float32)  19.9 us
    unnamed x10, local copies, waits for them, and re-layouts  18.1 us
    dot_general x1, matrix products, shards(): jnp.dot(all_hidden, down_weight[0], preferred_element_type=jnp.float32)  13.2 us
    gather x1, local copies, waits for them, and re-layouts, shards(): picked = jnp.take(returned, slot, axis=0).astype(jnp.float32)  12.1 us
  transfers between devices with their start and end apart: 3, of which 3 were waited for; matrix products, arithmetic and copies ran while one was open for 3% of the time, Pallas kernels for 0%

commit v1 on v0

v1 whole, which is shorter than its diff:
```python
import functools

import jax
import jax.numpy as jnp
from jax import lax
from jax.experimental import pallas as pl
from jax.experimental.pallas import tpu as pltpu
from jax.sharding import PartitionSpec as P

UNITS = 64
SCALE = 1.0 / 256.0


def group_of(capacity):
    count = 2
    while (count * capacity) % 16:
        count *= 2
    return count


def slot_map(code, group, capacity):
    line = jnp.concatenate(
        [code[i : i + 1] + jnp.where(code[i : i + 1] >= 0, i * capacity * 256, 0) for i in range(group)], axis=1
    )
    slot, weight = line >> 8, line & 255
    places = lax.broadcasted_iota(jnp.int32, (group * capacity, line.shape[1]), 0)
    return places == slot, weight


def up_kernel(group, capacity, code_ref, tokens_ref, weight_ref, hidden_ref, rows_ref):
    groups = tokens_ref.shape[0] // group
    sections, rows, width = tokens_ref.shape[1:]
    size = group * capacity
    for g in range(groups):
        onehot, _ = slot_map(code_ref[0, g * group : (g + 1) * group], group, capacity)
        onehot = onehot.astype(jnp.bfloat16)
        for s in range(sections):
            block = jnp.concatenate([tokens_ref[g * group + i, s] for i in range(group)], axis=0)
            picked = jnp.dot(onehot, block, preferred_element_type=jnp.float32)
            rows_ref[g * size : (g + 1) * size, s * width : (s + 1) * width] = picked.astype(jnp.bfloat16)
    columns = weight_ref.shape[1]
    pair = 4 * UNITS

    def products(first, count):
        return jnp.dot(rows_ref[...], weight_ref[:, pl.ds(first, count)], preferred_element_type=jnp.float32)

    def mix(gate, up):
        return (gate / (1.0 + jnp.exp(-gate)) * up).astype(jnp.bfloat16)

    @pl.loop(0, columns // pair)
    def _(p):
        both = products(pl.multiple_of(p * pair, pair), pair)
        one, two = both[:, : 2 * UNITS], both[:, 2 * UNITS :]
        low = lax.broadcasted_iota(jnp.int32, one.shape, 1) < UNITS
        gate = jnp.where(low, one, pltpu.roll(two, UNITS, 1))
        up = jnp.where(low, pltpu.roll(one, UNITS, 1), two)
        hidden_ref[:, pl.ds(pl.multiple_of(p * 2 * UNITS, 2 * UNITS), 2 * UNITS)] = mix(gate, up)

    if columns % pair:
        start = columns // pair * pair
        both = products(start, 2 * UNITS)
        hidden_ref[:, start // 2 :] = mix(both, pltpu.roll(both, UNITS, 1))[:, :UNITS]


def down_kernel(group, capacity, code_ref, hidden_ref, weight_ref, out_ref, result_ref):
    sections, _, units = hidden_ref.shape
    groups = code_ref.shape[1] // group
    size = group * capacity
    wide = weight_ref.shape[1]
    step = min(512, wide)

    @pl.loop(0, wide // step)
    def _(p):
        at = pl.ds(pl.multiple_of(p * step, step), step)
        total = jnp.dot(hidden_ref[0], weight_ref[0:units, at], preferred_element_type=jnp.float32)
        for s in range(1, sections):
            total += jnp.dot(
                hidden_ref[s], weight_ref[s * units : (s + 1) * units, at], preferred_element_type=jnp.float32
            )
        result_ref[...] = total.astype(jnp.bfloat16)
        for g in range(groups):
            onehot, weight = slot_map(code_ref[0, g * group : (g + 1) * group], group, capacity)
            scaled = jnp.where(onehot, weight.astype(jnp.float32) * SCALE, 0.0).astype(jnp.bfloat16)
            mixed = lax.dot_general(
                scaled,
                result_ref[g * size : (g + 1) * size],
                (((0,), (0,)), ((), ())),
                preferred_element_type=jnp.float32,
            )
            tall = scaled.shape[1]
            out_ref[g * tall : (g + 1) * tall, at] = mixed.astype(jnp.bfloat16)


def up_call(code, tokens, weight, capacity):
    blocks, sections, rows, width = tokens.shape
    group = group_of(capacity)
    take = min(blocks, 2 * group)
    depth, columns = weight.shape
    tall = take * capacity
    flops = 2 * blocks * capacity * depth * (columns + group * rows)
    return pl.pallas_call(
        functools.partial(up_kernel, group, capacity),
        grid=(blocks // take,),
        in_specs=[
            pl.BlockSpec((1, take, rows), lambda i: (i, 0, 0)),
            pl.BlockSpec((take, sections, rows, width), lambda i: (i, 0, 0, 0)),
            pl.BlockSpec((depth, columns), lambda i: (0, 0), pipeline_mode=pl.Buffered(1)),
        ],
        out_specs=pl.BlockSpec((tall, columns // 2), lambda i: (i, 0)),
        out_shape=jax.ShapeDtypeStruct((blocks * capacity, columns // 2), jnp.bfloat16),
        scratch_shapes=[pltpu.VMEM((tall, depth), jnp.bfloat16)],
        compiler_params=pltpu.CompilerParams(vmem_limit_bytes=48 * 1024 * 1024),
        cost_estimate=pl.CostEstimate(
            flops=flops, bytes_accessed=2 * (tokens.size + weight.size), transcendentals=blocks * capacity * columns // 2
        ),
        name="gate_up",
    )(code.reshape(blocks // take, take, rows), tokens, weight)


def down_call(code, hidden, weight, capacity):
    blocks, rows = code.shape
    sections, _, units = hidden.shape
    group = group_of(capacity)
    take = min(blocks, 2 * group)
    depth, wide = weight.shape
    tall = take * capacity
    return pl.pallas_call(
        functools.partial(down_kernel, group, capacity),
        grid=(blocks // take,),
        in_specs=[
            pl.BlockSpec((1, take, rows), lambda i: (i, 0, 0)),
            pl.BlockSpec((sections, tall, units), lambda i: (0, i, 0)),
            pl.BlockSpec((depth, wide), lambda i: (0, 0), pipeline_mode=pl.Buffered(1)),
        ],
        out_specs=pl.BlockSpec((take * rows, wide), lambda i: (i, 0)),
        out_shape=jax.ShapeDtypeStruct((blocks * rows, wide), jnp.bfloat16),
        scratch_shapes=[pltpu.VMEM((tall, min(512, wide)), jnp.bfloat16)],
        compiler_params=pltpu.CompilerParams(vmem_limit_bytes=48 * 1024 * 1024),
        cost_estimate=pl.CostEstimate(
            flops=2 * blocks * capacity * wide * (depth + group * rows),
            bytes_accessed=2 * (hidden.size + weight.size + blocks * rows * wide),
            transcendentals=0,
        ),
        name="down",
    )(code.reshape(blocks // take, take, rows), hidden, weight)


def codes_of(expert_ids, numerators, experts):
    rows = expert_ids.shape[0]
    named = expert_ids.T[None] == jnp.arange(experts, dtype=jnp.int32)[:, None, None]
    hits = jnp.any(named, axis=1)
    weight = jnp.sum(jnp.where(named, numerators.T[None], 0), axis=1)
    earlier = jnp.arange(rows)[:, None] < jnp.arange(rows)[None, :]
    rank = jnp.dot(hits.astype(jnp.bfloat16), earlier.astype(jnp.bfloat16), preferred_element_type=jnp.float32)
    return jnp.where(hits, rank.astype(jnp.int32) * 256 + weight, -1)


def shards(tokens, expert_ids, numerators, gate_up_weight, down_weight):
    rows, width = tokens.shape
    experts = lax.axis_size("expert")
    capacity = rows * expert_ids.shape[1] * 5 // (4 * experts)
    chips = experts // 2
    across = [[2 * i + c for i in range(chips)] for c in range(2)]
    pairs = [[2 * i, 2 * i + 1] for i in range(chips)]

    codes = lax.all_gather(codes_of(expert_ids, numerators, experts), "expert", axis=0)
    code = lax.dynamic_index_in_dim(codes, lax.axis_index("expert"), 1, keepdims=False)
    code = code.reshape(chips, 2, rows).swapaxes(0, 1).reshape(experts, rows)

    wide = lax.all_gather(tokens, "section", axis=0)
    half = lax.all_gather(wide, "expert", axis=0, axis_index_groups=across)
    whole = lax.all_gather(half, "expert", axis=0, axis_index_groups=pairs)
    whole = whole.reshape((experts,) + wide.shape)

    hidden = up_call(code, whole, gate_up_weight[0], capacity)
    hidden = lax.all_gather(hidden, "section", axis=0)
    part = down_call(code, hidden, down_weight[0], capacity)

    part = part.reshape(2, chips * rows, width)
    part = lax.psum_scatter(part, "expert", scatter_dimension=0, axis_index_groups=pairs, tiled=False)
    return lax.psum_scatter(part, "expert", scatter_dimension=0, axis_index_groups=across, tiled=True)


def solution(mesh):
    in_specs = (
        P("expert", "section"),
        P("expert", None),
        P("expert", None),
        P("expert", None, "section"),
        P("expert", None, "section"),
    )
    out_specs = P("expert", "section")
    return jax.shard_map(shards, mesh=mesh, in_specs=in_specs, out_specs=out_specs, check_vma=False)
```

time: 515 us -> 417 us (0.81)
  the two profiles are of different devices: /device:TPU:13 before, /device:TPU:0 now
where the time goes in v1:
time: 417 us
  waiting for transfers between devices  330 us (79%)
  Pallas kernels  51.8 us (12%)
  blocking collectives  18.8 us (5%)
  between operations  13.5 us (3%)
    all_gather x1, waiting for transfers between devices, shards(): half = lax.all_gather(wide, 'expert', axis=0, axis_index_groups=across)  127 us
    reduce_scatter x1, waiting for transfers between devices, shards(): lax.psum_scatter(part, 'expert', scatter_dimension=0, axis_index_groups=a...  93.7 us
    all_gather x1, waiting for transfers between devices, shards(): hidden = lax.all_gather(hidden, 'section', axis=0)  55.1 us
    pallas_call x1, Pallas kernels, up_call(): pl.pallas_call(functools.partial(up_kernel, group, capacity), grid=(block...  32.7 us
    all_gather x1, waiting for transfers between devices, shards(): wide = lax.all_gather(tokens, 'section', axis=0)  25.6 us
    pallas_call x1, Pallas kernels, down_call(): pl.pallas_call(functools.partial(down_kernel, group, capacity), grid=(blo...  19.1 us
    all_gather x1, blocking collectives, shards(): lax.all_gather(codes_of(expert_ids, numerators, experts), 'expert', axis=0)  18.8 us
    reduce_scatter x1, waiting for transfers between devices, shards(): lax.psum_scatter(part, 'expert', scatter_dimension=0, axis_index_groups=p...  16.9 us
  transfers between devices with their start and end apart: 6, of which 6 were waited for; matrix products, arithmetic and copies ran while one was open for 0% of the time, Pallas kernels for 0%

profile of v1, /device:TPU:0, one launch (start us, length us, event | category | flops | bytes accessed | tf_op | source)
XLA Modules:
  0.0 416.5 jit_solution(178533229025440229)
XLA Ops:
  6.5 0.0 all-gather.10.cloned.1.call-start
  6.5 0.7 all-gather.10.cloned.1.call-update
  7.3 0.0 all-gather.12.cloned.1.call-start
  7.3 25.6 %all-gather.10.cloned.1.call-done = bf16[256,2048]{1,0:T(8,128)(2,1)} async-done(((bf16[128,2048]{1,0:T(8,128)(2,1)}), bf16[256,2048]{1,0:T(8,128)(2,1)}) %all-gather.10.cloned.1.call-update) | async-done | bytes 1048592 | tf_op jit(solution)/shard_map/all_gather | solution.py:170
  32.9 0.0 all-gather.12.cloned.1.call-update
  33.0 0.0 all-gather.14.cloned.1.call-start
  33.0 127.0 %all-gather.12.cloned.1.call-done = bf16[16,128,2048]{2,1,0:T(8,128)(2,1)} async-done(((bf16[2,128,2048]{2,1,0:T(8,128)(2,1)}), bf16[16,128,2048]{2,1,0:T(8,128)(2,1)}) %all-gather.12.cloned.1.call-update) | async-done | bytes 8388624 | tf_op jit(solution)/shard_map/all_gather | solution.py:171
  160.0 0.0 all-gather.14.cloned.1.call-update
  160.1 0.0 all-gather.16.cloned.1.call-start
  160.1 0.0 copy-done.1
  160.2 0.1 fusion.2
  160.3 18.8 %all-gather = s32[256,128]{1,0:T(8,128)S(1)} all-gather(s32[16,128]{1,0:T(8,128)S(1)} %fusion.2), channel_id=2, replica_groups=mesh['section'=2,'expert'=16] {'expert'}, dimensions={0}, use_global_device_ids=true | all-gather | bytes 139264 | tf_op jit(solution)/shard_map/all_gather | solution.py:166
  179.1 10.8 %all-gather.14.cloned.1.call-done.tokens_ref = bf16[16,2,128,2048]{3,2,1,0:T(8,128)(2,1)} async-done(((bf16[8,2,128,2048]{3,2,1,0:T(8,128)(2,1)}), bf16[16,2,128,2048]{3,2,1,0:T(8,128)(2,1)}) %all-gather.14.cloned.1.call-update) | async-done | bytes 16777232 | tf_op jit(solution)/shard_map/all_gather | solution.py:172
  189.9 32.7 %gate_up.1 = bf16[1280,768]{1,0:T(8,128)(2,1)} custom-call(s32[4,4,128]{2,1,0:T(4,128)S(1)} %bitcast.17, bf16[16,2,128,2048]{3,2,1,0:T(8,128)(2,1)} %all-gather.14.cloned.1.call-done.tokens_ref, bf16[4096,1536]{1,0:T(8,128)(2,1)} %bitcast.29), custom_call_target="tpu_custom_call" | custom-call | flops 18790481920 | bytes 29360128 | tf_op jit(solution)/shard_map/gate_up/pallas_call | solution.py:101
  222.6 0.0 all-gather.16.cloned.1.call-update
  222.6 0.0 reduce-scatter.3.cloned.1.call-start
  222.7 55.1 %all-gather.16.cloned.1.call-done = bf16[2560,768]{1,0:T(8,128)(2,1)} async-done(((bf16[1280,768]{1,0:T(8,128)(2,1)}), bf16[2560,768]{1,0:T(8,128)(2,1)}) %all-gather.16.cloned.1.call-update) | async-done | bytes 3932176 | tf_op jit(solution)/shard_map/all_gather | solution.py:176
  277.7 2.1 copy-done
  279.9 19.1 %down.1 = bf16[2048,2048]{1,0:T(8,128)(2,1)} custom-call(s32[4,4,128]{2,1,0:T(4,128)S(1)} %bitcast.18, bf16[2,1280,768]{2,1,0:T(8,128)(2,1)S(1)} %bitcast.19, bf16[1536,2048]{1,0:T(8,128)(2,1)} %bitcast.30), custom_call_target="tpu_custom_call" | custom-call | flops 9395240960 | bytes 18612224 | tf_op jit(solution)/shard_map/down/pallas_call | solution.py:127
  299.0 0.0 reduce-scatter.3.cloned.1.call-update
  299.0 0.0 reduce-scatter.5.cloned.1.call-start
  299.0 16.9 %reduce-scatter.3.cloned.1.call-done = bf16[1,1024,2048]{2,1,0:T(8,128)(2,1)} async-done(((bf16[2,1024,2048]{2,1,0:T(8,128)(2,1)}), bf16[1,1024,2048]{2,1,0:T(8,128)(2,1)}) %reduce-scatter.3.cloned.1.call-update) | async-done | bytes 4194320 | tf_op jit(solution)/shard_map/reduce_scatter | solution.py:180
  316.0 0.0 reduce-scatter.5.cloned.1.call-update
  316.0 93.7 %reduce-scatter.5.cloned.1.call-done = bf16[128,2048]{1,0:T(8,128)(2,1)} async-done(((bf16[1024,2048]{1,0:T(8,128)(2,1)}), bf16[128,2048]{1,0:T(8,128)(2,1)}) %reduce-scatter.5.cloned.1.call-update) | async-done | bytes 524304 | tf_op jit(solution)/shard_map/reduce_scatter | solution.py:181
  (8 shorter events, 0.1 us)
Async XLA Ops:
  6.5 153.6 %copy-start.1 = (s32[128,8]{0,1:T(8,128)S(1)}, s32[128,8]{0,1:T(8,128)}, u32[]{:S(2)}) copy-start(s32[128,8]{0,1:T(8,128)} %param.6) | copy-start | bytes 12292
  6.5 153.6 %copy-start.2 = (s32[128,8]{0,1:T(8,128)S(1)}, s32[128,8]{0,1:T(8,128)}, u32[]{:S(2)}) copy-start(s32[128,8]{0,1:T(8,128)} %param.7) | copy-start | bytes 12292
  6.5 26.4 %all-gather.10.cloned.1.call-start = ((), (), s32[]{:S(2)}) async-start(), calls=%async_computation.4 | async-start | bytes 1572864 | tf_op jit(solution)/shard_map/all_gather | solution.py:170
  7.3 152.8 %all-gather.12.cloned.1.call-start = ((), (), s32[]{:S(2)}) async-start(), calls=%async_computation.5 | async-start | bytes 9437184 | tf_op jit(solution)/shard_map/all_gather | solution.py:171
  33.0 156.9 %all-gather.14.cloned.1.call-start = ((), (), s32[]{:S(2)}) async-start(), calls=%async_computation.6 | async-start | bytes 25165824 | tf_op jit(solution)/shard_map/all_gather | solution.py:172
  160.1 117.7 %all-gather.16.cloned.1.call-start = ((), (), s32[]{:S(2)}) async-start(), calls=%async_computation.7 | async-start | bytes 5898240 | tf_op jit(solution)/shard_map/all_gather | solution.py:176
  222.6 93.3 %reduce-scatter.3.cloned.1.call-start = ((), (), s32[]{:S(2)}) async-start(), calls=%async_computation.2 | async-start | bytes 12582912 | tf_op jit(solution)/shard_map/reduce_scatter | solution.py:180
  277.7 2.1 copy-start
  299.0 110.7 %reduce-scatter.5.cloned.1.call-start = ((), (), s32[]{:S(2)}) async-start(), calls=%async_computation.3 | async-start | bytes 4718592 | tf_op jit(solution)/shard_map/reduce_scatter | solution.py:181
Sparse Core Ops, SparseCore 0:
  8.9 23.9 all-gather.9
  35.1 124.9 all-gather.11
  161.6 28.2 all-gather.13
  222.7 54.9 all-gather.15
  299.1 16.8 reduce-scatter.2
  319.9 89.7 reduce-scatter.4

commit v2 on v1

--- a/solution.py
+++ b/solution.py
@@ -145,6 +145,113 @@
     )(code.reshape(blocks // take, take, rows), hidden, weight)
 
 
+def pick_kernel(capacity, where_ref, code_ref, *refs):
+    pieces, weight_ref, hidden_ref, rows_ref = refs[:8], refs[8], refs[9], refs[10]
+    rows, width = pieces[0].shape
+
+    @pl.when(pl.program_id(0) == 0)
+    def _():
+        for i, piece in enumerate(pieces):
+            block, section = where_ref[4 + 2 * i], where_ref[5 + 2 * i]
+            code = code_ref[pl.ds(where_ref[block], 1), :]
+            places = lax.broadcasted_iota(jnp.int32, (capacity, rows), 0)
+            onehot = (places == code >> 8).astype(jnp.bfloat16)
+            picked = jnp.dot(onehot, piece[...], preferred_element_type=jnp.float32)
+            down = pl.ds(pl.multiple_of(block * capacity, capacity), capacity)
+            rows_ref[down, pl.ds(pl.multiple_of(section * width, width), width)] = picked.astype(jnp.bfloat16)
+
+    both = jnp.dot(rows_ref[...], weight_ref[...], preferred_element_type=jnp.float32)
+    one, two = both[:, : 2 * UNITS], both[:, 2 * UNITS :]
+    low = lax.broadcasted_iota(jnp.int32, one.shape, 1) < UNITS
+    gate = jnp.where(low, one, pltpu.roll(two, UNITS, 1))
+    up = jnp.where(low, pltpu.roll(one, UNITS, 1), two)
+    hidden_ref[...] = (gate / (1.0 + jnp.exp(-gate)) * up).astype(jnp.bfloat16)
+
+
+def sum_kernel(capacity, where_ref, code_ref, mine_ref, other_ref, weight_ref, keep_ref, send_ref):
+    rows = code_ref.shape[1]
+    units = mine_ref.shape[1]
+    me = where_ref[5]
+    total = jnp.dot(
+        mine_ref[...],
+        weight_ref[pl.ds(pl.multiple_of(me * units, units), units), :],
+        preferred_element_type=jnp.float32,
+    )
+    total += jnp.dot(
+        other_ref[...],
+        weight_ref[pl.ds(pl.multiple_of((1 - me) * units, units), units), :],
+        preferred_element_type=jnp.float32,
+    )
+    result = total.astype(jnp.bfloat16)
+    for b in range(4):
+        code = code_ref[pl.ds(where_ref[b], 1), :]
+        places = lax.broadcasted_iota(jnp.int32, (capacity, rows), 0)
+        scale = (code & 255).astype(jnp.float32) * SCALE
+        scaled = jnp.where(places == code >> 8, scale, 0.0).astype(jnp.bfloat16)
+        mixed = lax.dot_general(
+            scaled,
+            result[b * capacity : (b + 1) * capacity],
+            (((0,), (0,)), ((), ())),
+            preferred_element_type=jnp.float32,
+        )
+        out_ref = keep_ref if b < 2 else send_ref
+        out_ref[b % 2] = mixed.astype(jnp.bfloat16)
+
+
+def pick_call(where, code, pieces, weight, capacity):
+    rows, width = pieces[0].shape
+    depth, columns = weight.shape
+    tall = 4 * capacity
+    pair = 4 * UNITS
+    return pl.pallas_call(
+        functools.partial(pick_kernel, capacity),
+        grid=(columns // pair,),
+        in_specs=[
+            pl.BlockSpec(memory_space=pltpu.SMEM),
+            pl.BlockSpec(code.shape, lambda i: (0, 0)),
+            *[pl.BlockSpec((rows, width), lambda i: (0, 0), pipeline_mode=pl.Buffered(1)) for _ in pieces],
+            pl.BlockSpec((depth, pair), lambda i: (0, i)),
+        ],
+        out_specs=pl.BlockSpec((tall, pair // 2), lambda i: (0, i)),
+        out_shape=jax.ShapeDtypeStruct((tall, columns // 2), jnp.bfloat16),
+        scratch_shapes=[pltpu.VMEM((tall, depth), jnp.bfloat16)],
+        compiler_params=pltpu.CompilerParams(vmem_limit_bytes=28 * 1024 * 1024),
+        cost_estimate=pl.CostEstimate(
+            flops=2 * tall * depth * (columns + rows),
+            bytes_accessed=2 * (8 * rows * width + weight.size + tall * columns // 2),
+            transcendentals=tall * columns // 2,
+        ),
+        name="gate_up",
+    )(where, code, *pieces, weight)
+
+
+def sum_call(where, code, mine, other, weight, capacity):
+    rows = code.shape[1]
+    depth, wide = weight.shape
+    tall, units = mine.shape
+    step = 512
+    return pl.pallas_call(
+        functools.partial(sum_kernel, capacity),
+        grid=(wide // step,),
+        in_specs=[
+            pl.BlockSpec(memory_space=pltpu.SMEM),
+            pl.BlockSpec(code.shape, lambda i: (0, 0)),
+            pl.BlockSpec((tall, units), lambda i: (0, 0), pipeline_mode=pl.Buffered(1)),
+            pl.BlockSpec((tall, units), lambda i: (0, 0), pipeline_mode=pl.Buffered(1)),
+            pl.BlockSpec((depth, step), lambda i: (0, i)),
+        ],
+        out_specs=[pl.BlockSpec((2, rows, step), lambda i: (0, 0, i))] * 2,
+        out_shape=[jax.ShapeDtypeStruct((2, rows, wide), jnp.bfloat16)] * 2,
+        compiler_params=pltpu.CompilerParams(vmem_limit_bytes=28 * 1024 * 1024),
+        cost_estimate=pl.CostEstimate(
+            flops=2 * wide * (tall * depth + 4 * rows * capacity),
+            bytes_accessed=2 * (2 * mine.size + weight.size + 4 * rows * wide),
+            transcendentals=0,
+        ),
+        name="down",
+    )(where, code, mine, other, weight)
+
+
 def codes_of(expert_ids, numerators, experts):
     rows = expert_ids.shape[0]
     named = expert_ids.T[None] == jnp.arange(experts, dtype=jnp.int32)[:, None, None]
@@ -179,6 +286,80 @@
     part = part.reshape(2, chips * rows, width)
     part = lax.psum_scatter(part, "expert", scatter_dimension=0, axis_index_groups=pairs, tiled=False)
     return lax.psum_scatter(part, "expert", scatter_dimension=0, axis_index_groups=across, tiled=True)
+
+
+def pair_shards(tokens, expert_ids, numerators, gate_up_weight, down_weight):
+    rows, width = tokens.shape
+    experts = lax.axis_size("expert")
+    layers = experts // 4
+    capacity = rows * expert_ids.shape[1] * 5 // (4 * experts)
+    axes = ("section", "expert")
+    ring = [0, *range(1, layers, 2), *reversed(range(2, layers, 2))]
+    following = {z: ring[(p + 1) % layers] for p, z in enumerate(ring)}
+
+    def perm(place):
+        moves = []
+        for x in range(2):
+            for z in range(layers):
+                for y in range(2):
+                    for c in range(2):
+                        tx, tz, ty, tc = place(x, z, y, c)
+                        moves.append(((x * layers + z) * 4 + y * 2 + c, (tx * layers + tz) * 4 + ty * 2 + tc))
+        return moves
+
+    onward = perm(lambda x, z, y, c: (x, following[z], y, c))
+    first = perm(lambda x, z, y, c: (x ^ (1 - c), z, y ^ c, c))
+    second = perm(lambda x, z, y, c: (x ^ c, z, y ^ (1 - c), c))
+    sibling = perm(lambda x, z, y, c: (x, z, y, 1 - c))
+    over_x = perm(lambda x, z, y, c: (1 - x, z, y, c))
+    over_y = perm(lambda x, z, y, c: (x, z, 1 - y, c))
+
+    def move(value, moves):
+        return lax.ppermute(value, axes, moves)
+
+    x, e = lax.axis_index("section"), lax.axis_index("expert")
+    z, y, c = e // 4, e // 2 % 2, e % 2
+    places = jnp.array([ring.index(i) for i in range(layers)], jnp.int32)
+    code = lax.all_to_all(codes_of(expert_ids, numerators, experts), "expert", split_axis=0, concat_axis=0, tiled=True)
+
+    def where(k):
+        at = jnp.array(ring, jnp.int32)[(places[z] - k) % layers] * 4
+        blocks = [at + (y ^ (i & 1)) * 2 + (c ^ (i >> 1)) for i in range(4)]
+        spots = []
+        for own in (0, 1):
+            core = c ^ own
+            base = 2 * own
+            spots += [base, x]
+            spots += [base + core, x ^ (1 - core)]
+            spots += [base + 1 - core, x ^ core]
+            spots += [base + 1, 1 - x]
+        return jnp.stack([jnp.asarray(v, jnp.int32) for v in blocks + spots])
+
+    wheres = [where(k) for k in range(layers)]
+    shard, kept = tokens, []
+    for k in range(layers):
+        later = move(shard, onward) if k < layers - 1 else None
+        a = move(shard, first)
+        b = move(shard, second)
+        d = move(a, second)
+        pieces = [shard, a, b, d]
+        pieces += [move(v, sibling) for v in pieces]
+        mine = pick_call(wheres[k], code, pieces, gate_up_weight[0], capacity)
+        other = move(mine, over_x)
+        keep, send = sum_call(wheres[k], code, mine, other, down_weight[0], capacity)
+        got = move(send, sibling)
+        away = (keep[1].astype(jnp.float32) + got[1].astype(jnp.float32)).astype(jnp.bfloat16)
+        back = move(away, over_y)
+        kept.append((keep[0], got[0], back))
+        shard = later
+
+    total = None
+    for k in [*range(1, layers), 0]:
+        terms = [v.astype(jnp.float32) for v in kept[k]]
+        if total is not None:
+            terms.append(move(total, onward).astype(jnp.float32))
+        total = functools.reduce(jnp.add, terms).astype(jnp.bfloat16)
+    return total
 
 
 def solution(mesh):
@@ -190,4 +371,5 @@
         P("expert", None, "section"),
     )
     out_specs = P("expert", "section")
-    return jax.shard_map(shards, mesh=mesh, in_specs=in_specs, out_specs=out_specs, check_vma=False)
+    fits = mesh.shape["section"] == 2 and mesh.shape["expert"] % 4 == 0
+    return jax.shard_map(pair_shards if fits else shards, mesh=mesh, in_specs=in_specs, out_specs=out_specs, check_vma=False)

time: 417 us -> 240 us (0.58)
  waiting for transfers between devices: 330 us -> 71.5 us
  starting transfers between devices: 0.2 us -> 61.9 us
  local copies, waits for them, and re-layouts: 2.13 us -> 37.2 us
  blocking collectives: 18.8 us -> 0 us
  between operations: 13.5 us -> 6.57 us
  other arithmetic: 0.06 us -> 6.05 us
    all_gather x4 -> x0, waiting for transfers between devices: 218 us -> none  [the longest x1 127 us: shards(): half = lax.all_gather(wide, 'expert', axis=0, axis_index_groups=across)]
    reduce_scatter x2 -> x0, waiting for transfers between devices: 111 us -> none  [the longest x1 93.7 us: shards(): lax.psum_scatter(part, 'expert', scatter_dimension=0, axis_index_groups=a...]
    ppermute x0 -> x46, waiting for transfers between devices: none -> 71.5 us  [move(): return lax.ppermute(value, axes, moves)]
    ppermute x0 -> x46, starting transfers between devices: none -> 56.2 us  [move(): return lax.ppermute(value, axes, moves)]
    unnamed x6 -> x64, local copies, waits for them, and re-layouts: 2.12 us -> 34.1 us
    all_gather x1 -> x0, blocking collectives: 18.8 us -> none  [shards(): lax.all_gather(codes_of(expert_ids, numerators, experts), 'expert', axis=0)]
    all_to_all x0 -> x1, starting transfers between devices: none -> 5.75 us  [pair_shards(): lax.all_to_all(codes_of(expert_ids, numerators, experts), 'expert', split...]
    convert_element_type x0 -> x8, other arithmetic: none -> 4.61 us  [the longest x4 3.07 us: pair_shards(): total = functools.reduce(jnp.add, terms).astype(jnp.bfloat16)]
  transfers between devices with their start and end apart: 6 -> 47, of which waited for: 6 -> 13; matrix products, arithmetic and copies ran while one was open for 0% -> 4% of each run, Pallas kernels for 0% -> 23%
where the time goes in v2:
time: 240 us; the launch traced here: 239 us
  waiting for transfers between devices  71.5 us (30%)
  starting transfers between devices  61.9 us (26%)
  Pallas kernels  54.8 us (23%)
  local copies, waits for them, and re-layouts  37.2 us (16%)
  between operations  6.57 us (3%)
  other arithmetic  6.05 us (3%)
    ppermute x46, waiting for transfers between devices, move(): return lax.ppermute(value, axes, moves)  71.5 us
    ppermute x46, starting transfers between devices, move(): return lax.ppermute(value, axes, moves)  56.2 us
    pallas_call x4, Pallas kernels, pick_call(): pl.pallas_call(functools.partial(pick_kernel, capacity), grid=(columns //...  35 us
    unnamed x64, local copies, waits for them, and re-layouts  34.1 us
    pallas_call x4, Pallas kernels, sum_call(): pl.pallas_call(functools.partial(sum_kernel, capacity), grid=(wide // ste...  19.9 us
    all_to_all x1, starting transfers between devices, pair_shards(): lax.all_to_all(codes_of(expert_ids, numerators, experts), 'expert', split...  5.75 us
  transfers between devices with their start and end apart: 47, of which 13 were waited for; matrix products, arithmetic and copies ran while one was open for 4% of the time, Pallas kernels for 23%

profile of v2, /device:TPU:0, one launch (start us, length us, event | category | flops | bytes accessed | tf_op | source)
XLA Modules:
  0.0 238.8 jit_solution(5467202236429268791)
XLA Ops:
  3.0 13.1 %collective-permute-done.10.refs_0_ = bf16[128,2048]{1,0:T(8,128)(2,1)S(1)} collective-permute-done((bf16[128,2048]{1,0:T(8,128)(2,1)}, bf16[128,2048]{1,0:T(8,128)(2,1)S(1)}, u32[]{:S(2)}, u32[]{:S(2)}) %collective-permute-start.10) | collective-permute-done | bytes 524320 | tf_op jit(solution)/shard_map/ppermute | solution.py:318
  21.5 9.4 %collective-permute-done.33.refs_1_ = bf16[128,2048]{1,0:T(8,128)(2,1)S(1)} collective-permute-done((bf16[128,2048]{1,0:T(8,128)(2,1)S(1)}, bf16[128,2048]{1,0:T(8,128)(2,1)S(1)}, u32[]{:S(2)}, u32[]{:S(2)}) %collective-permute-start.33) | collective-permute-done | bytes 524320 | tf_op jit(solution)/shard_map/ppermute | solution.py:318
  32.5 9.6 %collective-permute-done.refs_1_ = bf16[128,2048]{1,0:T(8,128)(2,1)S(1)} collective-permute-done((bf16[128,2048]{1,0:T(8,128)(2,1)}, bf16[128,2048]{1,0:T(8,128)(2,1)S(1)}, u32[]{:S(2)}, u32[]{:S(2)}) %collective-permute-start) | collective-permute-done | bytes 524320 | tf_op jit(solution)/shard_map/ppermute | solution.py:318
  49.3 5.5 %collective-permute-done.23.refs_1_ = bf16[128,2048]{1,0:T(8,128)(2,1)S(1)} collective-permute-done((bf16[128,2048]{1,0:T(8,128)(2,1)S(1)}, bf16[128,2048]{1,0:T(8,128)(2,1)S(1)}, u32[]{:S(2)}, u32[]{:S(2)}) %collective-permute-start.23) | collective-permute-done | bytes 524320 | tf_op jit(solution)/shard_map/ppermute | solution.py:318
  64.9 5.8 %all-to-all-start = ((s32[16,1,128]{2,1,0:T(1,128)}), s32[16,1,128]{2,1,0:T(1,128)S(1)}, u32[]{:S(2)}, u32[]{:S(2)}) async-start(s32[16,1,128]{2,1,0:T(1,128)} %bitcast.19), calls=%async_computation | async-start | bytes 16384 | tf_op jit(solution)/shard_map/all_to_all | solution.py:323
  77.7 4.6 %copy-done = bf16[1,4096,1536]{2,1,0:T(8,128)(2,1)S(1)} copy-done((bf16[1,4096,1536]{2,1,0:T(8,128)(2,1)S(1)}, bf16[1,4096,1536]{2,1,0:T(8,128)(2,1)}, u32[]{:S(2)}) %copy-start) | copy-done | bytes 12582936
  90.6 8.5 %gate_up.7.mine_ref = bf16[320,768]{1,0:T(8,128)(2,1)} custom-call(s32[20]{0:T(128)S(1)} %stack.157.where_ref, s32[16,128]{1,0:T(8,128)S(1)} %bitcast.74, bf16[128,2048]{1,0:T(8,128)(2,1)S(1)} %copy-done.5, bf16[128,2048]{1,0:T(8,128)(2,1)S(1)} %copy-done.7, bf16[128,2048]{1,0:T(8,128)(2,1)S(1)} %copy-done.9, bf16[128,2048]{1,0:T(8,128)(2,1)S(1)} %copy-done.13, ...), custom_call_target="tpu_custom_call" | custom-call | flops 4362076160 | bytes 17268736 | tf_op jit(solution)/shard_map/gate_up/pallas_call | solution.py:206
  106.4 4.6 %copy-done.1 = bf16[1,4096,1536]{2,1,0:T(8,128)(2,1)S(1)} copy-done((bf16[1,4096,1536]{2,1,0:T(8,128)(2,1)S(1)}, bf16[1,4096,1536]{2,1,0:T(8,128)(2,1)}, u32[]{:S(2)}) %copy-start.1) | copy-done | bytes 12582936
  111.0 9.4 %gate_up.6.mine_ref = bf16[320,768]{1,0:T(8,128)(2,1)S(1)} custom-call(s32[20]{0:T(128)S(1)} %stack.152.where_ref, s32[16,128]{1,0:T(8,128)S(1)} %bitcast.75, bf16[128,2048]{1,0:T(8,128)(2,1)S(1)} %collective-permute-done.11.refs_0_, bf16[128,2048]{1,0:T(8,128)(2,1)S(1)} %collective-permute-done.23.refs_1_, ...), custom_call_target="tpu_custom_call" | custom-call | flops 4362076160 | bytes 17268736 | tf_op jit(solution)/shard_map/gate_up/pallas_call | solution.py:206
  120.5 6.0 %down.7 = (bf16[2,128,2048]{2,1,0:T(8,128)(2,1)S(1)}, bf16[2,128,2048]{2,1,0:T(8,128)(2,1)}) custom-call(s32[20]{0:T(128)S(1)} %stack.157.where_ref, s32[16,128]{1,0:T(8,128)S(1)} %bitcast.76, bf16[320,768]{1,0:T(8,128)(2,1)} %gate_up.7.mine_ref, bf16[320,768]{1,0:T(8,128)(2,1)} %collective-permute-done.40.other_ref, bf16[1536,2048]{1,0:T(8,128)(2,1)S(1)} %bitcast.82), custom_call_target="tpu_custom_call" | custom-call | flops 2181038080 | bytes 9371648 | tf_op jit(solution)/shard_map/down/pallas_call | solution.py:233
  127.0 8.5 %collective-permute-start.17 = (bf16[128,2048]{1,0:T(8,128)(2,1)S(1)}, bf16[128,2048]{1,0:T(8,128)(2,1)}, u32[]{:S(2)}, u32[]{:S(2)}) collective-permute-start(bf16[128,2048]{1,0:T(8,128)(2,1)S(1)} %collective-permute-done.13.refs_1_), channel_id=1, source_target_pairs={{0,1},{1,0},{2,3},{3,2},{4,5},{5,4},{6,7},{7,6},{8,9},{9,8},{10,11... | collective-permute-start | bytes 1572872 | tf_op jit(solution)/shard_map/ppermute | solution.py:318
  135.5 5.6 %collective-permute-start.18 = (bf16[128,2048]{1,0:T(8,128)(2,1)}, bf16[128,2048]{1,0:T(8,128)(2,1)}, u32[]{:S(2)}, u32[]{:S(2)}) collective-permute-start(bf16[128,2048]{1,0:T(8,128)(2,1)} %collective-permute-done.14.refs_2_), channel_id=1, source_target_pairs={{0,1},{1,0},{2,3},{3,2},{4,5},{5,4},{6,7},{7,6},{8,9},{9,8},{10,11... | collective-permute-start | bytes 1572872 | tf_op jit(solution)/shard_map/ppermute | solution.py:318
  141.9 5.1 %collective-permute-start.19 = (bf16[128,2048]{1,0:T(8,128)(2,1)}, bf16[128,2048]{1,0:T(8,128)(2,1)}, u32[]{:S(2)}, u32[]{:S(2)}) collective-permute-start(bf16[128,2048]{1,0:T(8,128)(2,1)} %collective-permute-done.15.refs_3_), channel_id=1, source_target_pairs={{0,1},{1,0},{2,3},{3,2},{4,5},{5,4},{6,7},{7,6},{8,9},{9,8},{10,11... | collective-permute-start | bytes 1572872 | tf_op jit(solution)/shard_map/ppermute | solution.py:318
  153.5 4.6 %down.6 = (bf16[2,128,2048]{2,1,0:T(8,128)(2,1)S(1)}, bf16[2,128,2048]{2,1,0:T(8,128)(2,1)S(1)}) custom-call(s32[20]{0:T(128)S(1)} %stack.152.where_ref, s32[16,128]{1,0:T(8,128)S(1)} %bitcast.77, bf16[320,768]{1,0:T(8,128)(2,1)S(1)} %copy-done.25, bf16[320,768]{1,0:T(8,128)(2,1)S(1)} %copy-done.29, bf16[1536,2048]{1,0:T(8,128)(2,1)S(1)} %bitcast.83), custom_call_target="tpu_custom_call" | custom-call | flops 2181038080 | bytes 9371648 | tf_op jit(solution)/shard_map/down/pallas_call | solution.py:233
  159.2 4.6 %copy-done.2 = bf16[1,4096,1536]{2,1,0:T(8,128)(2,1)S(1)} copy-done((bf16[1,4096,1536]{2,1,0:T(8,128)(2,1)S(1)}, bf16[1,4096,1536]{2,1,0:T(8,128)(2,1)}, u32[]{:S(2)}) %copy-start.2) | copy-done | bytes 12582936
  163.8 9.2 %gate_up.5.mine_ref = bf16[320,768]{1,0:T(8,128)(2,1)S(1)} custom-call(s32[20]{0:T(128)S(1)} %stack.147.where_ref, s32[16,128]{1,0:T(8,128)S(1)} %bitcast.78, bf16[128,2048]{1,0:T(8,128)(2,1)S(1)} %collective-permute-done.12.refs_0_, bf16[128,2048]{1,0:T(8,128)(2,1)S(1)} %collective-permute-done.13.refs_1_, ...), custom_call_target="tpu_custom_call" | custom-call | flops 4362076160 | bytes 17268736 | tf_op jit(solution)/shard_map/gate_up/pallas_call | solution.py:206
  177.9 7.9 %gate_up.4.mine_ref = bf16[320,768]{1,0:T(8,128)(2,1)S(1)} custom-call(s32[20]{0:T(128)S(1)} %stack.142.where_ref, s32[16,128]{1,0:T(8,128)S(1)} %bitcast.79, bf16[128,2048]{1,0:T(8,128)(2,1)S(1)} %copy-done.3, bf16[128,2048]{1,0:T(8,128)(2,1)S(1)} %collective-permute-done.refs_1_, bf16[128,2048]{1,0:T(8,128)(2,1)S(1)} %copy-done.21, ...), custom_call_target="tpu_custom_call" | custom-call | flops 4362076160 | bytes 17268736 | tf_op jit(solution)/shard_map/gate_up/pallas_call | solution.py:206
  186.4 4.6 %down.5 = (bf16[2,128,2048]{2,1,0:T(8,128)(2,1)S(1)}, bf16[2,128,2048]{2,1,0:T(8,128)(2,1)S(1)}) custom-call(s32[20]{0:T(128)S(1)} %stack.147.where_ref, s32[16,128]{1,0:T(8,128)S(1)} %bitcast.80, bf16[320,768]{1,0:T(8,128)(2,1)S(1)} %gate_up.5.mine_ref, bf16[320,768]{1,0:T(8,128)(2,1)S(1)} %collective-permute-done.20.other_ref, bf16[1536,2048]{1,0:T(8,128)(2,1)S(1)} %bitcast.86), custom_call_target="tpu_custom_call" | custom-call | flops 2181038080 | bytes 9371648 | tf_op jit(solution)/shard_map/down/pallas_call | solution.py:233
  195.9 3.2 %collective-permute-done.7.other_ref = bf16[320,768]{1,0:T(8,128)(2,1)S(1)} collective-permute-done((bf16[320,768]{1,0:T(8,128)(2,1)S(1)}, bf16[320,768]{1,0:T(8,128)(2,1)S(1)}, u32[]{:S(2)}, u32[]{:S(2)}) %collective-permute-start.7) | collective-permute-done | bytes 491552 | tf_op jit(solution)/shard_map/ppermute | solution.py:318
  199.1 4.6 %down.4 = (bf16[2,128,2048]{2,1,0:T(8,128)(2,1)S(1)}, bf16[2,128,2048]{2,1,0:T(8,128)(2,1)S(1)}) custom-call(s32[20]{0:T(128)S(1)} %stack.142.where_ref, s32[16,128]{1,0:T(8,128)S(1)} %bitcast.81, bf16[320,768]{1,0:T(8,128)(2,1)S(1)} %gate_up.4.mine_ref, bf16[320,768]{1,0:T(8,128)(2,1)S(1)} %collective-permute-done.7.other_ref, bf16[1536,2048]{1,0:T(8,128)(2,1)S(1)} %bitcast.87), custom_call_target="tpu_custom_call" | custom-call | flops 2181038080 | bytes 9371648 | tf_op jit(solution)/shard_map/down/pallas_call | solution.py:233
  203.8 4.0 %collective-permute-done.43 = bf16[128,2048]{1,0:T(8,128)(2,1)S(1)} collective-permute-done((bf16[128,2048]{1,0:T(8,128)(2,1)S(1)}, bf16[128,2048]{1,0:T(8,128)(2,1)S(1)}, u32[]{:S(2)}, u32[]{:S(2)}) %collective-permute-start.43) | collective-permute-done | bytes 524320 | tf_op jit(solution)/shard_map/ppermute | solution.py:318
  213.7 9.3 %collective-permute-done.44 = bf16[128,2048]{1,0:T(8,128)(2,1)S(1)} collective-permute-done((bf16[128,2048]{1,0:T(8,128)(2,1)S(1)}, bf16[128,2048]{1,0:T(8,128)(2,1)S(1)}, u32[]{:S(2)}, u32[]{:S(2)}) %collective-permute-start.44) | collective-permute-done | bytes 524320 | tf_op jit(solution)/shard_map/ppermute | solution.py:318
  223.0 3.3 %collective-permute-done.22 = bf16[128,2048]{1,0:T(8,128)(2,1)S(1)} collective-permute-done((bf16[128,2048]{1,0:T(8,128)(2,1)S(1)}, bf16[128,2048]{1,0:T(8,128)(2,1)S(1)}, u32[]{:S(2)}, u32[]{:S(2)}) %collective-permute-start.22) | collective-permute-done | bytes 524320 | tf_op jit(solution)/shard_map/ppermute | solution.py:318
  227.7 7.9 %collective-permute-done.9 = bf16[128,2048]{1,0:T(8,128)(2,1)S(1)} collective-permute-done((bf16[128,2048]{1,0:T(8,128)(2,1)S(1)}, bf16[128,2048]{1,0:T(8,128)(2,1)S(1)}, u32[]{:S(2)}, u32[]{:S(2)}) %collective-permute-start.9) | collective-permute-done | bytes 524320 | tf_op jit(solution)/shard_map/ppermute | solution.py:318
  (160 shorter events, 73.2 us)
Async XLA Ops:
  17.7 24.4 %collective-permute-start = (bf16[128,2048]{1,0:T(8,128)(2,1)}, bf16[128,2048]{1,0:T(8,128)(2,1)S(1)}, u32[]{:S(2)}, u32[]{:S(2)}) collective-permute-start(bf16[128,2048]{1,0:T(8,128)(2,1)} %refs_0_.1), channel_id=1, source_target_pairs={{0,16},{1,3},{2,18},{3,1},{4,20},{5,7},{6,22},{7,5},{8,24},{9,11},... | collective-permute-start | bytes 1572872 | tf_op jit(solution)/shard_map/ppermute | solution.py:318
  18.2 24.7 %collective-permute-start.11 = (bf16[128,2048]{1,0:T(8,128)(2,1)S(1)}, bf16[128,2048]{1,0:T(8,128)(2,1)S(1)}, u32[]{:S(2)}, u32[]{:S(2)}) collective-permute-start(bf16[128,2048]{1,0:T(8,128)(2,1)S(1)} %collective-permute-done.10.refs_0_), channel_id=1, source_target_pairs={{0,4},{1,5},{2,6},{3,7},{4,12},{5,13},{6,14},{7,15},{8,0},{9,1},{1... | collective-permute-start | bytes 1572872 | tf_op jit(solution)/shard_map/ppermute | solution.py:318
  19.1 25.3 %collective-permute-start.34 = (bf16[128,2048]{1,0:T(8,128)(2,1)S(1)}, bf16[128,2048]{1,0:T(8,128)(2,1)S(1)}, u32[]{:S(2)}, u32[]{:S(2)}) collective-permute-start(bf16[128,2048]{1,0:T(8,128)(2,1)S(1)} %collective-permute-done.10.refs_0_), channel_id=1, source_target_pairs={{0,2},{1,17},{2,0},{3,19},{4,6},{5,21},{6,4},{7,23},{8,10},{9,25},... | collective-permute-start | bytes 1572872 | tf_op jit(solution)/shard_map/ppermute | solution.py:318
  20.7 24.9 %collective-permute-start.36 = (bf16[128,2048]{1,0:T(8,128)(2,1)S(1)}, bf16[128,2048]{1,0:T(8,128)(2,1)S(1)}, u32[]{:S(2)}, u32[]{:S(2)}) collective-permute-start(bf16[128,2048]{1,0:T(8,128)(2,1)S(1)} %collective-permute-done.10.refs_0_), channel_id=1, source_target_pairs={{0,1},{1,0},{2,3},{3,2},{4,5},{5,4},{6,7},{7,6},{8,9},{9,8},{10,11... | collective-permute-start | bytes 1572872 | tf_op jit(solution)/shard_map/ppermute | solution.py:318
  58.8 40.3 %collective-permute-start.26 = (bf16[128,2048]{1,0:T(8,128)(2,1)S(1)}, bf16[128,2048]{1,0:T(8,128)(2,1)}, u32[]{:S(2)}, u32[]{:S(2)}) collective-permute-start(bf16[128,2048]{1,0:T(8,128)(2,1)S(1)} %collective-permute-done.11.refs_0_), channel_id=1, source_target_pairs={{0,1},{1,0},{2,3},{3,2},{4,5},{5,4},{6,7},{7,6},{8,9},{9,8},{10,11... | collective-permute-start | bytes 1572872 | tf_op jit(solution)/shard_map/ppermute | solution.py:318
  58.8 43.5 %collective-permute-start.27 = (bf16[128,2048]{1,0:T(8,128)(2,1)S(1)}, bf16[128,2048]{1,0:T(8,128)(2,1)}, u32[]{:S(2)}, u32[]{:S(2)}) collective-permute-start(bf16[128,2048]{1,0:T(8,128)(2,1)S(1)} %collective-permute-done.23.refs_1_), channel_id=1, source_target_pairs={{0,1},{1,0},{2,3},{3,2},{4,5},{5,4},{6,7},{7,6},{8,9},{9,8},{10,11... | collective-permute-start | bytes 1572872 | tf_op jit(solution)/shard_map/ppermute | solution.py:318
  62.3 41.9 %collective-permute-start.28 = (bf16[128,2048]{1,0:T(8,128)(2,1)}, bf16[128,2048]{1,0:T(8,128)(2,1)}, u32[]{:S(2)}, u32[]{:S(2)}) collective-permute-start(bf16[128,2048]{1,0:T(8,128)(2,1)} %collective-permute-done.24.refs_2_), channel_id=1, source_target_pairs={{0,1},{1,0},{2,3},{3,2},{4,5},{5,4},{6,7},{7,6},{8,9},{9,8},{10,11... | collective-permute-start | bytes 1572872 | tf_op jit(solution)/shard_map/ppermute | solution.py:318
  63.1 41.3 %collective-permute-start.13 = (bf16[128,2048]{1,0:T(8,128)(2,1)S(1)}, bf16[128,2048]{1,0:T(8,128)(2,1)S(1)}, u32[]{:S(2)}, u32[]{:S(2)}) collective-permute-start(bf16[128,2048]{1,0:T(8,128)(2,1)S(1)} %collective-permute-done.12.refs_0_), channel_id=1, source_target_pairs={{0,16},{1,3},{2,18},{3,1},{4,20},{5,7},{6,22},{7,5},{8,24},{9,11},... | collective-permute-start | bytes 1572872 | tf_op jit(solution)/shard_map/ppermute | solution.py:318
  64.1 42.2 %collective-permute-start.29 = (bf16[128,2048]{1,0:T(8,128)(2,1)}, bf16[128,2048]{1,0:T(8,128)(2,1)}, u32[]{:S(2)}, u32[]{:S(2)}) collective-permute-start(bf16[128,2048]{1,0:T(8,128)(2,1)} %collective-permute-done.25.refs_3_), channel_id=1, source_target_pairs={{0,1},{1,0},{2,3},{3,2},{4,5},{5,4},{6,7},{7,6},{8,9},{9,8},{10,11... | collective-permute-start | bytes 1572872 | tf_op jit(solution)/shard_map/ppermute | solution.py:318
  99.1 21.3 %collective-permute-start.40 = (bf16[320,768]{1,0:T(8,128)(2,1)}, bf16[320,768]{1,0:T(8,128)(2,1)}, u32[]{:S(2)}, u32[]{:S(2)}) collective-permute-start(bf16[320,768]{1,0:T(8,128)(2,1)} %gate_up.7.mine_ref), channel_id=1, source_target_pairs={{0,16},{1,17},{2,18},{3,19},{4,20},{5,21},{6,22},{7,23},{8,24},{9,... | collective-permute-start | bytes 1474568 | tf_op jit(solution)/shard_map/ppermute | solution.py:318
  102.3 24.2 %collective-permute-start.1 = (bf16[128,2048]{1,0:T(8,128)(2,1)S(1)}, bf16[128,2048]{1,0:T(8,128)(2,1)S(1)}, u32[]{:S(2)}, u32[]{:S(2)}) collective-permute-start(bf16[128,2048]{1,0:T(8,128)(2,1)S(1)} %copy-done.3), channel_id=1, source_target_pairs={{0,2},{1,17},{2,0},{3,19},{4,6},{5,21},{6,4},{7,23},{8,10},{9,25},... | collective-permute-start | bytes 1572872 | tf_op jit(solution)/shard_map/ppermute | solution.py:318
  104.3 22.2 %collective-permute-start.2 = (bf16[128,2048]{1,0:T(8,128)(2,1)S(1)}, bf16[128,2048]{1,0:T(8,128)(2,1)S(1)}, u32[]{:S(2)}, u32[]{:S(2)}) collective-permute-start(bf16[128,2048]{1,0:T(8,128)(2,1)S(1)} %collective-permute-done.refs_1_), channel_id=1, source_target_pairs={{0,2},{1,17},{2,0},{3,19},{4,6},{5,21},{6,4},{7,23},{8,10},{9,25},... | collective-permute-start | bytes 1572872 | tf_op jit(solution)/shard_map/ppermute | solution.py:318
  104.4 22.6 %collective-permute-start.14 = (bf16[128,2048]{1,0:T(8,128)(2,1)S(1)}, bf16[128,2048]{1,0:T(8,128)(2,1)}, u32[]{:S(2)}, u32[]{:S(2)}) collective-permute-start(bf16[128,2048]{1,0:T(8,128)(2,1)S(1)} %collective-permute-done.12.refs_0_), channel_id=1, source_target_pairs={{0,2},{1,17},{2,0},{3,19},{4,6},{5,21},{6,4},{7,23},{8,10},{9,25},... | collective-permute-start | bytes 1572872 | tf_op jit(solution)/shard_map/ppermute | solution.py:318
  106.3 29.2 %collective-permute-start.15 = (bf16[128,2048]{1,0:T(8,128)(2,1)S(1)}, bf16[128,2048]{1,0:T(8,128)(2,1)}, u32[]{:S(2)}, u32[]{:S(2)}) collective-permute-start(bf16[128,2048]{1,0:T(8,128)(2,1)S(1)} %collective-permute-done.13.refs_1_), channel_id=1, source_target_pairs={{0,2},{1,17},{2,0},{3,19},{4,6},{5,21},{6,4},{7,23},{8,10},{9,25},... | collective-permute-start | bytes 1572872 | tf_op jit(solution)/shard_map/ppermute | solution.py:318
  120.4 20.7 %collective-permute-start.30 = (bf16[320,768]{1,0:T(8,128)(2,1)S(1)}, bf16[320,768]{1,0:T(8,128)(2,1)S(1)}, u32[]{:S(2)}, u32[]{:S(2)}) collective-permute-start(bf16[320,768]{1,0:T(8,128)(2,1)S(1)} %gate_up.6.mine_ref), channel_id=1, source_target_pairs={{0,16},{1,17},{2,18},{3,19},{4,20},{5,21},{6,22},{7,23},{8,24},{9,... | collective-permute-start | bytes 1474568 | tf_op jit(solution)/shard_map/ppermute | solution.py:318
  126.5 46.6 %collective-permute-start.41 = (bf16[2,128,2048]{2,1,0:T(8,128)(2,1)}, bf16[2,128,2048]{2,1,0:T(8,128)(2,1)}, u32[]{:S(2)}, u32[]{:S(2)}) collective-permute-start(bf16[2,128,2048]{2,1,0:T(8,128)(2,1)} %get-tuple-element.20), channel_id=1, source_target_pairs={{0,1},{1,0},{2,3},{3,2},{4,5},{5,4},{6,7},{7,6},{8,9},{9,8},{10,11... | collective-permute-start | bytes 3145736 | tf_op jit(solution)/shard_map/ppermute | solution.py:318
  126.5 31.6 %collective-permute-start.16 = (bf16[128,2048]{1,0:T(8,128)(2,1)S(1)}, bf16[128,2048]{1,0:T(8,128)(2,1)}, u32[]{:S(2)}, u32[]{:S(2)}) collective-permute-start(bf16[128,2048]{1,0:T(8,128)(2,1)S(1)} %collective-permute-done.12.refs_0_), channel_id=1, source_target_pairs={{0,1},{1,0},{2,3},{3,2},{4,5},{5,4},{6,7},{7,6},{8,9},{9,8},{10,11... | collective-permute-start | bytes 1572872 | tf_op jit(solution)/shard_map/ppermute | solution.py:318
  127.0 31.2 %collective-permute-start.17 = (bf16[128,2048]{1,0:T(8,128)(2,1)S(1)}, bf16[128,2048]{1,0:T(8,128)(2,1)}, u32[]{:S(2)}, u32[]{:S(2)}) collective-permute-start(bf16[128,2048]{1,0:T(8,128)(2,1)S(1)} %collective-permute-done.13.refs_1_), channel_id=1, source_target_pairs={{0,1},{1,0},{2,3},{3,2},{4,5},{5,4},{6,7},{7,6},{8,9},{9,8},{10,11... | collective-permute-start | bytes 1572872 | tf_op jit(solution)/shard_map/ppermute | solution.py:318
  135.5 23.2 %collective-permute-start.18 = (bf16[128,2048]{1,0:T(8,128)(2,1)}, bf16[128,2048]{1,0:T(8,128)(2,1)}, u32[]{:S(2)}, u32[]{:S(2)}) collective-permute-start(bf16[128,2048]{1,0:T(8,128)(2,1)} %collective-permute-done.14.refs_2_), channel_id=1, source_target_pairs={{0,1},{1,0},{2,3},{3,2},{4,5},{5,4},{6,7},{7,6},{8,9},{9,8},{10,11... | collective-permute-start | bytes 1572872 | tf_op jit(solution)/shard_map/ppermute | solution.py:318
  158.7 19.2 %collective-permute-start.5 = (bf16[128,2048]{1,0:T(8,128)(2,1)}, bf16[128,2048]{1,0:T(8,128)(2,1)S(1)}, u32[]{:S(2)}, u32[]{:S(2)}) collective-permute-start(bf16[128,2048]{1,0:T(8,128)(2,1)} %copy-done.20), channel_id=1, source_target_pairs={{0,1},{1,0},{2,3},{3,2},{4,5},{5,4},{6,7},{7,6},{8,9},{9,8},{10,11... | collective-permute-start | bytes 1572872 | tf_op jit(solution)/shard_map/ppermute | solution.py:318
  158.8 19.1 %collective-permute-start.6 = (bf16[128,2048]{1,0:T(8,128)(2,1)}, bf16[128,2048]{1,0:T(8,128)(2,1)S(1)}, u32[]{:S(2)}, u32[]{:S(2)}) collective-permute-start(bf16[128,2048]{1,0:T(8,128)(2,1)} %copy-done.22), channel_id=1, source_target_pairs={{0,1},{1,0},{2,3},{3,2},{4,5},{5,4},{6,7},{7,6},{8,9},{9,8},{10,11... | collective-permute-start | bytes 1572872 | tf_op jit(solution)/shard_map/ppermute | solution.py:318
  176.1 18.2 %collective-permute-start.31 = (bf16[2,128,2048]{2,1,0:T(8,128)(2,1)S(1)}, bf16[2,128,2048]{2,1,0:T(8,128)(2,1)S(1)}, u32[]{:S(2)}, u32[]{:S(2)}) collective-permute-start(bf16[2,128,2048]{2,1,0:T(8,128)(2,1)S(1)} %get-tuple-element.18), channel_id=1, source_target_pairs={{0,1},{1,0},{2,3},{3,2},{4,5},{5,4},{6,7},{7,6},{8,9},{9,8},{10,11... | collective-permute-start | bytes 3145736 | tf_op jit(solution)/shard_map/ppermute | solution.py:318
  191.0 20.2 %collective-permute-start.21 = (bf16[2,128,2048]{2,1,0:T(8,128)(2,1)S(1)}, bf16[2,128,2048]{2,1,0:T(8,128)(2,1)S(1)}, u32[]{:S(2)}, u32[]{:S(2)}) collective-permute-start(bf16[2,128,2048]{2,1,0:T(8,128)(2,1)S(1)} %get-tuple-element.16), channel_id=1, source_target_pairs={{0,1},{1,0},{2,3},{3,2},{4,5},{5,4},{6,7},{7,6},{8,9},{9,8},{10,11... | collective-permute-start | bytes 3145736 | tf_op jit(solution)/shard_map/ppermute | solution.py:318
  213.1 22.6 %collective-permute-start.9 = (bf16[128,2048]{1,0:T(8,128)(2,1)S(1)}, bf16[128,2048]{1,0:T(8,128)(2,1)S(1)}, u32[]{:S(2)}, u32[]{:S(2)}) collective-permute-start(bf16[128,2048]{1,0:T(8,128)(2,1)S(1)} %fusion.10), channel_id=1, source_target_pairs={{0,2},{1,3},{2,0},{3,1},{4,6},{5,7},{6,4},{7,5},{8,10},{9,11},{10,... | collective-permute-start | bytes 1572872 | tf_op jit(solution)/shard_map/ppermute | solution.py:318
  (55 other events, 487.1 us)

commit v3 on v2

--- a/solution.py
+++ b/solution.py
@@ -2,6 +2,7 @@
 
 import jax
 import jax.numpy as jnp
+import numpy as np
 from jax import lax
 from jax.experimental import pallas as pl
 from jax.experimental.pallas import tpu as pltpu
@@ -9,6 +10,7 @@
 
 UNITS = 64
 SCALE = 1.0 / 256.0
+VMEM = 60 * 1024 * 1024
 
 
 def group_of(capacity):
@@ -145,15 +147,16 @@
     )(code.reshape(blocks // take, take, rows), hidden, weight)
 
 
-def pick_kernel(capacity, where_ref, code_ref, *refs):
-    pieces, weight_ref, hidden_ref, rows_ref = refs[:8], refs[8], refs[9], refs[10]
+def pick_kernel(capacity, k, where_ref, code_ref, *refs):
+    pieces, weight_ref = refs[:8], refs[8]
+    hidden_ref, rows_ref = refs[-2:]
     rows, width = pieces[0].shape
 
     @pl.when(pl.program_id(0) == 0)
     def _():
         for i, piece in enumerate(pieces):
-            block, section = where_ref[4 + 2 * i], where_ref[5 + 2 * i]
-            code = code_ref[pl.ds(where_ref[block], 1), :]
+            block, section = where_ref[k, 4 + 2 * i], where_ref[k, 5 + 2 * i]
+            code = code_ref[pl.ds(where_ref[k, block], 1), :]
             places = lax.broadcasted_iota(jnp.int32, (capacity, rows), 0)
             onehot = (places == code >> 8).astype(jnp.bfloat16)
             picked = jnp.dot(onehot, piece[...], preferred_element_type=jnp.float32)
@@ -168,10 +171,10 @@
     hidden_ref[...] = (gate / (1.0 + jnp.exp(-gate)) * up).astype(jnp.bfloat16)
 
 
-def sum_kernel(capacity, where_ref, code_ref, mine_ref, other_ref, weight_ref, keep_ref, send_ref):
+def sum_kernel(capacity, k, where_ref, code_ref, mine_ref, other_ref, weight_ref, keep_ref, send_ref):
     rows = code_ref.shape[1]
     units = mine_ref.shape[1]
-    me = where_ref[5]
+    me = where_ref[k, 5]
     total = jnp.dot(
         mine_ref[...],
         weight_ref[pl.ds(pl.multiple_of(me * units, units), units), :],
@@ -184,7 +187,7 @@
     )
     result = total.astype(jnp.bfloat16)
     for b in range(4):
-        code = code_ref[pl.ds(where_ref[b], 1), :]
+        code = code_ref[pl.ds(where_ref[k, b], 1), :]
         places = lax.broadcasted_iota(jnp.int32, (capacity, rows), 0)
         scale = (code & 255).astype(jnp.float32) * SCALE
         scaled = jnp.where(places == code >> 8, scale, 0.0).astype(jnp.bfloat16)
@@ -198,40 +201,41 @@
         out_ref[b % 2] = mixed.astype(jnp.bfloat16)
 
 
-def pick_call(where, code, pieces, weight, capacity):
+def pick_call(k, where, code, pieces, weight, earlier, capacity):
     rows, width = pieces[0].shape
     depth, columns = weight.shape
     tall = 4 * capacity
     pair = 4 * UNITS
     return pl.pallas_call(
-        functools.partial(pick_kernel, capacity),
+        functools.partial(pick_kernel, capacity, k),
         grid=(columns // pair,),
         in_specs=[
             pl.BlockSpec(memory_space=pltpu.SMEM),
             pl.BlockSpec(code.shape, lambda i: (0, 0)),
             *[pl.BlockSpec((rows, width), lambda i: (0, 0), pipeline_mode=pl.Buffered(1)) for _ in pieces],
             pl.BlockSpec((depth, pair), lambda i: (0, i)),
+            *[pl.BlockSpec(memory_space=pl.ANY) for _ in earlier],
         ],
         out_specs=pl.BlockSpec((tall, pair // 2), lambda i: (0, i)),
         out_shape=jax.ShapeDtypeStruct((tall, columns // 2), jnp.bfloat16),
         scratch_shapes=[pltpu.VMEM((tall, depth), jnp.bfloat16)],
-        compiler_params=pltpu.CompilerParams(vmem_limit_bytes=28 * 1024 * 1024),
+        compiler_params=pltpu.CompilerParams(vmem_limit_bytes=VMEM),
         cost_estimate=pl.CostEstimate(
             flops=2 * tall * depth * (columns + rows),
             bytes_accessed=2 * (8 * rows * width + weight.size + tall * columns // 2),
             transcendentals=tall * columns // 2,
         ),
         name="gate_up",
-    )(where, code, *pieces, weight)
-
-
-def sum_call(where, code, mine, other, weight, capacity):
+    )(where, code, *pieces, weight, *earlier)
+
+
+def sum_call(k, where, code, mine, other, weight, capacity):
     rows = code.shape[1]
     depth, wide = weight.shape
     tall, units = mine.shape
     step = 512
     return pl.pallas_call(
-        functools.partial(sum_kernel, capacity),
+        functools.partial(sum_kernel, capacity, k),
         grid=(wide // step,),
         in_specs=[
             pl.BlockSpec(memory_space=pltpu.SMEM),
@@ -242,7 +246,7 @@
         ],
         out_specs=[pl.BlockSpec((2, rows, step), lambda i: (0, 0, i))] * 2,
         out_shape=[jax.ShapeDtypeStruct((2, rows, wide), jnp.bfloat16)] * 2,
-        compiler_params=pltpu.CompilerParams(vmem_limit_bytes=28 * 1024 * 1024),
+        compiler_params=pltpu.CompilerParams(vmem_limit_bytes=VMEM),
         cost_estimate=pl.CostEstimate(
             flops=2 * wide * (tall * depth + 4 * rows * capacity),
             bytes_accessed=2 * (2 * mine.size + weight.size + 4 * rows * wide),
@@ -317,45 +321,43 @@
     def move(value, moves):
         return lax.ppermute(value, axes, moves)
 
-    x, e = lax.axis_index("section"), lax.axis_index("expert")
-    z, y, c = e // 4, e // 2 % 2, e % 2
-    places = jnp.array([ring.index(i) for i in range(layers)], jnp.int32)
+    table = np.zeros((2, layers, 2, 2, layers, 20), np.int32)
+    for x, z, y, c, k in np.ndindex(2, layers, 2, 2, layers):
+        at = ring[(ring.index(z) - k) % layers] * 4
+        row = [at + (y ^ (i & 1)) * 2 + (c ^ (i >> 1)) for i in range(4)]
+        for own in (0, 1):
+            core, base = c ^ own, 2 * own
+            row += [base, x, base + core, x ^ (1 - core), base + 1 - core, x ^ core, base + 1, 1 - x]
+        table[x, z, y, c, k] = row
+    device = lax.axis_index("section") * experts + lax.axis_index("expert")
+    where = lax.dynamic_index_in_dim(jnp.asarray(table.reshape(2 * experts, layers, 20)), device, 0, keepdims=False)
     code = lax.all_to_all(codes_of(expert_ids, numerators, experts), "expert", split_axis=0, concat_axis=0, tiled=True)
 
-    def where(k):
-        at = jnp.array(ring, jnp.int32)[(places[z] - k) % layers] * 4
-        blocks = [at + (y ^ (i & 1)) * 2 + (c ^ (i >> 1)) for i in range(4)]
-        spots = []
-        for own in (0, 1):
-            core = c ^ own
-            base = 2 * own
-            spots += [base, x]
-            spots += [base + core, x ^ (1 - core)]
-            spots += [base + 1 - core, x ^ core]
-            spots += [base + 1, 1 - x]
-        return jnp.stack([jnp.asarray(v, jnp.int32) for v in blocks + spots])
-
-    wheres = [where(k) for k in range(layers)]
-    shard, kept = tokens, []
+    shard, kept, hiddens = tokens, [], []
     for k in range(layers):
         later = move(shard, onward) if k < layers - 1 else None
         a = move(shard, first)
         b = move(shard, second)
+        if k == 0:
+            a, code, where = lax.optimization_barrier((a, code, where))
         d = move(a, second)
         pieces = [shard, a, b, d]
         pieces += [move(v, sibling) for v in pieces]
-        mine = pick_call(wheres[k], code, pieces, gate_up_weight[0], capacity)
+        earlier = hiddens[-1:] + [keep for keep, _, _ in kept[-2:-1]]
+        mine = pick_call(k, where, code, pieces, gate_up_weight[0], earlier, capacity)
         other = move(mine, over_x)
-        keep, send = sum_call(wheres[k], code, mine, other, down_weight[0], capacity)
+        keep, send = sum_call(k, where, code, mine, other, down_weight[0], capacity)
         got = move(send, sibling)
         away = (keep[1].astype(jnp.float32) + got[1].astype(jnp.float32)).astype(jnp.bfloat16)
         back = move(away, over_y)
-        kept.append((keep[0], got[0], back))
+        kept.append((keep, got, back))
+        hiddens.append(mine)
         shard = later
 
     total = None
     for k in [*range(1, layers), 0]:
-        terms = [v.astype(jnp.float32) for v in kept[k]]
+        keep, got, back = kept[k]
+        terms = [v.astype(jnp.float32) for v in (keep[0], got[0], back)]
         if total is not None:
             terms.append(move(total, onward).astype(jnp.float32))
         total = functools.reduce(jnp.add, terms).astype(jnp.bfloat16)

time: 240 us -> 233 us (0.971)
  local copies, waits for them, and re-layouts: 37.2 us -> 4.22 us
  waiting for transfers between devices: 71.5 us -> 96.5 us
  Pallas kernels: 54.8 us -> 74.2 us
  starting transfers between devices: 61.9 us -> 45.8 us
  between operations: 6.57 us -> 0.34 us
  other arithmetic: 6.05 us -> 10.4 us
    unnamed x64 -> x50, local copies, waits for them, and re-layouts: 34.1 us -> 2.95 us
    ppermute x46, waiting for transfers between devices: 71.5 us -> 91.4 us  [move(): return lax.ppermute(value, axes, moves)]
    pallas_call x8, Pallas kernels: 54.8 us -> 74.2 us  [the longest x4 46.9 us: pick_call(): pl.pallas_call(functools.partial(pick_kernel, capacity, k), grid=(columns...]
    ppermute x46, starting transfers between devices: 56.2 us -> 40.8 us  [move(): return lax.ppermute(value, axes, moves)]
    all_to_all x1, waiting for transfers between devices: 0.01 us -> 5.14 us  [pair_shards(): lax.all_to_all(codes_of(expert_ids, numerators, experts), 'expert', split...]
    dynamic_slice x2 -> x0, local copies, waits for them, and re-layouts: 2.71 us -> none  [where(): at = jnp.array(ring, jnp.int32)[(places[z] - k) % layers] * 4]
  transfers between devices with their start and end apart: 47 -> 47, of which waited for: 13 -> 13; matrix products, arithmetic and copies ran while one was open for 4% -> 5% of each run, Pallas kernels for 23% -> 32%
where the time goes in v3:
time: 233 us; the launch traced here: 232 us
  waiting for transfers between devices  96.5 us (41%)
  Pallas kernels  74.2 us (32%)
  starting transfers between devices  45.8 us (20%)
  other arithmetic  10.4 us (4%)
  local copies, waits for them, and re-layouts  4.22 us (2%)
    ppermute x46, waiting for transfers between devices, move(): return lax.ppermute(value, axes, moves)  91.4 us
    pallas_call x4, Pallas kernels, pick_call(): pl.pallas_call(functools.partial(pick_kernel, capacity, k), grid=(columns...  46.9 us
    ppermute x46, starting transfers between devices, move(): return lax.ppermute(value, axes, moves)  40.8 us
    pallas_call x4, Pallas kernels, sum_call(): pl.pallas_call(functools.partial(sum_kernel, capacity, k), grid=(wide //...  27.3 us
    convert_element_type x4, other arithmetic, pair_shards(): total = functools.reduce(jnp.add, terms).astype(jnp.bfloat16)  5.3 us
    all_to_all x1, waiting for transfers between devices, pair_shards(): lax.all_to_all(codes_of(expert_ids, numerators, experts), 'expert', split...  5.14 us
    all_to_all x1, starting transfers between devices, pair_shards(): lax.all_to_all(codes_of(expert_ids, numerators, experts), 'expert', split...  4.98 us
  transfers between devices with their start and end apart: 47, of which 13 were waited for; matrix products, arithmetic and copies ran while one was open for 5% of the time, Pallas kernels for 32%

profile of v3, /device:TPU:0, one launch (start us, length us, event | category | flops | bytes accessed | tf_op | source)
XLA Modules:
  0.0 232.1 jit_solution(18095920414629123888)
XLA Ops:
  0.0 3.0 %collective-permute-start.10 = (bf16[128,2048]{1,0:T(8,128)(2,1)}, bf16[128,2048]{1,0:T(8,128)(2,1)S(1)}, u32[]{:S(2)}, u32[]{:S(2)}) collective-permute-start(bf16[128,2048]{1,0:T(8,128)(2,1)} %refs_0_.1), channel_id=1, source_target_pairs={{0,4},{1,5},{2,6},{3,7},{4,12},{5,13},{6,14},{7,15},{8,0},{9,1},{1... | collective-permute-start | bytes 1572872 | tf_op jit(solution)/shard_map/ppermute | solution.py:322
  6.0 10.1 %collective-permute-done.10.refs_0_ = bf16[128,2048]{1,0:T(8,128)(2,1)S(1)} collective-permute-done((bf16[128,2048]{1,0:T(8,128)(2,1)}, bf16[128,2048]{1,0:T(8,128)(2,1)S(1)}, u32[]{:S(2)}, u32[]{:S(2)}) %collective-permute-start.10) | collective-permute-done | bytes 524320 | tf_op jit(solution)/shard_map/ppermute | solution.py:322
  21.5 5.0 %all-to-all-start = ((s32[16,1,128]{2,1,0:T(1,128)}), s32[16,1,128]{2,1,0:T(1,128)S(1)}, u32[]{:S(2)}, u32[]{:S(2)}) async-start(s32[16,1,128]{2,1,0:T(1,128)} %bitcast.3), calls=%async_computation | async-start | bytes 16384 | tf_op jit(solution)/shard_map/all_to_all | solution.py:334
  27.7 5.1 %all-to-all-done = s32[16,1,128]{2,1,0:T(1,128)S(1)} async-done(((s32[16,1,128]{2,1,0:T(1,128)}), s32[16,1,128]{2,1,0:T(1,128)S(1)}, u32[]{:S(2)}, u32[]{:S(2)}) %all-to-all-start) | async-done | bytes 8224 | tf_op jit(solution)/shard_map/all_to_all | solution.py:334
  36.5 5.7 %collective-permute-done.2.refs_3_ = bf16[128,2048]{1,0:T(8,128)(2,1)S(1)} collective-permute-done((bf16[128,2048]{1,0:T(8,128)(2,1)S(1)}, bf16[128,2048]{1,0:T(8,128)(2,1)S(1)}, u32[]{:S(2)}, u32[]{:S(2)}) %collective-permute-start.2) | collective-permute-done | bytes 524320 | tf_op jit(solution)/shard_map/ppermute | solution.py:322
  42.7 6.5 %collective-permute-done.11.refs_0_ = bf16[128,2048]{1,0:T(8,128)(2,1)S(1)} collective-permute-done((bf16[128,2048]{1,0:T(8,128)(2,1)S(1)}, bf16[128,2048]{1,0:T(8,128)(2,1)S(1)}, u32[]{:S(2)}, u32[]{:S(2)}) %collective-permute-start.11) | collective-permute-done | bytes 524320 | tf_op jit(solution)/shard_map/ppermute | solution.py:322
  51.6 11.5 %collective-permute-done.20.refs_1_ = bf16[128,2048]{1,0:T(8,128)(2,1)} collective-permute-done((bf16[128,2048]{1,0:T(8,128)(2,1)S(1)}, bf16[128,2048]{1,0:T(8,128)(2,1)}, u32[]{:S(2)}, u32[]{:S(2)}) %collective-permute-start.20) | collective-permute-done | bytes 524320 | tf_op jit(solution)/shard_map/ppermute | solution.py:322
  65.0 11.7 %gate_up.4.mine_ref.refs_9_ = bf16[320,768]{1,0:T(8,128)(2,1)} custom-call(s32[4,20]{1,0:T(4,128)} %dynamic-slice_bitcast_fusion.where_ref, s32[16,128]{1,0:T(8,128)} %bitcast.45, bf16[128,2048]{1,0:T(8,128)(2,1)} %refs_0_.1, bf16[128,2048]{1,0:T(8,128)(2,1)} %copy-done.7, bf16[128,2048]{1,0:T(8,128)(2,1)} %copy-done.9, bf16[128,2048]{1,0:T(8,128)(2,1)} %copy-done.15, ...), custom_call_target="tpu_custom_call" | custom-call | flops 4362076160 | bytes 17268736 | tf_op jit(solution)/shard_map/gate_up/pallas_call | solution.py:209
  77.9 9.9 %collective-permute-done.7.other_ref = bf16[320,768]{1,0:T(8,128)(2,1)S(1)} collective-permute-done((bf16[320,768]{1,0:T(8,128)(2,1)}, bf16[320,768]{1,0:T(8,128)(2,1)S(1)}, u32[]{:S(2)}, u32[]{:S(2)}) %collective-permute-start.7) | collective-permute-done | bytes 491552 | tf_op jit(solution)/shard_map/ppermute | solution.py:322
  88.9 6.8 %down.4 = (bf16[2,128,2048]{2,1,0:T(8,128)(2,1)}, bf16[2,128,2048]{2,1,0:T(8,128)(2,1)}) custom-call(s32[4,20]{1,0:T(4,128)} %dynamic-slice_bitcast_fusion.where_ref, s32[16,128]{1,0:T(8,128)} %bitcast.46, bf16[320,768]{1,0:T(8,128)(2,1)} %gate_up.4.mine_ref.refs_9_, bf16[320,768]{1,0:T(8,128)(2,1)} %copy-done.23, bf16[1536,2048]{1,0:T(8,128)(2,1)} %bitcast.56), custom_call_target="tpu_custom_call" | custom-call | flops 2181038080 | bytes 9371648 | tf_op jit(solution)/shard_map/down/pallas_call | solution.py:237
  95.8 11.7 %gate_up.5.refs_9_.mine_ref = bf16[320,768]{1,0:T(8,128)(2,1)} custom-call(s32[4,20]{1,0:T(4,128)} %dynamic-slice_bitcast_fusion.where_ref, s32[16,128]{1,0:T(8,128)} %bitcast.47, bf16[128,2048]{1,0:T(8,128)(2,1)} %copy-done.3, bf16[128,2048]{1,0:T(8,128)(2,1)} %copy-done.4, bf16[128,2048]{1,0:T(8,128)(2,1)} %copy-done.5, ...), custom_call_target="tpu_custom_call" | custom-call | flops 4362076160 | bytes 17268736 | tf_op jit(solution)/shard_map/gate_up/pallas_call | solution.py:209
  111.4 11.7 %gate_up.6.refs_9_.mine_ref = bf16[320,768]{1,0:T(8,128)(2,1)} custom-call(s32[4,20]{1,0:T(4,128)} %dynamic-slice_bitcast_fusion.where_ref, s32[16,128]{1,0:T(8,128)} %bitcast.48, bf16[128,2048]{1,0:T(8,128)(2,1)} %copy-done.8, bf16[128,2048]{1,0:T(8,128)(2,1)} %collective-permute-done.20.refs_1_, bf16[128,2048]{1,0:T(8,128)(2,1)} %collective-permute-done.21.refs_2_, ...), custom_call_target="tpu_custom_call" | custom-call | flops 4362076160 | bytes 17268736 | tf_op jit(solution)/shard_map/gate_up/pallas_call | solution.py:209
  124.1 6.8 %down.5 = (bf16[2,128,2048]{2,1,0:T(8,128)(2,1)}, bf16[2,128,2048]{2,1,0:T(8,128)(2,1)}) custom-call(s32[4,20]{1,0:T(4,128)} %dynamic-slice_bitcast_fusion.where_ref, s32[16,128]{1,0:T(8,128)} %bitcast.49, bf16[320,768]{1,0:T(8,128)(2,1)} %gate_up.5.refs_9_.mine_ref, bf16[320,768]{1,0:T(8,128)(2,1)} %copy-done.24, bf16[1536,2048]{1,0:T(8,128)(2,1)} %bitcast.57), custom_call_target="tpu_custom_call" | custom-call | flops 2181038080 | bytes 9371648 | tf_op jit(solution)/shard_map/down/pallas_call | solution.py:237
  131.0 4.2 %collective-permute-start.41 = (bf16[2,128,2048]{2,1,0:T(8,128)(2,1)}, bf16[2,128,2048]{2,1,0:T(8,128)(2,1)}, u32[]{:S(2)}, u32[]{:S(2)}) collective-permute-start(bf16[2,128,2048]{2,1,0:T(8,128)(2,1)} %get-tuple-element.26), channel_id=1, source_target_pairs={{0,1},{1,0},{2,3},{3,2},{4,5},{5,4},{6,7},{7,6},{8,9},{9,8},{10,11... | collective-permute-start | bytes 3145736 | tf_op jit(solution)/shard_map/ppermute | solution.py:322
  137.7 5.2 %collective-permute-start.19 = (bf16[128,2048]{1,0:T(8,128)(2,1)S(1)}, bf16[128,2048]{1,0:T(8,128)(2,1)}, u32[]{:S(2)}, u32[]{:S(2)}) collective-permute-start(bf16[128,2048]{1,0:T(8,128)(2,1)S(1)} %collective-permute-done.15.refs_3_), channel_id=1, source_target_pairs={{0,1},{1,0},{2,3},{3,2},{4,5},{5,4},{6,7},{7,6},{8,9},{9,8},{10,11... | collective-permute-start | bytes 1572872 | tf_op jit(solution)/shard_map/ppermute | solution.py:322
  142.9 6.8 %down.7 = (bf16[2,128,2048]{2,1,0:T(8,128)(2,1)}, bf16[2,128,2048]{2,1,0:T(8,128)(2,1)}) custom-call(s32[4,20]{1,0:T(4,128)} %dynamic-slice_bitcast_fusion.where_ref, s32[16,128]{1,0:T(8,128)} %bitcast.50, bf16[320,768]{1,0:T(8,128)(2,1)} %gate_up.6.refs_9_.mine_ref, bf16[320,768]{1,0:T(8,128)(2,1)} %collective-permute-done.38.other_ref, ...), custom_call_target="tpu_custom_call" | custom-call | flops 2181038080 | bytes 9371648 | tf_op jit(solution)/shard_map/down/pallas_call | solution.py:237
  150.5 11.8 %gate_up.7.mine_ref = bf16[320,768]{1,0:T(8,128)(2,1)} custom-call(s32[4,20]{1,0:T(4,128)} %dynamic-slice_bitcast_fusion.where_ref, s32[16,128]{1,0:T(8,128)} %bitcast.51, bf16[128,2048]{1,0:T(8,128)(2,1)} %copy-done.6, bf16[128,2048]{1,0:T(8,128)(2,1)} %copy-done.12, bf16[128,2048]{1,0:T(8,128)(2,1)} %copy-done.14, bf16[128,2048]{1,0:T(8,128)(2,1)} %copy-done.17, ...), custom_call_target="tpu_custom_call" | custom-call | flops 4362076160 | bytes 17268736 | tf_op jit(solution)/shard_map/gate_up/pallas_call | solution.py:209
  165.3 10.5 %collective-permute-done.35.other_ref = bf16[320,768]{1,0:T(8,128)(2,1)} collective-permute-done((bf16[320,768]{1,0:T(8,128)(2,1)}, bf16[320,768]{1,0:T(8,128)(2,1)}, u32[]{:S(2)}, u32[]{:S(2)}) %collective-permute-start.35) | collective-permute-done | bytes 491552 | tf_op jit(solution)/shard_map/ppermute | solution.py:322
  175.8 6.8 %down.6 = (bf16[2,128,2048]{2,1,0:T(8,128)(2,1)}, bf16[2,128,2048]{2,1,0:T(8,128)(2,1)}) custom-call(s32[4,20]{1,0:T(4,128)} %dynamic-slice_bitcast_fusion.where_ref, s32[16,128]{1,0:T(8,128)} %bitcast.52, bf16[320,768]{1,0:T(8,128)(2,1)} %gate_up.7.mine_ref, bf16[320,768]{1,0:T(8,128)(2,1)} %collective-permute-done.35.other_ref, bf16[1536,2048]{1,0:T(8,128)(2,1)} %bitcast.59), custom_call_target="tpu_custom_call" | custom-call | flops 2181038080 | bytes 9371648 | tf_op jit(solution)/shard_map/down/pallas_call | solution.py:237
  186.3 13.0 %collective-permute-done.43 = bf16[128,2048]{1,0:T(8,128)(2,1)S(1)} collective-permute-done((bf16[128,2048]{1,0:T(8,128)(2,1)S(1)}, bf16[128,2048]{1,0:T(8,128)(2,1)S(1)}, u32[]{:S(2)}, u32[]{:S(2)}) %collective-permute-start.43) | collective-permute-done | bytes 524320 | tf_op jit(solution)/shard_map/ppermute | solution.py:322
  205.3 10.3 %collective-permute-done.44 = bf16[128,2048]{1,0:T(8,128)(2,1)S(1)} collective-permute-done((bf16[128,2048]{1,0:T(8,128)(2,1)S(1)}, bf16[128,2048]{1,0:T(8,128)(2,1)S(1)}, u32[]{:S(2)}, u32[]{:S(2)}) %collective-permute-start.44) | collective-permute-done | bytes 524320 | tf_op jit(solution)/shard_map/ppermute | solution.py:322
  215.6 2.4 %collective-permute-done.37 = bf16[128,2048]{1,0:T(8,128)(2,1)S(1)} collective-permute-done((bf16[128,2048]{1,0:T(8,128)(2,1)S(1)}, bf16[128,2048]{1,0:T(8,128)(2,1)S(1)}, u32[]{:S(2)}, u32[]{:S(2)}) %collective-permute-start.37) | collective-permute-done | bytes 524320 | tf_op jit(solution)/shard_map/ppermute | solution.py:322
  220.0 7.6 %collective-permute-done.9 = bf16[128,2048]{1,0:T(8,128)(2,1)S(1)} collective-permute-done((bf16[128,2048]{1,0:T(8,128)(2,1)S(1)}, bf16[128,2048]{1,0:T(8,128)(2,1)S(1)}, u32[]{:S(2)}, u32[]{:S(2)}) %collective-permute-start.9) | collective-permute-done | bytes 524320 | tf_op jit(solution)/shard_map/ppermute | solution.py:322
  227.6 3.4 %collective-permute-done.45 = bf16[128,2048]{1,0:T(8,128)(2,1)S(1)} collective-permute-done((bf16[128,2048]{1,0:T(8,128)(2,1)S(1)}, bf16[128,2048]{1,0:T(8,128)(2,1)S(1)}, u32[]{:S(2)}, u32[]{:S(2)}) %collective-permute-start.45) | collective-permute-done | bytes 524320 | tf_op jit(solution)/shard_map/ppermute | solution.py:322
  (140 shorter events, 44.2 us)
Async XLA Ops:
  0.0 16.2 %collective-permute-start.10 = (bf16[128,2048]{1,0:T(8,128)(2,1)}, bf16[128,2048]{1,0:T(8,128)(2,1)S(1)}, u32[]{:S(2)}, u32[]{:S(2)}) collective-permute-start(bf16[128,2048]{1,0:T(8,128)(2,1)} %refs_0_.1), channel_id=1, source_target_pairs={{0,4},{1,5},{2,6},{3,7},{4,12},{5,13},{6,14},{7,15},{8,0},{9,1},{1... | collective-permute-start | bytes 1572872 | tf_op jit(solution)/shard_map/ppermute | solution.py:322
  3.0 29.9 %collective-permute-start = (bf16[128,2048]{1,0:T(8,128)(2,1)}, bf16[128,2048]{1,0:T(8,128)(2,1)S(1)}, u32[]{:S(2)}, u32[]{:S(2)}) collective-permute-start(bf16[128,2048]{1,0:T(8,128)(2,1)} %refs_0_.1), channel_id=1, source_target_pairs={{0,16},{1,3},{2,18},{3,1},{4,20},{5,7},{6,22},{7,5},{8,24},{9,11},... | collective-permute-start | bytes 1572872 | tf_op jit(solution)/shard_map/ppermute | solution.py:322
  4.5 28.4 %collective-permute-start.1 = (bf16[128,2048]{1,0:T(8,128)(2,1)}, bf16[128,2048]{1,0:T(8,128)(2,1)S(1)}, u32[]{:S(2)}, u32[]{:S(2)}) collective-permute-start(bf16[128,2048]{1,0:T(8,128)(2,1)} %refs_0_.1), channel_id=1, source_target_pairs={{0,2},{1,17},{2,0},{3,19},{4,6},{5,21},{6,4},{7,23},{8,10},{9,25},... | collective-permute-start | bytes 1572872 | tf_op jit(solution)/shard_map/ppermute | solution.py:322
  6.0 27.5 %collective-permute-start.3 = (bf16[128,2048]{1,0:T(8,128)(2,1)}, bf16[128,2048]{1,0:T(8,128)(2,1)S(1)}, u32[]{:S(2)}, u32[]{:S(2)}) collective-permute-start(bf16[128,2048]{1,0:T(8,128)(2,1)} %refs_0_.1), channel_id=1, source_target_pairs={{0,1},{1,0},{2,3},{3,2},{4,5},{5,4},{6,7},{7,6},{8,9},{9,8},{10,11... | collective-permute-start | bytes 1572872 | tf_op jit(solution)/shard_map/ppermute | solution.py:322
  16.2 18.2 %collective-permute-start.27 = (bf16[128,2048]{1,0:T(8,128)(2,1)S(1)}, bf16[128,2048]{1,0:T(8,128)(2,1)S(1)}, u32[]{:S(2)}, u32[]{:S(2)}) collective-permute-start(bf16[128,2048]{1,0:T(8,128)(2,1)S(1)} %collective-permute-done.10.refs_0_), channel_id=1, source_target_pairs={{0,16},{1,3},{2,18},{3,1},{4,20},{5,7},{6,22},{7,5},{8,24},{9,11},... | collective-permute-start | bytes 1572872 | tf_op jit(solution)/shard_map/ppermute | solution.py:322
  34.9 15.8 %collective-permute-start.5 = (bf16[128,2048]{1,0:T(8,128)(2,1)S(1)}, bf16[128,2048]{1,0:T(8,128)(2,1)S(1)}, u32[]{:S(2)}, u32[]{:S(2)}) collective-permute-start(bf16[128,2048]{1,0:T(8,128)(2,1)S(1)} %collective-permute-done.1.refs_2_), channel_id=1, source_target_pairs={{0,1},{1,0},{2,3},{3,2},{4,5},{5,4},{6,7},{7,6},{8,9},{9,8},{10,11... | collective-permute-start | bytes 1572872 | tf_op jit(solution)/shard_map/ppermute | solution.py:322
  50.8 26.0 %collective-permute-start.32 = (bf16[128,2048]{1,0:T(8,128)(2,1)S(1)}, bf16[128,2048]{1,0:T(8,128)(2,1)}, u32[]{:S(2)}, u32[]{:S(2)}) collective-permute-start(bf16[128,2048]{1,0:T(8,128)(2,1)S(1)} %collective-permute-done.28.refs_2_), channel_id=1, source_target_pairs={{0,1},{1,0},{2,3},{3,2},{4,5},{5,4},{6,7},{7,6},{8,9},{9,8},{10,11... | collective-permute-start | bytes 1572872 | tf_op jit(solution)/shard_map/ppermute | solution.py:322
  50.8 26.7 %collective-permute-start.21 = (bf16[128,2048]{1,0:T(8,128)(2,1)S(1)}, bf16[128,2048]{1,0:T(8,128)(2,1)}, u32[]{:S(2)}, u32[]{:S(2)}) collective-permute-start(bf16[128,2048]{1,0:T(8,128)(2,1)S(1)} %collective-permute-done.11.refs_0_), channel_id=1, source_target_pairs={{0,2},{1,17},{2,0},{3,19},{4,6},{5,21},{6,4},{7,23},{8,10},{9,25},... | collective-permute-start | bytes 1572872 | tf_op jit(solution)/shard_map/ppermute | solution.py:322
  51.3 26.1 %collective-permute-start.12 = (bf16[128,2048]{1,0:T(8,128)(2,1)S(1)}, bf16[128,2048]{1,0:T(8,128)(2,1)S(1)}, u32[]{:S(2)}, u32[]{:S(2)}) collective-permute-start(bf16[128,2048]{1,0:T(8,128)(2,1)S(1)} %collective-permute-done.11.refs_0_), channel_id=1, source_target_pairs={{0,4},{1,5},{2,6},{3,7},{4,12},{5,13},{6,14},{7,15},{8,0},{9,1},{1... | collective-permute-start | bytes 1572872 | tf_op jit(solution)/shard_map/ppermute | solution.py:322
  51.4 37.2 %collective-permute-start.33 = (bf16[128,2048]{1,0:T(8,128)(2,1)}, bf16[128,2048]{1,0:T(8,128)(2,1)}, u32[]{:S(2)}, u32[]{:S(2)}) collective-permute-start(bf16[128,2048]{1,0:T(8,128)(2,1)} %collective-permute-done.29.refs_3_), channel_id=1, source_target_pairs={{0,1},{1,0},{2,3},{3,2},{4,5},{5,4},{6,7},{7,6},{8,9},{9,8},{10,11... | collective-permute-start | bytes 1572872 | tf_op jit(solution)/shard_map/ppermute | solution.py:322
  63.1 25.8 %collective-permute-start.22 = (bf16[128,2048]{1,0:T(8,128)(2,1)}, bf16[128,2048]{1,0:T(8,128)(2,1)}, u32[]{:S(2)}, u32[]{:S(2)}) collective-permute-start(bf16[128,2048]{1,0:T(8,128)(2,1)} %collective-permute-done.20.refs_1_), channel_id=1, source_target_pairs={{0,2},{1,17},{2,0},{3,19},{4,6},{5,21},{6,4},{7,23},{8,10},{9,25},... | collective-permute-start | bytes 1572872 | tf_op jit(solution)/shard_map/ppermute | solution.py:322
  77.4 30.0 %collective-permute-start.23 = (bf16[128,2048]{1,0:T(8,128)(2,1)S(1)}, bf16[128,2048]{1,0:T(8,128)(2,1)S(1)}, u32[]{:S(2)}, u32[]{:S(2)}) collective-permute-start(bf16[128,2048]{1,0:T(8,128)(2,1)S(1)} %collective-permute-done.11.refs_0_), channel_id=1, source_target_pairs={{0,1},{1,0},{2,3},{3,2},{4,5},{5,4},{6,7},{7,6},{8,9},{9,8},{10,11... | collective-permute-start | bytes 1572872 | tf_op jit(solution)/shard_map/ppermute | solution.py:322
  77.4 31.3 %collective-permute-start.24 = (bf16[128,2048]{1,0:T(8,128)(2,1)}, bf16[128,2048]{1,0:T(8,128)(2,1)}, u32[]{:S(2)}, u32[]{:S(2)}) collective-permute-start(bf16[128,2048]{1,0:T(8,128)(2,1)} %collective-permute-done.20.refs_1_), channel_id=1, source_target_pairs={{0,1},{1,0},{2,3},{3,2},{4,5},{5,4},{6,7},{7,6},{8,9},{9,8},{10,11... | collective-permute-start | bytes 1572872 | tf_op jit(solution)/shard_map/ppermute | solution.py:322
  87.8 23.5 %collective-permute-start.25 = (bf16[128,2048]{1,0:T(8,128)(2,1)}, bf16[128,2048]{1,0:T(8,128)(2,1)}, u32[]{:S(2)}, u32[]{:S(2)}) collective-permute-start(bf16[128,2048]{1,0:T(8,128)(2,1)} %collective-permute-done.21.refs_2_), channel_id=1, source_target_pairs={{0,1},{1,0},{2,3},{3,2},{4,5},{5,4},{6,7},{7,6},{8,9},{9,8},{10,11... | collective-permute-start | bytes 1572872 | tf_op jit(solution)/shard_map/ppermute | solution.py:322
  88.6 20.8 %collective-permute-start.13 = (bf16[128,2048]{1,0:T(8,128)(2,1)S(1)}, bf16[128,2048]{1,0:T(8,128)(2,1)S(1)}, u32[]{:S(2)}, u32[]{:S(2)}) collective-permute-start(bf16[128,2048]{1,0:T(8,128)(2,1)S(1)} %collective-permute-done.12.refs_0_), channel_id=1, source_target_pairs={{0,16},{1,3},{2,18},{3,1},{4,20},{5,7},{6,22},{7,5},{8,24},{9,11},... | collective-permute-start | bytes 1572872 | tf_op jit(solution)/shard_map/ppermute | solution.py:322
  88.9 22.5 %collective-permute-start.26 = (bf16[128,2048]{1,0:T(8,128)(2,1)}, bf16[128,2048]{1,0:T(8,128)(2,1)}, u32[]{:S(2)}, u32[]{:S(2)}) collective-permute-start(bf16[128,2048]{1,0:T(8,128)(2,1)} %collective-permute-done.22.refs_3_), channel_id=1, source_target_pairs={{0,1},{1,0},{2,3},{3,2},{4,5},{5,4},{6,7},{7,6},{8,9},{9,8},{10,11... | collective-permute-start | bytes 1572872 | tf_op jit(solution)/shard_map/ppermute | solution.py:322
  107.5 27.8 %collective-permute-start.14 = (bf16[128,2048]{1,0:T(8,128)(2,1)S(1)}, bf16[128,2048]{1,0:T(8,128)(2,1)S(1)}, u32[]{:S(2)}, u32[]{:S(2)}) collective-permute-start(bf16[128,2048]{1,0:T(8,128)(2,1)S(1)} %collective-permute-done.12.refs_0_), channel_id=1, source_target_pairs={{0,2},{1,17},{2,0},{3,19},{4,6},{5,21},{6,4},{7,23},{8,10},{9,25},... | collective-permute-start | bytes 1572872 | tf_op jit(solution)/shard_map/ppermute | solution.py:322
  109.3 26.4 %collective-permute-start.15 = (bf16[128,2048]{1,0:T(8,128)(2,1)S(1)}, bf16[128,2048]{1,0:T(8,128)(2,1)S(1)}, u32[]{:S(2)}, u32[]{:S(2)}) collective-permute-start(bf16[128,2048]{1,0:T(8,128)(2,1)S(1)} %collective-permute-done.13.refs_1_), channel_id=1, source_target_pairs={{0,2},{1,17},{2,0},{3,19},{4,6},{5,21},{6,4},{7,23},{8,10},{9,25},... | collective-permute-start | bytes 1572872 | tf_op jit(solution)/shard_map/ppermute | solution.py:322
  131.0 33.0 %collective-permute-start.41 = (bf16[2,128,2048]{2,1,0:T(8,128)(2,1)}, bf16[2,128,2048]{2,1,0:T(8,128)(2,1)}, u32[]{:S(2)}, u32[]{:S(2)}) collective-permute-start(bf16[2,128,2048]{2,1,0:T(8,128)(2,1)} %get-tuple-element.26), channel_id=1, source_target_pairs={{0,1},{1,0},{2,3},{3,2},{4,5},{5,4},{6,7},{7,6},{8,9},{9,8},{10,11... | collective-permute-start | bytes 3145736 | tf_op jit(solution)/shard_map/ppermute | solution.py:322
  149.7 34.4 %collective-permute-start.39 = (bf16[2,128,2048]{2,1,0:T(8,128)(2,1)}, bf16[2,128,2048]{2,1,0:T(8,128)(2,1)}, u32[]{:S(2)}, u32[]{:S(2)}) collective-permute-start(bf16[2,128,2048]{2,1,0:T(8,128)(2,1)} %get-tuple-element.25), channel_id=1, source_target_pairs={{0,1},{1,0},{2,3},{3,2},{4,5},{5,4},{6,7},{7,6},{8,9},{9,8},{10,11... | collective-permute-start | bytes 3145736 | tf_op jit(solution)/shard_map/ppermute | solution.py:322
  165.2 17.4 %collective-permute-start.42 = (bf16[128,2048]{1,0:T(8,128)(2,1)S(1)}, bf16[128,2048]{1,0:T(8,128)(2,1)}, u32[]{:S(2)}, u32[]{:S(2)}) collective-permute-start(bf16[128,2048]{1,0:T(8,128)(2,1)S(1)} %fusion.13), channel_id=1, source_target_pairs={{0,2},{1,3},{2,0},{3,1},{4,6},{5,7},{6,4},{7,5},{8,10},{9,11},{10,... | collective-permute-start | bytes 1572872 | tf_op jit(solution)/shard_map/ppermute | solution.py:322
  182.6 19.3 %collective-permute-start.36 = (bf16[2,128,2048]{2,1,0:T(8,128)(2,1)}, bf16[2,128,2048]{2,1,0:T(8,128)(2,1)S(1)}, u32[]{:S(2)}, u32[]{:S(2)}) collective-permute-start(bf16[2,128,2048]{2,1,0:T(8,128)(2,1)} %get-tuple-element.23), channel_id=1, source_target_pairs={{0,1},{1,0},{2,3},{3,2},{4,5},{5,4},{6,7},{7,6},{8,9},{9,8},{10,11... | collective-permute-start | bytes 3145736 | tf_op jit(solution)/shard_map/ppermute | solution.py:322
  186.0 18.8 %collective-permute-start.8 = (bf16[2,128,2048]{2,1,0:T(8,128)(2,1)}, bf16[2,128,2048]{2,1,0:T(8,128)(2,1)S(1)}, u32[]{:S(2)}, u32[]{:S(2)}) collective-permute-start(bf16[2,128,2048]{2,1,0:T(8,128)(2,1)} %get-tuple-element.20), channel_id=1, source_target_pairs={{0,1},{1,0},{2,3},{3,2},{4,5},{5,4},{6,7},{7,6},{8,9},{9,8},{10,11... | collective-permute-start | bytes 3145736 | tf_op jit(solution)/shard_map/ppermute | solution.py:322
  205.0 22.6 %collective-permute-start.9 = (bf16[128,2048]{1,0:T(8,128)(2,1)S(1)}, bf16[128,2048]{1,0:T(8,128)(2,1)S(1)}, u32[]{:S(2)}, u32[]{:S(2)}) collective-permute-start(bf16[128,2048]{1,0:T(8,128)(2,1)S(1)} %fusion.10), channel_id=1, source_target_pairs={{0,2},{1,3},{2,0},{3,1},{4,6},{5,7},{6,4},{7,5},{8,10},{9,11},{10,... | collective-permute-start | bytes 1572872 | tf_op jit(solution)/shard_map/ppermute | solution.py:322
  (48 other events, 976.3 us)

commit v4 on v3

--- a/solution.py
+++ b/solution.py
@@ -147,78 +147,124 @@
     )(code.reshape(blocks // take, take, rows), hidden, weight)
 
 
+def onehot_of(code, capacity):
+    return lax.broadcasted_iota(jnp.int32, (capacity, code.shape[1]), 0) == code >> 8
+
+
 def pick_kernel(capacity, k, where_ref, code_ref, *refs):
-    pieces, weight_ref = refs[:8], refs[8]
-    hidden_ref, rows_ref = refs[-2:]
-    rows, width = pieces[0].shape
-
-    @pl.when(pl.program_id(0) == 0)
-    def _():
-        for i, piece in enumerate(pieces):
-            block, section = where_ref[k, 4 + 2 * i], where_ref[k, 5 + 2 * i]
-            code = code_ref[pl.ds(where_ref[k, block], 1), :]
-            places = lax.broadcasted_iota(jnp.int32, (capacity, rows), 0)
-            onehot = (places == code >> 8).astype(jnp.bfloat16)
-            picked = jnp.dot(onehot, piece[...], preferred_element_type=jnp.float32)
+    pairs, weight_hbm = refs[:4], refs[4]
+    hidden_ref, pair_ref, weight_ref, rows_ref, sems = refs[-5:]
+    rows, width = pairs[0].shape[1:]
+    span = 4 * UNITS
+    spans = weight_hbm.shape[1] // span
+
+    def weight_copy(j):
+        at = pl.ds(pl.multiple_of(j * span, span), span)
+        return pltpu.make_async_copy(weight_hbm.at[:, at], weight_ref.at[:, at], sems.at[4 + j])
+
+    copies = [pltpu.make_async_copy(v, pair_ref.at[i], sems.at[i]) for i, v in enumerate(pairs)]
+    for copy in copies:
+        copy.start()
+    for j in range(spans):
+        weight_copy(j).start()
+    for i, copy in enumerate(copies):
+        copy.wait()
+        for h in range(2):
+            spot = 4 + 2 * (2 * i + h)
+            block, section = where_ref[k, spot], where_ref[k, spot + 1]
+            onehot = onehot_of(code_ref[pl.ds(where_ref[k, block], 1), :], capacity).astype(jnp.bfloat16)
+            picked = jnp.dot(onehot, pair_ref[i, h], preferred_element_type=jnp.float32)
             down = pl.ds(pl.multiple_of(block * capacity, capacity), capacity)
             rows_ref[down, pl.ds(pl.multiple_of(section * width, width), width)] = picked.astype(jnp.bfloat16)
 
-    both = jnp.dot(rows_ref[...], weight_ref[...], preferred_element_type=jnp.float32)
-    one, two = both[:, : 2 * UNITS], both[:, 2 * UNITS :]
-    low = lax.broadcasted_iota(jnp.int32, one.shape, 1) < UNITS
-    gate = jnp.where(low, one, pltpu.roll(two, UNITS, 1))
-    up = jnp.where(low, pltpu.roll(one, UNITS, 1), two)
-    hidden_ref[...] = (gate / (1.0 + jnp.exp(-gate)) * up).astype(jnp.bfloat16)
-
-
-def sum_kernel(capacity, k, where_ref, code_ref, mine_ref, other_ref, weight_ref, keep_ref, send_ref):
+    @pl.loop(0, spans)
+    def _(j):
+        weight_copy(j).wait()
+        at = pl.ds(pl.multiple_of(j * span, span), span)
+        both = jnp.dot(rows_ref[...], weight_ref[:, at], preferred_element_type=jnp.float32)
+        one, two = both[:, : 2 * UNITS], both[:, 2 * UNITS :]
+        low = lax.broadcasted_iota(jnp.int32, one.shape, 1) < UNITS
+        gate = jnp.where(low, one, pltpu.roll(two, UNITS, 1))
+        up = jnp.where(low, pltpu.roll(one, UNITS, 1), two)
+        half = pl.ds(pl.multiple_of(j * 2 * UNITS, 2 * UNITS), 2 * UNITS)
+        hidden_ref[:, half] = (gate / (1.0 + jnp.exp(-gate)) * up).astype(jnp.bfloat16)
+
+
+def sum_kernel(capacity, k, where_ref, code_ref, mine_hbm, other_hbm, weight_hbm, keep_hbm, send_hbm, *refs):
+    hidden_ref, weight_ref, out_ref, sems = refs
     rows = code_ref.shape[1]
-    units = mine_ref.shape[1]
-    me = where_ref[k, 5]
-    total = jnp.dot(
-        mine_ref[...],
-        weight_ref[pl.ds(pl.multiple_of(me * units, units), units), :],
-        preferred_element_type=jnp.float32,
-    )
-    total += jnp.dot(
-        other_ref[...],
-        weight_ref[pl.ds(pl.multiple_of((1 - me) * units, units), units), :],
-        preferred_element_type=jnp.float32,
-    )
-    result = total.astype(jnp.bfloat16)
+    units = mine_hbm.shape[1]
+    span = 512
+    spans = weight_hbm.shape[1] // span
+
+    def weight_copy(j):
+        at = pl.ds(pl.multiple_of(j * span, span), span)
+        return pltpu.make_async_copy(weight_hbm.at[:, at], weight_ref.at[:, at], sems.at[2 + j])
+
+    def out_copy(j, i, to):
+        at = pl.ds(pl.multiple_of(j * span, span), span)
+        sem = sems.at[2 + spans + 2 * j + i]
+        return pltpu.make_async_copy(out_ref.at[pl.ds(2 * i, 2), :, at], to.at[:, :, at], sem)
+
+    copies = [pltpu.make_async_copy(v, hidden_ref.at[i], sems.at[i]) for i, v in enumerate((mine_hbm, other_hbm))]
+    for copy in copies:
+        copy.start()
+    for j in range(spans):
+        weight_copy(j).start()
+    scaled = []
     for b in range(4):
         code = code_ref[pl.ds(where_ref[k, b], 1), :]
-        places = lax.broadcasted_iota(jnp.int32, (capacity, rows), 0)
         scale = (code & 255).astype(jnp.float32) * SCALE
-        scaled = jnp.where(places == code >> 8, scale, 0.0).astype(jnp.bfloat16)
-        mixed = lax.dot_general(
-            scaled,
-            result[b * capacity : (b + 1) * capacity],
-            (((0,), (0,)), ((), ())),
-            preferred_element_type=jnp.float32,
-        )
-        out_ref = keep_ref if b < 2 else send_ref
-        out_ref[b % 2] = mixed.astype(jnp.bfloat16)
-
-
-def pick_call(k, where, code, pieces, weight, earlier, capacity):
-    rows, width = pieces[0].shape
+        scaled.append(jnp.where(onehot_of(code, capacity), scale, 0.0).astype(jnp.bfloat16))
+    me = where_ref[k, 5]
+    mine_at = pl.ds(pl.multiple_of(me * units, units), units)
+    other_at = pl.ds(pl.multiple_of((1 - me) * units, units), units)
+    for copy in copies:
+        copy.wait()
+
+    @pl.loop(0, spans)
+    def _(j):
+        weight_copy(j).wait()
+        at = pl.ds(pl.multiple_of(j * span, span), span)
+        total = jnp.dot(hidden_ref[0], weight_ref[mine_at, at], preferred_element_type=jnp.float32)
+        total += jnp.dot(hidden_ref[1], weight_ref[other_at, at], preferred_element_type=jnp.float32)
+        result = total.astype(jnp.bfloat16)
+        for b in range(4):
+            mixed = lax.dot_general(
+                scaled[b],
+                result[b * capacity : (b + 1) * capacity],
+                (((0,), (0,)), ((), ())),
+                preferred_element_type=jnp.float32,
+            )
+            out_ref[b, :, at] = mixed.astype(jnp.bfloat16)
+        out_copy(j, 0, keep_hbm).start()
+        out_copy(j, 1, send_hbm).start()
+
+    for j in range(spans):
+        out_copy(j, 0, keep_hbm).wait()
+        out_copy(j, 1, send_hbm).wait()
+
+
+def pick_call(k, where, code, pairs, weight, earlier, capacity):
+    _, rows, width = pairs[0].shape
     depth, columns = weight.shape
     tall = 4 * capacity
-    pair = 4 * UNITS
+    anywhere = pl.BlockSpec(memory_space=pl.ANY)
     return pl.pallas_call(
         functools.partial(pick_kernel, capacity, k),
-        grid=(columns // pair,),
         in_specs=[
             pl.BlockSpec(memory_space=pltpu.SMEM),
-            pl.BlockSpec(code.shape, lambda i: (0, 0)),
-            *[pl.BlockSpec((rows, width), lambda i: (0, 0), pipeline_mode=pl.Buffered(1)) for _ in pieces],
-            pl.BlockSpec((depth, pair), lambda i: (0, i)),
-            *[pl.BlockSpec(memory_space=pl.ANY) for _ in earlier],
-        ],
-        out_specs=pl.BlockSpec((tall, pair // 2), lambda i: (0, i)),
+            pl.BlockSpec(memory_space=pltpu.VMEM),
+            *[anywhere] * (5 + len(earlier)),
+        ],
+        out_specs=pl.BlockSpec(memory_space=pltpu.VMEM),
         out_shape=jax.ShapeDtypeStruct((tall, columns // 2), jnp.bfloat16),
-        scratch_shapes=[pltpu.VMEM((tall, depth), jnp.bfloat16)],
+        scratch_shapes=[
+            pltpu.VMEM((4, 2, rows, width), jnp.bfloat16),
+            pltpu.VMEM((depth, columns), jnp.bfloat16),
+            pltpu.VMEM((tall, depth), jnp.bfloat16),
+            pltpu.SemaphoreType.DMA((4 + columns // (4 * UNITS),)),
+        ],
         compiler_params=pltpu.CompilerParams(vmem_limit_bytes=VMEM),
         cost_estimate=pl.CostEstimate(
             flops=2 * tall * depth * (columns + rows),
@@ -226,26 +272,29 @@
             transcendentals=tall * columns // 2,
         ),
         name="gate_up",
-    )(where, code, *pieces, weight, *earlier)
+    )(where, code, *pairs, weight, *earlier)
 
 
 def sum_call(k, where, code, mine, other, weight, capacity):
     rows = code.shape[1]
     depth, wide = weight.shape
     tall, units = mine.shape
-    step = 512
+    anywhere = pl.BlockSpec(memory_space=pl.ANY)
     return pl.pallas_call(
         functools.partial(sum_kernel, capacity, k),
-        grid=(wide // step,),
         in_specs=[
             pl.BlockSpec(memory_space=pltpu.SMEM),
-            pl.BlockSpec(code.shape, lambda i: (0, 0)),
-            pl.BlockSpec((tall, units), lambda i: (0, 0), pipeline_mode=pl.Buffered(1)),
-            pl.BlockSpec((tall, units), lambda i: (0, 0), pipeline_mode=pl.Buffered(1)),
-            pl.BlockSpec((depth, step), lambda i: (0, i)),
-        ],
-        out_specs=[pl.BlockSpec((2, rows, step), lambda i: (0, 0, i))] * 2,
+            pl.BlockSpec(memory_space=pltpu.VMEM),
+            *[anywhere] * 3,
+        ],
+        out_specs=[anywhere] * 2,
         out_shape=[jax.ShapeDtypeStruct((2, rows, wide), jnp.bfloat16)] * 2,
+        scratch_shapes=[
+            pltpu.VMEM((2, tall, units), jnp.bfloat16),
+            pltpu.VMEM((depth, wide), jnp.bfloat16),
+            pltpu.VMEM((4, rows, wide), jnp.bfloat16),
+            pltpu.SemaphoreType.DMA((2 + 3 * (wide // 512),)),
+        ],
         compiler_params=pltpu.CompilerParams(vmem_limit_bytes=VMEM),
         cost_estimate=pl.CostEstimate(
             flops=2 * wide * (tall * depth + 4 * rows * capacity),
@@ -333,18 +382,21 @@
     where = lax.dynamic_index_in_dim(jnp.asarray(table.reshape(2 * experts, layers, 20)), device, 0, keepdims=False)
     code = lax.all_to_all(codes_of(expert_ids, numerators, experts), "expert", split_axis=0, concat_axis=0, tiled=True)
 
-    shard, kept, hiddens = tokens, [], []
+    kept, hiddens = [], []
+    near = move(tokens, first)
+    later = move(tokens, onward)
+    near, code, where = lax.optimization_barrier((near, code, where))
+    near_later = move(near, onward)
+    pair = jnp.stack([tokens, near])
     for k in range(layers):
-        later = move(shard, onward) if k < layers - 1 else None
-        a = move(shard, first)
-        b = move(shard, second)
         if k == 0:
-            a, code, where = lax.optimization_barrier((a, code, where))
-        d = move(a, second)
-        pieces = [shard, a, b, d]
-        pieces += [move(v, sibling) for v in pieces]
+            after = jnp.stack([later, near_later])
+        else:
+            after = move(pair, onward) if k < layers - 1 else None
+        cross = move(pair, second)
+        pairs = [pair, cross, move(pair, sibling), move(cross, sibling)]
         earlier = hiddens[-1:] + [keep for keep, _, _ in kept[-2:-1]]
-        mine = pick_call(k, where, code, pieces, gate_up_weight[0], earlier, capacity)
+        mine = pick_call(k, where, code, pairs, gate_up_weight[0], earlier, capacity)
         other = move(mine, over_x)
         keep, send = sum_call(k, where, code, mine, other, down_weight[0], capacity)
         got = move(send, sibling)
@@ -352,7 +404,7 @@
         back = move(away, over_y)
         kept.append((keep, got, back))
         hiddens.append(mine)
-        shard = later
+        pair = after
 
     total = None
     for k in [*range(1, layers), 0]:

time: 233 us -> 238 us (1.021)
  waiting for transfers between devices: 96.5 us -> 104 us
  Pallas kernels: 74.2 us -> 68.6 us
    ppermute x46 -> x32, waiting for transfers between devices: 91.4 us -> 98.4 us  [move(): return lax.ppermute(value, axes, moves)]
    pallas_call x8, Pallas kernels: 74.2 us -> 68.6 us  [the longest x4 40.6 us: pick_call(): pl.pallas_call(functools.partial(pick_kernel, capacity, k), in_specs=[pl....]
    unnamed x50 -> x32, local copies, waits for them, and re-layouts: 2.95 us -> 5.31 us
    ppermute x46 -> x32, starting transfers between devices: 40.8 us -> 39.1 us  [move(): return lax.ppermute(value, axes, moves)]
  transfers between devices with their start and end apart: 47 -> 33, of which waited for: 13 -> 14; matrix products, arithmetic and copies ran while one was open for 5% -> 6% of each run, Pallas kernels for 32% -> 29%
where the time goes in v4:
time: 238 us; the launch traced here: 237 us
  waiting for transfers between devices  104 us (44%)
  Pallas kernels  68.6 us (29%)
  starting transfers between devices  44.1 us (19%)
  other arithmetic  12.4 us (5%)
  local copies, waits for them, and re-layouts  6.58 us (3%)
    ppermute x32, waiting for transfers between devices, move(): return lax.ppermute(value, axes, moves)  98.4 us
    pallas_call x4, Pallas kernels, pick_call(): pl.pallas_call(functools.partial(pick_kernel, capacity, k), in_specs=[pl....  40.6 us
    ppermute x32, starting transfers between devices, move(): return lax.ppermute(value, axes, moves)  39.1 us
    pallas_call x4, Pallas kernels, sum_call(): pl.pallas_call(functools.partial(sum_kernel, capacity, k), in_specs=[pl.B...  28 us
    convert_element_type x4, other arithmetic, pair_shards(): total = functools.reduce(jnp.add, terms).astype(jnp.bfloat16)  6.1 us
    all_to_all x1, waiting for transfers between devices, pair_shards(): lax.all_to_all(codes_of(expert_ids, numerators, experts), 'expert', split...  5.71 us
    unnamed x32, local copies, waits for them, and re-layouts  5.31 us
    all_to_all x1, starting transfers between devices, pair_shards(): lax.all_to_all(codes_of(expert_ids, numerators, experts), 'expert', split...  4.93 us
  transfers between devices with their start and end apart: 33, of which 14 were waited for; matrix products, arithmetic and copies ran while one was open for 6% of the time, Pallas kernels for 29%

profile of v4, /device:TPU:0, one launch (start us, length us, event | category | flops | bytes accessed | tf_op | source)
XLA Modules:
  0.0 236.9 jit_solution(6049000659975138463)
XLA Ops:
  0.0 2.9 %collective-permute-start = (bf16[128,2048]{1,0:T(8,128)(2,1)}, bf16[128,2048]{1,0:T(8,128)(2,1)S(1)}, u32[]{:S(2)}, u32[]{:S(2)}) collective-permute-start(bf16[128,2048]{1,0:T(8,128)(2,1)} %param.6), channel_id=1, source_target_pairs={{0,16},{1,3},{2,18},{3,1},{4,20},{5,7},{6,22},{7,5},{8,24},{9,11},... | collective-permute-start | bytes 1572872 | tf_op jit(solution)/shard_map/ppermute | solution.py:371
  6.7 4.9 %all-to-all-start = ((s32[16,1,128]{2,1,0:T(1,128)}), s32[16,1,128]{2,1,0:T(1,128)S(1)}, u32[]{:S(2)}, u32[]{:S(2)}) async-start(s32[16,1,128]{2,1,0:T(1,128)} %bitcast.3), calls=%async_computation | async-start | bytes 16384 | tf_op jit(solution)/shard_map/all_to_all | solution.py:383
  12.9 5.7 %all-to-all-done = s32[16,1,128]{2,1,0:T(1,128)S(1)} async-done(((s32[16,1,128]{2,1,0:T(1,128)}), s32[16,1,128]{2,1,0:T(1,128)S(1)}, u32[]{:S(2)}, u32[]{:S(2)}) %all-to-all-start) | async-done | bytes 8224 | tf_op jit(solution)/shard_map/all_to_all | solution.py:383
  21.9 11.3 %collective-permute-done.8 = bf16[128,2048]{1,0:T(8,128)(2,1)S(1)} collective-permute-done((bf16[128,2048]{1,0:T(8,128)(2,1)S(1)}, bf16[128,2048]{1,0:T(8,128)(2,1)S(1)}, u32[]{:S(2)}, u32[]{:S(2)}) %collective-permute-start.8) | collective-permute-done | bytes 524320 | tf_op jit(solution)/shard_map/ppermute | solution.py:371
  35.7 12.6 %collective-permute-done.17.refs_1_ = bf16[2,128,2048]{2,1,0:T(8,128)(2,1)} collective-permute-done((bf16[2,128,2048]{2,1,0:T(8,128)(2,1)S(1)}, bf16[2,128,2048]{2,1,0:T(8,128)(2,1)}, u32[]{:S(2)}, u32[]{:S(2)}) %collective-permute-start.17) | collective-permute-done | bytes 1048608 | tf_op jit(solution)/shard_map/ppermute | solution.py:371
  48.3 11.3 %collective-permute-done.9.refs_0_ = bf16[2,128,2048]{2,1,0:T(8,128)(2,1)} collective-permute-done((bf16[2,128,2048]{2,1,0:T(8,128)(2,1)S(1)}, bf16[2,128,2048]{2,1,0:T(8,128)(2,1)}, u32[]{:S(2)}, u32[]{:S(2)}) %collective-permute-start.9) | collective-permute-done | bytes 1048608 | tf_op jit(solution)/shard_map/ppermute | solution.py:371
  63.1 10.1 %gate_up.4.mine_hbm.refs_5_ = bf16[320,768]{1,0:T(8,128)(2,1)} custom-call(s32[4,20]{1,0:T(4,128)} %dynamic-slice_bitcast_fusion.where_ref, s32[16,128]{1,0:T(8,128)} %bitcast.53, bf16[2,128,2048]{2,1,0:T(8,128)(2,1)} %copy-done.3, bf16[2,128,2048]{2,1,0:T(8,128)(2,1)} %copy-done.8, bf16[2,128,2048]{2,1,0:T(8,128)(2,1)} %copy-done.10, ...), custom_call_target="tpu_custom_call" | custom-call | flops 4362076160 | bytes 17268736 | tf_op jit(solution)/shard_map/gate_up/pallas_call | solution.py:253
  73.2 10.2 %gate_up.5.refs_5_.mine_hbm = bf16[320,768]{1,0:T(8,128)(2,1)} custom-call(s32[4,20]{1,0:T(4,128)} %dynamic-slice_bitcast_fusion.where_ref, s32[16,128]{1,0:T(8,128)} %bitcast.54, bf16[2,128,2048]{2,1,0:T(8,128)(2,1)} %copy-done.4, bf16[2,128,2048]{2,1,0:T(8,128)(2,1)} %collective-permute-done.17.refs_1_, ...), custom_call_target="tpu_custom_call" | custom-call | flops 4362076160 | bytes 17268736 | tf_op jit(solution)/shard_map/gate_up/pallas_call | solution.py:253
  88.4 9.5 %collective-permute-done.20.other_hbm = bf16[320,768]{1,0:T(8,128)(2,1)S(1)} collective-permute-done((bf16[320,768]{1,0:T(8,128)(2,1)}, bf16[320,768]{1,0:T(8,128)(2,1)S(1)}, u32[]{:S(2)}, u32[]{:S(2)}) %collective-permute-start.20) | collective-permute-done | bytes 491552 | tf_op jit(solution)/shard_map/ppermute | solution.py:371
  98.7 7.0 %down.5 = (bf16[2,128,2048]{2,1,0:T(8,128)(2,1)}, bf16[2,128,2048]{2,1,0:T(8,128)(2,1)}) custom-call(s32[4,20]{1,0:T(4,128)} %dynamic-slice_bitcast_fusion.where_ref, s32[16,128]{1,0:T(8,128)} %bitcast.55, bf16[320,768]{1,0:T(8,128)(2,1)} %gate_up.5.refs_5_.mine_hbm, bf16[320,768]{1,0:T(8,128)(2,1)} %copy-done.13, bf16[1536,2048]{1,0:T(8,128)(2,1)} %bitcast.64), custom_call_target="tpu_custom_call" | custom-call | flops 2181038080 | bytes 9371648 | tf_op jit(solution)/shard_map/down/pallas_call | solution.py:283
  109.2 7.0 %down.4 = (bf16[2,128,2048]{2,1,0:T(8,128)(2,1)}, bf16[2,128,2048]{2,1,0:T(8,128)(2,1)}) custom-call(s32[4,20]{1,0:T(4,128)} %dynamic-slice_bitcast_fusion.where_ref, s32[16,128]{1,0:T(8,128)} %bitcast.56, bf16[320,768]{1,0:T(8,128)(2,1)} %gate_up.4.mine_hbm.refs_5_, bf16[320,768]{1,0:T(8,128)(2,1)} %copy-done.14, bf16[1536,2048]{1,0:T(8,128)(2,1)} %bitcast.65), custom_call_target="tpu_custom_call" | custom-call | flops 2181038080 | bytes 9371648 | tf_op jit(solution)/shard_map/down/pallas_call | solution.py:283
  116.2 6.4 %collective-permute-start.12 = (bf16[2,128,2048]{2,1,0:T(8,128)(2,1)S(1)}, bf16[2,128,2048]{2,1,0:T(8,128)(2,1)}, u32[]{:S(2)}, u32[]{:S(2)}) collective-permute-start(bf16[2,128,2048]{2,1,0:T(8,128)(2,1)S(1)} %collective-permute-done.10.refs_0_), channel_id=1, source_target_pairs={{0,1},{1,0},{2,3},{3,2},{4,5},{5,4},{6,7},{7,6},{8,9},{9,8},{10,11... | collective-permute-start | bytes 3145736 | tf_op jit(solution)/shard_map/ppermute | solution.py:371
  123.7 10.1 %gate_up.6.refs_5_.mine_hbm = bf16[320,768]{1,0:T(8,128)(2,1)} custom-call(s32[4,20]{1,0:T(4,128)} %dynamic-slice_bitcast_fusion.where_ref, s32[16,128]{1,0:T(8,128)} %bitcast.57, bf16[2,128,2048]{2,1,0:T(8,128)(2,1)} %collective-permute-done.9.refs_0_, bf16[2,128,2048]{2,1,0:T(8,128)(2,1)} %collective-permute-done.14.refs_1_, ...), custom_call_target="tpu_custom_call" | custom-call | flops 4362076160 | bytes 17268736 | tf_op jit(solution)/shard_map/gate_up/pallas_call | solution.py:253
  139.3 8.4 %collective-permute-done.24.other_hbm = bf16[320,768]{1,0:T(8,128)(2,1)S(1)} collective-permute-done((bf16[320,768]{1,0:T(8,128)(2,1)}, bf16[320,768]{1,0:T(8,128)(2,1)S(1)}, u32[]{:S(2)}, u32[]{:S(2)}) %collective-permute-start.24) | collective-permute-done | bytes 491552 | tf_op jit(solution)/shard_map/ppermute | solution.py:371
  148.5 7.0 %down.7 = (bf16[2,128,2048]{2,1,0:T(8,128)(2,1)}, bf16[2,128,2048]{2,1,0:T(8,128)(2,1)}) custom-call(s32[4,20]{1,0:T(4,128)} %dynamic-slice_bitcast_fusion.where_ref, s32[16,128]{1,0:T(8,128)} %bitcast.58, bf16[320,768]{1,0:T(8,128)(2,1)} %gate_up.6.refs_5_.mine_hbm, bf16[320,768]{1,0:T(8,128)(2,1)} %copy-done.15, bf16[1536,2048]{1,0:T(8,128)(2,1)} %bitcast.66), custom_call_target="tpu_custom_call" | custom-call | flops 2181038080 | bytes 9371648 | tf_op jit(solution)/shard_map/down/pallas_call | solution.py:283
  155.6 10.2 %gate_up.7.mine_hbm = bf16[320,768]{1,0:T(8,128)(2,1)} custom-call(s32[4,20]{1,0:T(4,128)} %dynamic-slice_bitcast_fusion.where_ref, s32[16,128]{1,0:T(8,128)} %bitcast.59, bf16[2,128,2048]{2,1,0:T(8,128)(2,1)} %copy-done.6, bf16[2,128,2048]{2,1,0:T(8,128)(2,1)} %collective-permute-done.11.refs_1_, bf16[2,128,2048]{2,1,0:T(8,128)(2,1)} %collective-permute-done.12.refs_2_, ...), custom_call_target="tpu_custom_call" | custom-call | flops 4362076160 | bytes 17268736 | tf_op jit(solution)/shard_map/gate_up/pallas_call | solution.py:253
  169.9 2.9 %collective-permute-start.29 = (bf16[128,2048]{1,0:T(8,128)(2,1)}, bf16[128,2048]{1,0:T(8,128)(2,1)S(1)}, u32[]{:S(2)}, u32[]{:S(2)}) collective-permute-start(bf16[128,2048]{1,0:T(8,128)(2,1)} %fusion.3), channel_id=1, source_target_pairs={{0,4},{1,5},{2,6},{3,7},{4,12},{5,13},{6,14},{7,15},{8,0},{9,1},{1... | collective-permute-start | bytes 1572872 | tf_op jit(solution)/shard_map/ppermute | solution.py:371
  172.8 6.9 %collective-permute-done.21.other_hbm = bf16[320,768]{1,0:T(8,128)(2,1)} collective-permute-done((bf16[320,768]{1,0:T(8,128)(2,1)}, bf16[320,768]{1,0:T(8,128)(2,1)}, u32[]{:S(2)}, u32[]{:S(2)}) %collective-permute-start.21) | collective-permute-done | bytes 491552 | tf_op jit(solution)/shard_map/ppermute | solution.py:371
  179.7 7.0 %down.6 = (bf16[2,128,2048]{2,1,0:T(8,128)(2,1)}, bf16[2,128,2048]{2,1,0:T(8,128)(2,1)}) custom-call(s32[4,20]{1,0:T(4,128)} %dynamic-slice_bitcast_fusion.where_ref, s32[16,128]{1,0:T(8,128)} %bitcast.60, bf16[320,768]{1,0:T(8,128)(2,1)} %gate_up.7.mine_hbm, bf16[320,768]{1,0:T(8,128)(2,1)} %collective-permute-done.21.other_hbm, bf16[1536,2048]{1,0:T(8,128)(2,1)} %bitcast.67), custom_call_target="tpu_custom_call" | custom-call | flops 2181038080 | bytes 9371648 | tf_op jit(solution)/shard_map/down/pallas_call | solution.py:283
  190.7 12.4 %collective-permute-done.26 = bf16[128,2048]{1,0:T(8,128)(2,1)S(1)} collective-permute-done((bf16[128,2048]{1,0:T(8,128)(2,1)S(1)}, bf16[128,2048]{1,0:T(8,128)(2,1)S(1)}, u32[]{:S(2)}, u32[]{:S(2)}) %collective-permute-start.26) | collective-permute-done | bytes 524320 | tf_op jit(solution)/shard_map/ppermute | solution.py:371
  210.1 9.0 %collective-permute-done.30 = bf16[128,2048]{1,0:T(8,128)(2,1)S(1)} collective-permute-done((bf16[128,2048]{1,0:T(8,128)(2,1)S(1)}, bf16[128,2048]{1,0:T(8,128)(2,1)S(1)}, u32[]{:S(2)}, u32[]{:S(2)}) %collective-permute-start.30) | collective-permute-done | bytes 524320 | tf_op jit(solution)/shard_map/ppermute | solution.py:371
  219.1 3.7 %collective-permute-done.23 = bf16[128,2048]{1,0:T(8,128)(2,1)S(1)} collective-permute-done((bf16[128,2048]{1,0:T(8,128)(2,1)S(1)}, bf16[128,2048]{1,0:T(8,128)(2,1)S(1)}, u32[]{:S(2)}, u32[]{:S(2)}) %collective-permute-start.23) | collective-permute-done | bytes 524320 | tf_op jit(solution)/shard_map/ppermute | solution.py:371
  225.4 7.0 %collective-permute-done.6 = bf16[128,2048]{1,0:T(8,128)(2,1)S(1)} collective-permute-done((bf16[128,2048]{1,0:T(8,128)(2,1)S(1)}, bf16[128,2048]{1,0:T(8,128)(2,1)S(1)}, u32[]{:S(2)}, u32[]{:S(2)}) %collective-permute-start.6) | collective-permute-done | bytes 524320 | tf_op jit(solution)/shard_map/ppermute | solution.py:371
  232.4 3.4 %collective-permute-done.31 = bf16[128,2048]{1,0:T(8,128)(2,1)S(1)} collective-permute-done((bf16[128,2048]{1,0:T(8,128)(2,1)S(1)}, bf16[128,2048]{1,0:T(8,128)(2,1)S(1)}, u32[]{:S(2)}, u32[]{:S(2)}) %collective-permute-start.31) | collective-permute-done | bytes 524320 | tf_op jit(solution)/shard_map/ppermute | solution.py:371
  (96 shorter events, 49.6 us)
Async XLA Ops:
  0.0 18.6 %collective-permute-start = (bf16[128,2048]{1,0:T(8,128)(2,1)}, bf16[128,2048]{1,0:T(8,128)(2,1)S(1)}, u32[]{:S(2)}, u32[]{:S(2)}) collective-permute-start(bf16[128,2048]{1,0:T(8,128)(2,1)} %param.6), channel_id=1, source_target_pairs={{0,16},{1,3},{2,18},{3,1},{4,20},{5,7},{6,22},{7,5},{8,24},{9,11},... | collective-permute-start | bytes 1572872 | tf_op jit(solution)/shard_map/ppermute | solution.py:371
  2.9 19.0 %collective-permute-start.7 = (bf16[128,2048]{1,0:T(8,128)(2,1)}, bf16[128,2048]{1,0:T(8,128)(2,1)S(1)}, u32[]{:S(2)}, u32[]{:S(2)}) collective-permute-start(bf16[128,2048]{1,0:T(8,128)(2,1)} %param.6), channel_id=1, source_target_pairs={{0,4},{1,5},{2,6},{3,7},{4,12},{5,13},{6,14},{7,15},{8,0},{9,1},{1... | collective-permute-start | bytes 1572872 | tf_op jit(solution)/shard_map/ppermute | solution.py:371
  33.3 15.0 %collective-permute-start.17 = (bf16[2,128,2048]{2,1,0:T(8,128)(2,1)S(1)}, bf16[2,128,2048]{2,1,0:T(8,128)(2,1)}, u32[]{:S(2)}, u32[]{:S(2)}) collective-permute-start(bf16[2,128,2048]{2,1,0:T(8,128)(2,1)S(1)} %pad_maximum_fusion.1.refs_0_), channel_id=1, source_target_pairs={{0,2},{1,17},{2,0},{3,19},{4,6},{5,21},{6,4},{7,23},{8,10},{9,25},... | collective-permute-start | bytes 3145736 | tf_op jit(solution)/shard_map/ppermute | solution.py:371
  34.9 24.8 %collective-permute-start.9 = (bf16[2,128,2048]{2,1,0:T(8,128)(2,1)S(1)}, bf16[2,128,2048]{2,1,0:T(8,128)(2,1)}, u32[]{:S(2)}, u32[]{:S(2)}) collective-permute-start(bf16[2,128,2048]{2,1,0:T(8,128)(2,1)S(1)} %pad_maximum_fusion.1.refs_0_), channel_id=1, source_target_pairs={{0,4},{1,5},{2,6},{3,7},{4,12},{5,13},{6,14},{7,15},{8,0},{9,1},{1... | collective-permute-start | bytes 3145736 | tf_op jit(solution)/shard_map/ppermute | solution.py:371
  34.9 26.3 %collective-permute-start.2 = (bf16[2,128,2048]{2,1,0:T(8,128)(2,1)S(1)}, bf16[2,128,2048]{2,1,0:T(8,128)(2,1)S(1)}, u32[]{:S(2)}, u32[]{:S(2)}) collective-permute-start(bf16[2,128,2048]{2,1,0:T(8,128)(2,1)S(1)} %pad_maximum_fusion.refs_0_), channel_id=1, source_target_pairs={{0,1},{1,0},{2,3},{3,2},{4,5},{5,4},{6,7},{7,6},{8,9},{9,8},{10,11... | collective-permute-start | bytes 3145736 | tf_op jit(solution)/shard_map/ppermute | solution.py:371
  35.2 26.0 %collective-permute-start.3 = (bf16[2,128,2048]{2,1,0:T(8,128)(2,1)S(1)}, bf16[2,128,2048]{2,1,0:T(8,128)(2,1)S(1)}, u32[]{:S(2)}, u32[]{:S(2)}) collective-permute-start(bf16[2,128,2048]{2,1,0:T(8,128)(2,1)S(1)} %collective-permute-done.1.refs_1_), channel_id=1, source_target_pairs={{0,1},{1,0},{2,3},{3,2},{4,5},{5,4},{6,7},{7,6},{8,9},{9,8},{10,11... | collective-permute-start | bytes 3145736 | tf_op jit(solution)/shard_map/ppermute | solution.py:371
  35.4 37.8 %collective-permute-start.18 = (bf16[2,128,2048]{2,1,0:T(8,128)(2,1)S(1)}, bf16[2,128,2048]{2,1,0:T(8,128)(2,1)}, u32[]{:S(2)}, u32[]{:S(2)}) collective-permute-start(bf16[2,128,2048]{2,1,0:T(8,128)(2,1)S(1)} %pad_maximum_fusion.1.refs_0_), channel_id=1, source_target_pairs={{0,1},{1,0},{2,3},{3,2},{4,5},{5,4},{6,7},{7,6},{8,9},{9,8},{10,11... | collective-permute-start | bytes 3145736 | tf_op jit(solution)/shard_map/ppermute | solution.py:371
  48.3 24.9 %collective-permute-start.19 = (bf16[2,128,2048]{2,1,0:T(8,128)(2,1)}, bf16[2,128,2048]{2,1,0:T(8,128)(2,1)}, u32[]{:S(2)}, u32[]{:S(2)}) collective-permute-start(bf16[2,128,2048]{2,1,0:T(8,128)(2,1)} %collective-permute-done.17.refs_1_), channel_id=1, source_target_pairs={{0,1},{1,0},{2,3},{3,2},{4,5},{5,4},{6,7},{7,6},{8,9},{9,8},{10,11... | collective-permute-start | bytes 3145736 | tf_op jit(solution)/shard_map/ppermute | solution.py:371
  59.6 26.5 %collective-permute-start.14 = (bf16[2,128,2048]{2,1,0:T(8,128)(2,1)}, bf16[2,128,2048]{2,1,0:T(8,128)(2,1)}, u32[]{:S(2)}, u32[]{:S(2)}) collective-permute-start(bf16[2,128,2048]{2,1,0:T(8,128)(2,1)} %collective-permute-done.9.refs_0_), channel_id=1, source_target_pairs={{0,2},{1,17},{2,0},{3,19},{4,6},{5,21},{6,4},{7,23},{8,10},{9,25},... | collective-permute-start | bytes 3145736 | tf_op jit(solution)/shard_map/ppermute | solution.py:371
  61.1 22.9 %collective-permute-start.10 = (bf16[2,128,2048]{2,1,0:T(8,128)(2,1)}, bf16[2,128,2048]{2,1,0:T(8,128)(2,1)S(1)}, u32[]{:S(2)}, u32[]{:S(2)}) collective-permute-start(bf16[2,128,2048]{2,1,0:T(8,128)(2,1)} %collective-permute-done.9.refs_0_), channel_id=1, source_target_pairs={{0,4},{1,5},{2,6},{3,7},{4,12},{5,13},{6,14},{7,15},{8,0},{9,1},{1... | collective-permute-start | bytes 3145736 | tf_op jit(solution)/shard_map/ppermute | solution.py:371
  84.1 38.6 %collective-permute-start.11 = (bf16[2,128,2048]{2,1,0:T(8,128)(2,1)S(1)}, bf16[2,128,2048]{2,1,0:T(8,128)(2,1)}, u32[]{:S(2)}, u32[]{:S(2)}) collective-permute-start(bf16[2,128,2048]{2,1,0:T(8,128)(2,1)S(1)} %collective-permute-done.10.refs_0_), channel_id=1, source_target_pairs={{0,2},{1,17},{2,0},{3,19},{4,6},{5,21},{6,4},{7,23},{8,10},{9,25},... | collective-permute-start | bytes 3145736 | tf_op jit(solution)/shard_map/ppermute | solution.py:371
  86.1 36.6 %collective-permute-start.15 = (bf16[2,128,2048]{2,1,0:T(8,128)(2,1)}, bf16[2,128,2048]{2,1,0:T(8,128)(2,1)S(1)}, u32[]{:S(2)}, u32[]{:S(2)}) collective-permute-start(bf16[2,128,2048]{2,1,0:T(8,128)(2,1)} %collective-permute-done.9.refs_0_), channel_id=1, source_target_pairs={{0,1},{1,0},{2,3},{3,2},{4,5},{5,4},{6,7},{7,6},{8,9},{9,8},{10,11... | collective-permute-start | bytes 3145736 | tf_op jit(solution)/shard_map/ppermute | solution.py:371
  86.1 36.6 %collective-permute-start.16 = (bf16[2,128,2048]{2,1,0:T(8,128)(2,1)}, bf16[2,128,2048]{2,1,0:T(8,128)(2,1)}, u32[]{:S(2)}, u32[]{:S(2)}) collective-permute-start(bf16[2,128,2048]{2,1,0:T(8,128)(2,1)} %collective-permute-done.14.refs_1_), channel_id=1, source_target_pairs={{0,1},{1,0},{2,3},{3,2},{4,5},{5,4},{6,7},{7,6},{8,9},{9,8},{10,11... | collective-permute-start | bytes 3145736 | tf_op jit(solution)/shard_map/ppermute | solution.py:371
  86.6 21.8 %collective-permute-start.4 = (bf16[320,768]{1,0:T(8,128)(2,1)S(1)}, bf16[320,768]{1,0:T(8,128)(2,1)S(1)}, u32[]{:S(2)}, u32[]{:S(2)}) collective-permute-start(bf16[320,768]{1,0:T(8,128)(2,1)S(1)} %copy-done.5), channel_id=1, source_target_pairs={{0,16},{1,17},{2,18},{3,19},{4,20},{5,21},{6,22},{7,23},{8,24},{9,... | collective-permute-start | bytes 1474568 | tf_op jit(solution)/shard_map/ppermute | solution.py:371
  105.8 29.9 %collective-permute-start.27 = (bf16[2,128,2048]{2,1,0:T(8,128)(2,1)}, bf16[2,128,2048]{2,1,0:T(8,128)(2,1)}, u32[]{:S(2)}, u32[]{:S(2)}) collective-permute-start(bf16[2,128,2048]{2,1,0:T(8,128)(2,1)} %get-tuple-element.26), channel_id=1, source_target_pairs={{0,1},{1,0},{2,3},{3,2},{4,5},{5,4},{6,7},{7,6},{8,9},{9,8},{10,11... | collective-permute-start | bytes 3145736 | tf_op jit(solution)/shard_map/ppermute | solution.py:371
  116.2 39.4 %collective-permute-start.12 = (bf16[2,128,2048]{2,1,0:T(8,128)(2,1)S(1)}, bf16[2,128,2048]{2,1,0:T(8,128)(2,1)}, u32[]{:S(2)}, u32[]{:S(2)}) collective-permute-start(bf16[2,128,2048]{2,1,0:T(8,128)(2,1)S(1)} %collective-permute-done.10.refs_0_), channel_id=1, source_target_pairs={{0,1},{1,0},{2,3},{3,2},{4,5},{5,4},{6,7},{7,6},{8,9},{9,8},{10,11... | collective-permute-start | bytes 3145736 | tf_op jit(solution)/shard_map/ppermute | solution.py:371
  122.6 33.0 %collective-permute-start.13 = (bf16[2,128,2048]{2,1,0:T(8,128)(2,1)}, bf16[2,128,2048]{2,1,0:T(8,128)(2,1)}, u32[]{:S(2)}, u32[]{:S(2)}) collective-permute-start(bf16[2,128,2048]{2,1,0:T(8,128)(2,1)} %collective-permute-done.11.refs_1_), channel_id=1, source_target_pairs={{0,1},{1,0},{2,3},{3,2},{4,5},{5,4},{6,7},{7,6},{8,9},{9,8},{10,11... | collective-permute-start | bytes 3145736 | tf_op jit(solution)/shard_map/ppermute | solution.py:371
  136.8 30.9 %collective-permute-start.28 = (bf16[128,2048]{1,0:T(8,128)(2,1)S(1)}, bf16[128,2048]{1,0:T(8,128)(2,1)}, u32[]{:S(2)}, u32[]{:S(2)}) collective-permute-start(bf16[128,2048]{1,0:T(8,128)(2,1)S(1)} %fusion.13), channel_id=1, source_target_pairs={{0,2},{1,3},{2,0},{3,1},{4,6},{5,7},{6,4},{7,5},{8,10},{9,11},{10,... | collective-permute-start | bytes 1572872 | tf_op jit(solution)/shard_map/ppermute | solution.py:371
  155.5 31.3 %collective-permute-start.25 = (bf16[2,128,2048]{2,1,0:T(8,128)(2,1)}, bf16[2,128,2048]{2,1,0:T(8,128)(2,1)}, u32[]{:S(2)}, u32[]{:S(2)}) collective-permute-start(bf16[2,128,2048]{2,1,0:T(8,128)(2,1)} %get-tuple-element.25), channel_id=1, source_target_pairs={{0,1},{1,0},{2,3},{3,2},{4,5},{5,4},{6,7},{7,6},{8,9},{9,8},{10,11... | collective-permute-start | bytes 3145736 | tf_op jit(solution)/shard_map/ppermute | solution.py:371
  169.9 20.7 %collective-permute-start.29 = (bf16[128,2048]{1,0:T(8,128)(2,1)}, bf16[128,2048]{1,0:T(8,128)(2,1)S(1)}, u32[]{:S(2)}, u32[]{:S(2)}) collective-permute-start(bf16[128,2048]{1,0:T(8,128)(2,1)} %fusion.3), channel_id=1, source_target_pairs={{0,4},{1,5},{2,6},{3,7},{4,12},{5,13},{6,14},{7,15},{8,0},{9,1},{1... | collective-permute-start | bytes 1572872 | tf_op jit(solution)/shard_map/ppermute | solution.py:371
  186.7 20.0 %collective-permute-start.22 = (bf16[2,128,2048]{2,1,0:T(8,128)(2,1)}, bf16[2,128,2048]{2,1,0:T(8,128)(2,1)S(1)}, u32[]{:S(2)}, u32[]{:S(2)}) collective-permute-start(bf16[2,128,2048]{2,1,0:T(8,128)(2,1)} %get-tuple-element.23), channel_id=1, source_target_pairs={{0,1},{1,0},{2,3},{3,2},{4,5},{5,4},{6,7},{7,6},{8,9},{9,8},{10,11... | collective-permute-start | bytes 3145736 | tf_op jit(solution)/shard_map/ppermute | solution.py:371
  188.0 15.0 %collective-permute-start.26 = (bf16[128,2048]{1,0:T(8,128)(2,1)S(1)}, bf16[128,2048]{1,0:T(8,128)(2,1)S(1)}, u32[]{:S(2)}, u32[]{:S(2)}) collective-permute-start(bf16[128,2048]{1,0:T(8,128)(2,1)S(1)} %fusion.12), channel_id=1, source_target_pairs={{0,2},{1,3},{2,0},{3,1},{4,6},{5,7},{6,4},{7,5},{8,10},{9,11},{10,... | collective-permute-start | bytes 1572872 | tf_op jit(solution)/shard_map/ppermute | solution.py:371
  190.5 18.5 %collective-permute-start.5 = (bf16[2,128,2048]{2,1,0:T(8,128)(2,1)}, bf16[2,128,2048]{2,1,0:T(8,128)(2,1)S(1)}, u32[]{:S(2)}, u32[]{:S(2)}) collective-permute-start(bf16[2,128,2048]{2,1,0:T(8,128)(2,1)} %get-tuple-element.20), channel_id=1, source_target_pairs={{0,1},{1,0},{2,3},{3,2},{4,5},{5,4},{6,7},{7,6},{8,9},{9,8},{10,11... | collective-permute-start | bytes 3145736 | tf_op jit(solution)/shard_map/ppermute | solution.py:371
  209.1 23.2 %collective-permute-start.6 = (bf16[128,2048]{1,0:T(8,128)(2,1)S(1)}, bf16[128,2048]{1,0:T(8,128)(2,1)S(1)}, u32[]{:S(2)}, u32[]{:S(2)}) collective-permute-start(bf16[128,2048]{1,0:T(8,128)(2,1)S(1)} %fusion.10), channel_id=1, source_target_pairs={{0,2},{1,3},{2,0},{3,1},{4,6},{5,7},{6,4},{7,5},{8,10},{9,11},{10,... | collective-permute-start | bytes 1572872 | tf_op jit(solution)/shard_map/ppermute | solution.py:371
  (25 other events, 481.5 us)

commit v5 on v4

--- a/solution.py
+++ b/solution.py
@@ -147,51 +147,56 @@
     )(code.reshape(blocks // take, take, rows), hidden, weight)
 
 
-def onehot_of(code, capacity):
-    return lax.broadcasted_iota(jnp.int32, (capacity, code.shape[1]), 0) == code >> 8
+def block_codes(k, own, where_ref, code_ref):
+    return jnp.concatenate([code_ref[pl.ds(where_ref[k, 2 * own + i], 1), :] for i in range(2)], axis=0)
 
 
 def pick_kernel(capacity, k, where_ref, code_ref, *refs):
     pairs, weight_hbm = refs[:4], refs[4]
     hidden_ref, pair_ref, weight_ref, rows_ref, sems = refs[-5:]
     rows, width = pairs[0].shape[1:]
-    span = 4 * UNITS
+    span = 8 * UNITS
     spans = weight_hbm.shape[1] // span
+    x, c = where_ref[k, 4], where_ref[k, 5]
 
     def weight_copy(j):
         at = pl.ds(pl.multiple_of(j * span, span), span)
         return pltpu.make_async_copy(weight_hbm.at[:, at], weight_ref.at[:, at], sems.at[4 + j])
 
-    copies = [pltpu.make_async_copy(v, pair_ref.at[i], sems.at[i]) for i, v in enumerate(pairs)]
+    copies = [pltpu.make_async_copy(v, pair_ref.at[pl.ds(2 * i, 2)], sems.at[i]) for i, v in enumerate(pairs)]
     for copy in copies:
         copy.start()
     for j in range(spans):
         weight_copy(j).start()
-    for i, copy in enumerate(copies):
-        copy.wait()
-        for h in range(2):
-            spot = 4 + 2 * (2 * i + h)
-            block, section = where_ref[k, spot], where_ref[k, spot + 1]
-            onehot = onehot_of(code_ref[pl.ds(where_ref[k, block], 1), :], capacity).astype(jnp.bfloat16)
-            picked = jnp.dot(onehot, pair_ref[i, h], preferred_element_type=jnp.float32)
-            down = pl.ds(pl.multiple_of(block * capacity, capacity), capacity)
-            rows_ref[down, pl.ds(pl.multiple_of(section * width, width), width)] = picked.astype(jnp.bfloat16)
+    for own in range(2):
+        core = c ^ own
+        onehot, _ = slot_map(block_codes(k, own, where_ref, code_ref), 2, capacity)
+        onehot = onehot.astype(jnp.bfloat16)
+        copies[2 * own].wait()
+        copies[2 * own + 1].wait()
+        for section, near, far in ((x, 0, 2 - core), (1 - x, 1 + core, 3)):
+            block = jnp.concatenate([pair_ref[4 * own + near], pair_ref[4 * own + far]], axis=0)
+            picked = jnp.dot(onehot, block, preferred_element_type=jnp.float32)
+            at = pl.ds(pl.multiple_of(section * width, width), width)
+            rows_ref[2 * own * capacity : 2 * (own + 1) * capacity, at] = picked.astype(jnp.bfloat16)
 
     @pl.loop(0, spans)
     def _(j):
         weight_copy(j).wait()
         at = pl.ds(pl.multiple_of(j * span, span), span)
         both = jnp.dot(rows_ref[...], weight_ref[:, at], preferred_element_type=jnp.float32)
-        one, two = both[:, : 2 * UNITS], both[:, 2 * UNITS :]
-        low = lax.broadcasted_iota(jnp.int32, one.shape, 1) < UNITS
-        gate = jnp.where(low, one, pltpu.roll(two, UNITS, 1))
-        up = jnp.where(low, pltpu.roll(one, UNITS, 1), two)
-        half = pl.ds(pl.multiple_of(j * 2 * UNITS, 2 * UNITS), 2 * UNITS)
-        hidden_ref[:, half] = (gate / (1.0 + jnp.exp(-gate)) * up).astype(jnp.bfloat16)
-
-
-def sum_kernel(capacity, k, where_ref, code_ref, mine_hbm, other_hbm, weight_hbm, keep_hbm, send_hbm, *refs):
-    hidden_ref, weight_ref, out_ref, sems = refs
+        for p in range(2):
+            one, two = both[:, 4 * p * UNITS : (4 * p + 2) * UNITS], both[:, (4 * p + 2) * UNITS : 4 * (p + 1) * UNITS]
+            low = lax.broadcasted_iota(jnp.int32, one.shape, 1) < UNITS
+            gate = jnp.where(low, one, pltpu.roll(two, UNITS, 1))
+            up = jnp.where(low, pltpu.roll(one, UNITS, 1), two)
+            half = pl.ds(pl.multiple_of((2 * j + p) * 2 * UNITS, 2 * UNITS), 2 * UNITS)
+            hidden_ref[:, half] = (gate / (1.0 + jnp.exp(-gate)) * up).astype(jnp.bfloat16)
+
+
+def sum_kernel(capacity, k, where_ref, code_ref, *refs):
+    mine_hbm, other_hbm, weight_hbm = refs[:3]
+    keep_hbm, send_hbm, hidden_ref, weight_ref, out_ref, sems = refs[-6:]
     rows = code_ref.shape[1]
     units = mine_hbm.shape[1]
     span = 512
@@ -212,11 +217,10 @@
     for j in range(spans):
         weight_copy(j).start()
     scaled = []
-    for b in range(4):
-        code = code_ref[pl.ds(where_ref[k, b], 1), :]
-        scale = (code & 255).astype(jnp.float32) * SCALE
-        scaled.append(jnp.where(onehot_of(code, capacity), scale, 0.0).astype(jnp.bfloat16))
-    me = where_ref[k, 5]
+    for own in range(2):
+        onehot, weight = slot_map(block_codes(k, own, where_ref, code_ref), 2, capacity)
+        scaled.append(jnp.where(onehot, weight.astype(jnp.float32) * SCALE, 0.0).astype(jnp.bfloat16))
+    me = where_ref[k, 4]
     mine_at = pl.ds(pl.multiple_of(me * units, units), units)
     other_at = pl.ds(pl.multiple_of((1 - me) * units, units), units)
     for copy in copies:
@@ -229,14 +233,14 @@
         total = jnp.dot(hidden_ref[0], weight_ref[mine_at, at], preferred_element_type=jnp.float32)
         total += jnp.dot(hidden_ref[1], weight_ref[other_at, at], preferred_element_type=jnp.float32)
         result = total.astype(jnp.bfloat16)
-        for b in range(4):
+        for own in range(2):
             mixed = lax.dot_general(
-                scaled[b],
-                result[b * capacity : (b + 1) * capacity],
+                scaled[own],
+                result[2 * own * capacity : 2 * (own + 1) * capacity],
                 (((0,), (0,)), ((), ())),
                 preferred_element_type=jnp.float32,
             )
-            out_ref[b, :, at] = mixed.astype(jnp.bfloat16)
+            out_ref[2 * own : 2 * own + 2, :, at] = mixed.astype(jnp.bfloat16).reshape(2, rows, span)
         out_copy(j, 0, keep_hbm).start()
         out_copy(j, 1, send_hbm).start()
 
@@ -260,10 +264,10 @@
         out_specs=pl.BlockSpec(memory_space=pltpu.VMEM),
         out_shape=jax.ShapeDtypeStruct((tall, columns // 2), jnp.bfloat16),
         scratch_shapes=[
-            pltpu.VMEM((4, 2, rows, width), jnp.bfloat16),
+            pltpu.VMEM((8, rows, width), jnp.bfloat16),
             pltpu.VMEM((depth, columns), jnp.bfloat16),
             pltpu.VMEM((tall, depth), jnp.bfloat16),
-            pltpu.SemaphoreType.DMA((4 + columns // (4 * UNITS),)),
+            pltpu.SemaphoreType.DMA((4 + columns // (8 * UNITS),)),
         ],
         compiler_params=pltpu.CompilerParams(vmem_limit_bytes=VMEM),
         cost_estimate=pl.CostEstimate(
@@ -275,7 +279,7 @@
     )(where, code, *pairs, weight, *earlier)
 
 
-def sum_call(k, where, code, mine, other, weight, capacity):
+def sum_call(k, where, code, mine, other, weight, earlier, capacity):
     rows = code.shape[1]
     depth, wide = weight.shape
     tall, units = mine.shape
@@ -285,7 +289,7 @@
         in_specs=[
             pl.BlockSpec(memory_space=pltpu.SMEM),
             pl.BlockSpec(memory_space=pltpu.VMEM),
-            *[anywhere] * 3,
+            *[anywhere] * (3 + len(earlier)),
         ],
         out_specs=[anywhere] * 2,
         out_shape=[jax.ShapeDtypeStruct((2, rows, wide), jnp.bfloat16)] * 2,
@@ -302,7 +306,7 @@
             transcendentals=0,
         ),
         name="down",
-    )(where, code, mine, other, weight)
+    )(where, code, mine, other, weight, *earlier)
 
 
 def codes_of(expert_ids, numerators, experts):
@@ -370,50 +374,64 @@
     def move(value, moves):
         return lax.ppermute(value, axes, moves)
 
-    table = np.zeros((2, layers, 2, 2, layers, 20), np.int32)
+    table = np.zeros((2, layers, 2, 2, layers, 6), np.int32)
     for x, z, y, c, k in np.ndindex(2, layers, 2, 2, layers):
         at = ring[(ring.index(z) - k) % layers] * 4
-        row = [at + (y ^ (i & 1)) * 2 + (c ^ (i >> 1)) for i in range(4)]
-        for own in (0, 1):
-            core, base = c ^ own, 2 * own
-            row += [base, x, base + core, x ^ (1 - core), base + 1 - core, x ^ core, base + 1, 1 - x]
-        table[x, z, y, c, k] = row
+        table[x, z, y, c, k] = [at + (y ^ (i & 1)) * 2 + (c ^ (i >> 1)) for i in range(4)] + [x, c]
     device = lax.axis_index("section") * experts + lax.axis_index("expert")
-    where = lax.dynamic_index_in_dim(jnp.asarray(table.reshape(2 * experts, layers, 20)), device, 0, keepdims=False)
+    where = lax.dynamic_index_in_dim(jnp.asarray(table.reshape(2 * experts, layers, 6)), device, 0, keepdims=False)
     code = lax.all_to_all(codes_of(expert_ids, numerators, experts), "expert", split_axis=0, concat_axis=0, tiled=True)
 
-    kept, hiddens = [], []
-    near = move(tokens, first)
     later = move(tokens, onward)
-    near, code, where = lax.optimization_barrier((near, code, where))
-    near_later = move(near, onward)
-    pair = jnp.stack([tokens, near])
-    for k in range(layers):
+    pairs = [jnp.stack([v, move(v, first)]) for v in (tokens, later)]
+
+    mine, keeps, backs, hops, sums = [], [], [], [], []
+
+    def spread(k):
+        nonlocal code, where
+        cross = move(pairs[k], second)
         if k == 0:
-            after = jnp.stack([later, near_later])
-        else:
-            after = move(pair, onward) if k < layers - 1 else None
-        cross = move(pair, second)
-        pairs = [pair, cross, move(pair, sibling), move(cross, sibling)]
-        earlier = hiddens[-1:] + [keep for keep, _, _ in kept[-2:-1]]
-        mine = pick_call(k, where, code, pairs, gate_up_weight[0], earlier, capacity)
-        other = move(mine, over_x)
-        keep, send = sum_call(k, where, code, mine, other, down_weight[0], capacity)
+            cross, code, where = lax.optimization_barrier((cross, code, where))
+        return [pairs[k], cross, move(pairs[k], sibling), move(cross, sibling)]
+
+    def gate_up(k, shards_of, *earlier):
+        mine.append(pick_call(k, where, code, shards_of, gate_up_weight[0], mine[-1:] + list(earlier), capacity))
+
+    def down(k, *earlier):
+        other = move(mine[k], over_x)
+        keep, send = sum_call(k, where, code, mine[k], other, down_weight[0], keeps[-1:] + list(earlier), capacity)
         got = move(send, sibling)
         away = (keep[1].astype(jnp.float32) + got[1].astype(jnp.float32)).astype(jnp.bfloat16)
-        back = move(away, over_y)
-        kept.append((keep, got, back))
-        hiddens.append(mine)
-        pair = after
-
-    total = None
-    for k in [*range(1, layers), 0]:
-        keep, got, back = kept[k]
-        terms = [v.astype(jnp.float32) for v in (keep[0], got[0], back)]
-        if total is not None:
-            terms.append(move(total, onward).astype(jnp.float32))
+        keeps.append(keep)
+        backs.append(move(away, over_y))
+        sums.append((keep[0], got[0], backs[-1]))
+
+    def hop(k):
+        terms = [v.astype(jnp.float32) for v in [*sums[k], *hops[-1:]]]
         total = functools.reduce(jnp.add, terms).astype(jnp.bfloat16)
-    return total
+        if k:
+            hops.append(move(total, onward))
+        return total
+
+    for k in range(layers):
+        shards_of = spread(k)
+        if k + 2 < layers:
+            pairs.append(move(pairs[k + 1], onward))
+        gate_up(k, shards_of, *keeps[-1:], *pairs[k + 1 : k + 2], *backs[:-1][-1:])
+        if k == 0 and layers > 2:
+            pairs[2], _ = lax.optimization_barrier((pairs[2], mine[0]))
+        if k == 1:
+            down(0, mine[1])
+            if layers > 3:
+                pairs[3], _ = lax.optimization_barrier((pairs[3], keeps[0]))
+            down(1)
+        if k > 2:
+            down(k - 1, mine[k], backs[k - 2])
+            hop(k - 2)
+    hop(layers - 2)
+    down(layers - 1, *hops[:1])
+    hop(layers - 1)
+    return hop(0)
 
 
 def solution(mesh):
@@ -425,5 +443,5 @@
         P("expert", None, "section"),
     )
     out_specs = P("expert", "section")
-    fits = mesh.shape["section"] == 2 and mesh.shape["expert"] % 4 == 0
+    fits = mesh.shape["section"] == 2 and mesh.shape["expert"] == 16
     return jax.shard_map(pair_shards if fits else shards, mesh=mesh, in_specs=in_specs, out_specs=out_specs, check_vma=False)

time: 238 us -> 227 us (0.954)
  starting transfers between devices: 44.1 us -> 36.1 us
  local copies, waits for them, and re-layouts: 6.58 us -> 2.91 us
    ppermute x32, starting transfers between devices: 39.1 us -> 31.2 us  [move(): return lax.ppermute(value, axes, moves)]
    unnamed x32, local copies, waits for them, and re-layouts: 5.31 us -> 1.64 us
  transfers between devices with their start and end apart: 33 -> 33, of which waited for: 14 -> 13; matrix products, arithmetic and copies ran while one was open for 6% -> 6% of each run, Pallas kernels for 29% -> 30%
where the time goes in v5:
time: 227 us; the launch traced here: 226 us
  waiting for transfers between devices  103 us (45%)
  Pallas kernels  68.9 us (30%)
  starting transfers between devices  36.1 us (16%)
  other arithmetic  14.3 us (6%)
  local copies, waits for them, and re-layouts  2.91 us (1%)
    ppermute x32, waiting for transfers between devices, move(): return lax.ppermute(value, axes, moves)  98 us
    pallas_call x4, Pallas kernels, pick_call(): pl.pallas_call(functools.partial(pick_kernel, capacity, k), in_specs=[pl....  40.2 us
    ppermute x32, starting transfers between devices, move(): return lax.ppermute(value, axes, moves)  31.2 us
    pallas_call x4, Pallas kernels, sum_call(): pl.pallas_call(functools.partial(sum_kernel, capacity, k), in_specs=[pl.B...  28.6 us
    convert_element_type x4, other arithmetic, hop(): total = functools.reduce(jnp.add, terms).astype(jnp.bfloat16)  6.45 us
    convert_element_type x4, other arithmetic, down(): (keep[1].astype(jnp.float32) + got[1].astype(jnp.float32)).astype(jnp.bfl...  5.14 us
    all_to_all x1, starting transfers between devices, pair_shards(): lax.all_to_all(codes_of(expert_ids, numerators, experts), 'expert', split...  4.92 us
    all_to_all x1, waiting for transfers between devices, pair_shards(): lax.all_to_all(codes_of(expert_ids, numerators, experts), 'expert', split...  4.76 us
  transfers between devices with their start and end apart: 33, of which 13 were waited for; matrix products, arithmetic and copies ran while one was open for 6% of the time, Pallas kernels for 30%

profile of v5, /device:TPU:0, one launch (start us, length us, event | category | flops | bytes accessed | tf_op | source)
XLA Modules:
  0.0 226.1 jit_solution(12771978534000412756)
XLA Ops:
  0.0 3.0 %collective-permute-start.4 = (bf16[128,2048]{1,0:T(8,128)(2,1)}, bf16[128,2048]{1,0:T(8,128)(2,1)S(1)}, u32[]{:S(2)}, u32[]{:S(2)}) collective-permute-start(bf16[128,2048]{1,0:T(8,128)(2,1)} %param.6), channel_id=1, source_target_pairs={{0,4},{1,5},{2,6},{3,7},{4,12},{5,13},{6,14},{7,15},{8,0},{9,1},{1... | collective-permute-start | bytes 1572872 | tf_op jit(solution)/shard_map/ppermute | solution.py:375
  4.5 11.7 %collective-permute-done.4 = bf16[128,2048]{1,0:T(8,128)(2,1)S(1)} collective-permute-done((bf16[128,2048]{1,0:T(8,128)(2,1)}, bf16[128,2048]{1,0:T(8,128)(2,1)S(1)}, u32[]{:S(2)}, u32[]{:S(2)}) %collective-permute-start.4) | collective-permute-done | bytes 524320 | tf_op jit(solution)/shard_map/ppermute | solution.py:375
  20.5 10.1 %collective-permute-done.5 = bf16[128,2048]{1,0:T(8,128)(2,1)S(1)} collective-permute-done((bf16[128,2048]{1,0:T(8,128)(2,1)S(1)}, bf16[128,2048]{1,0:T(8,128)(2,1)S(1)}, u32[]{:S(2)}, u32[]{:S(2)}) %collective-permute-start.5) | collective-permute-done | bytes 524320 | tf_op jit(solution)/shard_map/ppermute | solution.py:375
  30.6 2.1 collective-permute-start.7
  34.9 4.9 %all-to-all-start = ((s32[16,1,128]{2,1,0:T(1,128)}), s32[16,1,128]{2,1,0:T(1,128)S(1)}, u32[]{:S(2)}, u32[]{:S(2)}) async-start(s32[16,1,128]{2,1,0:T(1,128)} %bitcast.5), calls=%async_computation | async-start | bytes 16384 | tf_op jit(solution)/shard_map/all_to_all | solution.py:383
  41.5 4.8 %all-to-all-done = s32[16,1,128]{2,1,0:T(1,128)S(1)} async-done(((s32[16,1,128]{2,1,0:T(1,128)}), s32[16,1,128]{2,1,0:T(1,128)S(1)}, u32[]{:S(2)}, u32[]{:S(2)}) %all-to-all-start) | async-done | bytes 8224 | tf_op jit(solution)/shard_map/all_to_all | solution.py:383
  49.3 10.1 %gate_up.4.refs_5_.refs_0_ = bf16[320,768]{1,0:T(8,128)(2,1)} custom-call(s32[4,6]{1,0:T(4,128)} %dynamic-slice_bitcast_fusion.where_ref, s32[16,128]{1,0:T(8,128)} %bitcast.57, bf16[2,128,2048]{2,1,0:T(8,128)(2,1)} %copy-done.5, bf16[2,128,2048]{2,1,0:T(8,128)(2,1)} %collective-permute-done.1.refs_1_, bf16[2,128,2048]{2,1,0:T(8,128)(2,1)} %collective-permute-done.2.refs_2_, ...), custom_call_target="tpu_custom_call" | custom-call | flops 4362076160 | bytes 17268736 | tf_op jit(solution)/shard_map/gate_up/pallas_call | solution.py:257
  60.8 12.1 %collective-permute-done.10.refs_6_.refs_0_ = bf16[2,128,2048]{2,1,0:T(8,128)(2,1)} collective-permute-done((bf16[2,128,2048]{2,1,0:T(8,128)(2,1)S(1)}, bf16[2,128,2048]{2,1,0:T(8,128)(2,1)}, u32[]{:S(2)}, u32[]{:S(2)}) %collective-permute-start.10) | collective-permute-done | bytes 1048608 | tf_op jit(solution)/shard_map/ppermute | solution.py:375
  73.3 10.1 %gate_up.5.refs_3_.refs_0_.refs_5_ = bf16[320,768]{1,0:T(8,128)(2,1)} custom-call(s32[4,6]{1,0:T(4,128)} %dynamic-slice_bitcast_fusion.where_ref, s32[16,128]{1,0:T(8,128)} %bitcast.58, bf16[2,128,2048]{2,1,0:T(8,128)(2,1)} %copy-done.1, bf16[2,128,2048]{2,1,0:T(8,128)(2,1)} %copy-done.11, bf16[2,128,2048]{2,1,0:T(8,128)(2,1)} %collective-permute-done.8.refs_2_, ...), custom_call_target="tpu_custom_call" | custom-call | flops 4362076160 | bytes 17268736 | tf_op jit(solution)/shard_map/gate_up/pallas_call | solution.py:257
  86.5 7.1 %down.4 = (bf16[2,128,2048]{2,1,0:T(8,128)(2,1)}, bf16[2,128,2048]{2,1,0:T(8,128)(2,1)}) custom-call(s32[4,6]{1,0:T(4,128)} %dynamic-slice_bitcast_fusion.where_ref, s32[16,128]{1,0:T(8,128)} %bitcast.59, bf16[320,768]{1,0:T(8,128)(2,1)} %gate_up.4.refs_5_.refs_0_, bf16[320,768]{1,0:T(8,128)(2,1)} %collective-permute-done.6.refs_1_, ...), custom_call_target="tpu_custom_call" | custom-call | flops 2181038080 | bytes 9371648 | tf_op jit(solution)/shard_map/down/pallas_call | solution.py:287
  93.7 4.1 %collective-permute-done.20.refs_1_ = bf16[320,768]{1,0:T(8,128)(2,1)S(1)} collective-permute-done((bf16[320,768]{1,0:T(8,128)(2,1)}, bf16[320,768]{1,0:T(8,128)(2,1)S(1)}, u32[]{:S(2)}, u32[]{:S(2)}) %collective-permute-start.20) | collective-permute-done | bytes 491552 | tf_op jit(solution)/shard_map/ppermute | solution.py:375
  98.6 7.1 %down.5 = (bf16[2,128,2048]{2,1,0:T(8,128)(2,1)}, bf16[2,128,2048]{2,1,0:T(8,128)(2,1)}) custom-call(s32[4,6]{1,0:T(4,128)} %dynamic-slice_bitcast_fusion.where_ref, s32[16,128]{1,0:T(8,128)} %bitcast.60, bf16[320,768]{1,0:T(8,128)(2,1)} %gate_up.5.refs_3_.refs_0_.refs_5_, bf16[320,768]{1,0:T(8,128)(2,1)} %copy-done.15, bf16[1536,2048]{1,0:T(8,128)(2,1)} %bitcast.50, ...), custom_call_target="tpu_custom_call" | custom-call | flops 2181038080 | bytes 9371648 | tf_op jit(solution)/shard_map/down/pallas_call | solution.py:287
  110.9 15.5 %collective-permute-done.14.refs_1_ = bf16[2,128,2048]{2,1,0:T(8,128)(2,1)} collective-permute-done((bf16[2,128,2048]{2,1,0:T(8,128)(2,1)S(1)}, bf16[2,128,2048]{2,1,0:T(8,128)(2,1)}, u32[]{:S(2)}, u32[]{:S(2)}) %collective-permute-start.14) | collective-permute-done | bytes 1048608 | tf_op jit(solution)/shard_map/ppermute | solution.py:375
  129.3 3.7 %collective-permute-done.12.refs_8_.refs_7_ = bf16[128,2048]{1,0:T(8,128)(2,1)S(1)} collective-permute-done((bf16[128,2048]{1,0:T(8,128)(2,1)S(1)}, bf16[128,2048]{1,0:T(8,128)(2,1)S(1)}, u32[]{:S(2)}, u32[]{:S(2)}) %collective-permute-start.12) | collective-permute-done | bytes 524320 | tf_op jit(solution)/shard_map/ppermute | solution.py:375
  133.8 10.0 %gate_up.6.refs_5_.refs_0_ = bf16[320,768]{1,0:T(8,128)(2,1)} custom-call(s32[4,6]{1,0:T(4,128)} %dynamic-slice_bitcast_fusion.where_ref, s32[16,128]{1,0:T(8,128)} %bitcast.61, bf16[2,128,2048]{2,1,0:T(8,128)(2,1)} %collective-permute-done.10.refs_6_.refs_0_, bf16[2,128,2048]{2,1,0:T(8,128)(2,1)} %collective-permute-done.17.refs_1_, ...), custom_call_target="tpu_custom_call" | custom-call | flops 4362076160 | bytes 17268736 | tf_op jit(solution)/shard_map/gate_up/pallas_call | solution.py:257
  145.5 2.3 %fusion.7 = bf16[128,2048]{1,0:T(8,128)(2,1)} fusion(bf16[128,2048]{1,0:T(8,128)(2,1)S(1)} %collective-permute-done.24.refs_5_, bf16[2,128,2048]{2,1,0:T(8,128)(2,1)} %copy-done.13, bf16[2,128,2048]{2,1,0:T(8,128)(2,1)S(1)} %copy-done), kind=kLoop, calls=%fused_computation.13 | loop fusion | flops 1572864 | bytes 2097152 | tf_op jit(solution)/shard_map/convert_element_type | solution.py:411
  147.7 3.5 %collective-permute-start.25 = (bf16[128,2048]{1,0:T(8,128)(2,1)}, bf16[128,2048]{1,0:T(8,128)(2,1)S(1)}, u32[]{:S(2)}, u32[]{:S(2)}) collective-permute-start(bf16[128,2048]{1,0:T(8,128)(2,1)} %fusion.7), channel_id=1, source_target_pairs={{0,4},{1,5},{2,6},{3,7},{4,12},{5,13},{6,14},{7,15},{8,0},{9,1},{1... | collective-permute-start | bytes 1572872 | tf_op jit(solution)/shard_map/ppermute | solution.py:375
  151.2 10.1 %gate_up.7.refs_4_.refs_0_ = bf16[320,768]{1,0:T(8,128)(2,1)} custom-call(s32[4,6]{1,0:T(4,128)} %dynamic-slice_bitcast_fusion.where_ref, s32[16,128]{1,0:T(8,128)} %bitcast.62, bf16[2,128,2048]{2,1,0:T(8,128)(2,1)} %copy-done.4, bf16[2,128,2048]{2,1,0:T(8,128)(2,1)} %collective-permute-done.14.refs_1_, ...), custom_call_target="tpu_custom_call" | custom-call | flops 4362076160 | bytes 17268736 | tf_op jit(solution)/shard_map/gate_up/pallas_call | solution.py:257
  161.9 7.3 %down.6 = (bf16[2,128,2048]{2,1,0:T(8,128)(2,1)}, bf16[2,128,2048]{2,1,0:T(8,128)(2,1)}) custom-call(s32[4,6]{1,0:T(4,128)} %dynamic-slice_bitcast_fusion.where_ref, s32[16,128]{1,0:T(8,128)} %bitcast.63, bf16[320,768]{1,0:T(8,128)(2,1)} %gate_up.6.refs_5_.refs_0_, bf16[320,768]{1,0:T(8,128)(2,1)} %collective-permute-done.22.refs_1_, ...), custom_call_target="tpu_custom_call" | custom-call | flops 2181038080 | bytes 9371648 | tf_op jit(solution)/shard_map/down/pallas_call | solution.py:287
  171.3 7.1 %down.7 = (bf16[2,128,2048]{2,1,0:T(8,128)(2,1)}, bf16[2,128,2048]{2,1,0:T(8,128)(2,1)}) custom-call(s32[4,6]{1,0:T(4,128)} %dynamic-slice_bitcast_fusion.where_ref, s32[16,128]{1,0:T(8,128)} %bitcast.64, bf16[320,768]{1,0:T(8,128)(2,1)} %gate_up.7.refs_4_.refs_0_, bf16[320,768]{1,0:T(8,128)(2,1)} %collective-permute-done.21.refs_1_, ...), custom_call_target="tpu_custom_call" | custom-call | flops 2181038080 | bytes 9371648 | tf_op jit(solution)/shard_map/down/pallas_call | solution.py:287
  184.2 10.4 %collective-permute-done.29 = bf16[128,2048]{1,0:T(8,128)(2,1)S(1)} collective-permute-done((bf16[128,2048]{1,0:T(8,128)(2,1)S(1)}, bf16[128,2048]{1,0:T(8,128)(2,1)S(1)}, u32[]{:S(2)}, u32[]{:S(2)}) %collective-permute-start.29) | collective-permute-done | bytes 524320 | tf_op jit(solution)/shard_map/ppermute | solution.py:375
  196.6 8.8 %collective-permute-done.27 = bf16[128,2048]{1,0:T(8,128)(2,1)S(1)} collective-permute-done((bf16[128,2048]{1,0:T(8,128)(2,1)S(1)}, bf16[128,2048]{1,0:T(8,128)(2,1)S(1)}, u32[]{:S(2)}, u32[]{:S(2)}) %collective-permute-start.27) | collective-permute-done | bytes 524320 | tf_op jit(solution)/shard_map/ppermute | solution.py:375
  205.4 4.9 %collective-permute-done.30 = bf16[128,2048]{1,0:T(8,128)(2,1)S(1)} collective-permute-done((bf16[128,2048]{1,0:T(8,128)(2,1)S(1)}, bf16[128,2048]{1,0:T(8,128)(2,1)S(1)}, u32[]{:S(2)}, u32[]{:S(2)}) %collective-permute-start.30) | collective-permute-done | bytes 524320 | tf_op jit(solution)/shard_map/ppermute | solution.py:375
  211.8 13.1 %collective-permute-done.31 = bf16[128,2048]{1,0:T(8,128)(2,1)S(1)} collective-permute-done((bf16[128,2048]{1,0:T(8,128)(2,1)S(1)}, bf16[128,2048]{1,0:T(8,128)(2,1)S(1)}, u32[]{:S(2)}, u32[]{:S(2)}) %collective-permute-start.31) | collective-permute-done | bytes 524320 | tf_op jit(solution)/shard_map/ppermute | solution.py:375
  (96 shorter events, 41.9 us)
Async XLA Ops:
  0.0 16.2 %collective-permute-start.4 = (bf16[128,2048]{1,0:T(8,128)(2,1)}, bf16[128,2048]{1,0:T(8,128)(2,1)S(1)}, u32[]{:S(2)}, u32[]{:S(2)}) collective-permute-start(bf16[128,2048]{1,0:T(8,128)(2,1)} %param.6), channel_id=1, source_target_pairs={{0,4},{1,5},{2,6},{3,7},{4,12},{5,13},{6,14},{7,15},{8,0},{9,1},{1... | collective-permute-start | bytes 1572872 | tf_op jit(solution)/shard_map/ppermute | solution.py:375
  3.0 14.7 %collective-permute-start = (bf16[128,2048]{1,0:T(8,128)(2,1)}, bf16[128,2048]{1,0:T(8,128)(2,1)S(1)}, u32[]{:S(2)}, u32[]{:S(2)}) collective-permute-start(bf16[128,2048]{1,0:T(8,128)(2,1)} %param.6), channel_id=1, source_target_pairs={{0,16},{1,3},{2,18},{3,1},{4,20},{5,7},{6,22},{7,5},{8,24},{9,11},... | collective-permute-start | bytes 1572872 | tf_op jit(solution)/shard_map/ppermute | solution.py:375
  16.2 14.4 %collective-permute-start.5 = (bf16[128,2048]{1,0:T(8,128)(2,1)S(1)}, bf16[128,2048]{1,0:T(8,128)(2,1)S(1)}, u32[]{:S(2)}, u32[]{:S(2)}) collective-permute-start(bf16[128,2048]{1,0:T(8,128)(2,1)S(1)} %collective-permute-done.4), channel_id=1, source_target_pairs={{0,16},{1,3},{2,18},{3,1},{4,20},{5,7},{6,22},{7,5},{8,24},{9,11},... | collective-permute-start | bytes 1572872 | tf_op jit(solution)/shard_map/ppermute | solution.py:375
  18.9 27.4 %collective-permute-start.1 = (bf16[2,128,2048]{2,1,0:T(8,128)(2,1)S(1)}, bf16[2,128,2048]{2,1,0:T(8,128)(2,1)}, u32[]{:S(2)}, u32[]{:S(2)}) collective-permute-start(bf16[2,128,2048]{2,1,0:T(8,128)(2,1)S(1)} %pad_maximum_fusion.refs_0_), channel_id=1, source_target_pairs={{0,2},{1,17},{2,0},{3,19},{4,6},{5,21},{6,4},{7,23},{8,10},{9,25},... | collective-permute-start | bytes 3145736 | tf_op jit(solution)/shard_map/ppermute | solution.py:375
  30.6 16.5 %collective-permute-start.7 = (bf16[2,128,2048]{2,1,0:T(8,128)(2,1)S(1)}, bf16[2,128,2048]{2,1,0:T(8,128)(2,1)S(1)}, u32[]{:S(2)}, u32[]{:S(2)}) collective-permute-start(bf16[2,128,2048]{2,1,0:T(8,128)(2,1)S(1)} %pad_maximum_fusion.1.refs_5_.refs_0_), channel_id=1, source_target_pairs={{0,2},{1,17},{2,0},{3,19},{4,6},{5,21},{6,4},{7,23},{8,10},{9,25},... | collective-permute-start | bytes 3145736 | tf_op jit(solution)/shard_map/ppermute | solution.py:375
  46.3 26.5 %collective-permute-start.10 = (bf16[2,128,2048]{2,1,0:T(8,128)(2,1)S(1)}, bf16[2,128,2048]{2,1,0:T(8,128)(2,1)}, u32[]{:S(2)}, u32[]{:S(2)}) collective-permute-start(bf16[2,128,2048]{2,1,0:T(8,128)(2,1)S(1)} %pad_maximum_fusion.1.refs_5_.refs_0_), channel_id=1, source_target_pairs={{0,4},{1,5},{2,6},{3,7},{4,12},{5,13},{6,14},{7,15},{8,0},{9,1},{1... | collective-permute-start | bytes 3145736 | tf_op jit(solution)/shard_map/ppermute | solution.py:375
  47.0 26.3 %collective-permute-start.8 = (bf16[2,128,2048]{2,1,0:T(8,128)(2,1)S(1)}, bf16[2,128,2048]{2,1,0:T(8,128)(2,1)}, u32[]{:S(2)}, u32[]{:S(2)}) collective-permute-start(bf16[2,128,2048]{2,1,0:T(8,128)(2,1)S(1)} %pad_maximum_fusion.1.refs_5_.refs_0_), channel_id=1, source_target_pairs={{0,1},{1,0},{2,3},{3,2},{4,5},{5,4},{6,7},{7,6},{8,9},{9,8},{10,11... | collective-permute-start | bytes 3145736 | tf_op jit(solution)/shard_map/ppermute | solution.py:375
  47.1 26.1 %collective-permute-start.9 = (bf16[2,128,2048]{2,1,0:T(8,128)(2,1)S(1)}, bf16[2,128,2048]{2,1,0:T(8,128)(2,1)}, u32[]{:S(2)}, u32[]{:S(2)}) collective-permute-start(bf16[2,128,2048]{2,1,0:T(8,128)(2,1)S(1)} %collective-permute-done.7.refs_1_), channel_id=1, source_target_pairs={{0,1},{1,0},{2,3},{3,2},{4,5},{5,4},{6,7},{7,6},{8,9},{9,8},{10,11... | collective-permute-start | bytes 3145736 | tf_op jit(solution)/shard_map/ppermute | solution.py:375
  59.4 27.2 %collective-permute-start.6 = (bf16[320,768]{1,0:T(8,128)(2,1)}, bf16[320,768]{1,0:T(8,128)(2,1)}, u32[]{:S(2)}, u32[]{:S(2)}) collective-permute-start(bf16[320,768]{1,0:T(8,128)(2,1)} %gate_up.4.refs_5_.refs_0_), channel_id=1, source_target_pairs={{0,16},{1,17},{2,18},{3,19},{4,20},{5,21},{6,22},{7,23},{8,24},{9,... | collective-permute-start | bytes 1474568 | tf_op jit(solution)/shard_map/ppermute | solution.py:375
  72.9 33.0 %collective-permute-start.13 = (bf16[2,128,2048]{2,1,0:T(8,128)(2,1)}, bf16[2,128,2048]{2,1,0:T(8,128)(2,1)S(1)}, u32[]{:S(2)}, u32[]{:S(2)}) collective-permute-start(bf16[2,128,2048]{2,1,0:T(8,128)(2,1)} %collective-permute-done.10.refs_6_.refs_0_), channel_id=1, source_target_pairs={{0,4},{1,5},{2,6},{3,7},{4,12},{5,13},{6,14},{7,15},{8,0},{9,1},{1... | collective-permute-start | bytes 3145736 | tf_op jit(solution)/shard_map/ppermute | solution.py:375
  83.4 14.4 %collective-permute-start.20 = (bf16[320,768]{1,0:T(8,128)(2,1)}, bf16[320,768]{1,0:T(8,128)(2,1)S(1)}, u32[]{:S(2)}, u32[]{:S(2)}) collective-permute-start(bf16[320,768]{1,0:T(8,128)(2,1)} %gate_up.5.refs_3_.refs_0_.refs_5_), channel_id=1, source_target_pairs={{0,16},{1,17},{2,18},{3,19},{4,20},{5,21},{6,22},{7,23},{8,24},{9,... | collective-permute-start | bytes 1474568 | tf_op jit(solution)/shard_map/ppermute | solution.py:375
  84.9 22.6 %collective-permute-start.17 = (bf16[2,128,2048]{2,1,0:T(8,128)(2,1)}, bf16[2,128,2048]{2,1,0:T(8,128)(2,1)}, u32[]{:S(2)}, u32[]{:S(2)}) collective-permute-start(bf16[2,128,2048]{2,1,0:T(8,128)(2,1)} %collective-permute-done.10.refs_6_.refs_0_), channel_id=1, source_target_pairs={{0,2},{1,17},{2,0},{3,19},{4,6},{5,21},{6,4},{7,23},{8,10},{9,25},... | collective-permute-start | bytes 3145736 | tf_op jit(solution)/shard_map/ppermute | solution.py:375
  93.6 14.4 %collective-permute-start.11 = (bf16[2,128,2048]{2,1,0:T(8,128)(2,1)}, bf16[2,128,2048]{2,1,0:T(8,128)(2,1)S(1)}, u32[]{:S(2)}, u32[]{:S(2)}) collective-permute-start(bf16[2,128,2048]{2,1,0:T(8,128)(2,1)} %get-tuple-element.23), channel_id=1, source_target_pairs={{0,1},{1,0},{2,3},{3,2},{4,5},{5,4},{6,7},{7,6},{8,9},{9,8},{10,11... | collective-permute-start | bytes 3145736 | tf_op jit(solution)/shard_map/ppermute | solution.py:375
  105.8 20.6 %collective-permute-start.14 = (bf16[2,128,2048]{2,1,0:T(8,128)(2,1)S(1)}, bf16[2,128,2048]{2,1,0:T(8,128)(2,1)}, u32[]{:S(2)}, u32[]{:S(2)}) collective-permute-start(bf16[2,128,2048]{2,1,0:T(8,128)(2,1)S(1)} %collective-permute-done.13.refs_7_.refs_0_), channel_id=1, source_target_pairs={{0,2},{1,17},{2,0},{3,19},{4,6},{5,21},{6,4},{7,23},{8,10},{9,25},... | collective-permute-start | bytes 3145736 | tf_op jit(solution)/shard_map/ppermute | solution.py:375
  107.5 20.1 %collective-permute-start.18 = (bf16[2,128,2048]{2,1,0:T(8,128)(2,1)}, bf16[2,128,2048]{2,1,0:T(8,128)(2,1)S(1)}, u32[]{:S(2)}, u32[]{:S(2)}) collective-permute-start(bf16[2,128,2048]{2,1,0:T(8,128)(2,1)} %collective-permute-done.10.refs_6_.refs_0_), channel_id=1, source_target_pairs={{0,1},{1,0},{2,3},{3,2},{4,5},{5,4},{6,7},{7,6},{8,9},{9,8},{10,11... | collective-permute-start | bytes 3145736 | tf_op jit(solution)/shard_map/ppermute | solution.py:375
  107.5 43.7 %collective-permute-start.15 = (bf16[2,128,2048]{2,1,0:T(8,128)(2,1)S(1)}, bf16[2,128,2048]{2,1,0:T(8,128)(2,1)}, u32[]{:S(2)}, u32[]{:S(2)}) collective-permute-start(bf16[2,128,2048]{2,1,0:T(8,128)(2,1)S(1)} %collective-permute-done.13.refs_7_.refs_0_), channel_id=1, source_target_pairs={{0,1},{1,0},{2,3},{3,2},{4,5},{5,4},{6,7},{7,6},{8,9},{9,8},{10,11... | collective-permute-start | bytes 3145736 | tf_op jit(solution)/shard_map/ppermute | solution.py:375
  108.0 25.0 %collective-permute-start.19 = (bf16[2,128,2048]{2,1,0:T(8,128)(2,1)}, bf16[2,128,2048]{2,1,0:T(8,128)(2,1)}, u32[]{:S(2)}, u32[]{:S(2)}) collective-permute-start(bf16[2,128,2048]{2,1,0:T(8,128)(2,1)} %collective-permute-done.17.refs_1_), channel_id=1, source_target_pairs={{0,1},{1,0},{2,3},{3,2},{4,5},{5,4},{6,7},{7,6},{8,9},{9,8},{10,11... | collective-permute-start | bytes 3145736 | tf_op jit(solution)/shard_map/ppermute | solution.py:375
  109.6 23.4 %collective-permute-start.12 = (bf16[128,2048]{1,0:T(8,128)(2,1)S(1)}, bf16[128,2048]{1,0:T(8,128)(2,1)S(1)}, u32[]{:S(2)}, u32[]{:S(2)}) collective-permute-start(bf16[128,2048]{1,0:T(8,128)(2,1)S(1)} %fusion.10), channel_id=1, source_target_pairs={{0,2},{1,3},{2,0},{3,1},{4,6},{5,7},{6,4},{7,5},{8,10},{9,11},{10,... | collective-permute-start | bytes 1572872 | tf_op jit(solution)/shard_map/ppermute | solution.py:375
  126.4 24.8 %collective-permute-start.16 = (bf16[2,128,2048]{2,1,0:T(8,128)(2,1)}, bf16[2,128,2048]{2,1,0:T(8,128)(2,1)}, u32[]{:S(2)}, u32[]{:S(2)}) collective-permute-start(bf16[2,128,2048]{2,1,0:T(8,128)(2,1)} %collective-permute-done.14.refs_1_), channel_id=1, source_target_pairs={{0,1},{1,0},{2,3},{3,2},{4,5},{5,4},{6,7},{7,6},{8,9},{9,8},{10,11... | collective-permute-start | bytes 3145736 | tf_op jit(solution)/shard_map/ppermute | solution.py:375
  127.6 17.8 %collective-permute-start.24 = (bf16[128,2048]{1,0:T(8,128)(2,1)S(1)}, bf16[128,2048]{1,0:T(8,128)(2,1)S(1)}, u32[]{:S(2)}, u32[]{:S(2)}) collective-permute-start(bf16[128,2048]{1,0:T(8,128)(2,1)S(1)} %fusion.11), channel_id=1, source_target_pairs={{0,2},{1,3},{2,0},{3,1},{4,6},{5,7},{6,4},{7,5},{8,10},{9,11},{10,... | collective-permute-start | bytes 1572872 | tf_op jit(solution)/shard_map/ppermute | solution.py:375
  143.9 18.0 %collective-permute-start.22 = (bf16[320,768]{1,0:T(8,128)(2,1)}, bf16[320,768]{1,0:T(8,128)(2,1)}, u32[]{:S(2)}, u32[]{:S(2)}) collective-permute-start(bf16[320,768]{1,0:T(8,128)(2,1)} %gate_up.6.refs_5_.refs_0_), channel_id=1, source_target_pairs={{0,16},{1,17},{2,18},{3,19},{4,20},{5,21},{6,22},{7,23},{8,24},{9,... | collective-permute-start | bytes 1474568 | tf_op jit(solution)/shard_map/ppermute | solution.py:375
  147.7 21.6 %collective-permute-start.25 = (bf16[128,2048]{1,0:T(8,128)(2,1)}, bf16[128,2048]{1,0:T(8,128)(2,1)S(1)}, u32[]{:S(2)}, u32[]{:S(2)}) collective-permute-start(bf16[128,2048]{1,0:T(8,128)(2,1)} %fusion.7), channel_id=1, source_target_pairs={{0,4},{1,5},{2,6},{3,7},{4,12},{5,13},{6,14},{7,15},{8,0},{9,1},{1... | collective-permute-start | bytes 1572872 | tf_op jit(solution)/shard_map/ppermute | solution.py:375
  179.8 14.8 %collective-permute-start.29 = (bf16[128,2048]{1,0:T(8,128)(2,1)S(1)}, bf16[128,2048]{1,0:T(8,128)(2,1)S(1)}, u32[]{:S(2)}, u32[]{:S(2)}) collective-permute-start(bf16[128,2048]{1,0:T(8,128)(2,1)S(1)} %fusion.13), channel_id=1, source_target_pairs={{0,2},{1,3},{2,0},{3,1},{4,6},{5,7},{6,4},{7,5},{8,10},{9,11},{10,... | collective-permute-start | bytes 1572872 | tf_op jit(solution)/shard_map/ppermute | solution.py:375
  182.7 22.8 %collective-permute-start.27 = (bf16[128,2048]{1,0:T(8,128)(2,1)S(1)}, bf16[128,2048]{1,0:T(8,128)(2,1)S(1)}, u32[]{:S(2)}, u32[]{:S(2)}) collective-permute-start(bf16[128,2048]{1,0:T(8,128)(2,1)S(1)} %fusion.12), channel_id=1, source_target_pairs={{0,2},{1,3},{2,0},{3,1},{4,6},{5,7},{6,4},{7,5},{8,10},{9,11},{10,... | collective-permute-start | bytes 1572872 | tf_op jit(solution)/shard_map/ppermute | solution.py:375
  (25 other events, 460.9 us)

commit v6 on v5

--- a/solution.py
+++ b/solution.py
@@ -383,54 +383,57 @@
     code = lax.all_to_all(codes_of(expert_ids, numerators, experts), "expert", split_axis=0, concat_axis=0, tiled=True)
 
     later = move(tokens, onward)
-    pairs = [jnp.stack([v, move(v, first)]) for v in (tokens, later)]
-
-    mine, keeps, backs, hops, sums = [], [], [], [], []
-
-    def spread(k):
-        nonlocal code, where
+    near = move(tokens, first)
+    later, near, code, where = lax.optimization_barrier((later, near, code, where))
+    pairs = [jnp.stack([tokens, near]), jnp.stack([later, move(later, first)])]
+    pairs.append(move(pairs[1], onward))
+
+    mine, others, keeps, gots, backs, hops = [], [], [], [], [], []
+
+    def after(value, *done):
+        return lax.optimization_barrier((value, *done))[0]
+
+    def spread(k, *done):
         cross = move(pairs[k], second)
-        if k == 0:
-            cross, code, where = lax.optimization_barrier((cross, code, where))
-        return [pairs[k], cross, move(pairs[k], sibling), move(cross, sibling)]
+        return [pairs[k], cross, move(pairs[k], sibling), move(after(cross, *done), sibling)]
 
     def gate_up(k, shards_of, *earlier):
         mine.append(pick_call(k, where, code, shards_of, gate_up_weight[0], mine[-1:] + list(earlier), capacity))
+        others.append(move(mine[k], over_x))
 
     def down(k, *earlier):
-        other = move(mine[k], over_x)
-        keep, send = sum_call(k, where, code, mine[k], other, down_weight[0], keeps[-1:] + list(earlier), capacity)
-        got = move(send, sibling)
-        away = (keep[1].astype(jnp.float32) + got[1].astype(jnp.float32)).astype(jnp.bfloat16)
+        keep, send = sum_call(k, where, code, mine[k], others[k], down_weight[0], keeps[-1:] + list(earlier), capacity)
         keeps.append(keep)
-        backs.append(move(away, over_y))
-        sums.append((keep[0], got[0], backs[-1]))
+        gots.append(move(send, sibling))
+
+    def away(k):
+        return (keeps[k][1].astype(jnp.float32) + gots[k][1].astype(jnp.float32)).astype(jnp.bfloat16)
 
     def hop(k):
-        terms = [v.astype(jnp.float32) for v in [*sums[k], *hops[-1:]]]
+        terms = [v.astype(jnp.float32) for v in [keeps[k][0], gots[k][0], backs[k], *hops[-1:]]]
         total = functools.reduce(jnp.add, terms).astype(jnp.bfloat16)
         if k:
             hops.append(move(total, onward))
         return total
 
-    for k in range(layers):
-        shards_of = spread(k)
-        if k + 2 < layers:
-            pairs.append(move(pairs[k + 1], onward))
-        gate_up(k, shards_of, *keeps[-1:], *pairs[k + 1 : k + 2], *backs[:-1][-1:])
-        if k == 0 and layers > 2:
-            pairs[2], _ = lax.optimization_barrier((pairs[2], mine[0]))
-        if k == 1:
-            down(0, mine[1])
-            if layers > 3:
-                pairs[3], _ = lax.optimization_barrier((pairs[3], keeps[0]))
-            down(1)
-        if k > 2:
-            down(k - 1, mine[k], backs[k - 2])
-            hop(k - 2)
-    hop(layers - 2)
-    down(layers - 1, *hops[:1])
-    hop(layers - 1)
+    gate_up(0, spread(0))
+    gate_up(1, spread(1), pairs[2])
+    pairs[2] = after(pairs[2], mine[0])
+    pairs.append(move(pairs[2], onward))
+    down(0, mine[1])
+    pairs[3] = after(pairs[3], keeps[0])
+    down(1)
+    both = move(jnp.stack([away(0), away(1)]), over_y)
+    backs += [both[0], both[1]]
+    gate_up(2, spread(2), keeps[1], pairs[3])
+    gate_up(3, spread(3, mine[2]))
+    hop(1)
+    down(2, mine[3])
+    backs.append(move(away(2), over_y))
+    down(3, both)
+    backs.append(move(after(away(3), hops[0]), over_y))
+    hop(2)
+    hop(3)
     return hop(0)
 
 

time: 227 us -> 219 us (0.965)
  waiting for transfers between devices: 103 us -> 95.9 us
  starting transfers between devices: 36.1 us -> 30.1 us
  local copies, waits for them, and re-layouts: 2.91 us -> 6.78 us
    ppermute x32 -> x31, waiting for transfers between devices: 98 us -> 90.4 us  [move(): return lax.ppermute(value, axes, moves)]
    ppermute x32 -> x31, starting transfers between devices: 31.2 us -> 25.2 us  [move(): return lax.ppermute(value, axes, moves)]
    unnamed x32 -> x34, local copies, waits for them, and re-layouts: 1.64 us -> 5.51 us
  transfers between devices with their start and end apart: 33 -> 32, of which waited for: 13 -> 12; matrix products, arithmetic and copies ran while one was open for 6% -> 6% of each run, Pallas kernels for 30% -> 32%
where the time goes in v6:
time: 219 us; the launch traced here: 218 us
  waiting for transfers between devices  95.9 us (44%)
  Pallas kernels  68.7 us (31%)
  starting transfers between devices  30.1 us (14%)
  other arithmetic  15.4 us (7%)
  local copies, waits for them, and re-layouts  6.78 us (3%)
    ppermute x31, waiting for transfers between devices, move(): return lax.ppermute(value, axes, moves)  90.4 us
    pallas_call x4, Pallas kernels, pick_call(): pl.pallas_call(functools.partial(pick_kernel, capacity, k), in_specs=[pl....  40.2 us
    pallas_call x4, Pallas kernels, sum_call(): pl.pallas_call(functools.partial(sum_kernel, capacity, k), in_specs=[pl.B...  28.5 us
    ppermute x31, starting transfers between devices, move(): return lax.ppermute(value, axes, moves)  25.2 us
    convert_element_type x4, other arithmetic, hop(): total = functools.reduce(jnp.add, terms).astype(jnp.bfloat16)  6.66 us
    unnamed x34, local copies, waits for them, and re-layouts  5.51 us
    all_to_all x1, waiting for transfers between devices, pair_shards(): lax.all_to_all(codes_of(expert_ids, numerators, experts), 'expert', split...  5.49 us
    convert_element_type x4, other arithmetic, away(): (keeps[k][1].astype(jnp.float32) + gots[k][1].astype(jnp.float32)).astype...  4.99 us
  transfers between devices with their start and end apart: 32, of which 12 were waited for; matrix products, arithmetic and copies ran while one was open for 6% of the time, Pallas kernels for 32%

profile of v6, /device:TPU:0, one launch (start us, length us, event | category | flops | bytes accessed | tf_op | source)
XLA Modules:
  0.0 218.0 jit_solution(542874601395006558)
XLA Ops:
  0.0 3.0 %collective-permute-start = (bf16[128,2048]{1,0:T(8,128)(2,1)}, bf16[128,2048]{1,0:T(8,128)(2,1)S(1)}, u32[]{:S(2)}, u32[]{:S(2)}) collective-permute-start(bf16[128,2048]{1,0:T(8,128)(2,1)} %param.6), channel_id=1, source_target_pairs={{0,4},{1,5},{2,6},{3,7},{4,12},{5,13},{6,14},{7,15},{8,0},{9,1},{1... | collective-permute-start | bytes 1572872 | tf_op jit(solution)/shard_map/ppermute | solution.py:375
  6.7 4.9 %all-to-all-start = ((s32[16,1,128]{2,1,0:T(1,128)}), s32[16,1,128]{2,1,0:T(1,128)S(1)}, u32[]{:S(2)}, u32[]{:S(2)}) async-start(s32[16,1,128]{2,1,0:T(1,128)} %bitcast.3), calls=%async_computation | async-start | bytes 16384 | tf_op jit(solution)/shard_map/all_to_all | solution.py:383
  12.9 5.5 %all-to-all-done = s32[16,1,128]{2,1,0:T(1,128)S(1)} async-done(((s32[16,1,128]{2,1,0:T(1,128)}), s32[16,1,128]{2,1,0:T(1,128)S(1)}, u32[]{:S(2)}, u32[]{:S(2)}) %all-to-all-start) | async-done | bytes 8224 | tf_op jit(solution)/shard_map/all_to_all | solution.py:383
  21.6 18.4 %collective-permute-done.2.refs_1_ = bf16[2,128,2048]{2,1,0:T(8,128)(2,1)S(1)} collective-permute-done((bf16[2,128,2048]{2,1,0:T(8,128)(2,1)S(1)}, bf16[2,128,2048]{2,1,0:T(8,128)(2,1)S(1)}, u32[]{:S(2)}, u32[]{:S(2)}) %collective-permute-start.2) | collective-permute-done | bytes 1048608 | tf_op jit(solution)/shard_map/ppermute | solution.py:375
  43.7 10.0 %gate_up.4.refs_5_.refs_0_ = bf16[320,768]{1,0:T(8,128)(2,1)} custom-call(s32[4,6]{1,0:T(4,128)} %dynamic-slice_bitcast_fusion.where_ref, s32[16,128]{1,0:T(8,128)} %bitcast.49, bf16[2,128,2048]{2,1,0:T(8,128)(2,1)} %copy-done.7, bf16[2,128,2048]{2,1,0:T(8,128)(2,1)} %copy-done.8, bf16[2,128,2048]{2,1,0:T(8,128)(2,1)} %copy-done.10, ...), custom_call_target="tpu_custom_call" | custom-call | flops 4362076160 | bytes 17268736 | tf_op jit(solution)/shard_map/gate_up/pallas_call | solution.py:257
  53.8 12.9 %collective-permute-done.10.refs_6_.refs_0_ = bf16[2,128,2048]{2,1,0:T(8,128)(2,1)S(1)} collective-permute-done((bf16[2,128,2048]{2,1,0:T(8,128)(2,1)S(1)}, bf16[2,128,2048]{2,1,0:T(8,128)(2,1)S(1)}, u32[]{:S(2)}, u32[]{:S(2)}) %collective-permute-start.10) | collective-permute-done | bytes 1048608 | tf_op jit(solution)/shard_map/ppermute | solution.py:375
  68.4 13.2 %collective-permute-done.18.refs_1_ = bf16[2,128,2048]{2,1,0:T(8,128)(2,1)} collective-permute-done((bf16[2,128,2048]{2,1,0:T(8,128)(2,1)S(1)}, bf16[2,128,2048]{2,1,0:T(8,128)(2,1)}, u32[]{:S(2)}, u32[]{:S(2)}) %collective-permute-start.18) | collective-permute-done | bytes 1048608 | tf_op jit(solution)/shard_map/ppermute | solution.py:375
  81.6 4.0 %collective-permute-start.19 = (bf16[2,128,2048]{2,1,0:T(8,128)(2,1)S(1)}, bf16[2,128,2048]{2,1,0:T(8,128)(2,1)}, u32[]{:S(2)}, u32[]{:S(2)}) collective-permute-start(bf16[2,128,2048]{2,1,0:T(8,128)(2,1)S(1)} %collective-permute-done.10.refs_6_.refs_0_), channel_id=1, source_target_pairs={{0,1},{1,0},{2,3},{3,2},{4,5},{5,4},{6,7},{7,6},{8,9},{9,8},{10,11... | collective-permute-start | bytes 3145736 | tf_op jit(solution)/shard_map/ppermute | solution.py:375
  86.6 10.1 %gate_up.5.refs_3_.refs_0_.refs_5_ = bf16[320,768]{1,0:T(8,128)(2,1)} custom-call(s32[4,6]{1,0:T(4,128)} %dynamic-slice_bitcast_fusion.where_ref, s32[16,128]{1,0:T(8,128)} %bitcast.50, bf16[2,128,2048]{2,1,0:T(8,128)(2,1)} %copy-done.6, bf16[2,128,2048]{2,1,0:T(8,128)(2,1)} %collective-permute-done.7.refs_1_, bf16[2,128,2048]{2,1,0:T(8,128)(2,1)} %copy-done.9, ...), custom_call_target="tpu_custom_call" | custom-call | flops 4362076160 | bytes 17268736 | tf_op jit(solution)/shard_map/gate_up/pallas_call | solution.py:257
  98.1 7.1 %down.4 = (bf16[2,128,2048]{2,1,0:T(8,128)(2,1)}, bf16[2,128,2048]{2,1,0:T(8,128)(2,1)}) custom-call(s32[4,6]{1,0:T(4,128)} %dynamic-slice_bitcast_fusion.where_ref, s32[16,128]{1,0:T(8,128)} %bitcast.51, bf16[320,768]{1,0:T(8,128)(2,1)} %gate_up.4.refs_5_.refs_0_, bf16[320,768]{1,0:T(8,128)(2,1)} %copy-done.16, bf16[1536,2048]{1,0:T(8,128)(2,1)} %bitcast.41, ...), custom_call_target="tpu_custom_call" | custom-call | flops 2181038080 | bytes 9371648 | tf_op jit(solution)/shard_map/down/pallas_call | solution.py:287
  106.7 4.3 %collective-permute-done.12.refs_1_ = bf16[320,768]{1,0:T(8,128)(2,1)S(1)} collective-permute-done((bf16[320,768]{1,0:T(8,128)(2,1)}, bf16[320,768]{1,0:T(8,128)(2,1)S(1)}, u32[]{:S(2)}, u32[]{:S(2)}) %collective-permute-start.12) | collective-permute-done | bytes 491552 | tf_op jit(solution)/shard_map/ppermute | solution.py:375
  111.8 7.1 %down.5 = (bf16[2,128,2048]{2,1,0:T(8,128)(2,1)}, bf16[2,128,2048]{2,1,0:T(8,128)(2,1)}) custom-call(s32[4,6]{1,0:T(4,128)} %dynamic-slice_bitcast_fusion.where_ref, s32[16,128]{1,0:T(8,128)} %bitcast.52, bf16[320,768]{1,0:T(8,128)(2,1)} %gate_up.5.refs_3_.refs_0_.refs_5_, bf16[320,768]{1,0:T(8,128)(2,1)} %copy-done.15, bf16[1536,2048]{1,0:T(8,128)(2,1)} %bitcast.42, ...), custom_call_target="tpu_custom_call" | custom-call | flops 2181038080 | bytes 9371648 | tf_op jit(solution)/shard_map/down/pallas_call | solution.py:287
  119.5 10.0 %gate_up.6.refs_5_.refs_0_ = bf16[320,768]{1,0:T(8,128)(2,1)} custom-call(s32[4,6]{1,0:T(4,128)} %dynamic-slice_bitcast_fusion.where_ref, s32[16,128]{1,0:T(8,128)} %bitcast.53, bf16[2,128,2048]{2,1,0:T(8,128)(2,1)} %copy-done.3, bf16[2,128,2048]{2,1,0:T(8,128)(2,1)} %collective-permute-done.18.refs_1_, ...), custom_call_target="tpu_custom_call" | custom-call | flops 4362076160 | bytes 17268736 | tf_op jit(solution)/shard_map/gate_up/pallas_call | solution.py:257
  134.5 10.1 %gate_up.7.refs_4_.refs_0_ = bf16[320,768]{1,0:T(8,128)(2,1)} custom-call(s32[4,6]{1,0:T(4,128)} %dynamic-slice_bitcast_fusion.where_ref, s32[16,128]{1,0:T(8,128)} %bitcast.54, bf16[2,128,2048]{2,1,0:T(8,128)(2,1)} %copy-done.2, bf16[2,128,2048]{2,1,0:T(8,128)(2,1)} %collective-permute-done.16.refs_1_, ...), custom_call_target="tpu_custom_call" | custom-call | flops 4362076160 | bytes 17268736 | tf_op jit(solution)/shard_map/gate_up/pallas_call | solution.py:257
  148.2 7.1 %down.6 = (bf16[2,128,2048]{2,1,0:T(8,128)(2,1)}, bf16[2,128,2048]{2,1,0:T(8,128)(2,1)}) custom-call(s32[4,6]{1,0:T(4,128)} %dynamic-slice_bitcast_fusion.where_ref, s32[16,128]{1,0:T(8,128)} %bitcast.55, bf16[320,768]{1,0:T(8,128)(2,1)} %gate_up.6.refs_5_.refs_0_, bf16[320,768]{1,0:T(8,128)(2,1)} %copy-done.14, bf16[1536,2048]{1,0:T(8,128)(2,1)} %bitcast.43, ...), custom_call_target="tpu_custom_call" | custom-call | flops 2181038080 | bytes 9371648 | tf_op jit(solution)/shard_map/down/pallas_call | solution.py:287
  155.4 3.7 %collective-permute-done.14.refs_4_ = bf16[2,128,2048]{2,1,0:T(8,128)(2,1)S(1)} collective-permute-done((bf16[2,128,2048]{2,1,0:T(8,128)(2,1)}, bf16[2,128,2048]{2,1,0:T(8,128)(2,1)S(1)}, u32[]{:S(2)}, u32[]{:S(2)}) %collective-permute-start.14) | collective-permute-done | bytes 1048608 | tf_op jit(solution)/shard_map/ppermute | solution.py:375
  160.2 7.1 %down.7 = (bf16[2,128,2048]{2,1,0:T(8,128)(2,1)}, bf16[2,128,2048]{2,1,0:T(8,128)(2,1)}) custom-call(s32[4,6]{1,0:T(4,128)} %dynamic-slice_bitcast_fusion.where_ref, s32[16,128]{1,0:T(8,128)} %bitcast.56, bf16[320,768]{1,0:T(8,128)(2,1)} %gate_up.7.refs_4_.refs_0_, bf16[320,768]{1,0:T(8,128)(2,1)} %copy-done.13, bf16[1536,2048]{1,0:T(8,128)(2,1)} %bitcast.44, ...), custom_call_target="tpu_custom_call" | custom-call | flops 2181038080 | bytes 9371648 | tf_op jit(solution)/shard_map/down/pallas_call | solution.py:287
  172.0 12.1 %collective-permute-done.25 = bf16[128,2048]{1,0:T(8,128)(2,1)S(1)} collective-permute-done((bf16[128,2048]{1,0:T(8,128)(2,1)S(1)}, bf16[128,2048]{1,0:T(8,128)(2,1)S(1)}, u32[]{:S(2)}, u32[]{:S(2)}) %collective-permute-start.25) | collective-permute-done | bytes 524320 | tf_op jit(solution)/shard_map/ppermute | solution.py:375
  186.0 3.5 %collective-permute-start.29 = (bf16[128,2048]{1,0:T(8,128)(2,1)S(1)}, bf16[128,2048]{1,0:T(8,128)(2,1)S(1)}, u32[]{:S(2)}, u32[]{:S(2)}) collective-permute-start(bf16[128,2048]{1,0:T(8,128)(2,1)S(1)} %fusion.4), channel_id=1, source_target_pairs={{0,4},{1,5},{2,6},{3,7},{4,12},{5,13},{6,14},{7,15},{8,0},{9,1},{1... | collective-permute-start | bytes 1572872 | tf_op jit(solution)/shard_map/ppermute | solution.py:375
  189.6 8.1 %collective-permute-done.26 = bf16[128,2048]{1,0:T(8,128)(2,1)S(1)} collective-permute-done((bf16[128,2048]{1,0:T(8,128)(2,1)S(1)}, bf16[128,2048]{1,0:T(8,128)(2,1)S(1)}, u32[]{:S(2)}, u32[]{:S(2)}) %collective-permute-start.26) | collective-permute-done | bytes 524320 | tf_op jit(solution)/shard_map/ppermute | solution.py:375
  197.7 2.9 %collective-permute-done.29 = bf16[128,2048]{1,0:T(8,128)(2,1)S(1)} collective-permute-done((bf16[128,2048]{1,0:T(8,128)(2,1)S(1)}, bf16[128,2048]{1,0:T(8,128)(2,1)S(1)}, u32[]{:S(2)}, u32[]{:S(2)}) %collective-permute-start.29) | collective-permute-done | bytes 524320 | tf_op jit(solution)/shard_map/ppermute | solution.py:375
  201.9 1.6 collective-permute-start.30
  203.5 12.0 %collective-permute-done.30 = bf16[128,2048]{1,0:T(8,128)(2,1)S(1)} collective-permute-done((bf16[128,2048]{1,0:T(8,128)(2,1)S(1)}, bf16[128,2048]{1,0:T(8,128)(2,1)S(1)}, u32[]{:S(2)}, u32[]{:S(2)}) %collective-permute-start.30) | collective-permute-done | bytes 524320 | tf_op jit(solution)/shard_map/ppermute | solution.py:375
  215.5 2.5 %fusion.7 = bf16[128,2048]{1,0:T(8,128)(2,1)} fusion(bf16[128,2048]{1,0:T(8,128)(2,1)S(1)} %collective-permute-done.30, bf16[2,128,2048]{2,1,0:T(8,128)(2,1)} %copy-done.5, bf16[2,128,2048]{2,1,0:T(8,128)(2,1)} %collective-permute-done.11, bf16[2,128,2048]{2,1,0:T(8,128)(2,1)} %get-tuple-element.25.refs_3_), kind=kLoop, calls=%fused_computation.14 | loop fusion | flops 2097152 | bytes 2621440 | tf_op jit(solution)/shard_map/convert_element_type | solution.py:414
  (97 shorter events, 36.3 us)
Async XLA Ops:
  0.0 18.4 %collective-permute-start = (bf16[128,2048]{1,0:T(8,128)(2,1)}, bf16[128,2048]{1,0:T(8,128)(2,1)S(1)}, u32[]{:S(2)}, u32[]{:S(2)}) collective-permute-start(bf16[128,2048]{1,0:T(8,128)(2,1)} %param.6), channel_id=1, source_target_pairs={{0,4},{1,5},{2,6},{3,7},{4,12},{5,13},{6,14},{7,15},{8,0},{9,1},{1... | collective-permute-start | bytes 1572872 | tf_op jit(solution)/shard_map/ppermute | solution.py:375
  3.0 15.4 %collective-permute-start.1 = (bf16[128,2048]{1,0:T(8,128)(2,1)}, bf16[128,2048]{1,0:T(8,128)(2,1)S(1)}, u32[]{:S(2)}, u32[]{:S(2)}) collective-permute-start(bf16[128,2048]{1,0:T(8,128)(2,1)} %param.6), channel_id=1, source_target_pairs={{0,16},{1,3},{2,18},{3,1},{4,20},{5,7},{6,22},{7,5},{8,24},{9,11},... | collective-permute-start | bytes 1572872 | tf_op jit(solution)/shard_map/ppermute | solution.py:375
  19.6 20.5 %collective-permute-start.2 = (bf16[2,128,2048]{2,1,0:T(8,128)(2,1)S(1)}, bf16[2,128,2048]{2,1,0:T(8,128)(2,1)S(1)}, u32[]{:S(2)}, u32[]{:S(2)}) collective-permute-start(bf16[2,128,2048]{2,1,0:T(8,128)(2,1)S(1)} %pad_maximum_fusion.refs_0_), channel_id=1, source_target_pairs={{0,2},{1,17},{2,0},{3,19},{4,6},{5,21},{6,4},{7,23},{8,10},{9,25},... | collective-permute-start | bytes 3145736 | tf_op jit(solution)/shard_map/ppermute | solution.py:375
  20.1 19.9 %collective-permute-start.6 = (bf16[128,2048]{1,0:T(8,128)(2,1)S(1)}, bf16[128,2048]{1,0:T(8,128)(2,1)S(1)}, u32[]{:S(2)}, u32[]{:S(2)}) collective-permute-start(bf16[128,2048]{1,0:T(8,128)(2,1)S(1)} %collective-permute-done), channel_id=1, source_target_pairs={{0,16},{1,3},{2,18},{3,1},{4,20},{5,7},{6,22},{7,5},{8,24},{9,11},... | collective-permute-start | bytes 1572872 | tf_op jit(solution)/shard_map/ppermute | solution.py:375
  21.6 19.7 %collective-permute-start.3 = (bf16[2,128,2048]{2,1,0:T(8,128)(2,1)S(1)}, bf16[2,128,2048]{2,1,0:T(8,128)(2,1)S(1)}, u32[]{:S(2)}, u32[]{:S(2)}) collective-permute-start(bf16[2,128,2048]{2,1,0:T(8,128)(2,1)S(1)} %pad_maximum_fusion.refs_0_), channel_id=1, source_target_pairs={{0,1},{1,0},{2,3},{3,2},{4,5},{5,4},{6,7},{7,6},{8,9},{9,8},{10,11... | collective-permute-start | bytes 3145736 | tf_op jit(solution)/shard_map/ppermute | solution.py:375
  40.2 26.5 %collective-permute-start.10 = (bf16[2,128,2048]{2,1,0:T(8,128)(2,1)S(1)}, bf16[2,128,2048]{2,1,0:T(8,128)(2,1)S(1)}, u32[]{:S(2)}, u32[]{:S(2)}) collective-permute-start(bf16[2,128,2048]{2,1,0:T(8,128)(2,1)S(1)} %pad_maximum_fusion.1.refs_0_), channel_id=1, source_target_pairs={{0,4},{1,5},{2,6},{3,7},{4,12},{5,13},{6,14},{7,15},{8,0},{9,1},{1... | collective-permute-start | bytes 3145736 | tf_op jit(solution)/shard_map/ppermute | solution.py:375
  40.7 26.5 %collective-permute-start.7 = (bf16[2,128,2048]{2,1,0:T(8,128)(2,1)S(1)}, bf16[2,128,2048]{2,1,0:T(8,128)(2,1)}, u32[]{:S(2)}, u32[]{:S(2)}) collective-permute-start(bf16[2,128,2048]{2,1,0:T(8,128)(2,1)S(1)} %pad_maximum_fusion.1.refs_0_), channel_id=1, source_target_pairs={{0,2},{1,17},{2,0},{3,19},{4,6},{5,21},{6,4},{7,23},{8,10},{9,25},... | collective-permute-start | bytes 3145736 | tf_op jit(solution)/shard_map/ppermute | solution.py:375
  66.7 14.9 %collective-permute-start.18 = (bf16[2,128,2048]{2,1,0:T(8,128)(2,1)S(1)}, bf16[2,128,2048]{2,1,0:T(8,128)(2,1)}, u32[]{:S(2)}, u32[]{:S(2)}) collective-permute-start(bf16[2,128,2048]{2,1,0:T(8,128)(2,1)S(1)} %collective-permute-done.10.refs_6_.refs_0_), channel_id=1, source_target_pairs={{0,2},{1,17},{2,0},{3,19},{4,6},{5,21},{6,4},{7,23},{8,10},{9,25},... | collective-permute-start | bytes 3145736 | tf_op jit(solution)/shard_map/ppermute | solution.py:375
  67.2 18.4 %collective-permute-start.8 = (bf16[2,128,2048]{2,1,0:T(8,128)(2,1)S(1)}, bf16[2,128,2048]{2,1,0:T(8,128)(2,1)S(1)}, u32[]{:S(2)}, u32[]{:S(2)}) collective-permute-start(bf16[2,128,2048]{2,1,0:T(8,128)(2,1)S(1)} %pad_maximum_fusion.1.refs_0_), channel_id=1, source_target_pairs={{0,1},{1,0},{2,3},{3,2},{4,5},{5,4},{6,7},{7,6},{8,9},{9,8},{10,11... | collective-permute-start | bytes 3145736 | tf_op jit(solution)/shard_map/ppermute | solution.py:375
  67.2 19.4 %collective-permute-start.9 = (bf16[2,128,2048]{2,1,0:T(8,128)(2,1)}, bf16[2,128,2048]{2,1,0:T(8,128)(2,1)}, u32[]{:S(2)}, u32[]{:S(2)}) collective-permute-start(bf16[2,128,2048]{2,1,0:T(8,128)(2,1)} %collective-permute-done.7.refs_1_), channel_id=1, source_target_pairs={{0,1},{1,0},{2,3},{3,2},{4,5},{5,4},{6,7},{7,6},{8,9},{9,8},{10,11... | collective-permute-start | bytes 3145736 | tf_op jit(solution)/shard_map/ppermute | solution.py:375
  67.7 37.5 %collective-permute-start.15 = (bf16[2,128,2048]{2,1,0:T(8,128)(2,1)S(1)}, bf16[2,128,2048]{2,1,0:T(8,128)(2,1)S(1)}, u32[]{:S(2)}, u32[]{:S(2)}) collective-permute-start(bf16[2,128,2048]{2,1,0:T(8,128)(2,1)S(1)} %collective-permute-done.10.refs_6_.refs_0_), channel_id=1, source_target_pairs={{0,4},{1,5},{2,6},{3,7},{4,12},{5,13},{6,14},{7,15},{8,0},{9,1},{1... | collective-permute-start | bytes 3145736 | tf_op jit(solution)/shard_map/ppermute | solution.py:375
  67.7 29.6 %collective-permute-start.5 = (bf16[320,768]{1,0:T(8,128)(2,1)}, bf16[320,768]{1,0:T(8,128)(2,1)S(1)}, u32[]{:S(2)}, u32[]{:S(2)}) collective-permute-start(bf16[320,768]{1,0:T(8,128)(2,1)} %gate_up.4.refs_5_.refs_0_), channel_id=1, source_target_pairs={{0,16},{1,17},{2,18},{3,19},{4,20},{5,21},{6,22},{7,23},{8,24},{9,... | collective-permute-start | bytes 1474568 | tf_op jit(solution)/shard_map/ppermute | solution.py:375
  81.6 37.4 %collective-permute-start.19 = (bf16[2,128,2048]{2,1,0:T(8,128)(2,1)S(1)}, bf16[2,128,2048]{2,1,0:T(8,128)(2,1)}, u32[]{:S(2)}, u32[]{:S(2)}) collective-permute-start(bf16[2,128,2048]{2,1,0:T(8,128)(2,1)S(1)} %collective-permute-done.10.refs_6_.refs_0_), channel_id=1, source_target_pairs={{0,1},{1,0},{2,3},{3,2},{4,5},{5,4},{6,7},{7,6},{8,9},{9,8},{10,11... | collective-permute-start | bytes 3145736 | tf_op jit(solution)/shard_map/ppermute | solution.py:375
  86.6 32.9 %collective-permute-start.20 = (bf16[2,128,2048]{2,1,0:T(8,128)(2,1)}, bf16[2,128,2048]{2,1,0:T(8,128)(2,1)}, u32[]{:S(2)}, u32[]{:S(2)}) collective-permute-start(bf16[2,128,2048]{2,1,0:T(8,128)(2,1)} %collective-permute-done.18.refs_1_), channel_id=1, source_target_pairs={{0,1},{1,0},{2,3},{3,2},{4,5},{5,4},{6,7},{7,6},{8,9},{9,8},{10,11... | collective-permute-start | bytes 3145736 | tf_op jit(solution)/shard_map/ppermute | solution.py:375
  96.7 14.3 %collective-permute-start.12 = (bf16[320,768]{1,0:T(8,128)(2,1)}, bf16[320,768]{1,0:T(8,128)(2,1)S(1)}, u32[]{:S(2)}, u32[]{:S(2)}) collective-permute-start(bf16[320,768]{1,0:T(8,128)(2,1)} %gate_up.5.refs_3_.refs_0_.refs_5_), channel_id=1, source_target_pairs={{0,16},{1,17},{2,18},{3,19},{4,20},{5,21},{6,22},{7,23},{8,24},{9,... | collective-permute-start | bytes 1474568 | tf_op jit(solution)/shard_map/ppermute | solution.py:375
  105.3 24.3 %collective-permute-start.16 = (bf16[2,128,2048]{2,1,0:T(8,128)(2,1)S(1)}, bf16[2,128,2048]{2,1,0:T(8,128)(2,1)}, u32[]{:S(2)}, u32[]{:S(2)}) collective-permute-start(bf16[2,128,2048]{2,1,0:T(8,128)(2,1)S(1)} %collective-permute-done.15.refs_7_.refs_0_), channel_id=1, source_target_pairs={{0,2},{1,17},{2,0},{3,19},{4,6},{5,21},{6,4},{7,23},{8,10},{9,25},... | collective-permute-start | bytes 3145736 | tf_op jit(solution)/shard_map/ppermute | solution.py:375
  105.9 23.8 %collective-permute-start.11 = (bf16[2,128,2048]{2,1,0:T(8,128)(2,1)}, bf16[2,128,2048]{2,1,0:T(8,128)(2,1)}, u32[]{:S(2)}, u32[]{:S(2)}) collective-permute-start(bf16[2,128,2048]{2,1,0:T(8,128)(2,1)} %get-tuple-element.26), channel_id=1, source_target_pairs={{0,1},{1,0},{2,3},{3,2},{4,5},{5,4},{6,7},{7,6},{8,9},{9,8},{10,11... | collective-permute-start | bytes 3145736 | tf_op jit(solution)/shard_map/ppermute | solution.py:375
  119.0 15.5 %collective-permute-start.17 = (bf16[2,128,2048]{2,1,0:T(8,128)(2,1)S(1)}, bf16[2,128,2048]{2,1,0:T(8,128)(2,1)}, u32[]{:S(2)}, u32[]{:S(2)}) collective-permute-start(bf16[2,128,2048]{2,1,0:T(8,128)(2,1)S(1)} %collective-permute-done.15.refs_7_.refs_0_), channel_id=1, source_target_pairs={{0,1},{1,0},{2,3},{3,2},{4,5},{5,4},{6,7},{7,6},{8,9},{9,8},{10,11... | collective-permute-start | bytes 3145736 | tf_op jit(solution)/shard_map/ppermute | solution.py:375
  133.4 25.7 %collective-permute-start.14 = (bf16[2,128,2048]{2,1,0:T(8,128)(2,1)}, bf16[2,128,2048]{2,1,0:T(8,128)(2,1)S(1)}, u32[]{:S(2)}, u32[]{:S(2)}) collective-permute-start(bf16[2,128,2048]{2,1,0:T(8,128)(2,1)} %pad_maximum_fusion.2), channel_id=1, source_target_pairs={{0,2},{1,3},{2,0},{3,1},{4,6},{5,7},{6,4},{7,5},{8,10},{9,11},{10,... | collective-permute-start | bytes 3145736 | tf_op jit(solution)/shard_map/ppermute | solution.py:375
  144.6 14.5 %collective-permute-start.22 = (bf16[320,768]{1,0:T(8,128)(2,1)}, bf16[320,768]{1,0:T(8,128)(2,1)S(1)}, u32[]{:S(2)}, u32[]{:S(2)}) collective-permute-start(bf16[320,768]{1,0:T(8,128)(2,1)} %gate_up.7.refs_4_.refs_0_), channel_id=1, source_target_pairs={{0,16},{1,17},{2,18},{3,19},{4,20},{5,21},{6,22},{7,23},{8,24},{9,... | collective-permute-start | bytes 1474568 | tf_op jit(solution)/shard_map/ppermute | solution.py:375
  155.3 13.6 %collective-permute-start.27 = (bf16[2,128,2048]{2,1,0:T(8,128)(2,1)}, bf16[2,128,2048]{2,1,0:T(8,128)(2,1)}, u32[]{:S(2)}, u32[]{:S(2)}) collective-permute-start(bf16[2,128,2048]{2,1,0:T(8,128)(2,1)} %get-tuple-element.36), channel_id=1, source_target_pairs={{0,1},{1,0},{2,3},{3,2},{4,5},{5,4},{6,7},{7,6},{8,9},{9,8},{10,11... | collective-permute-start | bytes 3145736 | tf_op jit(solution)/shard_map/ppermute | solution.py:375
  168.9 15.3 %collective-permute-start.25 = (bf16[128,2048]{1,0:T(8,128)(2,1)S(1)}, bf16[128,2048]{1,0:T(8,128)(2,1)S(1)}, u32[]{:S(2)}, u32[]{:S(2)}) collective-permute-start(bf16[128,2048]{1,0:T(8,128)(2,1)S(1)} %fusion.9), channel_id=1, source_target_pairs={{0,4},{1,5},{2,6},{3,7},{4,12},{5,13},{6,14},{7,15},{8,0},{9,1},{1... | collective-permute-start | bytes 1572872 | tf_op jit(solution)/shard_map/ppermute | solution.py:375
  170.3 14.4 %collective-permute-start.28 = (bf16[128,2048]{1,0:T(8,128)(2,1)S(1)}, bf16[128,2048]{1,0:T(8,128)(2,1)S(1)}, u32[]{:S(2)}, u32[]{:S(2)}) collective-permute-start(bf16[128,2048]{1,0:T(8,128)(2,1)S(1)} %fusion.10), channel_id=1, source_target_pairs={{0,2},{1,3},{2,0},{3,1},{4,6},{5,7},{6,4},{7,5},{8,10},{9,11},{10,... | collective-permute-start | bytes 1572872 | tf_op jit(solution)/shard_map/ppermute | solution.py:375
  186.0 14.5 %collective-permute-start.29 = (bf16[128,2048]{1,0:T(8,128)(2,1)S(1)}, bf16[128,2048]{1,0:T(8,128)(2,1)S(1)}, u32[]{:S(2)}, u32[]{:S(2)}) collective-permute-start(bf16[128,2048]{1,0:T(8,128)(2,1)S(1)} %fusion.4), channel_id=1, source_target_pairs={{0,4},{1,5},{2,6},{3,7},{4,12},{5,13},{6,14},{7,15},{8,0},{9,1},{1... | collective-permute-start | bytes 1572872 | tf_op jit(solution)/shard_map/ppermute | solution.py:375
  (25 other events, 279.1 us)

commit v7 on v6

--- a/solution.py
+++ b/solution.py
@@ -10,7 +10,7 @@
 
 UNITS = 64
 SCALE = 1.0 / 256.0
-VMEM = 60 * 1024 * 1024
+VMEM = 40 * 1024 * 1024
 
 
 def group_of(capacity):
@@ -365,6 +365,7 @@
         return moves
 
     onward = perm(lambda x, z, y, c: (x, following[z], y, c))
+    backward = [(to, source) for source, to in onward]
     first = perm(lambda x, z, y, c: (x ^ (1 - c), z, y ^ c, c))
     second = perm(lambda x, z, y, c: (x ^ c, z, y ^ (1 - c), c))
     sibling = perm(lambda x, z, y, c: (x, z, y, 1 - c))
@@ -382,13 +383,12 @@
     where = lax.dynamic_index_in_dim(jnp.asarray(table.reshape(2 * experts, layers, 6)), device, 0, keepdims=False)
     code = lax.all_to_all(codes_of(expert_ids, numerators, experts), "expert", split_axis=0, concat_axis=0, tiled=True)
 
+    near = move(tokens, first)
     later = move(tokens, onward)
-    near = move(tokens, first)
+    last = move(later, onward)
     later, near, code, where = lax.optimization_barrier((later, near, code, where))
-    pairs = [jnp.stack([tokens, near]), jnp.stack([later, move(later, first)])]
-    pairs.append(move(pairs[1], onward))
-
-    mine, others, keeps, gots, backs, hops = [], [], [], [], [], []
+    pairs = [jnp.stack([tokens, near])] + [jnp.stack([v, move(v, first)]) for v in (later, last)]
+    pairs.append(move(pairs[2], onward))
 
     def after(value, *done):
         return lax.optimization_barrier((value, *done))[0]
@@ -398,43 +398,37 @@
         return [pairs[k], cross, move(pairs[k], sibling), move(after(cross, *done), sibling)]
 
     def gate_up(k, shards_of, *earlier):
-        mine.append(pick_call(k, where, code, shards_of, gate_up_weight[0], mine[-1:] + list(earlier), capacity))
-        others.append(move(mine[k], over_x))
-
-    def down(k, *earlier):
-        keep, send = sum_call(k, where, code, mine[k], others[k], down_weight[0], keeps[-1:] + list(earlier), capacity)
-        keeps.append(keep)
-        gots.append(move(send, sibling))
-
-    def away(k):
-        return (keeps[k][1].astype(jnp.float32) + gots[k][1].astype(jnp.float32)).astype(jnp.bfloat16)
-
-    def hop(k):
-        terms = [v.astype(jnp.float32) for v in [keeps[k][0], gots[k][0], backs[k], *hops[-1:]]]
-        total = functools.reduce(jnp.add, terms).astype(jnp.bfloat16)
-        if k:
-            hops.append(move(total, onward))
-        return total
-
-    gate_up(0, spread(0))
-    gate_up(1, spread(1), pairs[2])
-    pairs[2] = after(pairs[2], mine[0])
-    pairs.append(move(pairs[2], onward))
-    down(0, mine[1])
-    pairs[3] = after(pairs[3], keeps[0])
-    down(1)
-    both = move(jnp.stack([away(0), away(1)]), over_y)
-    backs += [both[0], both[1]]
-    gate_up(2, spread(2), keeps[1], pairs[3])
-    gate_up(3, spread(3, mine[2]))
-    hop(1)
-    down(2, mine[3])
-    backs.append(move(away(2), over_y))
-    down(3, both)
-    backs.append(move(after(away(3), hops[0]), over_y))
-    hop(2)
-    hop(3)
-    return hop(0)
+        mine = pick_call(k, where, code, shards_of, gate_up_weight[0], earlier, capacity)
+        return mine, move(mine, over_x)
+
+    def down(k, hidden, *earlier):
+        keep, send = sum_call(k, where, code, *hidden, down_weight[0], earlier, capacity)
+        return keep, move(send, sibling)
+
+    def away(part):
+        keep, got = part
+        return (keep[1].astype(jnp.float32) + got[1].astype(jnp.float32)).astype(jnp.bfloat16)
+
+    def total(part, back, *hop):
+        terms = [v.astype(jnp.float32) for v in (part[0][0], part[1][0], back, *hop)]
+        return functools.reduce(jnp.add, terms).astype(jnp.bfloat16)
+
+    hidden0 = gate_up(0, spread(0))
+    pairs[3] = after(pairs[3], hidden0[0])
+    shards2 = spread(2, hidden0[0])
+    hidden1 = gate_up(1, spread(1, hidden0[0]), pairs[3], shards2[1])
+    part0 = down(0, hidden0, hidden1[0])
+    hidden2 = gate_up(2, shards2, part0[0])
+    back0 = move(away(part0), over_y)
+    hidden3 = gate_up(3, spread(3, hidden1[0]), hidden2[0])
+    part1 = down(1, hidden1, hidden3[0], back0)
+    back1 = move(away(part1), over_y)
+    part2 = down(2, hidden2, part1[0], hidden3[1])
+    part3 = down(3, hidden3, part2[0], back1)
+    from_next = move(total(part1, back1), backward)
+    from_far = move(total(part2, move(away(part2), over_y)), onward)
+    from_last = move(total(part3, move(away(part3), over_y), after(from_far, from_next)), onward)
+    return total(part0, back0, from_next, from_last)
 
 
 def solution(mesh):

time: 219 us -> 207 us (0.945)
  waiting for transfers between devices: 95.9 us -> 111 us
  Pallas kernels: 68.7 us -> 57.6 us
  other arithmetic: 15.4 us -> 5.31 us
  local copies, waits for them, and re-layouts: 6.78 us -> 0.7 us
    ppermute x31 -> x33, waiting for transfers between devices: 90.4 us -> 105 us  [move(): return lax.ppermute(value, axes, moves)]
    convert_element_type x8, other arithmetic: 11.6 us -> 2.53 us  [the longest x4 2.03 us: total(): return functools.reduce(jnp.add, terms).astype(jnp.bfloat16)]
    pallas_call x4, Pallas kernels: 40.2 us -> 33 us  [pick_call(): pl.pallas_call(functools.partial(pick_kernel, capacity, k), in_specs=[pl....]
    unnamed x34 -> x4, local copies, waits for them, and re-layouts: 5.51 us -> 0.01 us
    pallas_call x4, Pallas kernels: 28.5 us -> 24.6 us  [sum_call(): pl.pallas_call(functools.partial(sum_kernel, capacity, k), in_specs=[pl.B...]
    ppermute x31 -> x33, starting transfers between devices: 25.2 us -> 26.2 us  [move(): return lax.ppermute(value, axes, moves)]
  transfers between devices with their start and end apart: 32 -> 34, of which waited for: 12 -> 13; matrix products, arithmetic and copies ran while one was open for 6% -> 2% of each run, Pallas kernels for 32% -> 28%
where the time goes in v7:
time: 207 us
  waiting for transfers between devices  111 us (54%)
  Pallas kernels  57.6 us (28%)
  starting transfers between devices  31.2 us (15%)
  other arithmetic  5.31 us (3%)
    ppermute x33, waiting for transfers between devices, move(): return lax.ppermute(value, axes, moves)  105 us
    pallas_call x4, Pallas kernels, pick_call(): pl.pallas_call(functools.partial(pick_kernel, capacity, k), in_specs=[pl....  33 us
    ppermute x33, starting transfers between devices, move(): return lax.ppermute(value, axes, moves)  26.2 us
    pallas_call x4, Pallas kernels, sum_call(): pl.pallas_call(functools.partial(sum_kernel, capacity, k), in_specs=[pl.B...  24.6 us
    all_to_all x1, waiting for transfers between devices, pair_shards(): lax.all_to_all(codes_of(expert_ids, numerators, experts), 'expert', split...  6.07 us
    all_to_all x1, starting transfers between devices, pair_shards(): lax.all_to_all(codes_of(expert_ids, numerators, experts), 'expert', split...  4.93 us
  transfers between devices with their start and end apart: 34, of which 13 were waited for; matrix products, arithmetic and copies ran while one was open for 2% of the time, Pallas kernels for 28%

profile of v7, /device:TPU:0, one launch (start us, length us, event | category | flops | bytes accessed | tf_op | source)
XLA Modules:
  0.0 206.5 jit_solution(10658911271369341929)
XLA Ops:
  0.0 3.0 %collective-permute-start = (bf16[128,2048]{1,0:T(8,128)(2,1)}, bf16[128,2048]{1,0:T(8,128)(2,1)S(1)}, u32[]{:S(2)}, u32[]{:S(2)}) collective-permute-start(bf16[128,2048]{1,0:T(8,128)(2,1)} %param.6), channel_id=1, source_target_pairs={{0,4},{1,5},{2,6},{3,7},{4,12},{5,13},{6,14},{7,15},{8,0},{9,1},{1... | collective-permute-start | bytes 1572872 | tf_op jit(solution)/shard_map/ppermute | solution.py:376
  6.7 4.9 %all-to-all-start = ((s32[16,1,128]{2,1,0:T(1,128)}), s32[16,1,128]{2,1,0:T(1,128)S(1)}, u32[]{:S(2)}, u32[]{:S(2)}) async-start(s32[16,1,128]{2,1,0:T(1,128)} %bitcast.3), calls=%async_computation | async-start | bytes 16384 | tf_op jit(solution)/shard_map/all_to_all | solution.py:384
  12.3 6.1 %all-to-all-done = s32[16,1,128]{2,1,0:T(1,128)S(1)} async-done(((s32[16,1,128]{2,1,0:T(1,128)}), s32[16,1,128]{2,1,0:T(1,128)S(1)}, u32[]{:S(2)}, u32[]{:S(2)}) %all-to-all-start) | async-done | bytes 8224 | tf_op jit(solution)/shard_map/all_to_all | solution.py:384
  22.2 17.8 %collective-permute-done.2.refs_1_ = bf16[2,128,2048]{2,1,0:T(8,128)(2,1)S(1)} collective-permute-done((bf16[2,128,2048]{2,1,0:T(8,128)(2,1)S(1)}, bf16[2,128,2048]{2,1,0:T(8,128)(2,1)S(1)}, u32[]{:S(2)}, u32[]{:S(2)}) %collective-permute-start.2) | collective-permute-done | bytes 1048608 | tf_op jit(solution)/shard_map/ppermute | solution.py:376
  41.7 13.2 %collective-permute-done.11 = bf16[128,2048]{1,0:T(8,128)(2,1)S(1)} collective-permute-done((bf16[128,2048]{1,0:T(8,128)(2,1)S(1)}, bf16[128,2048]{1,0:T(8,128)(2,1)S(1)}, u32[]{:S(2)}, u32[]{:S(2)}) %collective-permute-start.11) | collective-permute-done | bytes 524320 | tf_op jit(solution)/shard_map/ppermute | solution.py:376
  55.6 8.5 %gate_up.4.refs_0_ = bf16[320,768]{1,0:T(8,128)(2,1)S(1)} custom-call(s32[4,6]{1,0:T(4,128)S(1)} %dynamic-slice_bitcast_fusion.where_ref, s32[16,128]{1,0:T(8,128)S(1)} %bitcast.53, bf16[2,128,2048]{2,1,0:T(8,128)(2,1)S(1)} %pad_maximum_fusion.refs_0_, bf16[2,128,2048]{2,1,0:T(8,128)(2,1)S(1)} %collective-permute-done.2.refs_1_, ...), custom_call_target="tpu_custom_call" | custom-call | flops 4362076160 | bytes 17268736 | tf_op jit(solution)/shard_map/gate_up/pallas_call | solution.py:257
  65.8 13.8 %collective-permute-done.12.refs_5_.refs_0_ = bf16[2,128,2048]{2,1,0:T(8,128)(2,1)S(1)} collective-permute-done((bf16[2,128,2048]{2,1,0:T(8,128)(2,1)S(1)}, bf16[2,128,2048]{2,1,0:T(8,128)(2,1)S(1)}, u32[]{:S(2)}, u32[]{:S(2)}) %collective-permute-start.12) | collective-permute-done | bytes 1048608 | tf_op jit(solution)/shard_map/ppermute | solution.py:376
  80.2 8.2 %gate_up.5.refs_3_.refs_0_ = bf16[320,768]{1,0:T(8,128)(2,1)S(1)} custom-call(s32[4,6]{1,0:T(4,128)S(1)} %dynamic-slice_bitcast_fusion.where_ref, s32[16,128]{1,0:T(8,128)S(1)} %bitcast.54, bf16[2,128,2048]{2,1,0:T(8,128)(2,1)S(1)} %pad_maximum_fusion.1.refs_0_, bf16[2,128,2048]{2,1,0:T(8,128)(2,1)S(1)} %collective-permute-done.7.refs_1_, ...), custom_call_target="tpu_custom_call" | custom-call | flops 4362076160 | bytes 17268736 | tf_op jit(solution)/shard_map/gate_up/pallas_call | solution.py:257
  88.4 6.1 %down.4 = (bf16[2,128,2048]{2,1,0:T(8,128)(2,1)S(1)}, bf16[2,128,2048]{2,1,0:T(8,128)(2,1)S(1)}) custom-call(s32[4,6]{1,0:T(4,128)S(1)} %dynamic-slice_bitcast_fusion.where_ref, s32[16,128]{1,0:T(8,128)S(1)} %bitcast.55, bf16[320,768]{1,0:T(8,128)(2,1)S(1)} %gate_up.4.refs_0_, bf16[320,768]{1,0:T(8,128)(2,1)S(1)} %collective-permute-done.5.refs_1_, ...), custom_call_target="tpu_custom_call" | custom-call | flops 2181038080 | bytes 9371648 | tf_op jit(solution)/shard_map/down/pallas_call | solution.py:287
  100.2 8.1 %gate_up.6.refs_5_.refs_0_ = bf16[320,768]{1,0:T(8,128)(2,1)S(1)} custom-call(s32[4,6]{1,0:T(4,128)S(1)} %dynamic-slice_bitcast_fusion.where_ref, s32[16,128]{1,0:T(8,128)S(1)} %bitcast.56, bf16[2,128,2048]{2,1,0:T(8,128)(2,1)S(1)} %pad_maximum_fusion.2.refs_0_, bf16[2,128,2048]{2,1,0:T(8,128)(2,1)S(1)} %collective-permute-done.13.refs_6_.refs_1_, ...), custom_call_target="tpu_custom_call" | custom-call | flops 4362076160 | bytes 17268736 | tf_op jit(solution)/shard_map/gate_up/pallas_call | solution.py:257
  109.6 8.1 %gate_up.7.refs_3_.refs_0_ = bf16[320,768]{1,0:T(8,128)(2,1)S(1)} custom-call(s32[4,6]{1,0:T(4,128)S(1)} %dynamic-slice_bitcast_fusion.where_ref, s32[16,128]{1,0:T(8,128)S(1)} %bitcast.57, bf16[2,128,2048]{2,1,0:T(8,128)(2,1)S(1)} %collective-permute-done.12.refs_5_.refs_0_, bf16[2,128,2048]{2,1,0:T(8,128)(2,1)S(1)} %collective-permute-done.17.refs_1_, ...), custom_call_target="tpu_custom_call" | custom-call | flops 4362076160 | bytes 17268736 | tf_op jit(solution)/shard_map/gate_up/pallas_call | solution.py:257
  118.7 6.3 %down.5 = (bf16[2,128,2048]{2,1,0:T(8,128)(2,1)S(1)}, bf16[2,128,2048]{2,1,0:T(8,128)(2,1)S(1)}) custom-call(s32[4,6]{1,0:T(4,128)S(1)} %dynamic-slice_bitcast_fusion.where_ref, s32[16,128]{1,0:T(8,128)S(1)} %bitcast.58, bf16[320,768]{1,0:T(8,128)(2,1)S(1)} %gate_up.5.refs_3_.refs_0_, bf16[320,768]{1,0:T(8,128)(2,1)S(1)} %collective-permute-done.16.refs_1_, ...), custom_call_target="tpu_custom_call" | custom-call | flops 2181038080 | bytes 9371648 | tf_op jit(solution)/shard_map/down/pallas_call | solution.py:287
  125.1 7.1 %collective-permute-done.25.refs_4_.refs_1_ = bf16[320,768]{1,0:T(8,128)(2,1)S(1)} collective-permute-done((bf16[320,768]{1,0:T(8,128)(2,1)S(1)}, bf16[320,768]{1,0:T(8,128)(2,1)S(1)}, u32[]{:S(2)}, u32[]{:S(2)}) %collective-permute-start.25) | collective-permute-done | bytes 491552 | tf_op jit(solution)/shard_map/ppermute | solution.py:376
  132.2 6.1 %down.6 = (bf16[2,128,2048]{2,1,0:T(8,128)(2,1)S(1)}, bf16[2,128,2048]{2,1,0:T(8,128)(2,1)S(1)}) custom-call(s32[4,6]{1,0:T(4,128)S(1)} %dynamic-slice_bitcast_fusion.where_ref, s32[16,128]{1,0:T(8,128)S(1)} %bitcast.59, bf16[320,768]{1,0:T(8,128)(2,1)S(1)} %gate_up.6.refs_5_.refs_0_, bf16[320,768]{1,0:T(8,128)(2,1)S(1)} %collective-permute-done.26.refs_1_, ...), custom_call_target="tpu_custom_call" | custom-call | flops 2181038080 | bytes 9371648 | tf_op jit(solution)/shard_map/down/pallas_call | solution.py:287
  138.6 1.6 collective-permute-start.23
  141.2 1.6 collective-permute-start.30
  142.8 10.6 %collective-permute-done.23.refs_4_ = bf16[128,2048]{1,0:T(8,128)(2,1)S(1)} collective-permute-done((bf16[128,2048]{1,0:T(8,128)(2,1)S(1)}, bf16[128,2048]{1,0:T(8,128)(2,1)S(1)}, u32[]{:S(2)}, u32[]{:S(2)}) %collective-permute-start.23) | collective-permute-done | bytes 524320 | tf_op jit(solution)/shard_map/ppermute | solution.py:376
  153.3 6.1 %down.7 = (bf16[2,128,2048]{2,1,0:T(8,128)(2,1)S(1)}, bf16[2,128,2048]{2,1,0:T(8,128)(2,1)S(1)}) custom-call(s32[4,6]{1,0:T(4,128)S(1)} %dynamic-slice_bitcast_fusion.where_ref, s32[16,128]{1,0:T(8,128)S(1)} %bitcast.60, bf16[320,768]{1,0:T(8,128)(2,1)S(1)} %gate_up.7.refs_3_.refs_0_, bf16[320,768]{1,0:T(8,128)(2,1)S(1)} %collective-permute-done.25.refs_4_.refs_1_, ...), custom_call_target="tpu_custom_call" | custom-call | flops 2181038080 | bytes 9371648 | tf_op jit(solution)/shard_map/down/pallas_call | solution.py:287
  159.5 4.6 %collective-permute-done.30 = bf16[128,2048]{1,0:T(8,128)(2,1)S(1)} collective-permute-done((bf16[128,2048]{1,0:T(8,128)(2,1)S(1)}, bf16[128,2048]{1,0:T(8,128)(2,1)S(1)}, u32[]{:S(2)}, u32[]{:S(2)}) %collective-permute-start.30) | collective-permute-done | bytes 524320 | tf_op jit(solution)/shard_map/ppermute | solution.py:376
  165.4 2.3 %collective-permute-start.24 = (bf16[128,2048]{1,0:T(8,128)(2,1)S(1)}, bf16[128,2048]{1,0:T(8,128)(2,1)S(1)}, u32[]{:S(2)}, u32[]{:S(2)}) collective-permute-start(bf16[128,2048]{1,0:T(8,128)(2,1)S(1)} %fusion.6), channel_id=1, source_target_pairs={{4,0},{5,1},{6,2},{7,3},{12,4},{13,5},{14,6},{15,7},{0,8},{1,9},{2... | collective-permute-start | bytes 1572872 | tf_op jit(solution)/shard_map/ppermute | solution.py:376
  167.8 1.6 collective-permute-start.28
  169.4 10.6 %collective-permute-done.31 = bf16[128,2048]{1,0:T(8,128)(2,1)S(1)} collective-permute-done((bf16[128,2048]{1,0:T(8,128)(2,1)S(1)}, bf16[128,2048]{1,0:T(8,128)(2,1)S(1)}, u32[]{:S(2)}, u32[]{:S(2)}) %collective-permute-start.31) | collective-permute-done | bytes 524320 | tf_op jit(solution)/shard_map/ppermute | solution.py:376
  180.0 10.1 %collective-permute-done.24 = bf16[128,2048]{1,0:T(8,128)(2,1)S(1)} collective-permute-done((bf16[128,2048]{1,0:T(8,128)(2,1)S(1)}, bf16[128,2048]{1,0:T(8,128)(2,1)S(1)}, u32[]{:S(2)}, u32[]{:S(2)}) %collective-permute-start.24) | collective-permute-done | bytes 524320 | tf_op jit(solution)/shard_map/ppermute | solution.py:376
  191.4 13.9 %collective-permute-done.32 = bf16[128,2048]{1,0:T(8,128)(2,1)S(1)} collective-permute-done((bf16[128,2048]{1,0:T(8,128)(2,1)S(1)}, bf16[128,2048]{1,0:T(8,128)(2,1)S(1)}, u32[]{:S(2)}, u32[]{:S(2)}) %collective-permute-start.32) | collective-permute-done | bytes 524320 | tf_op jit(solution)/shard_map/ppermute | solution.py:376
  (72 shorter events, 25.8 us)
Async XLA Ops:
  0.0 18.4 %collective-permute-start = (bf16[128,2048]{1,0:T(8,128)(2,1)}, bf16[128,2048]{1,0:T(8,128)(2,1)S(1)}, u32[]{:S(2)}, u32[]{:S(2)}) collective-permute-start(bf16[128,2048]{1,0:T(8,128)(2,1)} %param.6), channel_id=1, source_target_pairs={{0,4},{1,5},{2,6},{3,7},{4,12},{5,13},{6,14},{7,15},{8,0},{9,1},{1... | collective-permute-start | bytes 1572872 | tf_op jit(solution)/shard_map/ppermute | solution.py:376
  3.0 15.4 %collective-permute-start.1 = (bf16[128,2048]{1,0:T(8,128)(2,1)}, bf16[128,2048]{1,0:T(8,128)(2,1)S(1)}, u32[]{:S(2)}, u32[]{:S(2)}) collective-permute-start(bf16[128,2048]{1,0:T(8,128)(2,1)} %param.6), channel_id=1, source_target_pairs={{0,16},{1,3},{2,18},{3,1},{4,20},{5,7},{6,22},{7,5},{8,24},{9,11},... | collective-permute-start | bytes 1572872 | tf_op jit(solution)/shard_map/ppermute | solution.py:376
  19.6 20.5 %collective-permute-start.2 = (bf16[2,128,2048]{2,1,0:T(8,128)(2,1)S(1)}, bf16[2,128,2048]{2,1,0:T(8,128)(2,1)S(1)}, u32[]{:S(2)}, u32[]{:S(2)}) collective-permute-start(bf16[2,128,2048]{2,1,0:T(8,128)(2,1)S(1)} %pad_maximum_fusion.refs_0_), channel_id=1, source_target_pairs={{0,2},{1,17},{2,0},{3,19},{4,6},{5,21},{6,4},{7,23},{8,10},{9,25},... | collective-permute-start | bytes 3145736 | tf_op jit(solution)/shard_map/ppermute | solution.py:376
  20.1 19.9 %collective-permute-start.10 = (bf16[128,2048]{1,0:T(8,128)(2,1)S(1)}, bf16[128,2048]{1,0:T(8,128)(2,1)S(1)}, u32[]{:S(2)}, u32[]{:S(2)}) collective-permute-start(bf16[128,2048]{1,0:T(8,128)(2,1)S(1)} %collective-permute-done), channel_id=1, source_target_pairs={{0,4},{1,5},{2,6},{3,7},{4,12},{5,13},{6,14},{7,15},{8,0},{9,1},{1... | collective-permute-start | bytes 1572872 | tf_op jit(solution)/shard_map/ppermute | solution.py:376
  20.7 20.2 %collective-permute-start.6 = (bf16[128,2048]{1,0:T(8,128)(2,1)S(1)}, bf16[128,2048]{1,0:T(8,128)(2,1)S(1)}, u32[]{:S(2)}, u32[]{:S(2)}) collective-permute-start(bf16[128,2048]{1,0:T(8,128)(2,1)S(1)} %collective-permute-done), channel_id=1, source_target_pairs={{0,16},{1,3},{2,18},{3,1},{4,20},{5,7},{6,22},{7,5},{8,24},{9,11},... | collective-permute-start | bytes 1572872 | tf_op jit(solution)/shard_map/ppermute | solution.py:376
  22.2 32.8 %collective-permute-start.3 = (bf16[2,128,2048]{2,1,0:T(8,128)(2,1)S(1)}, bf16[2,128,2048]{2,1,0:T(8,128)(2,1)S(1)}, u32[]{:S(2)}, u32[]{:S(2)}) collective-permute-start(bf16[2,128,2048]{2,1,0:T(8,128)(2,1)S(1)} %pad_maximum_fusion.refs_0_), channel_id=1, source_target_pairs={{0,1},{1,0},{2,3},{3,2},{4,5},{5,4},{6,7},{7,6},{8,9},{9,8},{10,11... | collective-permute-start | bytes 3145736 | tf_op jit(solution)/shard_map/ppermute | solution.py:376
  40.0 15.6 %collective-permute-start.4 = (bf16[2,128,2048]{2,1,0:T(8,128)(2,1)S(1)}, bf16[2,128,2048]{2,1,0:T(8,128)(2,1)S(1)}, u32[]{:S(2)}, u32[]{:S(2)}) collective-permute-start(bf16[2,128,2048]{2,1,0:T(8,128)(2,1)S(1)} %collective-permute-done.2.refs_1_), channel_id=1, source_target_pairs={{0,1},{1,0},{2,3},{3,2},{4,5},{5,4},{6,7},{7,6},{8,9},{9,8},{10,11... | collective-permute-start | bytes 3145736 | tf_op jit(solution)/shard_map/ppermute | solution.py:376
  40.0 14.8 %collective-permute-start.11 = (bf16[128,2048]{1,0:T(8,128)(2,1)S(1)}, bf16[128,2048]{1,0:T(8,128)(2,1)S(1)}, u32[]{:S(2)}, u32[]{:S(2)}) collective-permute-start(bf16[128,2048]{1,0:T(8,128)(2,1)S(1)} %collective-permute-done.10), channel_id=1, source_target_pairs={{0,16},{1,3},{2,18},{3,1},{4,20},{5,7},{6,22},{7,5},{8,24},{9,11},... | collective-permute-start | bytes 1572872 | tf_op jit(solution)/shard_map/ppermute | solution.py:376
  41.0 23.2 %collective-permute-start.7 = (bf16[2,128,2048]{2,1,0:T(8,128)(2,1)S(1)}, bf16[2,128,2048]{2,1,0:T(8,128)(2,1)S(1)}, u32[]{:S(2)}, u32[]{:S(2)}) collective-permute-start(bf16[2,128,2048]{2,1,0:T(8,128)(2,1)S(1)} %pad_maximum_fusion.1.refs_0_), channel_id=1, source_target_pairs={{0,2},{1,17},{2,0},{3,19},{4,6},{5,21},{6,4},{7,23},{8,10},{9,25},... | collective-permute-start | bytes 3145736 | tf_op jit(solution)/shard_map/ppermute | solution.py:376
  41.7 38.5 %collective-permute-start.8 = (bf16[2,128,2048]{2,1,0:T(8,128)(2,1)S(1)}, bf16[2,128,2048]{2,1,0:T(8,128)(2,1)S(1)}, u32[]{:S(2)}, u32[]{:S(2)}) collective-permute-start(bf16[2,128,2048]{2,1,0:T(8,128)(2,1)S(1)} %pad_maximum_fusion.1.refs_0_), channel_id=1, source_target_pairs={{0,1},{1,0},{2,3},{3,2},{4,5},{5,4},{6,7},{7,6},{8,9},{9,8},{10,11... | collective-permute-start | bytes 3145736 | tf_op jit(solution)/shard_map/ppermute | solution.py:376
  54.9 25.2 %collective-permute-start.13 = (bf16[2,128,2048]{2,1,0:T(8,128)(2,1)S(1)}, bf16[2,128,2048]{2,1,0:T(8,128)(2,1)S(1)}, u32[]{:S(2)}, u32[]{:S(2)}) collective-permute-start(bf16[2,128,2048]{2,1,0:T(8,128)(2,1)S(1)} %pad_maximum_fusion.2.refs_0_), channel_id=1, source_target_pairs={{0,2},{1,17},{2,0},{3,19},{4,6},{5,21},{6,4},{7,23},{8,10},{9,25},... | collective-permute-start | bytes 3145736 | tf_op jit(solution)/shard_map/ppermute | solution.py:376
  55.0 24.6 %collective-permute-start.12 = (bf16[2,128,2048]{2,1,0:T(8,128)(2,1)S(1)}, bf16[2,128,2048]{2,1,0:T(8,128)(2,1)S(1)}, u32[]{:S(2)}, u32[]{:S(2)}) collective-permute-start(bf16[2,128,2048]{2,1,0:T(8,128)(2,1)S(1)} %pad_maximum_fusion.2.refs_0_), channel_id=1, source_target_pairs={{0,4},{1,5},{2,6},{3,7},{4,12},{5,13},{6,14},{7,15},{8,0},{9,1},{1... | collective-permute-start | bytes 3145736 | tf_op jit(solution)/shard_map/ppermute | solution.py:376
  64.2 16.0 %collective-permute-start.9 = (bf16[2,128,2048]{2,1,0:T(8,128)(2,1)S(1)}, bf16[2,128,2048]{2,1,0:T(8,128)(2,1)S(1)}, u32[]{:S(2)}, u32[]{:S(2)}) collective-permute-start(bf16[2,128,2048]{2,1,0:T(8,128)(2,1)S(1)} %collective-permute-done.7.refs_1_), channel_id=1, source_target_pairs={{0,1},{1,0},{2,3},{3,2},{4,5},{5,4},{6,7},{7,6},{8,9},{9,8},{10,11... | collective-permute-start | bytes 3145736 | tf_op jit(solution)/shard_map/ppermute | solution.py:376
  64.3 24.1 %collective-permute-start.5 = (bf16[320,768]{1,0:T(8,128)(2,1)S(1)}, bf16[320,768]{1,0:T(8,128)(2,1)S(1)}, u32[]{:S(2)}, u32[]{:S(2)}) collective-permute-start(bf16[320,768]{1,0:T(8,128)(2,1)S(1)} %gate_up.4.refs_0_), channel_id=1, source_target_pairs={{0,16},{1,17},{2,18},{3,19},{4,20},{5,21},{6,22},{7,23},{8,24},{9,... | collective-permute-start | bytes 1474568 | tf_op jit(solution)/shard_map/ppermute | solution.py:376
  79.6 15.9 %collective-permute-start.17 = (bf16[2,128,2048]{2,1,0:T(8,128)(2,1)S(1)}, bf16[2,128,2048]{2,1,0:T(8,128)(2,1)S(1)}, u32[]{:S(2)}, u32[]{:S(2)}) collective-permute-start(bf16[2,128,2048]{2,1,0:T(8,128)(2,1)S(1)} %collective-permute-done.12.refs_5_.refs_0_), channel_id=1, source_target_pairs={{0,2},{1,17},{2,0},{3,19},{4,6},{5,21},{6,4},{7,23},{8,10},{9,25},... | collective-permute-start | bytes 3145736 | tf_op jit(solution)/shard_map/ppermute | solution.py:376
  97.2 21.5 %collective-permute-start.16 = (bf16[320,768]{1,0:T(8,128)(2,1)S(1)}, bf16[320,768]{1,0:T(8,128)(2,1)S(1)}, u32[]{:S(2)}, u32[]{:S(2)}) collective-permute-start(bf16[320,768]{1,0:T(8,128)(2,1)S(1)} %gate_up.5.refs_3_.refs_0_), channel_id=1, source_target_pairs={{0,16},{1,17},{2,18},{3,19},{4,20},{5,21},{6,22},{7,23},{8,24},{9,... | collective-permute-start | bytes 1474568 | tf_op jit(solution)/shard_map/ppermute | solution.py:376
  98.7 20.0 %collective-permute-start.15 = (bf16[128,2048]{1,0:T(8,128)(2,1)S(1)}, bf16[128,2048]{1,0:T(8,128)(2,1)S(1)}, u32[]{:S(2)}, u32[]{:S(2)}) collective-permute-start(bf16[128,2048]{1,0:T(8,128)(2,1)S(1)} %fusion.10), channel_id=1, source_target_pairs={{0,2},{1,3},{2,0},{3,1},{4,6},{5,7},{6,4},{7,5},{8,10},{9,11},{10,... | collective-permute-start | bytes 1572872 | tf_op jit(solution)/shard_map/ppermute | solution.py:376
  108.4 16.7 %collective-permute-start.26 = (bf16[320,768]{1,0:T(8,128)(2,1)S(1)}, bf16[320,768]{1,0:T(8,128)(2,1)S(1)}, u32[]{:S(2)}, u32[]{:S(2)}) collective-permute-start(bf16[320,768]{1,0:T(8,128)(2,1)S(1)} %gate_up.6.refs_5_.refs_0_), channel_id=1, source_target_pairs={{0,16},{1,17},{2,18},{3,19},{4,20},{5,21},{6,22},{7,23},{8,24},{9,... | collective-permute-start | bytes 1474568 | tf_op jit(solution)/shard_map/ppermute | solution.py:376
  138.6 14.8 %collective-permute-start.23 = (bf16[128,2048]{1,0:T(8,128)(2,1)S(1)}, bf16[128,2048]{1,0:T(8,128)(2,1)S(1)}, u32[]{:S(2)}, u32[]{:S(2)}) collective-permute-start(bf16[128,2048]{1,0:T(8,128)(2,1)S(1)} %fusion.11), channel_id=1, source_target_pairs={{0,2},{1,3},{2,0},{3,1},{4,6},{5,7},{6,4},{7,5},{8,10},{9,11},{10,... | collective-permute-start | bytes 1572872 | tf_op jit(solution)/shard_map/ppermute | solution.py:376
  141.2 23.0 %collective-permute-start.30 = (bf16[128,2048]{1,0:T(8,128)(2,1)S(1)}, bf16[128,2048]{1,0:T(8,128)(2,1)S(1)}, u32[]{:S(2)}, u32[]{:S(2)}) collective-permute-start(bf16[128,2048]{1,0:T(8,128)(2,1)S(1)} %fusion.13), channel_id=1, source_target_pairs={{0,2},{1,3},{2,0},{3,1},{4,6},{5,7},{6,4},{7,5},{8,10},{9,11},{10,... | collective-permute-start | bytes 1572872 | tf_op jit(solution)/shard_map/ppermute | solution.py:376
  164.4 15.6 %collective-permute-start.31 = (bf16[128,2048]{1,0:T(8,128)(2,1)S(1)}, bf16[128,2048]{1,0:T(8,128)(2,1)S(1)}, u32[]{:S(2)}, u32[]{:S(2)}) collective-permute-start(bf16[128,2048]{1,0:T(8,128)(2,1)S(1)} %fusion.3), channel_id=1, source_target_pairs={{0,4},{1,5},{2,6},{3,7},{4,12},{5,13},{6,14},{7,15},{8,0},{9,1},{1... | collective-permute-start | bytes 1572872 | tf_op jit(solution)/shard_map/ppermute | solution.py:376
  165.4 24.7 %collective-permute-start.24 = (bf16[128,2048]{1,0:T(8,128)(2,1)S(1)}, bf16[128,2048]{1,0:T(8,128)(2,1)S(1)}, u32[]{:S(2)}, u32[]{:S(2)}) collective-permute-start(bf16[128,2048]{1,0:T(8,128)(2,1)S(1)} %fusion.6), channel_id=1, source_target_pairs={{4,0},{5,1},{6,2},{7,3},{12,4},{13,5},{14,6},{15,7},{0,8},{1,9},{2... | collective-permute-start | bytes 1572872 | tf_op jit(solution)/shard_map/ppermute | solution.py:376
  167.8 22.3 %collective-permute-start.28 = (bf16[128,2048]{1,0:T(8,128)(2,1)S(1)}, bf16[128,2048]{1,0:T(8,128)(2,1)S(1)}, u32[]{:S(2)}, u32[]{:S(2)}) collective-permute-start(bf16[128,2048]{1,0:T(8,128)(2,1)S(1)} %fusion.12), channel_id=1, source_target_pairs={{0,2},{1,3},{2,0},{3,1},{4,6},{5,7},{6,4},{7,5},{8,10},{9,11},{10,... | collective-permute-start | bytes 1572872 | tf_op jit(solution)/shard_map/ppermute | solution.py:376
  190.5 14.8 %collective-permute-start.32 = (bf16[128,2048]{1,0:T(8,128)(2,1)S(1)}, bf16[128,2048]{1,0:T(8,128)(2,1)S(1)}, u32[]{:S(2)}, u32[]{:S(2)}) collective-permute-start(bf16[128,2048]{1,0:T(8,128)(2,1)S(1)} %fusion.5), channel_id=1, source_target_pairs={{0,4},{1,5},{2,6},{3,7},{4,12},{5,13},{6,14},{7,15},{8,0},{9,1},{1... | collective-permute-start | bytes 1572872 | tf_op jit(solution)/shard_map/ppermute | solution.py:376
  (12 other events, 148.0 us)

commit v8 on v7

--- a/solution.py
+++ b/solution.py
@@ -381,21 +381,25 @@
         table[x, z, y, c, k] = [at + (y ^ (i & 1)) * 2 + (c ^ (i >> 1)) for i in range(4)] + [x, c]
     device = lax.axis_index("section") * experts + lax.axis_index("expert")
     where = lax.dynamic_index_in_dim(jnp.asarray(table.reshape(2 * experts, layers, 6)), device, 0, keepdims=False)
-    code = lax.all_to_all(codes_of(expert_ids, numerators, experts), "expert", split_axis=0, concat_axis=0, tiled=True)
+    def after(value, *done):
+        return lax.optimization_barrier((value, *done))[0]
 
     near = move(tokens, first)
     later = move(tokens, onward)
+    near_later = move(later, first)
     last = move(later, onward)
-    later, near, code, where = lax.optimization_barrier((later, near, code, where))
-    pairs = [jnp.stack([tokens, near])] + [jnp.stack([v, move(v, first)]) for v in (later, last)]
+    named = codes_of(after(expert_ids, last), numerators, experts)
+    code = lax.all_to_all(named, "expert", split_axis=0, concat_axis=0, tiled=True)
+    pairs = [jnp.stack([tokens, near]), jnp.stack([later, near_later])]
+    crosses = [move(pairs[0], second)]
+    near_last = move(after(last, near_later, crosses[0]), first)
+    pairs.append(jnp.stack([after(last, code), near_last]))
     pairs.append(move(pairs[2], onward))
-
-    def after(value, *done):
-        return lax.optimization_barrier((value, *done))[0]
+    crosses.append(move(after(pairs[1], pairs[2]), second))
+    crosses.append(move(pairs[2], second))
 
     def spread(k, *done):
-        cross = move(pairs[k], second)
-        return [pairs[k], cross, move(pairs[k], sibling), move(after(cross, *done), sibling)]
+        return [pairs[k], crosses[k], move(pairs[k], sibling), move(after(crosses[k], *done), sibling)]
 
     def gate_up(k, shards_of, *earlier):
         mine = pick_call(k, where, code, shards_of, gate_up_weight[0], earlier, capacity)
@@ -414,20 +418,21 @@
         return functools.reduce(jnp.add, terms).astype(jnp.bfloat16)
 
     hidden0 = gate_up(0, spread(0))
-    pairs[3] = after(pairs[3], hidden0[0])
-    shards2 = spread(2, hidden0[0])
-    hidden1 = gate_up(1, spread(1, hidden0[0]), pairs[3], shards2[1])
-    part0 = down(0, hidden0, hidden1[0])
-    hidden2 = gate_up(2, shards2, part0[0])
-    back0 = move(away(part0), over_y)
-    hidden3 = gate_up(3, spread(3, hidden1[0]), hidden2[0])
-    part1 = down(1, hidden1, hidden3[0], back0)
+    crosses.append(move(after(pairs[3], hidden0[1]), second))
+    hidden1 = gate_up(1, spread(1, hidden0[0]), hidden0[0], pairs[3])
+    hidden2 = gate_up(2, spread(2, hidden0[0]), hidden1[0])
+    shards3 = spread(3, hidden1[0])
+    part1 = down(1, hidden1, hidden2[0], shards3[3])
     back1 = move(away(part1), over_y)
-    part2 = down(2, hidden2, part1[0], hidden3[1])
-    part3 = down(3, hidden3, part2[0], back1)
+    hidden3 = gate_up(3, shards3, part1[0])
+    part2 = down(2, hidden2, hidden3[0], back1)
+    part0 = down(0, hidden0, part2[0])
+    part3 = down(3, hidden3, part0[0])
     from_next = move(total(part1, back1), backward)
-    from_far = move(total(part2, move(away(part2), over_y)), onward)
-    from_last = move(total(part3, move(away(part3), over_y), after(from_far, from_next)), onward)
+    from_far = move(after(total(part2, move(away(part2), over_y)), from_next), onward)
+    back3 = move(away(part3), over_y)
+    from_last = move(total(part3, back3, from_far), onward)
+    back0 = move(after(away(part0), back3), over_y)
     return total(part0, back0, from_next, from_last)
 
 

time: 207 us -> 204 us (0.986)
  waiting for transfers between devices: 111 us -> 90.2 us
  starting transfers between devices: 31.2 us -> 44.6 us
    ppermute x33, waiting for transfers between devices: 105 us -> 84.4 us  [move(): return lax.ppermute(value, axes, moves)]
    ppermute x33, starting transfers between devices: 26.2 us -> 38.6 us  [move(): return lax.ppermute(value, axes, moves)]
  transfers between devices with their start and end apart: 34 -> 34, of which waited for: 13 -> 18; matrix products, arithmetic and copies ran while one was open for 2% -> 4% of each run, Pallas kernels for 28% -> 23%
where the time goes in v8:
time: 204 us
  waiting for transfers between devices  90.2 us (44%)
  Pallas kernels  59 us (29%)
  starting transfers between devices  44.6 us (22%)
  other arithmetic  7.33 us (4%)
    ppermute x33, waiting for transfers between devices, move(): return lax.ppermute(value, axes, moves)  84.4 us
    ppermute x33, starting transfers between devices, move(): return lax.ppermute(value, axes, moves)  38.6 us
    pallas_call x4, Pallas kernels, pick_call(): pl.pallas_call(functools.partial(pick_kernel, capacity, k), in_specs=[pl....  34 us
    pallas_call x4, Pallas kernels, sum_call(): pl.pallas_call(functools.partial(sum_kernel, capacity, k), in_specs=[pl.B...  25 us
    all_to_all x1, starting transfers between devices, pair_shards(): lax.all_to_all(named, 'expert', split_axis=0, concat_axis=0, tiled=True)  5.94 us
    all_to_all x1, waiting for transfers between devices, pair_shards(): lax.all_to_all(named, 'expert', split_axis=0, concat_axis=0, tiled=True)  5.82 us
  transfers between devices with their start and end apart: 34, of which 18 were waited for; matrix products, arithmetic and copies ran while one was open for 4% of the time, Pallas kernels for 23%

profile of v8, /device:TPU:0, one launch (start us, length us, event | category | flops | bytes accessed | tf_op | source)
XLA Modules:
  0.0 203.6 jit_solution(16177404183447579130)
XLA Ops:
  0.0 2.9 %collective-permute-start.2 = (bf16[128,2048]{1,0:T(8,128)(2,1)}, bf16[128,2048]{1,0:T(8,128)(2,1)S(1)}, u32[]{:S(2)}, u32[]{:S(2)}) collective-permute-start(bf16[128,2048]{1,0:T(8,128)(2,1)} %param.6), channel_id=1, source_target_pairs={{0,16},{1,3},{2,18},{3,1},{4,20},{5,7},{6,22},{7,5},{8,24},{9,11},... | collective-permute-start | bytes 1572872 | tf_op jit(solution)/shard_map/ppermute | solution.py:376
  4.5 5.8 %collective-permute-done.2 = bf16[128,2048]{1,0:T(8,128)(2,1)S(1)} collective-permute-done((bf16[128,2048]{1,0:T(8,128)(2,1)}, bf16[128,2048]{1,0:T(8,128)(2,1)S(1)}, u32[]{:S(2)}, u32[]{:S(2)}) %collective-permute-start.2) | collective-permute-done | bytes 524320 | tf_op jit(solution)/shard_map/ppermute | solution.py:376
  14.5 3.0 %collective-permute-done = bf16[128,2048]{1,0:T(8,128)(2,1)S(1)} collective-permute-done((bf16[128,2048]{1,0:T(8,128)(2,1)}, bf16[128,2048]{1,0:T(8,128)(2,1)S(1)}, u32[]{:S(2)}, u32[]{:S(2)}) %collective-permute-start) | collective-permute-done | bytes 524320 | tf_op jit(solution)/shard_map/ppermute | solution.py:376
  19.8 11.1 %collective-permute-done.1 = bf16[128,2048]{1,0:T(8,128)(2,1)S(1)} collective-permute-done((bf16[128,2048]{1,0:T(8,128)(2,1)S(1)}, bf16[128,2048]{1,0:T(8,128)(2,1)S(1)}, u32[]{:S(2)}, u32[]{:S(2)}) %collective-permute-start.1) | collective-permute-done | bytes 524320 | tf_op jit(solution)/shard_map/ppermute | solution.py:376
  36.6 5.9 %all-to-all-start = ((s32[16,1,128]{2,1,0:T(1,128)}), s32[16,1,128]{2,1,0:T(1,128)S(1)}, u32[]{:S(2)}, u32[]{:S(2)}) async-start(s32[16,1,128]{2,1,0:T(1,128)} %bitcast.4), calls=%async_computation | async-start | bytes 16384 | tf_op jit(solution)/shard_map/all_to_all | solution.py:392
  43.1 5.8 %all-to-all-done = s32[16,1,128]{2,1,0:T(1,128)S(1)} async-done(((s32[16,1,128]{2,1,0:T(1,128)}), s32[16,1,128]{2,1,0:T(1,128)S(1)}, u32[]{:S(2)}, u32[]{:S(2)}) %all-to-all-start) | async-done | bytes 8224 | tf_op jit(solution)/shard_map/all_to_all | solution.py:392
  52.7 9.4 %gate_up.4.refs_5_.refs_0_ = bf16[320,768]{1,0:T(8,128)(2,1)S(1)} custom-call(s32[4,6]{1,0:T(4,128)S(1)} %dynamic-slice_bitcast_fusion.where_ref, s32[16,128]{1,0:T(8,128)S(1)} %bitcast.53, bf16[2,128,2048]{2,1,0:T(8,128)(2,1)} %pad_maximum_fusion.refs_0_, bf16[2,128,2048]{2,1,0:T(8,128)(2,1)} %collective-permute-done.3.refs_1_, ...), custom_call_target="tpu_custom_call" | custom-call | flops 4362076160 | bytes 17268736 | tf_op jit(solution)/shard_map/gate_up/pallas_call | solution.py:257
  65.8 10.5 %collective-permute-done.6.refs_1_ = bf16[320,768]{1,0:T(8,128)(2,1)S(1)} collective-permute-done((bf16[320,768]{1,0:T(8,128)(2,1)S(1)}, bf16[320,768]{1,0:T(8,128)(2,1)S(1)}, u32[]{:S(2)}, u32[]{:S(2)}) %collective-permute-start.6) | collective-permute-done | bytes 491552 | tf_op jit(solution)/shard_map/ppermute | solution.py:376
  77.9 8.6 %collective-permute-start.11 = (bf16[2,128,2048]{2,1,0:T(8,128)(2,1)S(1)}, bf16[2,128,2048]{2,1,0:T(8,128)(2,1)S(1)}, u32[]{:S(2)}, u32[]{:S(2)}) collective-permute-start(bf16[2,128,2048]{2,1,0:T(8,128)(2,1)S(1)} %collective-permute-done.9.refs_1_), channel_id=1, source_target_pairs={{0,1},{1,0},{2,3},{3,2},{4,5},{5,4},{6,7},{7,6},{8,9},{9,8},{10,11... | collective-permute-start | bytes 3145736 | tf_op jit(solution)/shard_map/ppermute | solution.py:376
  86.4 8.3 %gate_up.5.refs_5_.refs_0_ = bf16[320,768]{1,0:T(8,128)(2,1)S(1)} custom-call(s32[4,6]{1,0:T(4,128)S(1)} %dynamic-slice_bitcast_fusion.where_ref, s32[16,128]{1,0:T(8,128)S(1)} %bitcast.54, bf16[2,128,2048]{2,1,0:T(8,128)(2,1)S(1)} %pad_maximum_fusion.2.refs_0_, bf16[2,128,2048]{2,1,0:T(8,128)(2,1)} %collective-permute-done.12.refs_1_, ...), custom_call_target="tpu_custom_call" | custom-call | flops 4362076160 | bytes 17268736 | tf_op jit(solution)/shard_map/gate_up/pallas_call | solution.py:257
  94.7 2.6 %collective-permute-start.19 = (bf16[2,128,2048]{2,1,0:T(8,128)(2,1)S(1)}, bf16[2,128,2048]{2,1,0:T(8,128)(2,1)S(1)}, u32[]{:S(2)}, u32[]{:S(2)}) collective-permute-start(bf16[2,128,2048]{2,1,0:T(8,128)(2,1)S(1)} %collective-permute-done.17.refs_1_), channel_id=1, source_target_pairs={{0,1},{1,0},{2,3},{3,2},{4,5},{5,4},{6,7},{7,6},{8,9},{9,8},{10,11... | collective-permute-start | bytes 3145736 | tf_op jit(solution)/shard_map/ppermute | solution.py:376
  98.4 8.1 %gate_up.6.refs_3_.refs_0_ = bf16[320,768]{1,0:T(8,128)(2,1)S(1)} custom-call(s32[4,6]{1,0:T(4,128)S(1)} %dynamic-slice_bitcast_fusion.where_ref, s32[16,128]{1,0:T(8,128)S(1)} %bitcast.55, bf16[2,128,2048]{2,1,0:T(8,128)(2,1)S(1)} %pad_maximum_fusion.1.refs_0_, bf16[2,128,2048]{2,1,0:T(8,128)(2,1)S(1)} %collective-permute-done.9.refs_1_, ...), custom_call_target="tpu_custom_call" | custom-call | flops 4362076160 | bytes 17268736 | tf_op jit(solution)/shard_map/gate_up/pallas_call | solution.py:257
  106.5 4.0 %collective-permute-done.20.refs_1_ = bf16[320,768]{1,0:T(8,128)(2,1)S(1)} collective-permute-done((bf16[320,768]{1,0:T(8,128)(2,1)S(1)}, bf16[320,768]{1,0:T(8,128)(2,1)S(1)}, u32[]{:S(2)}, u32[]{:S(2)}) %collective-permute-start.20) | collective-permute-done | bytes 491552 | tf_op jit(solution)/shard_map/ppermute | solution.py:376
  110.5 6.2 %down.4 = (bf16[2,128,2048]{2,1,0:T(8,128)(2,1)S(1)}, bf16[2,128,2048]{2,1,0:T(8,128)(2,1)S(1)}) custom-call(s32[4,6]{1,0:T(4,128)S(1)} %dynamic-slice_bitcast_fusion.where_ref, s32[16,128]{1,0:T(8,128)S(1)} %bitcast.56, bf16[320,768]{1,0:T(8,128)(2,1)S(1)} %gate_up.5.refs_5_.refs_0_, bf16[320,768]{1,0:T(8,128)(2,1)S(1)} %collective-permute-done.20.refs_1_, ...), custom_call_target="tpu_custom_call" | custom-call | flops 2181038080 | bytes 9371648 | tf_op jit(solution)/shard_map/down/pallas_call | solution.py:287
  121.2 8.1 %gate_up.7.refs_3_.refs_0_ = bf16[320,768]{1,0:T(8,128)(2,1)S(1)} custom-call(s32[4,6]{1,0:T(4,128)S(1)} %dynamic-slice_bitcast_fusion.where_ref, s32[16,128]{1,0:T(8,128)S(1)} %bitcast.57, bf16[2,128,2048]{2,1,0:T(8,128)(2,1)S(1)} %collective-permute-done.15.refs_6_.refs_0_, bf16[2,128,2048]{2,1,0:T(8,128)(2,1)S(1)} %collective-permute-done.17.refs_1_, ...), custom_call_target="tpu_custom_call" | custom-call | flops 4362076160 | bytes 17268736 | tf_op jit(solution)/shard_map/gate_up/pallas_call | solution.py:257
  129.4 3.8 %collective-permute-done.16.refs_1_ = bf16[320,768]{1,0:T(8,128)(2,1)S(1)} collective-permute-done((bf16[320,768]{1,0:T(8,128)(2,1)S(1)}, bf16[320,768]{1,0:T(8,128)(2,1)S(1)}, u32[]{:S(2)}, u32[]{:S(2)}) %collective-permute-start.16) | collective-permute-done | bytes 491552 | tf_op jit(solution)/shard_map/ppermute | solution.py:376
  133.6 6.2 %down.5 = (bf16[2,128,2048]{2,1,0:T(8,128)(2,1)S(1)}, bf16[2,128,2048]{2,1,0:T(8,128)(2,1)S(1)}) custom-call(s32[4,6]{1,0:T(4,128)S(1)} %dynamic-slice_bitcast_fusion.where_ref, s32[16,128]{1,0:T(8,128)S(1)} %bitcast.58, bf16[320,768]{1,0:T(8,128)(2,1)S(1)} %gate_up.6.refs_3_.refs_0_, bf16[320,768]{1,0:T(8,128)(2,1)S(1)} %collective-permute-done.16.refs_1_, ...), custom_call_target="tpu_custom_call" | custom-call | flops 2181038080 | bytes 9371648 | tf_op jit(solution)/shard_map/down/pallas_call | solution.py:287
  141.0 6.4 %down.6 = (bf16[2,128,2048]{2,1,0:T(8,128)(2,1)S(1)}, bf16[2,128,2048]{2,1,0:T(8,128)(2,1)S(1)}) custom-call(s32[4,6]{1,0:T(4,128)S(1)} %dynamic-slice_bitcast_fusion.where_ref, s32[16,128]{1,0:T(8,128)S(1)} %bitcast.59, bf16[320,768]{1,0:T(8,128)(2,1)S(1)} %gate_up.4.refs_5_.refs_0_, bf16[320,768]{1,0:T(8,128)(2,1)S(1)} %collective-permute-done.6.refs_1_, ...), custom_call_target="tpu_custom_call" | custom-call | flops 2181038080 | bytes 9371648 | tf_op jit(solution)/shard_map/down/pallas_call | solution.py:287
  147.4 6.1 %collective-permute-done.24.refs_1_ = bf16[320,768]{1,0:T(8,128)(2,1)S(1)} collective-permute-done((bf16[320,768]{1,0:T(8,128)(2,1)S(1)}, bf16[320,768]{1,0:T(8,128)(2,1)S(1)}, u32[]{:S(2)}, u32[]{:S(2)}) %collective-permute-start.24) | collective-permute-done | bytes 491552 | tf_op jit(solution)/shard_map/ppermute | solution.py:376
  153.5 6.2 %down.7 = (bf16[2,128,2048]{2,1,0:T(8,128)(2,1)S(1)}, bf16[2,128,2048]{2,1,0:T(8,128)(2,1)S(1)}) custom-call(s32[4,6]{1,0:T(4,128)S(1)} %dynamic-slice_bitcast_fusion.where_ref, s32[16,128]{1,0:T(8,128)S(1)} %bitcast.60, bf16[320,768]{1,0:T(8,128)(2,1)S(1)} %gate_up.7.refs_3_.refs_0_, bf16[320,768]{1,0:T(8,128)(2,1)S(1)} %collective-permute-done.24.refs_1_, ...), custom_call_target="tpu_custom_call" | custom-call | flops 2181038080 | bytes 9371648 | tf_op jit(solution)/shard_map/down/pallas_call | solution.py:287
  164.9 10.4 %collective-permute-done.30 = bf16[128,2048]{1,0:T(8,128)(2,1)S(1)} collective-permute-done((bf16[128,2048]{1,0:T(8,128)(2,1)S(1)}, bf16[128,2048]{1,0:T(8,128)(2,1)S(1)}, u32[]{:S(2)}, u32[]{:S(2)}) %collective-permute-start.30) | collective-permute-done | bytes 524320 | tf_op jit(solution)/shard_map/ppermute | solution.py:376
  177.1 8.5 %collective-permute-done.26 = bf16[128,2048]{1,0:T(8,128)(2,1)S(1)} collective-permute-done((bf16[128,2048]{1,0:T(8,128)(2,1)S(1)}, bf16[128,2048]{1,0:T(8,128)(2,1)S(1)}, u32[]{:S(2)}, u32[]{:S(2)}) %collective-permute-start.26) | collective-permute-done | bytes 524320 | tf_op jit(solution)/shard_map/ppermute | solution.py:376
  190.1 8.6 %collective-permute-done.27 = bf16[128,2048]{1,0:T(8,128)(2,1)S(1)} collective-permute-done((bf16[128,2048]{1,0:T(8,128)(2,1)S(1)}, bf16[128,2048]{1,0:T(8,128)(2,1)S(1)}, u32[]{:S(2)}, u32[]{:S(2)}) %collective-permute-start.27) | collective-permute-done | bytes 524320 | tf_op jit(solution)/shard_map/ppermute | solution.py:376
  198.7 3.6 %collective-permute-done.32 = bf16[128,2048]{1,0:T(8,128)(2,1)S(1)} collective-permute-done((bf16[128,2048]{1,0:T(8,128)(2,1)S(1)}, bf16[128,2048]{1,0:T(8,128)(2,1)S(1)}, u32[]{:S(2)}, u32[]{:S(2)}) %collective-permute-start.32) | collective-permute-done | bytes 524320 | tf_op jit(solution)/shard_map/ppermute | solution.py:376
  (74 shorter events, 42.9 us)
Async XLA Ops:
  2.9 14.5 %collective-permute-start = (bf16[128,2048]{1,0:T(8,128)(2,1)}, bf16[128,2048]{1,0:T(8,128)(2,1)S(1)}, u32[]{:S(2)}, u32[]{:S(2)}) collective-permute-start(bf16[128,2048]{1,0:T(8,128)(2,1)} %param.6), channel_id=1, source_target_pairs={{0,4},{1,5},{2,6},{3,7},{4,12},{5,13},{6,14},{7,15},{8,0},{9,1},{1... | collective-permute-start | bytes 1572872 | tf_op jit(solution)/shard_map/ppermute | solution.py:376
  12.4 20.8 %collective-permute-start.3 = (bf16[2,128,2048]{2,1,0:T(8,128)(2,1)}, bf16[2,128,2048]{2,1,0:T(8,128)(2,1)}, u32[]{:S(2)}, u32[]{:S(2)}) collective-permute-start(bf16[2,128,2048]{2,1,0:T(8,128)(2,1)} %pad_maximum_fusion.refs_0_), channel_id=1, source_target_pairs={{0,2},{1,17},{2,0},{3,19},{4,6},{5,21},{6,4},{7,23},{8,10},{9,25},... | collective-permute-start | bytes 3145736 | tf_op jit(solution)/shard_map/ppermute | solution.py:376
  17.5 13.4 %collective-permute-start.1 = (bf16[128,2048]{1,0:T(8,128)(2,1)S(1)}, bf16[128,2048]{1,0:T(8,128)(2,1)S(1)}, u32[]{:S(2)}, u32[]{:S(2)}) collective-permute-start(bf16[128,2048]{1,0:T(8,128)(2,1)S(1)} %collective-permute-done), channel_id=1, source_target_pairs={{0,4},{1,5},{2,6},{3,7},{4,12},{5,13},{6,14},{7,15},{8,0},{9,1},{1... | collective-permute-start | bytes 1572872 | tf_op jit(solution)/shard_map/ppermute | solution.py:376
  18.4 13.3 %collective-permute-start.7 = (bf16[128,2048]{1,0:T(8,128)(2,1)S(1)}, bf16[128,2048]{1,0:T(8,128)(2,1)S(1)}, u32[]{:S(2)}, u32[]{:S(2)}) collective-permute-start(bf16[128,2048]{1,0:T(8,128)(2,1)S(1)} %collective-permute-done), channel_id=1, source_target_pairs={{0,16},{1,3},{2,18},{3,1},{4,20},{5,7},{6,22},{7,5},{8,24},{9,11},... | collective-permute-start | bytes 1572872 | tf_op jit(solution)/shard_map/ppermute | solution.py:376
  19.8 32.9 %collective-permute-start.4 = (bf16[2,128,2048]{2,1,0:T(8,128)(2,1)}, bf16[2,128,2048]{2,1,0:T(8,128)(2,1)}, u32[]{:S(2)}, u32[]{:S(2)}) collective-permute-start(bf16[2,128,2048]{2,1,0:T(8,128)(2,1)} %pad_maximum_fusion.refs_0_), channel_id=1, source_target_pairs={{0,1},{1,0},{2,3},{3,2},{4,5},{5,4},{6,7},{7,6},{8,9},{9,8},{10,11... | collective-permute-start | bytes 3145736 | tf_op jit(solution)/shard_map/ppermute | solution.py:376
  33.2 15.7 %collective-permute-start.8 = (bf16[128,2048]{1,0:T(8,128)(2,1)S(1)}, bf16[128,2048]{1,0:T(8,128)(2,1)S(1)}, u32[]{:S(2)}, u32[]{:S(2)}) collective-permute-start(bf16[128,2048]{1,0:T(8,128)(2,1)S(1)} %collective-permute-done.1), channel_id=1, source_target_pairs={{0,16},{1,3},{2,18},{3,1},{4,20},{5,7},{6,22},{7,5},{8,24},{9,11},... | collective-permute-start | bytes 1572872 | tf_op jit(solution)/shard_map/ppermute | solution.py:376
  50.9 15.0 %collective-permute-start.12 = (bf16[2,128,2048]{2,1,0:T(8,128)(2,1)S(1)}, bf16[2,128,2048]{2,1,0:T(8,128)(2,1)}, u32[]{:S(2)}, u32[]{:S(2)}) collective-permute-start(bf16[2,128,2048]{2,1,0:T(8,128)(2,1)S(1)} %pad_maximum_fusion.2.refs_0_), channel_id=1, source_target_pairs={{0,2},{1,17},{2,0},{3,19},{4,6},{5,21},{6,4},{7,23},{8,10},{9,25},... | collective-permute-start | bytes 3145736 | tf_op jit(solution)/shard_map/ppermute | solution.py:376
  51.4 25.5 %collective-permute-start.15 = (bf16[2,128,2048]{2,1,0:T(8,128)(2,1)S(1)}, bf16[2,128,2048]{2,1,0:T(8,128)(2,1)S(1)}, u32[]{:S(2)}, u32[]{:S(2)}) collective-permute-start(bf16[2,128,2048]{2,1,0:T(8,128)(2,1)S(1)} %pad_maximum_fusion.1.refs_0_), channel_id=1, source_target_pairs={{0,4},{1,5},{2,6},{3,7},{4,12},{5,13},{6,14},{7,15},{8,0},{9,1},{1... | collective-permute-start | bytes 3145736 | tf_op jit(solution)/shard_map/ppermute | solution.py:376
  62.1 14.2 %collective-permute-start.6 = (bf16[320,768]{1,0:T(8,128)(2,1)S(1)}, bf16[320,768]{1,0:T(8,128)(2,1)S(1)}, u32[]{:S(2)}, u32[]{:S(2)}) collective-permute-start(bf16[320,768]{1,0:T(8,128)(2,1)S(1)} %gate_up.4.refs_5_.refs_0_), channel_id=1, source_target_pairs={{0,16},{1,17},{2,18},{3,19},{4,20},{5,21},{6,22},{7,23},{8,24},{9,... | collective-permute-start | bytes 1474568 | tf_op jit(solution)/shard_map/ppermute | solution.py:376
  62.7 15.1 %collective-permute-start.9 = (bf16[2,128,2048]{2,1,0:T(8,128)(2,1)S(1)}, bf16[2,128,2048]{2,1,0:T(8,128)(2,1)S(1)}, u32[]{:S(2)}, u32[]{:S(2)}) collective-permute-start(bf16[2,128,2048]{2,1,0:T(8,128)(2,1)S(1)} %pad_maximum_fusion.1.refs_0_), channel_id=1, source_target_pairs={{0,2},{1,17},{2,0},{3,19},{4,6},{5,21},{6,4},{7,23},{8,10},{9,25},... | collective-permute-start | bytes 3145736 | tf_op jit(solution)/shard_map/ppermute | solution.py:376
  64.2 22.3 %collective-permute-start.13 = (bf16[2,128,2048]{2,1,0:T(8,128)(2,1)S(1)}, bf16[2,128,2048]{2,1,0:T(8,128)(2,1)S(1)}, u32[]{:S(2)}, u32[]{:S(2)}) collective-permute-start(bf16[2,128,2048]{2,1,0:T(8,128)(2,1)S(1)} %pad_maximum_fusion.2.refs_0_), channel_id=1, source_target_pairs={{0,1},{1,0},{2,3},{3,2},{4,5},{5,4},{6,7},{7,6},{8,9},{9,8},{10,11... | collective-permute-start | bytes 3145736 | tf_op jit(solution)/shard_map/ppermute | solution.py:376
  65.8 20.6 %collective-permute-start.14 = (bf16[2,128,2048]{2,1,0:T(8,128)(2,1)}, bf16[2,128,2048]{2,1,0:T(8,128)(2,1)S(1)}, u32[]{:S(2)}, u32[]{:S(2)}) collective-permute-start(bf16[2,128,2048]{2,1,0:T(8,128)(2,1)} %collective-permute-done.12.refs_1_), channel_id=1, source_target_pairs={{0,1},{1,0},{2,3},{3,2},{4,5},{5,4},{6,7},{7,6},{8,9},{9,8},{10,11... | collective-permute-start | bytes 3145736 | tf_op jit(solution)/shard_map/ppermute | solution.py:376
  76.9 17.8 %collective-permute-start.17 = (bf16[2,128,2048]{2,1,0:T(8,128)(2,1)S(1)}, bf16[2,128,2048]{2,1,0:T(8,128)(2,1)S(1)}, u32[]{:S(2)}, u32[]{:S(2)}) collective-permute-start(bf16[2,128,2048]{2,1,0:T(8,128)(2,1)S(1)} %collective-permute-done.15.refs_6_.refs_0_), channel_id=1, source_target_pairs={{0,2},{1,17},{2,0},{3,19},{4,6},{5,21},{6,4},{7,23},{8,10},{9,25},... | collective-permute-start | bytes 3145736 | tf_op jit(solution)/shard_map/ppermute | solution.py:376
  77.8 20.6 %collective-permute-start.10 = (bf16[2,128,2048]{2,1,0:T(8,128)(2,1)S(1)}, bf16[2,128,2048]{2,1,0:T(8,128)(2,1)S(1)}, u32[]{:S(2)}, u32[]{:S(2)}) collective-permute-start(bf16[2,128,2048]{2,1,0:T(8,128)(2,1)S(1)} %pad_maximum_fusion.1.refs_0_), channel_id=1, source_target_pairs={{0,1},{1,0},{2,3},{3,2},{4,5},{5,4},{6,7},{7,6},{8,9},{9,8},{10,11... | collective-permute-start | bytes 3145736 | tf_op jit(solution)/shard_map/ppermute | solution.py:376
  77.9 20.5 %collective-permute-start.11 = (bf16[2,128,2048]{2,1,0:T(8,128)(2,1)S(1)}, bf16[2,128,2048]{2,1,0:T(8,128)(2,1)S(1)}, u32[]{:S(2)}, u32[]{:S(2)}) collective-permute-start(bf16[2,128,2048]{2,1,0:T(8,128)(2,1)S(1)} %collective-permute-done.9.refs_1_), channel_id=1, source_target_pairs={{0,1},{1,0},{2,3},{3,2},{4,5},{5,4},{6,7},{7,6},{8,9},{9,8},{10,11... | collective-permute-start | bytes 3145736 | tf_op jit(solution)/shard_map/ppermute | solution.py:376
  94.7 15.8 %collective-permute-start.19 = (bf16[2,128,2048]{2,1,0:T(8,128)(2,1)S(1)}, bf16[2,128,2048]{2,1,0:T(8,128)(2,1)S(1)}, u32[]{:S(2)}, u32[]{:S(2)}) collective-permute-start(bf16[2,128,2048]{2,1,0:T(8,128)(2,1)S(1)} %collective-permute-done.17.refs_1_), channel_id=1, source_target_pairs={{0,1},{1,0},{2,3},{3,2},{4,5},{5,4},{6,7},{7,6},{8,9},{9,8},{10,11... | collective-permute-start | bytes 3145736 | tf_op jit(solution)/shard_map/ppermute | solution.py:376
  119.6 14.0 %collective-permute-start.22 = (bf16[128,2048]{1,0:T(8,128)(2,1)S(1)}, bf16[128,2048]{1,0:T(8,128)(2,1)S(1)}, u32[]{:S(2)}, u32[]{:S(2)}) collective-permute-start(bf16[128,2048]{1,0:T(8,128)(2,1)S(1)} %fusion.10), channel_id=1, source_target_pairs={{0,2},{1,3},{2,0},{3,1},{4,6},{5,7},{6,4},{7,5},{8,10},{9,11},{10,... | collective-permute-start | bytes 1572872 | tf_op jit(solution)/shard_map/ppermute | solution.py:376
  139.8 20.5 %collective-permute-start.29 = (bf16[2,128,2048]{2,1,0:T(8,128)(2,1)S(1)}, bf16[2,128,2048]{2,1,0:T(8,128)(2,1)S(1)}, u32[]{:S(2)}, u32[]{:S(2)}) collective-permute-start(bf16[2,128,2048]{2,1,0:T(8,128)(2,1)S(1)} %get-tuple-element.39), channel_id=1, source_target_pairs={{0,1},{1,0},{2,3},{3,2},{4,5},{5,4},{6,7},{7,6},{8,9},{9,8},{10,11... | collective-permute-start | bytes 3145736 | tf_op jit(solution)/shard_map/ppermute | solution.py:376
  139.9 13.6 %collective-permute-start.24 = (bf16[320,768]{1,0:T(8,128)(2,1)S(1)}, bf16[320,768]{1,0:T(8,128)(2,1)S(1)}, u32[]{:S(2)}, u32[]{:S(2)}) collective-permute-start(bf16[320,768]{1,0:T(8,128)(2,1)S(1)} %gate_up.7.refs_3_.refs_0_), channel_id=1, source_target_pairs={{0,16},{1,17},{2,18},{3,19},{4,20},{5,21},{6,22},{7,23},{8,24},{9,... | collective-permute-start | bytes 1474568 | tf_op jit(solution)/shard_map/ppermute | solution.py:376
  159.8 17.2 %collective-permute-start.23 = (bf16[2,128,2048]{2,1,0:T(8,128)(2,1)S(1)}, bf16[2,128,2048]{2,1,0:T(8,128)(2,1)S(1)}, u32[]{:S(2)}, u32[]{:S(2)}) collective-permute-start(bf16[2,128,2048]{2,1,0:T(8,128)(2,1)S(1)} %get-tuple-element.35), channel_id=1, source_target_pairs={{0,1},{1,0},{2,3},{3,2},{4,5},{5,4},{6,7},{7,6},{8,9},{9,8},{10,11... | collective-permute-start | bytes 3145736 | tf_op jit(solution)/shard_map/ppermute | solution.py:376
  160.4 14.8 %collective-permute-start.30 = (bf16[128,2048]{1,0:T(8,128)(2,1)S(1)}, bf16[128,2048]{1,0:T(8,128)(2,1)S(1)}, u32[]{:S(2)}, u32[]{:S(2)}) collective-permute-start(bf16[128,2048]{1,0:T(8,128)(2,1)S(1)} %fusion.13), channel_id=1, source_target_pairs={{0,2},{1,3},{2,0},{3,1},{4,6},{5,7},{6,4},{7,5},{8,10},{9,11},{10,... | collective-permute-start | bytes 1572872 | tf_op jit(solution)/shard_map/ppermute | solution.py:376
  161.8 13.7 %collective-permute-start.28 = (bf16[128,2048]{1,0:T(8,128)(2,1)S(1)}, bf16[128,2048]{1,0:T(8,128)(2,1)S(1)}, u32[]{:S(2)}, u32[]{:S(2)}) collective-permute-start(bf16[128,2048]{1,0:T(8,128)(2,1)S(1)} %fusion.6), channel_id=1, source_target_pairs={{4,0},{5,1},{6,2},{7,3},{12,4},{13,5},{14,6},{15,7},{0,8},{1,9},{2... | collective-permute-start | bytes 1572872 | tf_op jit(solution)/shard_map/ppermute | solution.py:376
  163.8 21.8 %collective-permute-start.26 = (bf16[128,2048]{1,0:T(8,128)(2,1)S(1)}, bf16[128,2048]{1,0:T(8,128)(2,1)S(1)}, u32[]{:S(2)}, u32[]{:S(2)}) collective-permute-start(bf16[128,2048]{1,0:T(8,128)(2,1)S(1)} %fusion.12), channel_id=1, source_target_pairs={{0,2},{1,3},{2,0},{3,1},{4,6},{5,7},{6,4},{7,5},{8,10},{9,11},{10,... | collective-permute-start | bytes 1572872 | tf_op jit(solution)/shard_map/ppermute | solution.py:376
  175.6 13.7 %collective-permute-start.31 = (bf16[128,2048]{1,0:T(8,128)(2,1)S(1)}, bf16[128,2048]{1,0:T(8,128)(2,1)S(1)}, u32[]{:S(2)}, u32[]{:S(2)}) collective-permute-start(bf16[128,2048]{1,0:T(8,128)(2,1)S(1)} %fusion.3), channel_id=1, source_target_pairs={{0,4},{1,5},{2,6},{3,7},{4,12},{5,13},{6,14},{7,15},{8,0},{9,1},{1... | collective-permute-start | bytes 1572872 | tf_op jit(solution)/shard_map/ppermute | solution.py:376
  (13 other events, 202.8 us)

commit v9 on v8

--- a/solution.py
+++ b/solution.py
@@ -388,12 +388,12 @@
     later = move(tokens, onward)
     near_later = move(later, first)
     last = move(later, onward)
-    named = codes_of(after(expert_ids, last), numerators, experts)
+    named = codes_of(after(expert_ids, later), numerators, experts)
     code = lax.all_to_all(named, "expert", split_axis=0, concat_axis=0, tiled=True)
     pairs = [jnp.stack([tokens, near]), jnp.stack([later, near_later])]
     crosses = [move(pairs[0], second)]
-    near_last = move(after(last, near_later, crosses[0]), first)
-    pairs.append(jnp.stack([after(last, code), near_last]))
+    near_last = move(after(last, near_later, crosses[0], code), first)
+    pairs.append(jnp.stack([last, near_last]))
     pairs.append(move(pairs[2], onward))
     crosses.append(move(after(pairs[1], pairs[2]), second))
     crosses.append(move(pairs[2], second))
@@ -406,8 +406,10 @@
         return mine, move(mine, over_x)
 
     def down(k, hidden, *earlier):
-        keep, send = sum_call(k, where, code, *hidden, down_weight[0], earlier, capacity)
-        return keep, move(send, sibling)
+        return sum_call(k, where, code, *hidden, down_weight[0], earlier, capacity)
+
+    def give(part, *done):
+        return part[0], move(after(part[1], *done), sibling)
 
     def away(part):
         keep, got = part
@@ -422,14 +424,17 @@
     hidden1 = gate_up(1, spread(1, hidden0[0]), hidden0[0], pairs[3])
     hidden2 = gate_up(2, spread(2, hidden0[0]), hidden1[0])
     shards3 = spread(3, hidden1[0])
-    part1 = down(1, hidden1, hidden2[0], shards3[3])
+    part1 = down(1, hidden1, hidden2[0], *shards3[2:])
+    part2 = down(2, hidden2, part1[0])
+    part1 = give(part1, part2[0])
+    part2 = give(part2)
     back1 = move(away(part1), over_y)
-    hidden3 = gate_up(3, shards3, part1[0])
-    part2 = down(2, hidden2, hidden3[0], back1)
-    part0 = down(0, hidden0, part2[0])
-    part3 = down(3, hidden3, part0[0])
-    from_next = move(total(part1, back1), backward)
-    from_far = move(after(total(part2, move(away(part2), over_y)), from_next), onward)
+    hidden3 = gate_up(3, shards3, part2[0])
+    part0 = give(down(0, hidden0, hidden3[0], back1))
+    back2 = move(after(away(part2), back1, hidden3[0]), over_y)
+    from_next = move(total(part1, after(back1, hidden3[0])), backward)
+    part3 = give(down(3, hidden3, part0[0], back2, from_next))
+    from_far = move(total(part2, back2), onward)
     back3 = move(away(part3), over_y)
     from_last = move(total(part3, back3, from_far), onward)
     back0 = move(after(away(part0), back3), over_y)

time: 204 us -> 195 us (0.956)
  waiting for transfers between devices: 90.2 us -> 74.1 us
  blocking collectives: 0 us -> 11.8 us
    all_to_all x0 -> x1, blocking collectives: none -> 11.8 us  [pair_shards(): lax.all_to_all(named, 'expert', split_axis=0, concat_axis=0, tiled=True)]
    ppermute x33, waiting for transfers between devices: 84.4 us -> 74.1 us  [move(): return lax.ppermute(value, axes, moves)]
    all_to_all x1 -> x0, starting transfers between devices: 5.94 us -> none  [pair_shards(): lax.all_to_all(named, 'expert', split_axis=0, concat_axis=0, tiled=True)]
    all_to_all x1 -> x0, waiting for transfers between devices: 5.82 us -> none  [pair_shards(): lax.all_to_all(named, 'expert', split_axis=0, concat_axis=0, tiled=True)]
    ppermute x33, starting transfers between devices: 38.6 us -> 43.1 us  [move(): return lax.ppermute(value, axes, moves)]
  transfers between devices with their start and end apart: 34 -> 33, of which waited for: 18 -> 14; matrix products, arithmetic and copies ran while one was open for 4% -> 3% of each run, Pallas kernels for 23% -> 24%
where the time goes in v9:
time: 195 us
  waiting for transfers between devices  74.1 us (38%)
  Pallas kernels  58.7 us (30%)
  starting transfers between devices  43.1 us (22%)
  blocking collectives  11.8 us (6%)
  other arithmetic  6.28 us (3%)
    ppermute x33, waiting for transfers between devices, move(): return lax.ppermute(value, axes, moves)  74.1 us
    ppermute x33, starting transfers between devices, move(): return lax.ppermute(value, axes, moves)  43.1 us
    pallas_call x4, Pallas kernels, pick_call(): pl.pallas_call(functools.partial(pick_kernel, capacity, k), in_specs=[pl....  34 us
    pallas_call x4, Pallas kernels, sum_call(): pl.pallas_call(functools.partial(sum_kernel, capacity, k), in_specs=[pl.B...  24.7 us
    all_to_all x1, blocking collectives, pair_shards(): lax.all_to_all(named, 'expert', split_axis=0, concat_axis=0, tiled=True)  11.8 us
  transfers between devices with their start and end apart: 33, of which 14 were waited for; matrix products, arithmetic and copies ran while one was open for 3% of the time, Pallas kernels for 24%

profile of v9, /device:TPU:0, one launch (start us, length us, event | category | flops | bytes accessed | tf_op | source)
XLA Modules:
  0.0 195.0 jit_solution(4905577052298229903)
XLA Ops:
  0.0 2.9 %collective-permute-start.1 = (bf16[128,2048]{1,0:T(8,128)(2,1)}, bf16[128,2048]{1,0:T(8,128)(2,1)S(1)}, u32[]{:S(2)}, u32[]{:S(2)}) collective-permute-start(bf16[128,2048]{1,0:T(8,128)(2,1)} %param.6), channel_id=1, source_target_pairs={{0,16},{1,3},{2,18},{3,1},{4,20},{5,7},{6,22},{7,5},{8,24},{9,11},... | collective-permute-start | bytes 1572872 | tf_op jit(solution)/shard_map/ppermute | solution.py:376
  4.5 5.8 %collective-permute-done.1 = bf16[128,2048]{1,0:T(8,128)(2,1)S(1)} collective-permute-done((bf16[128,2048]{1,0:T(8,128)(2,1)}, bf16[128,2048]{1,0:T(8,128)(2,1)S(1)}, u32[]{:S(2)}, u32[]{:S(2)}) %collective-permute-start.1) | collective-permute-done | bytes 524320 | tf_op jit(solution)/shard_map/ppermute | solution.py:376
  14.5 3.0 %collective-permute-done = bf16[128,2048]{1,0:T(8,128)(2,1)S(1)} collective-permute-done((bf16[128,2048]{1,0:T(8,128)(2,1)}, bf16[128,2048]{1,0:T(8,128)(2,1)S(1)}, u32[]{:S(2)}, u32[]{:S(2)}) %collective-permute-start) | collective-permute-done | bytes 524320 | tf_op jit(solution)/shard_map/ppermute | solution.py:376
  21.4 11.8 %all_to_all.11 = s32[16,1,128]{2,1,0:T(1,128)S(1)} all-to-all(s32[16,1,128]{2,1,0:T(1,128)S(1)} %bitcast.73), channel_id=1, replica_groups=mesh['section'=2,'expert'=16] {'expert'}, dimensions={0} | all-to-all | bytes 16384 | tf_op jit(solution)/shard_map/all_to_all | solution.py:392
  35.9 6.6 %collective-permute-done.8 = bf16[128,2048]{1,0:T(8,128)(2,1)S(1)} collective-permute-done((bf16[128,2048]{1,0:T(8,128)(2,1)S(1)}, bf16[128,2048]{1,0:T(8,128)(2,1)S(1)}, u32[]{:S(2)}, u32[]{:S(2)}) %collective-permute-start.8) | collective-permute-done | bytes 524320 | tf_op jit(solution)/shard_map/ppermute | solution.py:376
  47.5 9.4 %gate_up.4.refs_5_.refs_0_ = bf16[320,768]{1,0:T(8,128)(2,1)S(1)} custom-call(s32[4,6]{1,0:T(4,128)S(1)} %dynamic-slice_bitcast_fusion.where_ref, s32[16,128]{1,0:T(8,128)S(1)} %bitcast.53, bf16[2,128,2048]{2,1,0:T(8,128)(2,1)} %pad_maximum_fusion.refs_0_, bf16[2,128,2048]{2,1,0:T(8,128)(2,1)} %collective-permute-done.2.refs_1_, ...), custom_call_target="tpu_custom_call" | custom-call | flops 4362076160 | bytes 17268736 | tf_op jit(solution)/shard_map/gate_up/pallas_call | solution.py:257
  59.0 12.2 %collective-permute-done.5.refs_1_ = bf16[320,768]{1,0:T(8,128)(2,1)S(1)} collective-permute-done((bf16[320,768]{1,0:T(8,128)(2,1)S(1)}, bf16[320,768]{1,0:T(8,128)(2,1)S(1)}, u32[]{:S(2)}, u32[]{:S(2)}) %collective-permute-start.5) | collective-permute-done | bytes 491552 | tf_op jit(solution)/shard_map/ppermute | solution.py:376
  72.6 6.7 %collective-permute-start.17 = (bf16[2,128,2048]{2,1,0:T(8,128)(2,1)S(1)}, bf16[2,128,2048]{2,1,0:T(8,128)(2,1)S(1)}, u32[]{:S(2)}, u32[]{:S(2)}) collective-permute-start(bf16[2,128,2048]{2,1,0:T(8,128)(2,1)S(1)} %pad_maximum_fusion.1.refs_0_), channel_id=1, source_target_pairs={{0,1},{1,0},{2,3},{3,2},{4,5},{5,4},{6,7},{7,6},{8,9},{9,8},{10,11... | collective-permute-start | bytes 3145736 | tf_op jit(solution)/shard_map/ppermute | solution.py:376
  79.9 8.3 %gate_up.5.refs_5_.refs_0_ = bf16[320,768]{1,0:T(8,128)(2,1)S(1)} custom-call(s32[4,6]{1,0:T(4,128)S(1)} %dynamic-slice_bitcast_fusion.where_ref, s32[16,128]{1,0:T(8,128)S(1)} %bitcast.54, bf16[2,128,2048]{2,1,0:T(8,128)(2,1)S(1)} %pad_maximum_fusion.2.refs_0_, bf16[2,128,2048]{2,1,0:T(8,128)(2,1)} %collective-permute-done.12.refs_1_, ...), custom_call_target="tpu_custom_call" | custom-call | flops 4362076160 | bytes 17268736 | tf_op jit(solution)/shard_map/gate_up/pallas_call | solution.py:257
  88.2 3.4 %collective-permute-start.15 = (bf16[2,128,2048]{2,1,0:T(8,128)(2,1)S(1)}, bf16[2,128,2048]{2,1,0:T(8,128)(2,1)S(1)}, u32[]{:S(2)}, u32[]{:S(2)}) collective-permute-start(bf16[2,128,2048]{2,1,0:T(8,128)(2,1)S(1)} %collective-permute-done.10.refs_1_), channel_id=1, source_target_pairs={{0,1},{1,0},{2,3},{3,2},{4,5},{5,4},{6,7},{7,6},{8,9},{9,8},{10,11... | collective-permute-start | bytes 3145736 | tf_op jit(solution)/shard_map/ppermute | solution.py:376
  93.3 8.1 %gate_up.6.refs_3_.refs_0_ = bf16[320,768]{1,0:T(8,128)(2,1)S(1)} custom-call(s32[4,6]{1,0:T(4,128)S(1)} %dynamic-slice_bitcast_fusion.where_ref, s32[16,128]{1,0:T(8,128)S(1)} %bitcast.55, bf16[2,128,2048]{2,1,0:T(8,128)(2,1)S(1)} %pad_maximum_fusion.1.refs_0_, bf16[2,128,2048]{2,1,0:T(8,128)(2,1)S(1)} %collective-permute-done.16.refs_1_, ...), custom_call_target="tpu_custom_call" | custom-call | flops 4362076160 | bytes 17268736 | tf_op jit(solution)/shard_map/gate_up/pallas_call | solution.py:257
  101.8 3.7 %collective-permute-done.20.refs_1_ = bf16[320,768]{1,0:T(8,128)(2,1)S(1)} collective-permute-done((bf16[320,768]{1,0:T(8,128)(2,1)S(1)}, bf16[320,768]{1,0:T(8,128)(2,1)S(1)}, u32[]{:S(2)}, u32[]{:S(2)}) %collective-permute-start.20) | collective-permute-done | bytes 491552 | tf_op jit(solution)/shard_map/ppermute | solution.py:376
  105.5 6.1 %down.4 = (bf16[2,128,2048]{2,1,0:T(8,128)(2,1)S(1)}, bf16[2,128,2048]{2,1,0:T(8,128)(2,1)S(1)}) custom-call(s32[4,6]{1,0:T(4,128)S(1)} %dynamic-slice_bitcast_fusion.where_ref, s32[16,128]{1,0:T(8,128)S(1)} %bitcast.56, bf16[320,768]{1,0:T(8,128)(2,1)S(1)} %gate_up.5.refs_5_.refs_0_, bf16[320,768]{1,0:T(8,128)(2,1)S(1)} %collective-permute-done.20.refs_1_, ...), custom_call_target="tpu_custom_call" | custom-call | flops 2181038080 | bytes 9371648 | tf_op jit(solution)/shard_map/down/pallas_call | solution.py:287
  111.6 3.6 %collective-permute-done.19.refs_1_ = bf16[320,768]{1,0:T(8,128)(2,1)S(1)} collective-permute-done((bf16[320,768]{1,0:T(8,128)(2,1)S(1)}, bf16[320,768]{1,0:T(8,128)(2,1)S(1)}, u32[]{:S(2)}, u32[]{:S(2)}) %collective-permute-start.19) | collective-permute-done | bytes 491552 | tf_op jit(solution)/shard_map/ppermute | solution.py:376
  115.2 6.1 %down.5 = (bf16[2,128,2048]{2,1,0:T(8,128)(2,1)S(1)}, bf16[2,128,2048]{2,1,0:T(8,128)(2,1)S(1)}) custom-call(s32[4,6]{1,0:T(4,128)S(1)} %dynamic-slice_bitcast_fusion.where_ref, s32[16,128]{1,0:T(8,128)S(1)} %bitcast.57, bf16[320,768]{1,0:T(8,128)(2,1)S(1)} %gate_up.6.refs_3_.refs_0_, bf16[320,768]{1,0:T(8,128)(2,1)S(1)} %collective-permute-done.19.refs_1_, ...), custom_call_target="tpu_custom_call" | custom-call | flops 2181038080 | bytes 9371648 | tf_op jit(solution)/shard_map/down/pallas_call | solution.py:287
  126.0 8.1 %gate_up.7.refs_3_.refs_0_ = bf16[320,768]{1,0:T(8,128)(2,1)S(1)} custom-call(s32[4,6]{1,0:T(4,128)S(1)} %dynamic-slice_bitcast_fusion.where_ref, s32[16,128]{1,0:T(8,128)S(1)} %bitcast.58, bf16[2,128,2048]{2,1,0:T(8,128)(2,1)S(1)} %collective-permute-done.9.refs_6_.refs_0_, bf16[2,128,2048]{2,1,0:T(8,128)(2,1)S(1)} %collective-permute-done.10.refs_1_, ...), custom_call_target="tpu_custom_call" | custom-call | flops 4362076160 | bytes 17268736 | tf_op jit(solution)/shard_map/gate_up/pallas_call | solution.py:257
  134.3 3.9 %collective-permute-done.22.refs_4_ = bf16[128,2048]{1,0:T(8,128)(2,1)S(1)} collective-permute-done((bf16[128,2048]{1,0:T(8,128)(2,1)S(1)}, bf16[128,2048]{1,0:T(8,128)(2,1)S(1)}, u32[]{:S(2)}, u32[]{:S(2)}) %collective-permute-start.22) | collective-permute-done | bytes 524320 | tf_op jit(solution)/shard_map/ppermute | solution.py:376
  138.5 2.9 %collective-permute-start.27 = (bf16[128,2048]{1,0:T(8,128)(2,1)S(1)}, bf16[128,2048]{1,0:T(8,128)(2,1)S(1)}, u32[]{:S(2)}, u32[]{:S(2)}) collective-permute-start(bf16[128,2048]{1,0:T(8,128)(2,1)S(1)} %fusion.6), channel_id=1, source_target_pairs={{4,0},{5,1},{6,2},{7,3},{12,4},{13,5},{14,6},{15,7},{0,8},{1,9},{2... | collective-permute-start | bytes 1572872 | tf_op jit(solution)/shard_map/ppermute | solution.py:376
  144.4 6.4 %down.6 = (bf16[2,128,2048]{2,1,0:T(8,128)(2,1)S(1)}, bf16[2,128,2048]{2,1,0:T(8,128)(2,1)S(1)}) custom-call(s32[4,6]{1,0:T(4,128)S(1)} %dynamic-slice_bitcast_fusion.where_ref, s32[16,128]{1,0:T(8,128)S(1)} %bitcast.59, bf16[320,768]{1,0:T(8,128)(2,1)S(1)} %gate_up.4.refs_5_.refs_0_, bf16[320,768]{1,0:T(8,128)(2,1)S(1)} %collective-permute-done.5.refs_1_, ...), custom_call_target="tpu_custom_call" | custom-call | flops 2181038080 | bytes 9371648 | tf_op jit(solution)/shard_map/down/pallas_call | solution.py:287
  150.7 4.0 %collective-permute-done.24.refs_1_ = bf16[320,768]{1,0:T(8,128)(2,1)S(1)} collective-permute-done((bf16[320,768]{1,0:T(8,128)(2,1)S(1)}, bf16[320,768]{1,0:T(8,128)(2,1)S(1)}, u32[]{:S(2)}, u32[]{:S(2)}) %collective-permute-start.24) | collective-permute-done | bytes 491552 | tf_op jit(solution)/shard_map/ppermute | solution.py:376
  154.8 6.1 %down.7 = (bf16[2,128,2048]{2,1,0:T(8,128)(2,1)S(1)}, bf16[2,128,2048]{2,1,0:T(8,128)(2,1)S(1)}) custom-call(s32[4,6]{1,0:T(4,128)S(1)} %dynamic-slice_bitcast_fusion.where_ref, s32[16,128]{1,0:T(8,128)S(1)} %bitcast.60, bf16[320,768]{1,0:T(8,128)(2,1)S(1)} %gate_up.7.refs_3_.refs_0_, bf16[320,768]{1,0:T(8,128)(2,1)S(1)} %collective-permute-done.24.refs_1_, ...), custom_call_target="tpu_custom_call" | custom-call | flops 2181038080 | bytes 9371648 | tf_op jit(solution)/shard_map/down/pallas_call | solution.py:287
  165.4 12.4 %collective-permute-done.29 = bf16[128,2048]{1,0:T(8,128)(2,1)S(1)} collective-permute-done((bf16[128,2048]{1,0:T(8,128)(2,1)S(1)}, bf16[128,2048]{1,0:T(8,128)(2,1)S(1)}, u32[]{:S(2)}, u32[]{:S(2)}) %collective-permute-start.29) | collective-permute-done | bytes 524320 | tf_op jit(solution)/shard_map/ppermute | solution.py:376
  180.1 10.8 %collective-permute-done.30 = bf16[128,2048]{1,0:T(8,128)(2,1)S(1)} collective-permute-done((bf16[128,2048]{1,0:T(8,128)(2,1)S(1)}, bf16[128,2048]{1,0:T(8,128)(2,1)S(1)}, u32[]{:S(2)}, u32[]{:S(2)}) %collective-permute-start.30) | collective-permute-done | bytes 524320 | tf_op jit(solution)/shard_map/ppermute | solution.py:376
  190.9 2.9 %collective-permute-done.32 = bf16[128,2048]{1,0:T(8,128)(2,1)S(1)} collective-permute-done((bf16[128,2048]{1,0:T(8,128)(2,1)S(1)}, bf16[128,2048]{1,0:T(8,128)(2,1)S(1)}, u32[]{:S(2)}, u32[]{:S(2)}) %collective-permute-start.32) | collective-permute-done | bytes 524320 | tf_op jit(solution)/shard_map/ppermute | solution.py:376
  (71 shorter events, 39.5 us)
Async XLA Ops:
  2.9 14.5 %collective-permute-start = (bf16[128,2048]{1,0:T(8,128)(2,1)}, bf16[128,2048]{1,0:T(8,128)(2,1)S(1)}, u32[]{:S(2)}, u32[]{:S(2)}) collective-permute-start(bf16[128,2048]{1,0:T(8,128)(2,1)} %param.6), channel_id=1, source_target_pairs={{0,4},{1,5},{2,6},{3,7},{4,12},{5,13},{6,14},{7,15},{8,0},{9,1},{1... | collective-permute-start | bytes 1572872 | tf_op jit(solution)/shard_map/ppermute | solution.py:376
  12.4 20.8 %collective-permute-start.2 = (bf16[2,128,2048]{2,1,0:T(8,128)(2,1)}, bf16[2,128,2048]{2,1,0:T(8,128)(2,1)}, u32[]{:S(2)}, u32[]{:S(2)}) collective-permute-start(bf16[2,128,2048]{2,1,0:T(8,128)(2,1)} %pad_maximum_fusion.refs_0_), channel_id=1, source_target_pairs={{0,2},{1,17},{2,0},{3,19},{4,6},{5,21},{6,4},{7,23},{8,10},{9,25},... | collective-permute-start | bytes 3145736 | tf_op jit(solution)/shard_map/ppermute | solution.py:376
  17.5 15.8 %collective-permute-start.6 = (bf16[128,2048]{1,0:T(8,128)(2,1)S(1)}, bf16[128,2048]{1,0:T(8,128)(2,1)S(1)}, u32[]{:S(2)}, u32[]{:S(2)}) collective-permute-start(bf16[128,2048]{1,0:T(8,128)(2,1)S(1)} %collective-permute-done), channel_id=1, source_target_pairs={{0,4},{1,5},{2,6},{3,7},{4,12},{5,13},{6,14},{7,15},{8,0},{9,1},{1... | collective-permute-start | bytes 1572872 | tf_op jit(solution)/shard_map/ppermute | solution.py:376
  18.4 14.9 %collective-permute-start.7 = (bf16[128,2048]{1,0:T(8,128)(2,1)S(1)}, bf16[128,2048]{1,0:T(8,128)(2,1)S(1)}, u32[]{:S(2)}, u32[]{:S(2)}) collective-permute-start(bf16[128,2048]{1,0:T(8,128)(2,1)S(1)} %collective-permute-done), channel_id=1, source_target_pairs={{0,16},{1,3},{2,18},{3,1},{4,20},{5,7},{6,22},{7,5},{8,24},{9,11},... | collective-permute-start | bytes 1572872 | tf_op jit(solution)/shard_map/ppermute | solution.py:376
  42.6 15.8 %collective-permute-start.12 = (bf16[2,128,2048]{2,1,0:T(8,128)(2,1)S(1)}, bf16[2,128,2048]{2,1,0:T(8,128)(2,1)}, u32[]{:S(2)}, u32[]{:S(2)}) collective-permute-start(bf16[2,128,2048]{2,1,0:T(8,128)(2,1)S(1)} %pad_maximum_fusion.2.refs_0_), channel_id=1, source_target_pairs={{0,2},{1,17},{2,0},{3,19},{4,6},{5,21},{6,4},{7,23},{8,10},{9,25},... | collective-permute-start | bytes 3145736 | tf_op jit(solution)/shard_map/ppermute | solution.py:376
  44.7 26.4 %collective-permute-start.9 = (bf16[2,128,2048]{2,1,0:T(8,128)(2,1)S(1)}, bf16[2,128,2048]{2,1,0:T(8,128)(2,1)S(1)}, u32[]{:S(2)}, u32[]{:S(2)}) collective-permute-start(bf16[2,128,2048]{2,1,0:T(8,128)(2,1)S(1)} %pad_maximum_fusion.1.refs_0_), channel_id=1, source_target_pairs={{0,4},{1,5},{2,6},{3,7},{4,12},{5,13},{6,14},{7,15},{8,0},{9,1},{1... | collective-permute-start | bytes 3145736 | tf_op jit(solution)/shard_map/ppermute | solution.py:376
  47.0 32.4 %collective-permute-start.16 = (bf16[2,128,2048]{2,1,0:T(8,128)(2,1)S(1)}, bf16[2,128,2048]{2,1,0:T(8,128)(2,1)S(1)}, u32[]{:S(2)}, u32[]{:S(2)}) collective-permute-start(bf16[2,128,2048]{2,1,0:T(8,128)(2,1)S(1)} %pad_maximum_fusion.1.refs_0_), channel_id=1, source_target_pairs={{0,2},{1,17},{2,0},{3,19},{4,6},{5,21},{6,4},{7,23},{8,10},{9,25},... | collective-permute-start | bytes 3145736 | tf_op jit(solution)/shard_map/ppermute | solution.py:376
  56.9 14.2 %collective-permute-start.5 = (bf16[320,768]{1,0:T(8,128)(2,1)S(1)}, bf16[320,768]{1,0:T(8,128)(2,1)S(1)}, u32[]{:S(2)}, u32[]{:S(2)}) collective-permute-start(bf16[320,768]{1,0:T(8,128)(2,1)S(1)} %gate_up.4.refs_5_.refs_0_), channel_id=1, source_target_pairs={{0,16},{1,17},{2,18},{3,19},{4,20},{5,21},{6,22},{7,23},{8,24},{9,... | collective-permute-start | bytes 1474568 | tf_op jit(solution)/shard_map/ppermute | solution.py:376
  58.5 20.9 %collective-permute-start.13 = (bf16[2,128,2048]{2,1,0:T(8,128)(2,1)S(1)}, bf16[2,128,2048]{2,1,0:T(8,128)(2,1)S(1)}, u32[]{:S(2)}, u32[]{:S(2)}) collective-permute-start(bf16[2,128,2048]{2,1,0:T(8,128)(2,1)S(1)} %pad_maximum_fusion.2.refs_0_), channel_id=1, source_target_pairs={{0,1},{1,0},{2,3},{3,2},{4,5},{5,4},{6,7},{7,6},{8,9},{9,8},{10,11... | collective-permute-start | bytes 3145736 | tf_op jit(solution)/shard_map/ppermute | solution.py:376
  58.5 21.4 %collective-permute-start.14 = (bf16[2,128,2048]{2,1,0:T(8,128)(2,1)}, bf16[2,128,2048]{2,1,0:T(8,128)(2,1)S(1)}, u32[]{:S(2)}, u32[]{:S(2)}) collective-permute-start(bf16[2,128,2048]{2,1,0:T(8,128)(2,1)} %collective-permute-done.12.refs_1_), channel_id=1, source_target_pairs={{0,1},{1,0},{2,3},{3,2},{4,5},{5,4},{6,7},{7,6},{8,9},{9,8},{10,11... | collective-permute-start | bytes 3145736 | tf_op jit(solution)/shard_map/ppermute | solution.py:376
  71.1 17.0 %collective-permute-start.10 = (bf16[2,128,2048]{2,1,0:T(8,128)(2,1)S(1)}, bf16[2,128,2048]{2,1,0:T(8,128)(2,1)S(1)}, u32[]{:S(2)}, u32[]{:S(2)}) collective-permute-start(bf16[2,128,2048]{2,1,0:T(8,128)(2,1)S(1)} %collective-permute-done.9.refs_6_.refs_0_), channel_id=1, source_target_pairs={{0,2},{1,17},{2,0},{3,19},{4,6},{5,21},{6,4},{7,23},{8,10},{9,25},... | collective-permute-start | bytes 3145736 | tf_op jit(solution)/shard_map/ppermute | solution.py:376
  72.6 20.6 %collective-permute-start.17 = (bf16[2,128,2048]{2,1,0:T(8,128)(2,1)S(1)}, bf16[2,128,2048]{2,1,0:T(8,128)(2,1)S(1)}, u32[]{:S(2)}, u32[]{:S(2)}) collective-permute-start(bf16[2,128,2048]{2,1,0:T(8,128)(2,1)S(1)} %pad_maximum_fusion.1.refs_0_), channel_id=1, source_target_pairs={{0,1},{1,0},{2,3},{3,2},{4,5},{5,4},{6,7},{7,6},{8,9},{9,8},{10,11... | collective-permute-start | bytes 3145736 | tf_op jit(solution)/shard_map/ppermute | solution.py:376
  79.4 13.9 %collective-permute-start.18 = (bf16[2,128,2048]{2,1,0:T(8,128)(2,1)S(1)}, bf16[2,128,2048]{2,1,0:T(8,128)(2,1)S(1)}, u32[]{:S(2)}, u32[]{:S(2)}) collective-permute-start(bf16[2,128,2048]{2,1,0:T(8,128)(2,1)S(1)} %collective-permute-done.16.refs_1_), channel_id=1, source_target_pairs={{0,1},{1,0},{2,3},{3,2},{4,5},{5,4},{6,7},{7,6},{8,9},{9,8},{10,11... | collective-permute-start | bytes 3145736 | tf_op jit(solution)/shard_map/ppermute | solution.py:376
  79.4 22.5 %collective-permute-start.11 = (bf16[2,128,2048]{2,1,0:T(8,128)(2,1)S(1)}, bf16[2,128,2048]{2,1,0:T(8,128)(2,1)S(1)}, u32[]{:S(2)}, u32[]{:S(2)}) collective-permute-start(bf16[2,128,2048]{2,1,0:T(8,128)(2,1)S(1)} %collective-permute-done.9.refs_6_.refs_0_), channel_id=1, source_target_pairs={{0,1},{1,0},{2,3},{3,2},{4,5},{5,4},{6,7},{7,6},{8,9},{9,8},{10,11... | collective-permute-start | bytes 3145736 | tf_op jit(solution)/shard_map/ppermute | solution.py:376
  88.2 17.3 %collective-permute-start.15 = (bf16[2,128,2048]{2,1,0:T(8,128)(2,1)S(1)}, bf16[2,128,2048]{2,1,0:T(8,128)(2,1)S(1)}, u32[]{:S(2)}, u32[]{:S(2)}) collective-permute-start(bf16[2,128,2048]{2,1,0:T(8,128)(2,1)S(1)} %collective-permute-done.10.refs_1_), channel_id=1, source_target_pairs={{0,1},{1,0},{2,3},{3,2},{4,5},{5,4},{6,7},{7,6},{8,9},{9,8},{10,11... | collective-permute-start | bytes 3145736 | tf_op jit(solution)/shard_map/ppermute | solution.py:376
  91.6 13.9 %collective-permute-start.20 = (bf16[320,768]{1,0:T(8,128)(2,1)S(1)}, bf16[320,768]{1,0:T(8,128)(2,1)S(1)}, u32[]{:S(2)}, u32[]{:S(2)}) collective-permute-start(bf16[320,768]{1,0:T(8,128)(2,1)S(1)} %gate_up.5.refs_5_.refs_0_), channel_id=1, source_target_pairs={{0,16},{1,17},{2,18},{3,19},{4,20},{5,21},{6,22},{7,23},{8,24},{9,... | collective-permute-start | bytes 1474568 | tf_op jit(solution)/shard_map/ppermute | solution.py:376
  101.4 13.8 %collective-permute-start.19 = (bf16[320,768]{1,0:T(8,128)(2,1)S(1)}, bf16[320,768]{1,0:T(8,128)(2,1)S(1)}, u32[]{:S(2)}, u32[]{:S(2)}) collective-permute-start(bf16[320,768]{1,0:T(8,128)(2,1)S(1)} %gate_up.6.refs_3_.refs_0_), channel_id=1, source_target_pairs={{0,16},{1,17},{2,18},{3,19},{4,20},{5,21},{6,22},{7,23},{8,24},{9,... | collective-permute-start | bytes 1474568 | tf_op jit(solution)/shard_map/ppermute | solution.py:376
  124.2 14.0 %collective-permute-start.22 = (bf16[128,2048]{1,0:T(8,128)(2,1)S(1)}, bf16[128,2048]{1,0:T(8,128)(2,1)S(1)}, u32[]{:S(2)}, u32[]{:S(2)}) collective-permute-start(bf16[128,2048]{1,0:T(8,128)(2,1)S(1)} %fusion.10), channel_id=1, source_target_pairs={{0,2},{1,3},{2,0},{3,1},{4,6},{5,7},{6,4},{7,5},{8,10},{9,11},{10,... | collective-permute-start | bytes 1572872 | tf_op jit(solution)/shard_map/ppermute | solution.py:376
  138.5 16.3 %collective-permute-start.27 = (bf16[128,2048]{1,0:T(8,128)(2,1)S(1)}, bf16[128,2048]{1,0:T(8,128)(2,1)S(1)}, u32[]{:S(2)}, u32[]{:S(2)}) collective-permute-start(bf16[128,2048]{1,0:T(8,128)(2,1)S(1)} %fusion.6), channel_id=1, source_target_pairs={{4,0},{5,1},{6,2},{7,3},{12,4},{13,5},{14,6},{15,7},{0,8},{1,9},{2... | collective-permute-start | bytes 1572872 | tf_op jit(solution)/shard_map/ppermute | solution.py:376
  141.4 13.4 %collective-permute-start.26 = (bf16[128,2048]{1,0:T(8,128)(2,1)S(1)}, bf16[128,2048]{1,0:T(8,128)(2,1)S(1)}, u32[]{:S(2)}, u32[]{:S(2)}) collective-permute-start(bf16[128,2048]{1,0:T(8,128)(2,1)S(1)} %fusion.12), channel_id=1, source_target_pairs={{0,2},{1,3},{2,0},{3,1},{4,6},{5,7},{6,4},{7,5},{8,10},{9,11},{10,... | collective-permute-start | bytes 1572872 | tf_op jit(solution)/shard_map/ppermute | solution.py:376
  163.7 14.0 %collective-permute-start.29 = (bf16[128,2048]{1,0:T(8,128)(2,1)S(1)}, bf16[128,2048]{1,0:T(8,128)(2,1)S(1)}, u32[]{:S(2)}, u32[]{:S(2)}) collective-permute-start(bf16[128,2048]{1,0:T(8,128)(2,1)S(1)} %fusion.13), channel_id=1, source_target_pairs={{0,2},{1,3},{2,0},{3,1},{4,6},{5,7},{6,4},{7,5},{8,10},{9,11},{10,... | collective-permute-start | bytes 1572872 | tf_op jit(solution)/shard_map/ppermute | solution.py:376
  165.0 14.6 %collective-permute-start.31 = (bf16[128,2048]{1,0:T(8,128)(2,1)S(1)}, bf16[128,2048]{1,0:T(8,128)(2,1)S(1)}, u32[]{:S(2)}, u32[]{:S(2)}) collective-permute-start(bf16[128,2048]{1,0:T(8,128)(2,1)S(1)} %fusion.3), channel_id=1, source_target_pairs={{0,4},{1,5},{2,6},{3,7},{4,12},{5,13},{6,14},{7,15},{8,0},{9,1},{1... | collective-permute-start | bytes 1572872 | tf_op jit(solution)/shard_map/ppermute | solution.py:376
  177.8 13.1 %collective-permute-start.30 = (bf16[128,2048]{1,0:T(8,128)(2,1)S(1)}, bf16[128,2048]{1,0:T(8,128)(2,1)S(1)}, u32[]{:S(2)}, u32[]{:S(2)}) collective-permute-start(bf16[128,2048]{1,0:T(8,128)(2,1)S(1)} %fusion.11), channel_id=1, source_target_pairs={{0,2},{1,3},{2,0},{3,1},{4,6},{5,7},{6,4},{7,5},{8,10},{9,11},{10,... | collective-permute-start | bytes 1572872 | tf_op jit(solution)/shard_map/ppermute | solution.py:376
  180.0 13.8 %collective-permute-start.32 = (bf16[128,2048]{1,0:T(8,128)(2,1)S(1)}, bf16[128,2048]{1,0:T(8,128)(2,1)S(1)}, u32[]{:S(2)}, u32[]{:S(2)}) collective-permute-start(bf16[128,2048]{1,0:T(8,128)(2,1)S(1)} %fusion.5), channel_id=1, source_target_pairs={{0,4},{1,5},{2,6},{3,7},{4,12},{5,13},{6,14},{7,15},{8,0},{9,1},{1... | collective-permute-start | bytes 1572872 | tf_op jit(solution)/shard_map/ppermute | solution.py:376
  (11 other events, 184.8 us)

commit v10 on v9

--- a/solution.py
+++ b/solution.py
@@ -396,14 +396,15 @@
     pairs.append(jnp.stack([last, near_last]))
     pairs.append(move(pairs[2], onward))
     crosses.append(move(after(pairs[1], pairs[2]), second))
-    crosses.append(move(pairs[2], second))
 
     def spread(k, *done):
         return [pairs[k], crosses[k], move(pairs[k], sibling), move(after(crosses[k], *done), sibling)]
 
     def gate_up(k, shards_of, *earlier):
-        mine = pick_call(k, where, code, shards_of, gate_up_weight[0], earlier, capacity)
-        return mine, move(mine, over_x)
+        return pick_call(k, where, code, shards_of, gate_up_weight[0], earlier, capacity)
+
+    def swap(mine, *done):
+        return mine, move(after(mine, *done), over_x)
 
     def down(k, hidden, *earlier):
         return sum_call(k, where, code, *hidden, down_weight[0], earlier, capacity)
@@ -419,21 +420,22 @@
         terms = [v.astype(jnp.float32) for v in (part[0][0], part[1][0], back, *hop)]
         return functools.reduce(jnp.add, terms).astype(jnp.bfloat16)
 
-    hidden0 = gate_up(0, spread(0))
-    crosses.append(move(after(pairs[3], hidden0[1]), second))
-    hidden1 = gate_up(1, spread(1, hidden0[0]), hidden0[0], pairs[3])
-    hidden2 = gate_up(2, spread(2, hidden0[0]), hidden1[0])
-    shards3 = spread(3, hidden1[0])
-    part1 = down(1, hidden1, hidden2[0], *shards3[2:])
-    part2 = down(2, hidden2, part1[0])
-    part1 = give(part1, part2[0])
-    part2 = give(part2)
+    hidden0 = swap(gate_up(0, spread(0)))
+    crosses.append(move(after(pairs[2], hidden0[0]), second))
+    hidden1 = swap(gate_up(1, spread(1, hidden0[0]), *hidden0))
+    pairs[3] = after(pairs[3], hidden1[0])
+    crosses.append(move(pairs[3], second))
+    hidden2 = swap(gate_up(2, spread(2, hidden1[0]), hidden1[0], pairs[3]))
+    part0 = give(down(0, hidden0, hidden2[0]))
+    part1 = down(1, hidden1, part0[0], crosses[3])
+    shards3 = spread(3, part1[0])
+    part1 = give(part1)
     back1 = move(away(part1), over_y)
-    hidden3 = gate_up(3, shards3, part2[0])
-    part0 = give(down(0, hidden0, hidden3[0], back1))
-    back2 = move(after(away(part2), back1, hidden3[0]), over_y)
+    hidden3 = swap(gate_up(3, shards3, part1[0]))
+    part2 = give(down(2, hidden2, hidden3[0], back1), hidden3[1])
     from_next = move(total(part1, after(back1, hidden3[0])), backward)
-    part3 = give(down(3, hidden3, part0[0], back2, from_next))
+    back2 = move(away(part2), over_y)
+    part3 = give(down(3, hidden3, part2[0]), from_next, back2)
     from_far = move(total(part2, back2), onward)
     back3 = move(away(part3), over_y)
     from_last = move(total(part3, back3, from_far), onward)

time: 195 us -> 198 us (1.015)
  starting transfers between devices: 43.1 us -> 53.9 us
  waiting for transfers between devices: 74.1 us -> 68.6 us
    ppermute x33, starting transfers between devices: 43.1 us -> 53.9 us  [move(): return lax.ppermute(value, axes, moves)]
    ppermute x33, waiting for transfers between devices: 74.1 us -> 68.6 us  [move(): return lax.ppermute(value, axes, moves)]
  transfers between devices with their start and end apart: 33 -> 33, of which waited for: 14 -> 14; matrix products, arithmetic and copies ran while one was open for 3% -> 2% of each run, Pallas kernels for 24% -> 26%
where the time goes in v10:
time: 198 us
  waiting for transfers between devices  68.6 us (35%)
  Pallas kernels  58.2 us (29%)
  starting transfers between devices  53.9 us (27%)
  blocking collectives  10.9 us (6%)
  other arithmetic  5.31 us (3%)
    ppermute x33, waiting for transfers between devices, move(): return lax.ppermute(value, axes, moves)  68.6 us
    ppermute x33, starting transfers between devices, move(): return lax.ppermute(value, axes, moves)  53.9 us
    pallas_call x4, Pallas kernels, pick_call(): pl.pallas_call(functools.partial(pick_kernel, capacity, k), in_specs=[pl....  33.7 us
    pallas_call x4, Pallas kernels, sum_call(): pl.pallas_call(functools.partial(sum_kernel, capacity, k), in_specs=[pl.B...  24.5 us
    all_to_all x1, blocking collectives, pair_shards(): lax.all_to_all(named, 'expert', split_axis=0, concat_axis=0, tiled=True)  10.9 us
  transfers between devices with their start and end apart: 33, of which 14 were waited for; matrix products, arithmetic and copies ran while one was open for 2% of the time, Pallas kernels for 26%

profile of v10, /device:TPU:0, one launch (start us, length us, event | category | flops | bytes accessed | tf_op | source)
XLA Modules:
  0.0 198.0 jit_solution(7305027672640898857)
XLA Ops:
  0.0 2.9 %collective-permute-start.1 = (bf16[128,2048]{1,0:T(8,128)(2,1)}, bf16[128,2048]{1,0:T(8,128)(2,1)S(1)}, u32[]{:S(2)}, u32[]{:S(2)}) collective-permute-start(bf16[128,2048]{1,0:T(8,128)(2,1)} %param.6), channel_id=1, source_target_pairs={{0,16},{1,3},{2,18},{3,1},{4,20},{5,7},{6,22},{7,5},{8,24},{9,11},... | collective-permute-start | bytes 1572872 | tf_op jit(solution)/shard_map/ppermute | solution.py:376
  4.5 5.8 %collective-permute-done.1 = bf16[128,2048]{1,0:T(8,128)(2,1)S(1)} collective-permute-done((bf16[128,2048]{1,0:T(8,128)(2,1)}, bf16[128,2048]{1,0:T(8,128)(2,1)S(1)}, u32[]{:S(2)}, u32[]{:S(2)}) %collective-permute-start.1) | collective-permute-done | bytes 524320 | tf_op jit(solution)/shard_map/ppermute | solution.py:376
  13.6 3.9 %collective-permute-done = bf16[128,2048]{1,0:T(8,128)(2,1)S(1)} collective-permute-done((bf16[128,2048]{1,0:T(8,128)(2,1)}, bf16[128,2048]{1,0:T(8,128)(2,1)S(1)}, u32[]{:S(2)}, u32[]{:S(2)}) %collective-permute-start) | collective-permute-done | bytes 524320 | tf_op jit(solution)/shard_map/ppermute | solution.py:376
  21.4 10.9 %all_to_all.11 = s32[16,1,128]{2,1,0:T(1,128)S(1)} all-to-all(s32[16,1,128]{2,1,0:T(1,128)S(1)} %bitcast.73), channel_id=1, replica_groups=mesh['section'=2,'expert'=16] {'expert'}, dimensions={0} | all-to-all | bytes 16384 | tf_op jit(solution)/shard_map/all_to_all | solution.py:392
  32.3 2.2 %collective-permute-start.8 = (bf16[128,2048]{1,0:T(8,128)(2,1)S(1)}, bf16[128,2048]{1,0:T(8,128)(2,1)S(1)}, u32[]{:S(2)}, u32[]{:S(2)}) collective-permute-start(bf16[128,2048]{1,0:T(8,128)(2,1)S(1)} %collective-permute-done.6), channel_id=1, source_target_pairs={{0,16},{1,3},{2,18},{3,1},{4,20},{5,7},{6,22},{7,5},{8,24},{9,11},... | collective-permute-start | bytes 1572872 | tf_op jit(solution)/shard_map/ppermute | solution.py:376
  35.1 6.5 %collective-permute-done.8 = bf16[128,2048]{1,0:T(8,128)(2,1)S(1)} collective-permute-done((bf16[128,2048]{1,0:T(8,128)(2,1)S(1)}, bf16[128,2048]{1,0:T(8,128)(2,1)S(1)}, u32[]{:S(2)}, u32[]{:S(2)}) %collective-permute-start.8) | collective-permute-done | bytes 524320 | tf_op jit(solution)/shard_map/ppermute | solution.py:376
  44.3 8.9 %gate_up.4.refs_5_.refs_0_ = bf16[320,768]{1,0:T(8,128)(2,1)S(1)} custom-call(s32[4,6]{1,0:T(4,128)S(1)} %dynamic-slice_bitcast_fusion.where_ref, s32[16,128]{1,0:T(8,128)S(1)} %bitcast.53, bf16[2,128,2048]{2,1,0:T(8,128)(2,1)S(1)} %pad_maximum_fusion.refs_0_, bf16[2,128,2048]{2,1,0:T(8,128)(2,1)} %collective-permute-done.2.refs_1_, ...), custom_call_target="tpu_custom_call" | custom-call | flops 4362076160 | bytes 17268736 | tf_op jit(solution)/shard_map/gate_up/pallas_call | solution.py:257
  53.2 3.6 %collective-permute-done.11.refs_1_ = bf16[2,128,2048]{2,1,0:T(8,128)(2,1)} collective-permute-done((bf16[2,128,2048]{2,1,0:T(8,128)(2,1)S(1)}, bf16[2,128,2048]{2,1,0:T(8,128)(2,1)}, u32[]{:S(2)}, u32[]{:S(2)}) %collective-permute-start.11) | collective-permute-done | bytes 1048608 | tf_op jit(solution)/shard_map/ppermute | solution.py:376
  61.6 11.1 %collective-permute-done.5.refs_6_.refs_1_ = bf16[320,768]{1,0:T(8,128)(2,1)S(1)} collective-permute-done((bf16[320,768]{1,0:T(8,128)(2,1)S(1)}, bf16[320,768]{1,0:T(8,128)(2,1)S(1)}, u32[]{:S(2)}, u32[]{:S(2)}) %collective-permute-start.5) | collective-permute-done | bytes 491552 | tf_op jit(solution)/shard_map/ppermute | solution.py:376
  72.7 8.6 %gate_up.5.refs_5_.refs_0_ = bf16[320,768]{1,0:T(8,128)(2,1)S(1)} custom-call(s32[4,6]{1,0:T(4,128)S(1)} %dynamic-slice_bitcast_fusion.where_ref, s32[16,128]{1,0:T(8,128)S(1)} %bitcast.54, bf16[2,128,2048]{2,1,0:T(8,128)(2,1)S(1)} %pad_maximum_fusion.2.refs_0_, bf16[2,128,2048]{2,1,0:T(8,128)(2,1)} %collective-permute-done.11.refs_1_, ...), custom_call_target="tpu_custom_call" | custom-call | flops 4362076160 | bytes 17268736 | tf_op jit(solution)/shard_map/gate_up/pallas_call | solution.py:257
  81.3 9.4 %collective-permute-start.14 = (bf16[2,128,2048]{2,1,0:T(8,128)(2,1)S(1)}, bf16[2,128,2048]{2,1,0:T(8,128)(2,1)S(1)}, u32[]{:S(2)}, u32[]{:S(2)}) collective-permute-start(bf16[2,128,2048]{2,1,0:T(8,128)(2,1)S(1)} %collective-permute-done.9.refs_1_), channel_id=1, source_target_pairs={{0,1},{1,0},{2,3},{3,2},{4,5},{5,4},{6,7},{7,6},{8,9},{9,8},{10,11... | collective-permute-start | bytes 3145736 | tf_op jit(solution)/shard_map/ppermute | solution.py:376
  93.9 8.1 %gate_up.6.refs_3_.refs_0_ = bf16[320,768]{1,0:T(8,128)(2,1)S(1)} custom-call(s32[4,6]{1,0:T(4,128)S(1)} %dynamic-slice_bitcast_fusion.where_ref, s32[16,128]{1,0:T(8,128)S(1)} %bitcast.55, bf16[2,128,2048]{2,1,0:T(8,128)(2,1)S(1)} %pad_maximum_fusion.1.refs_0_, bf16[2,128,2048]{2,1,0:T(8,128)(2,1)S(1)} %collective-permute-done.9.refs_1_, ...), custom_call_target="tpu_custom_call" | custom-call | flops 4362076160 | bytes 17268736 | tf_op jit(solution)/shard_map/gate_up/pallas_call | solution.py:257
  102.1 6.1 %down.4 = (bf16[2,128,2048]{2,1,0:T(8,128)(2,1)S(1)}, bf16[2,128,2048]{2,1,0:T(8,128)(2,1)S(1)}) custom-call(s32[4,6]{1,0:T(4,128)S(1)} %dynamic-slice_bitcast_fusion.where_ref, s32[16,128]{1,0:T(8,128)S(1)} %bitcast.56, bf16[320,768]{1,0:T(8,128)(2,1)S(1)} %gate_up.4.refs_5_.refs_0_, bf16[320,768]{1,0:T(8,128)(2,1)S(1)} %collective-permute-done.5.refs_6_.refs_1_, ...), custom_call_target="tpu_custom_call" | custom-call | flops 2181038080 | bytes 9371648 | tf_op jit(solution)/shard_map/down/pallas_call | solution.py:287
  108.2 6.1 %down.5 = (bf16[2,128,2048]{2,1,0:T(8,128)(2,1)S(1)}, bf16[2,128,2048]{2,1,0:T(8,128)(2,1)S(1)}) custom-call(s32[4,6]{1,0:T(4,128)S(1)} %dynamic-slice_bitcast_fusion.where_ref, s32[16,128]{1,0:T(8,128)S(1)} %bitcast.57, bf16[320,768]{1,0:T(8,128)(2,1)S(1)} %gate_up.5.refs_5_.refs_0_, bf16[320,768]{1,0:T(8,128)(2,1)S(1)} %collective-permute-done.19.refs_1_, ...), custom_call_target="tpu_custom_call" | custom-call | flops 2181038080 | bytes 9371648 | tf_op jit(solution)/shard_map/down/pallas_call | solution.py:287
  114.4 6.8 %collective-permute-start.23 = (bf16[2,128,2048]{2,1,0:T(8,128)(2,1)S(1)}, bf16[2,128,2048]{2,1,0:T(8,128)(2,1)S(1)}, u32[]{:S(2)}, u32[]{:S(2)}) collective-permute-start(bf16[2,128,2048]{2,1,0:T(8,128)(2,1)S(1)} %get-tuple-element.36), channel_id=1, source_target_pairs={{0,1},{1,0},{2,3},{3,2},{4,5},{5,4},{6,7},{7,6},{8,9},{9,8},{10,11... | collective-permute-start | bytes 3145736 | tf_op jit(solution)/shard_map/ppermute | solution.py:376
  126.4 8.1 %gate_up.7.refs_3_.refs_0_ = bf16[320,768]{1,0:T(8,128)(2,1)S(1)} custom-call(s32[4,6]{1,0:T(4,128)S(1)} %dynamic-slice_bitcast_fusion.where_ref, s32[16,128]{1,0:T(8,128)S(1)} %bitcast.58, bf16[2,128,2048]{2,1,0:T(8,128)(2,1)S(1)} %collective-permute-done.15.refs_6_.refs_0_, bf16[2,128,2048]{2,1,0:T(8,128)(2,1)S(1)} %collective-permute-done.17.refs_4_.refs_1_, ...), custom_call_target="tpu_custom_call" | custom-call | flops 4362076160 | bytes 17268736 | tf_op jit(solution)/shard_map/gate_up/pallas_call | solution.py:257
  137.8 6.1 %down.6 = (bf16[2,128,2048]{2,1,0:T(8,128)(2,1)S(1)}, bf16[2,128,2048]{2,1,0:T(8,128)(2,1)S(1)}) custom-call(s32[4,6]{1,0:T(4,128)S(1)} %dynamic-slice_bitcast_fusion.where_ref, s32[16,128]{1,0:T(8,128)S(1)} %bitcast.59, bf16[320,768]{1,0:T(8,128)(2,1)S(1)} %gate_up.6.refs_3_.refs_0_, bf16[320,768]{1,0:T(8,128)(2,1)S(1)} %collective-permute-done.22.refs_1_, ...), custom_call_target="tpu_custom_call" | custom-call | flops 2181038080 | bytes 9371648 | tf_op jit(solution)/shard_map/down/pallas_call | solution.py:287
  144.0 4.2 %collective-permute-done.21.refs_1_ = bf16[320,768]{1,0:T(8,128)(2,1)S(1)} collective-permute-done((bf16[320,768]{1,0:T(8,128)(2,1)S(1)}, bf16[320,768]{1,0:T(8,128)(2,1)S(1)}, u32[]{:S(2)}, u32[]{:S(2)}) %collective-permute-start.21) | collective-permute-done | bytes 491552 | tf_op jit(solution)/shard_map/ppermute | solution.py:376
  148.4 2.8 %collective-permute-start.25 = (bf16[128,2048]{1,0:T(8,128)(2,1)S(1)}, bf16[128,2048]{1,0:T(8,128)(2,1)S(1)}, u32[]{:S(2)}, u32[]{:S(2)}) collective-permute-start(bf16[128,2048]{1,0:T(8,128)(2,1)S(1)} %fusion.6), channel_id=1, source_target_pairs={{4,0},{5,1},{6,2},{7,3},{12,4},{13,5},{14,6},{15,7},{0,8},{1,9},{2... | collective-permute-start | bytes 1572872 | tf_op jit(solution)/shard_map/ppermute | solution.py:376
  152.9 6.1 %down.7 = (bf16[2,128,2048]{2,1,0:T(8,128)(2,1)S(1)}, bf16[2,128,2048]{2,1,0:T(8,128)(2,1)S(1)}) custom-call(s32[4,6]{1,0:T(4,128)S(1)} %dynamic-slice_bitcast_fusion.where_ref, s32[16,128]{1,0:T(8,128)S(1)} %bitcast.60, bf16[320,768]{1,0:T(8,128)(2,1)S(1)} %gate_up.7.refs_3_.refs_0_, bf16[320,768]{1,0:T(8,128)(2,1)S(1)} %collective-permute-done.21.refs_1_, ...), custom_call_target="tpu_custom_call" | custom-call | flops 2181038080 | bytes 9371648 | tf_op jit(solution)/shard_map/down/pallas_call | solution.py:287
  159.1 4.0 %collective-permute-done.25 = bf16[128,2048]{1,0:T(8,128)(2,1)S(1)} collective-permute-done((bf16[128,2048]{1,0:T(8,128)(2,1)S(1)}, bf16[128,2048]{1,0:T(8,128)(2,1)S(1)}, u32[]{:S(2)}, u32[]{:S(2)}) %collective-permute-start.25) | collective-permute-done | bytes 524320 | tf_op jit(solution)/shard_map/ppermute | solution.py:376
  163.1 2.4 %collective-permute-done.27 = bf16[128,2048]{1,0:T(8,128)(2,1)S(1)} collective-permute-done((bf16[128,2048]{1,0:T(8,128)(2,1)S(1)}, bf16[128,2048]{1,0:T(8,128)(2,1)S(1)}, u32[]{:S(2)}, u32[]{:S(2)}) %collective-permute-start.27) | collective-permute-done | bytes 524320 | tf_op jit(solution)/shard_map/ppermute | solution.py:376
  170.0 11.0 %collective-permute-done.31 = bf16[128,2048]{1,0:T(8,128)(2,1)S(1)} collective-permute-done((bf16[128,2048]{1,0:T(8,128)(2,1)S(1)}, bf16[128,2048]{1,0:T(8,128)(2,1)S(1)}, u32[]{:S(2)}, u32[]{:S(2)}) %collective-permute-start.31) | collective-permute-done | bytes 524320 | tf_op jit(solution)/shard_map/ppermute | solution.py:376
  185.6 11.2 %collective-permute-done.32 = bf16[128,2048]{1,0:T(8,128)(2,1)S(1)} collective-permute-done((bf16[128,2048]{1,0:T(8,128)(2,1)S(1)}, bf16[128,2048]{1,0:T(8,128)(2,1)S(1)}, u32[]{:S(2)}, u32[]{:S(2)}) %collective-permute-start.32) | collective-permute-done | bytes 524320 | tf_op jit(solution)/shard_map/ppermute | solution.py:376
  (71 shorter events, 40.8 us)
Async XLA Ops:
  0.0 10.3 %collective-permute-start.1 = (bf16[128,2048]{1,0:T(8,128)(2,1)}, bf16[128,2048]{1,0:T(8,128)(2,1)S(1)}, u32[]{:S(2)}, u32[]{:S(2)}) collective-permute-start(bf16[128,2048]{1,0:T(8,128)(2,1)} %param.6), channel_id=1, source_target_pairs={{0,16},{1,3},{2,18},{3,1},{4,20},{5,7},{6,22},{7,5},{8,24},{9,11},... | collective-permute-start | bytes 1572872 | tf_op jit(solution)/shard_map/ppermute | solution.py:376
  2.9 14.5 %collective-permute-start = (bf16[128,2048]{1,0:T(8,128)(2,1)}, bf16[128,2048]{1,0:T(8,128)(2,1)S(1)}, u32[]{:S(2)}, u32[]{:S(2)}) collective-permute-start(bf16[128,2048]{1,0:T(8,128)(2,1)} %param.6), channel_id=1, source_target_pairs={{0,4},{1,5},{2,6},{3,7},{4,12},{5,13},{6,14},{7,15},{8,0},{9,1},{1... | collective-permute-start | bytes 1572872 | tf_op jit(solution)/shard_map/ppermute | solution.py:376
  11.4 20.8 %collective-permute-start.2 = (bf16[2,128,2048]{2,1,0:T(8,128)(2,1)S(1)}, bf16[2,128,2048]{2,1,0:T(8,128)(2,1)}, u32[]{:S(2)}, u32[]{:S(2)}) collective-permute-start(bf16[2,128,2048]{2,1,0:T(8,128)(2,1)S(1)} %pad_maximum_fusion.refs_0_), channel_id=1, source_target_pairs={{0,2},{1,17},{2,0},{3,19},{4,6},{5,21},{6,4},{7,23},{8,10},{9,25},... | collective-permute-start | bytes 3145736 | tf_op jit(solution)/shard_map/ppermute | solution.py:376
  17.5 14.8 %collective-permute-start.6 = (bf16[128,2048]{1,0:T(8,128)(2,1)S(1)}, bf16[128,2048]{1,0:T(8,128)(2,1)S(1)}, u32[]{:S(2)}, u32[]{:S(2)}) collective-permute-start(bf16[128,2048]{1,0:T(8,128)(2,1)S(1)} %collective-permute-done), channel_id=1, source_target_pairs={{0,4},{1,5},{2,6},{3,7},{4,12},{5,13},{6,14},{7,15},{8,0},{9,1},{1... | collective-permute-start | bytes 1572872 | tf_op jit(solution)/shard_map/ppermute | solution.py:376
  18.4 13.9 %collective-permute-start.7 = (bf16[128,2048]{1,0:T(8,128)(2,1)S(1)}, bf16[128,2048]{1,0:T(8,128)(2,1)S(1)}, u32[]{:S(2)}, u32[]{:S(2)}) collective-permute-start(bf16[128,2048]{1,0:T(8,128)(2,1)S(1)} %collective-permute-done), channel_id=1, source_target_pairs={{0,16},{1,3},{2,18},{3,1},{4,20},{5,7},{6,22},{7,5},{8,24},{9,11},... | collective-permute-start | bytes 1572872 | tf_op jit(solution)/shard_map/ppermute | solution.py:376
  41.8 15.0 %collective-permute-start.11 = (bf16[2,128,2048]{2,1,0:T(8,128)(2,1)S(1)}, bf16[2,128,2048]{2,1,0:T(8,128)(2,1)}, u32[]{:S(2)}, u32[]{:S(2)}) collective-permute-start(bf16[2,128,2048]{2,1,0:T(8,128)(2,1)S(1)} %pad_maximum_fusion.2.refs_0_), channel_id=1, source_target_pairs={{0,2},{1,17},{2,0},{3,19},{4,6},{5,21},{6,4},{7,23},{8,10},{9,25},... | collective-permute-start | bytes 3145736 | tf_op jit(solution)/shard_map/ppermute | solution.py:376
  44.3 17.3 %collective-permute-start.12 = (bf16[2,128,2048]{2,1,0:T(8,128)(2,1)S(1)}, bf16[2,128,2048]{2,1,0:T(8,128)(2,1)S(1)}, u32[]{:S(2)}, u32[]{:S(2)}) collective-permute-start(bf16[2,128,2048]{2,1,0:T(8,128)(2,1)S(1)} %pad_maximum_fusion.2.refs_0_), channel_id=1, source_target_pairs={{0,1},{1,0},{2,3},{3,2},{4,5},{5,4},{6,7},{7,6},{8,9},{9,8},{10,11... | collective-permute-start | bytes 3145736 | tf_op jit(solution)/shard_map/ppermute | solution.py:376
  56.8 15.9 %collective-permute-start.13 = (bf16[2,128,2048]{2,1,0:T(8,128)(2,1)}, bf16[2,128,2048]{2,1,0:T(8,128)(2,1)S(1)}, u32[]{:S(2)}, u32[]{:S(2)}) collective-permute-start(bf16[2,128,2048]{2,1,0:T(8,128)(2,1)} %collective-permute-done.11.refs_1_), channel_id=1, source_target_pairs={{0,1},{1,0},{2,3},{3,2},{4,5},{5,4},{6,7},{7,6},{8,9},{9,8},{10,11... | collective-permute-start | bytes 3145736 | tf_op jit(solution)/shard_map/ppermute | solution.py:376
  56.8 24.5 %collective-permute-start.9 = (bf16[2,128,2048]{2,1,0:T(8,128)(2,1)S(1)}, bf16[2,128,2048]{2,1,0:T(8,128)(2,1)S(1)}, u32[]{:S(2)}, u32[]{:S(2)}) collective-permute-start(bf16[2,128,2048]{2,1,0:T(8,128)(2,1)S(1)} %pad_maximum_fusion.1.refs_0_), channel_id=1, source_target_pairs={{0,2},{1,17},{2,0},{3,19},{4,6},{5,21},{6,4},{7,23},{8,10},{9,25},... | collective-permute-start | bytes 3145736 | tf_op jit(solution)/shard_map/ppermute | solution.py:376
  58.5 14.2 %collective-permute-start.5 = (bf16[320,768]{1,0:T(8,128)(2,1)S(1)}, bf16[320,768]{1,0:T(8,128)(2,1)S(1)}, u32[]{:S(2)}, u32[]{:S(2)}) collective-permute-start(bf16[320,768]{1,0:T(8,128)(2,1)S(1)} %gate_up.4.refs_5_.refs_0_), channel_id=1, source_target_pairs={{0,16},{1,17},{2,18},{3,19},{4,20},{5,21},{6,22},{7,23},{8,24},{9,... | collective-permute-start | bytes 1474568 | tf_op jit(solution)/shard_map/ppermute | solution.py:376
  60.3 30.4 %collective-permute-start.15 = (bf16[2,128,2048]{2,1,0:T(8,128)(2,1)S(1)}, bf16[2,128,2048]{2,1,0:T(8,128)(2,1)S(1)}, u32[]{:S(2)}, u32[]{:S(2)}) collective-permute-start(bf16[2,128,2048]{2,1,0:T(8,128)(2,1)S(1)} %pad_maximum_fusion.1.refs_0_), channel_id=1, source_target_pairs={{0,4},{1,5},{2,6},{3,7},{4,12},{5,13},{6,14},{7,15},{8,0},{9,1},{1... | collective-permute-start | bytes 3145736 | tf_op jit(solution)/shard_map/ppermute | solution.py:376
  61.6 32.3 %collective-permute-start.10 = (bf16[2,128,2048]{2,1,0:T(8,128)(2,1)S(1)}, bf16[2,128,2048]{2,1,0:T(8,128)(2,1)S(1)}, u32[]{:S(2)}, u32[]{:S(2)}) collective-permute-start(bf16[2,128,2048]{2,1,0:T(8,128)(2,1)S(1)} %pad_maximum_fusion.1.refs_0_), channel_id=1, source_target_pairs={{0,1},{1,0},{2,3},{3,2},{4,5},{5,4},{6,7},{7,6},{8,9},{9,8},{10,11... | collective-permute-start | bytes 3145736 | tf_op jit(solution)/shard_map/ppermute | solution.py:376
  81.3 12.7 %collective-permute-start.14 = (bf16[2,128,2048]{2,1,0:T(8,128)(2,1)S(1)}, bf16[2,128,2048]{2,1,0:T(8,128)(2,1)S(1)}, u32[]{:S(2)}, u32[]{:S(2)}) collective-permute-start(bf16[2,128,2048]{2,1,0:T(8,128)(2,1)S(1)} %collective-permute-done.9.refs_1_), channel_id=1, source_target_pairs={{0,1},{1,0},{2,3},{3,2},{4,5},{5,4},{6,7},{7,6},{8,9},{9,8},{10,11... | collective-permute-start | bytes 3145736 | tf_op jit(solution)/shard_map/ppermute | solution.py:376
  90.7 17.5 %collective-permute-start.17 = (bf16[2,128,2048]{2,1,0:T(8,128)(2,1)S(1)}, bf16[2,128,2048]{2,1,0:T(8,128)(2,1)S(1)}, u32[]{:S(2)}, u32[]{:S(2)}) collective-permute-start(bf16[2,128,2048]{2,1,0:T(8,128)(2,1)S(1)} %collective-permute-done.15.refs_6_.refs_0_), channel_id=1, source_target_pairs={{0,2},{1,17},{2,0},{3,19},{4,6},{5,21},{6,4},{7,23},{8,10},{9,25},... | collective-permute-start | bytes 3145736 | tf_op jit(solution)/shard_map/ppermute | solution.py:376
  92.2 16.1 %collective-permute-start.19 = (bf16[320,768]{1,0:T(8,128)(2,1)S(1)}, bf16[320,768]{1,0:T(8,128)(2,1)S(1)}, u32[]{:S(2)}, u32[]{:S(2)}) collective-permute-start(bf16[320,768]{1,0:T(8,128)(2,1)S(1)} %gate_up.5.refs_5_.refs_0_), channel_id=1, source_target_pairs={{0,16},{1,17},{2,18},{3,19},{4,20},{5,21},{6,22},{7,23},{8,24},{9,... | collective-permute-start | bytes 1474568 | tf_op jit(solution)/shard_map/ppermute | solution.py:376
  121.7 14.7 %collective-permute-start.22 = (bf16[320,768]{1,0:T(8,128)(2,1)S(1)}, bf16[320,768]{1,0:T(8,128)(2,1)S(1)}, u32[]{:S(2)}, u32[]{:S(2)}) collective-permute-start(bf16[320,768]{1,0:T(8,128)(2,1)S(1)} %gate_up.6.refs_3_.refs_0_), channel_id=1, source_target_pairs={{0,16},{1,17},{2,18},{3,19},{4,20},{5,21},{6,22},{7,23},{8,24},{9,... | collective-permute-start | bytes 1474568 | tf_op jit(solution)/shard_map/ppermute | solution.py:376
  123.6 14.3 %collective-permute-start.24 = (bf16[128,2048]{1,0:T(8,128)(2,1)S(1)}, bf16[128,2048]{1,0:T(8,128)(2,1)S(1)}, u32[]{:S(2)}, u32[]{:S(2)}) collective-permute-start(bf16[128,2048]{1,0:T(8,128)(2,1)S(1)} %fusion.11), channel_id=1, source_target_pairs={{0,2},{1,3},{2,0},{3,1},{4,6},{5,7},{6,4},{7,5},{8,10},{9,11},{10,... | collective-permute-start | bytes 1572872 | tf_op jit(solution)/shard_map/ppermute | solution.py:376
  134.6 13.6 %collective-permute-start.21 = (bf16[320,768]{1,0:T(8,128)(2,1)S(1)}, bf16[320,768]{1,0:T(8,128)(2,1)S(1)}, u32[]{:S(2)}, u32[]{:S(2)}) collective-permute-start(bf16[320,768]{1,0:T(8,128)(2,1)S(1)} %gate_up.7.refs_3_.refs_0_), channel_id=1, source_target_pairs={{0,16},{1,17},{2,18},{3,19},{4,20},{5,21},{6,22},{7,23},{8,24},{9,... | collective-permute-start | bytes 1474568 | tf_op jit(solution)/shard_map/ppermute | solution.py:376
  148.4 14.7 %collective-permute-start.25 = (bf16[128,2048]{1,0:T(8,128)(2,1)S(1)}, bf16[128,2048]{1,0:T(8,128)(2,1)S(1)}, u32[]{:S(2)}, u32[]{:S(2)}) collective-permute-start(bf16[128,2048]{1,0:T(8,128)(2,1)S(1)} %fusion.6), channel_id=1, source_target_pairs={{4,0},{5,1},{6,2},{7,3},{12,4},{13,5},{14,6},{15,7},{0,8},{1,9},{2... | collective-permute-start | bytes 1572872 | tf_op jit(solution)/shard_map/ppermute | solution.py:376
  151.3 14.1 %collective-permute-start.27 = (bf16[128,2048]{1,0:T(8,128)(2,1)S(1)}, bf16[128,2048]{1,0:T(8,128)(2,1)S(1)}, u32[]{:S(2)}, u32[]{:S(2)}) collective-permute-start(bf16[128,2048]{1,0:T(8,128)(2,1)S(1)} %fusion.12), channel_id=1, source_target_pairs={{0,2},{1,3},{2,0},{3,1},{4,6},{5,7},{6,4},{7,5},{8,10},{9,11},{10,... | collective-permute-start | bytes 1572872 | tf_op jit(solution)/shard_map/ppermute | solution.py:376
  166.2 14.8 %collective-permute-start.31 = (bf16[128,2048]{1,0:T(8,128)(2,1)S(1)}, bf16[128,2048]{1,0:T(8,128)(2,1)S(1)}, u32[]{:S(2)}, u32[]{:S(2)}) collective-permute-start(bf16[128,2048]{1,0:T(8,128)(2,1)S(1)} %fusion.3), channel_id=1, source_target_pairs={{0,4},{1,5},{2,6},{3,7},{4,12},{5,13},{6,14},{7,15},{8,0},{9,1},{1... | collective-permute-start | bytes 1572872 | tf_op jit(solution)/shard_map/ppermute | solution.py:376
  168.3 14.0 %collective-permute-start.29 = (bf16[128,2048]{1,0:T(8,128)(2,1)S(1)}, bf16[128,2048]{1,0:T(8,128)(2,1)S(1)}, u32[]{:S(2)}, u32[]{:S(2)}) collective-permute-start(bf16[128,2048]{1,0:T(8,128)(2,1)S(1)} %fusion.13), channel_id=1, source_target_pairs={{0,2},{1,3},{2,0},{3,1},{4,6},{5,7},{6,4},{7,5},{8,10},{9,11},{10,... | collective-permute-start | bytes 1572872 | tf_op jit(solution)/shard_map/ppermute | solution.py:376
  182.6 14.1 %collective-permute-start.32 = (bf16[128,2048]{1,0:T(8,128)(2,1)S(1)}, bf16[128,2048]{1,0:T(8,128)(2,1)S(1)}, u32[]{:S(2)}, u32[]{:S(2)}) collective-permute-start(bf16[128,2048]{1,0:T(8,128)(2,1)S(1)} %fusion.5), channel_id=1, source_target_pairs={{0,4},{1,5},{2,6},{3,7},{4,12},{5,13},{6,14},{7,15},{8,0},{9,1},{1... | collective-permute-start | bytes 1572872 | tf_op jit(solution)/shard_map/ppermute | solution.py:376
  184.0 12.7 %collective-permute-start.30 = (bf16[128,2048]{1,0:T(8,128)(2,1)S(1)}, bf16[128,2048]{1,0:T(8,128)(2,1)S(1)}, u32[]{:S(2)}, u32[]{:S(2)}) collective-permute-start(bf16[128,2048]{1,0:T(8,128)(2,1)S(1)} %fusion.10), channel_id=1, source_target_pairs={{0,2},{1,3},{2,0},{3,1},{4,6},{5,7},{6,4},{7,5},{8,10},{9,11},{10,... | collective-permute-start | bytes 1572872 | tf_op jit(solution)/shard_map/ppermute | solution.py:376
  (11 other events, 107.5 us)

commit v11 on v10

--- a/solution.py
+++ b/solution.py
@@ -420,22 +420,24 @@
         terms = [v.astype(jnp.float32) for v in (part[0][0], part[1][0], back, *hop)]
         return functools.reduce(jnp.add, terms).astype(jnp.bfloat16)
 
-    hidden0 = swap(gate_up(0, spread(0)))
-    crosses.append(move(after(pairs[2], hidden0[0]), second))
-    hidden1 = swap(gate_up(1, spread(1, hidden0[0]), *hidden0))
+    mine0 = gate_up(0, spread(0))
+    crosses.append(move(after(pairs[2], mine0), second))
+    hidden1 = swap(gate_up(1, spread(1, mine0), mine0))
     pairs[3] = after(pairs[3], hidden1[0])
-    crosses.append(move(pairs[3], second))
+    crosses.append(move(after(pairs[3], hidden1[1]), second))
     hidden2 = swap(gate_up(2, spread(2, hidden1[0]), hidden1[0], pairs[3]))
-    part0 = give(down(0, hidden0, hidden2[0]))
-    part1 = down(1, hidden1, part0[0], crosses[3])
+    part1 = down(1, hidden1, hidden2[0], crosses[3])
     shards3 = spread(3, part1[0])
     part1 = give(part1)
     back1 = move(away(part1), over_y)
     hidden3 = swap(gate_up(3, shards3, part1[0]))
     part2 = give(down(2, hidden2, hidden3[0], back1), hidden3[1])
+    hidden0 = swap(mine0, hidden3[1])
     from_next = move(total(part1, after(back1, hidden3[0])), backward)
     back2 = move(away(part2), over_y)
-    part3 = give(down(3, hidden3, part2[0]), from_next, back2)
+    part3 = down(3, hidden3, part2[0])
+    part0 = give(down(0, hidden0, part3[0]))
+    part3 = give(part3, from_next, back2, part0[0])
     from_far = move(total(part2, back2), onward)
     back3 = move(away(part3), over_y)
     from_last = move(total(part3, back3, from_far), onward)

time: 198 us -> 186 us (0.939)
  starting transfers between devices: 53.9 us -> 27.5 us
  waiting for transfers between devices: 68.6 us -> 82.6 us
    ppermute x33, starting transfers between devices: 53.9 us -> 27.5 us  [move(): return lax.ppermute(value, axes, moves)]
    ppermute x33, waiting for transfers between devices: 68.6 us -> 82.6 us  [move(): return lax.ppermute(value, axes, moves)]
  transfers between devices with their start and end apart: 33 -> 33, of which waited for: 14 -> 20; matrix products, arithmetic and copies ran while one was open for 2% -> 2% of each run, Pallas kernels for 26% -> 28%
where the time goes in v11:
time: 186 us
  waiting for transfers between devices  82.6 us (44%)
  Pallas kernels  58.2 us (31%)
  starting transfers between devices  27.5 us (15%)
  blocking collectives  10.9 us (6%)
  other arithmetic  5.34 us (3%)
    ppermute x33, waiting for transfers between devices, move(): return lax.ppermute(value, axes, moves)  82.6 us
    pallas_call x4, Pallas kernels, pick_call(): pl.pallas_call(functools.partial(pick_kernel, capacity, k), in_specs=[pl....  33.7 us
    ppermute x33, starting transfers between devices, move(): return lax.ppermute(value, axes, moves)  27.5 us
    pallas_call x4, Pallas kernels, sum_call(): pl.pallas_call(functools.partial(sum_kernel, capacity, k), in_specs=[pl.B...  24.5 us
    all_to_all x1, blocking collectives, pair_shards(): lax.all_to_all(named, 'expert', split_axis=0, concat_axis=0, tiled=True)  10.9 us
  transfers between devices with their start and end apart: 33, of which 20 were waited for; matrix products, arithmetic and copies ran while one was open for 2% of the time, Pallas kernels for 28%

profile of v11, /device:TPU:0, one launch (start us, length us, event | category | flops | bytes accessed | tf_op | source)
XLA Modules:
  0.0 185.6 jit_solution(6956651103792161658)
XLA Ops:
  0.0 2.9 %collective-permute-start.1 = (bf16[128,2048]{1,0:T(8,128)(2,1)}, bf16[128,2048]{1,0:T(8,128)(2,1)S(1)}, u32[]{:S(2)}, u32[]{:S(2)}) collective-permute-start(bf16[128,2048]{1,0:T(8,128)(2,1)} %param.6), channel_id=1, source_target_pairs={{0,16},{1,3},{2,18},{3,1},{4,20},{5,7},{6,22},{7,5},{8,24},{9,11},... | collective-permute-start | bytes 1572872 | tf_op jit(solution)/shard_map/ppermute | solution.py:376
  4.5 5.8 %collective-permute-done.1 = bf16[128,2048]{1,0:T(8,128)(2,1)S(1)} collective-permute-done((bf16[128,2048]{1,0:T(8,128)(2,1)}, bf16[128,2048]{1,0:T(8,128)(2,1)S(1)}, u32[]{:S(2)}, u32[]{:S(2)}) %collective-permute-start.1) | collective-permute-done | bytes 524320 | tf_op jit(solution)/shard_map/ppermute | solution.py:376
  11.4 2.1 %collective-permute-start.2 = (bf16[2,128,2048]{2,1,0:T(8,128)(2,1)S(1)}, bf16[2,128,2048]{2,1,0:T(8,128)(2,1)}, u32[]{:S(2)}, u32[]{:S(2)}) collective-permute-start(bf16[2,128,2048]{2,1,0:T(8,128)(2,1)S(1)} %pad_maximum_fusion.refs_0_), channel_id=1, source_target_pairs={{0,2},{1,17},{2,0},{3,19},{4,6},{5,21},{6,4},{7,23},{8,10},{9,25},... | collective-permute-start | bytes 3145736 | tf_op jit(solution)/shard_map/ppermute | solution.py:376
  13.6 3.9 %collective-permute-done = bf16[128,2048]{1,0:T(8,128)(2,1)S(1)} collective-permute-done((bf16[128,2048]{1,0:T(8,128)(2,1)}, bf16[128,2048]{1,0:T(8,128)(2,1)S(1)}, u32[]{:S(2)}, u32[]{:S(2)}) %collective-permute-start) | collective-permute-done | bytes 524320 | tf_op jit(solution)/shard_map/ppermute | solution.py:376
  21.4 10.9 %all_to_all.11 = s32[16,1,128]{2,1,0:T(1,128)S(1)} all-to-all(s32[16,1,128]{2,1,0:T(1,128)S(1)} %bitcast.73), channel_id=1, replica_groups=mesh['section'=2,'expert'=16] {'expert'}, dimensions={0} | all-to-all | bytes 16384 | tf_op jit(solution)/shard_map/all_to_all | solution.py:392
  32.3 2.2 %collective-permute-start.7 = (bf16[128,2048]{1,0:T(8,128)(2,1)S(1)}, bf16[128,2048]{1,0:T(8,128)(2,1)S(1)}, u32[]{:S(2)}, u32[]{:S(2)}) collective-permute-start(bf16[128,2048]{1,0:T(8,128)(2,1)S(1)} %collective-permute-done.5), channel_id=1, source_target_pairs={{0,16},{1,3},{2,18},{3,1},{4,20},{5,7},{6,22},{7,5},{8,24},{9,11},... | collective-permute-start | bytes 1572872 | tf_op jit(solution)/shard_map/ppermute | solution.py:376
  35.1 6.5 %collective-permute-done.7 = bf16[128,2048]{1,0:T(8,128)(2,1)S(1)} collective-permute-done((bf16[128,2048]{1,0:T(8,128)(2,1)S(1)}, bf16[128,2048]{1,0:T(8,128)(2,1)S(1)}, u32[]{:S(2)}, u32[]{:S(2)}) %collective-permute-start.7) | collective-permute-done | bytes 524320 | tf_op jit(solution)/shard_map/ppermute | solution.py:376
  44.3 8.9 %gate_up.4.refs_5_.refs_0_ = bf16[320,768]{1,0:T(8,128)(2,1)S(1)} custom-call(s32[4,6]{1,0:T(4,128)S(1)} %dynamic-slice_bitcast_fusion.where_ref, s32[16,128]{1,0:T(8,128)S(1)} %bitcast.53, bf16[2,128,2048]{2,1,0:T(8,128)(2,1)S(1)} %pad_maximum_fusion.refs_0_, bf16[2,128,2048]{2,1,0:T(8,128)(2,1)} %collective-permute-done.2.refs_1_, ...), custom_call_target="tpu_custom_call" | custom-call | flops 4362076160 | bytes 17268736 | tf_op jit(solution)/shard_map/gate_up/pallas_call | solution.py:257
  53.2 3.6 %collective-permute-done.9.refs_1_ = bf16[2,128,2048]{2,1,0:T(8,128)(2,1)} collective-permute-done((bf16[2,128,2048]{2,1,0:T(8,128)(2,1)S(1)}, bf16[2,128,2048]{2,1,0:T(8,128)(2,1)}, u32[]{:S(2)}, u32[]{:S(2)}) %collective-permute-start.9) | collective-permute-done | bytes 1048608 | tf_op jit(solution)/shard_map/ppermute | solution.py:376
  60.1 8.6 %gate_up.5.refs_5_.refs_0_ = bf16[320,768]{1,0:T(8,128)(2,1)S(1)} custom-call(s32[4,6]{1,0:T(4,128)S(1)} %dynamic-slice_bitcast_fusion.where_ref, s32[16,128]{1,0:T(8,128)S(1)} %bitcast.54, bf16[2,128,2048]{2,1,0:T(8,128)(2,1)S(1)} %pad_maximum_fusion.2.refs_0_, bf16[2,128,2048]{2,1,0:T(8,128)(2,1)} %collective-permute-done.9.refs_1_, ...), custom_call_target="tpu_custom_call" | custom-call | flops 4362076160 | bytes 17268736 | tf_op jit(solution)/shard_map/gate_up/pallas_call | solution.py:257
  71.6 13.4 %collective-permute-done.8.refs_6_.refs_0_ = bf16[2,128,2048]{2,1,0:T(8,128)(2,1)S(1)} collective-permute-done((bf16[2,128,2048]{2,1,0:T(8,128)(2,1)S(1)}, bf16[2,128,2048]{2,1,0:T(8,128)(2,1)S(1)}, u32[]{:S(2)}, u32[]{:S(2)}) %collective-permute-start.8) | collective-permute-done | bytes 1048608 | tf_op jit(solution)/shard_map/ppermute | solution.py:376
  85.1 8.1 %gate_up.6.refs_3_.refs_0_ = bf16[320,768]{1,0:T(8,128)(2,1)S(1)} custom-call(s32[4,6]{1,0:T(4,128)S(1)} %dynamic-slice_bitcast_fusion.where_ref, s32[16,128]{1,0:T(8,128)S(1)} %bitcast.55, bf16[2,128,2048]{2,1,0:T(8,128)(2,1)S(1)} %pad_maximum_fusion.1.refs_0_, bf16[2,128,2048]{2,1,0:T(8,128)(2,1)S(1)} %collective-permute-done.15.refs_1_, ...), custom_call_target="tpu_custom_call" | custom-call | flops 4362076160 | bytes 17268736 | tf_op jit(solution)/shard_map/gate_up/pallas_call | solution.py:257
  93.2 6.6 %collective-permute-done.13.refs_4_.refs_1_ = bf16[2,128,2048]{2,1,0:T(8,128)(2,1)S(1)} collective-permute-done((bf16[2,128,2048]{2,1,0:T(8,128)(2,1)S(1)}, bf16[2,128,2048]{2,1,0:T(8,128)(2,1)S(1)}, u32[]{:S(2)}, u32[]{:S(2)}) %collective-permute-start.13) | collective-permute-done | bytes 1048608 | tf_op jit(solution)/shard_map/ppermute | solution.py:376
  99.8 6.1 %down.4 = (bf16[2,128,2048]{2,1,0:T(8,128)(2,1)S(1)}, bf16[2,128,2048]{2,1,0:T(8,128)(2,1)S(1)}) custom-call(s32[4,6]{1,0:T(4,128)S(1)} %dynamic-slice_bitcast_fusion.where_ref, s32[16,128]{1,0:T(8,128)S(1)} %bitcast.56, bf16[320,768]{1,0:T(8,128)(2,1)S(1)} %gate_up.5.refs_5_.refs_0_, bf16[320,768]{1,0:T(8,128)(2,1)S(1)} %collective-permute-done.12.refs_1_, ...), custom_call_target="tpu_custom_call" | custom-call | flops 2181038080 | bytes 9371648 | tf_op jit(solution)/shard_map/down/pallas_call | solution.py:287
  111.6 8.1 %gate_up.7.refs_3_.refs_0_ = bf16[320,768]{1,0:T(8,128)(2,1)S(1)} custom-call(s32[4,6]{1,0:T(4,128)S(1)} %dynamic-slice_bitcast_fusion.where_ref, s32[16,128]{1,0:T(8,128)S(1)} %bitcast.57, bf16[2,128,2048]{2,1,0:T(8,128)(2,1)S(1)} %collective-permute-done.8.refs_6_.refs_0_, bf16[2,128,2048]{2,1,0:T(8,128)(2,1)S(1)} %collective-permute-done.13.refs_4_.refs_1_, ...), custom_call_target="tpu_custom_call" | custom-call | flops 4362076160 | bytes 17268736 | tf_op jit(solution)/shard_map/gate_up/pallas_call | solution.py:257
  120.1 2.7 %collective-permute-done.23.refs_4_ = bf16[128,2048]{1,0:T(8,128)(2,1)S(1)} collective-permute-done((bf16[128,2048]{1,0:T(8,128)(2,1)S(1)}, bf16[128,2048]{1,0:T(8,128)(2,1)S(1)}, u32[]{:S(2)}, u32[]{:S(2)}) %collective-permute-start.23) | collective-permute-done | bytes 524320 | tf_op jit(solution)/shard_map/ppermute | solution.py:376
  122.8 6.1 %down.5 = (bf16[2,128,2048]{2,1,0:T(8,128)(2,1)S(1)}, bf16[2,128,2048]{2,1,0:T(8,128)(2,1)S(1)}) custom-call(s32[4,6]{1,0:T(4,128)S(1)} %dynamic-slice_bitcast_fusion.where_ref, s32[16,128]{1,0:T(8,128)S(1)} %bitcast.58, bf16[320,768]{1,0:T(8,128)(2,1)S(1)} %gate_up.6.refs_3_.refs_0_, bf16[320,768]{1,0:T(8,128)(2,1)S(1)} %collective-permute-done.21.refs_1_, ...), custom_call_target="tpu_custom_call" | custom-call | flops 2181038080 | bytes 9371648 | tf_op jit(solution)/shard_map/down/pallas_call | solution.py:287
  128.9 4.2 %collective-permute-done.19.refs_1_ = bf16[320,768]{1,0:T(8,128)(2,1)S(1)} collective-permute-done((bf16[320,768]{1,0:T(8,128)(2,1)S(1)}, bf16[320,768]{1,0:T(8,128)(2,1)S(1)}, u32[]{:S(2)}, u32[]{:S(2)}) %collective-permute-start.19) | collective-permute-done | bytes 491552 | tf_op jit(solution)/shard_map/ppermute | solution.py:376
  133.7 1.9 %collective-permute-start.25 = (bf16[128,2048]{1,0:T(8,128)(2,1)S(1)}, bf16[128,2048]{1,0:T(8,128)(2,1)S(1)}, u32[]{:S(2)}, u32[]{:S(2)}) collective-permute-start(bf16[128,2048]{1,0:T(8,128)(2,1)S(1)} %fusion.6), channel_id=1, source_target_pairs={{4,0},{5,1},{6,2},{7,3},{12,4},{13,5},{14,6},{15,7},{0,8},{1,9},{2... | collective-permute-start | bytes 1572872 | tf_op jit(solution)/shard_map/ppermute | solution.py:376
  137.3 6.1 %down.6 = (bf16[2,128,2048]{2,1,0:T(8,128)(2,1)S(1)}, bf16[2,128,2048]{2,1,0:T(8,128)(2,1)S(1)}) custom-call(s32[4,6]{1,0:T(4,128)S(1)} %dynamic-slice_bitcast_fusion.where_ref, s32[16,128]{1,0:T(8,128)S(1)} %bitcast.59, bf16[320,768]{1,0:T(8,128)(2,1)S(1)} %gate_up.7.refs_3_.refs_0_, bf16[320,768]{1,0:T(8,128)(2,1)S(1)} %collective-permute-done.19.refs_1_, ...), custom_call_target="tpu_custom_call" | custom-call | flops 2181038080 | bytes 9371648 | tf_op jit(solution)/shard_map/down/pallas_call | solution.py:287
  143.4 3.3 %collective-permute-done.20.refs_1_ = bf16[320,768]{1,0:T(8,128)(2,1)S(1)} collective-permute-done((bf16[320,768]{1,0:T(8,128)(2,1)S(1)}, bf16[320,768]{1,0:T(8,128)(2,1)S(1)}, u32[]{:S(2)}, u32[]{:S(2)}) %collective-permute-start.20) | collective-permute-done | bytes 491552 | tf_op jit(solution)/shard_map/ppermute | solution.py:376
  146.8 6.1 %down.7 = (bf16[2,128,2048]{2,1,0:T(8,128)(2,1)S(1)}, bf16[2,128,2048]{2,1,0:T(8,128)(2,1)S(1)}) custom-call(s32[4,6]{1,0:T(4,128)S(1)} %dynamic-slice_bitcast_fusion.where_ref, s32[16,128]{1,0:T(8,128)S(1)} %bitcast.60, bf16[320,768]{1,0:T(8,128)(2,1)S(1)} %gate_up.4.refs_5_.refs_0_, bf16[320,768]{1,0:T(8,128)(2,1)S(1)} %collective-permute-done.20.refs_1_, ...), custom_call_target="tpu_custom_call" | custom-call | flops 2181038080 | bytes 9371648 | tf_op jit(solution)/shard_map/down/pallas_call | solution.py:287
  157.3 11.4 %collective-permute-done.31 = bf16[128,2048]{1,0:T(8,128)(2,1)S(1)} collective-permute-done((bf16[128,2048]{1,0:T(8,128)(2,1)S(1)}, bf16[128,2048]{1,0:T(8,128)(2,1)S(1)}, u32[]{:S(2)}, u32[]{:S(2)}) %collective-permute-start.31) | collective-permute-done | bytes 524320 | tf_op jit(solution)/shard_map/ppermute | solution.py:376
  172.9 11.3 %collective-permute-done.32 = bf16[128,2048]{1,0:T(8,128)(2,1)S(1)} collective-permute-done((bf16[128,2048]{1,0:T(8,128)(2,1)S(1)}, bf16[128,2048]{1,0:T(8,128)(2,1)S(1)}, u32[]{:S(2)}, u32[]{:S(2)}) %collective-permute-start.32) | collective-permute-done | bytes 524320 | tf_op jit(solution)/shard_map/ppermute | solution.py:376
  (71 shorter events, 34.4 us)
Async XLA Ops:
  0.0 10.3 %collective-permute-start.1 = (bf16[128,2048]{1,0:T(8,128)(2,1)}, bf16[128,2048]{1,0:T(8,128)(2,1)S(1)}, u32[]{:S(2)}, u32[]{:S(2)}) collective-permute-start(bf16[128,2048]{1,0:T(8,128)(2,1)} %param.6), channel_id=1, source_target_pairs={{0,16},{1,3},{2,18},{3,1},{4,20},{5,7},{6,22},{7,5},{8,24},{9,11},... | collective-permute-start | bytes 1572872 | tf_op jit(solution)/shard_map/ppermute | solution.py:376
  2.9 14.5 %collective-permute-start = (bf16[128,2048]{1,0:T(8,128)(2,1)}, bf16[128,2048]{1,0:T(8,128)(2,1)S(1)}, u32[]{:S(2)}, u32[]{:S(2)}) collective-permute-start(bf16[128,2048]{1,0:T(8,128)(2,1)} %param.6), channel_id=1, source_target_pairs={{0,4},{1,5},{2,6},{3,7},{4,12},{5,13},{6,14},{7,15},{8,0},{9,1},{1... | collective-permute-start | bytes 1572872 | tf_op jit(solution)/shard_map/ppermute | solution.py:376
  11.4 20.8 %collective-permute-start.2 = (bf16[2,128,2048]{2,1,0:T(8,128)(2,1)S(1)}, bf16[2,128,2048]{2,1,0:T(8,128)(2,1)}, u32[]{:S(2)}, u32[]{:S(2)}) collective-permute-start(bf16[2,128,2048]{2,1,0:T(8,128)(2,1)S(1)} %pad_maximum_fusion.refs_0_), channel_id=1, source_target_pairs={{0,2},{1,17},{2,0},{3,19},{4,6},{5,21},{6,4},{7,23},{8,10},{9,25},... | collective-permute-start | bytes 3145736 | tf_op jit(solution)/shard_map/ppermute | solution.py:376
  17.5 14.8 %collective-permute-start.5 = (bf16[128,2048]{1,0:T(8,128)(2,1)S(1)}, bf16[128,2048]{1,0:T(8,128)(2,1)S(1)}, u32[]{:S(2)}, u32[]{:S(2)}) collective-permute-start(bf16[128,2048]{1,0:T(8,128)(2,1)S(1)} %collective-permute-done), channel_id=1, source_target_pairs={{0,4},{1,5},{2,6},{3,7},{4,12},{5,13},{6,14},{7,15},{8,0},{9,1},{1... | collective-permute-start | bytes 1572872 | tf_op jit(solution)/shard_map/ppermute | solution.py:376
  18.4 13.9 %collective-permute-start.6 = (bf16[128,2048]{1,0:T(8,128)(2,1)S(1)}, bf16[128,2048]{1,0:T(8,128)(2,1)S(1)}, u32[]{:S(2)}, u32[]{:S(2)}) collective-permute-start(bf16[128,2048]{1,0:T(8,128)(2,1)S(1)} %collective-permute-done), channel_id=1, source_target_pairs={{0,16},{1,3},{2,18},{3,1},{4,20},{5,7},{6,22},{7,5},{8,24},{9,11},... | collective-permute-start | bytes 1572872 | tf_op jit(solution)/shard_map/ppermute | solution.py:376
  34.5 9.8 %collective-permute-start.3 = (bf16[2,128,2048]{2,1,0:T(8,128)(2,1)S(1)}, bf16[2,128,2048]{2,1,0:T(8,128)(2,1)}, u32[]{:S(2)}, u32[]{:S(2)}) collective-permute-start(bf16[2,128,2048]{2,1,0:T(8,128)(2,1)S(1)} %pad_maximum_fusion.refs_0_), channel_id=1, source_target_pairs={{0,1},{1,0},{2,3},{3,2},{4,5},{5,4},{6,7},{7,6},{8,9},{9,8},{10,11... | collective-permute-start | bytes 3145736 | tf_op jit(solution)/shard_map/ppermute | solution.py:376
  41.8 15.0 %collective-permute-start.9 = (bf16[2,128,2048]{2,1,0:T(8,128)(2,1)S(1)}, bf16[2,128,2048]{2,1,0:T(8,128)(2,1)}, u32[]{:S(2)}, u32[]{:S(2)}) collective-permute-start(bf16[2,128,2048]{2,1,0:T(8,128)(2,1)S(1)} %pad_maximum_fusion.2.refs_0_), channel_id=1, source_target_pairs={{0,2},{1,17},{2,0},{3,19},{4,6},{5,21},{6,4},{7,23},{8,10},{9,25},... | collective-permute-start | bytes 3145736 | tf_op jit(solution)/shard_map/ppermute | solution.py:376
  44.3 15.8 %collective-permute-start.10 = (bf16[2,128,2048]{2,1,0:T(8,128)(2,1)S(1)}, bf16[2,128,2048]{2,1,0:T(8,128)(2,1)S(1)}, u32[]{:S(2)}, u32[]{:S(2)}) collective-permute-start(bf16[2,128,2048]{2,1,0:T(8,128)(2,1)S(1)} %pad_maximum_fusion.2.refs_0_), channel_id=1, source_target_pairs={{0,1},{1,0},{2,3},{3,2},{4,5},{5,4},{6,7},{7,6},{8,9},{9,8},{10,11... | collective-permute-start | bytes 3145736 | tf_op jit(solution)/shard_map/ppermute | solution.py:376
  56.8 14.8 %collective-permute-start.15 = (bf16[2,128,2048]{2,1,0:T(8,128)(2,1)S(1)}, bf16[2,128,2048]{2,1,0:T(8,128)(2,1)S(1)}, u32[]{:S(2)}, u32[]{:S(2)}) collective-permute-start(bf16[2,128,2048]{2,1,0:T(8,128)(2,1)S(1)} %pad_maximum_fusion.1.refs_0_), channel_id=1, source_target_pairs={{0,2},{1,17},{2,0},{3,19},{4,6},{5,21},{6,4},{7,23},{8,10},{9,25},... | collective-permute-start | bytes 3145736 | tf_op jit(solution)/shard_map/ppermute | solution.py:376
  58.5 26.5 %collective-permute-start.8 = (bf16[2,128,2048]{2,1,0:T(8,128)(2,1)S(1)}, bf16[2,128,2048]{2,1,0:T(8,128)(2,1)S(1)}, u32[]{:S(2)}, u32[]{:S(2)}) collective-permute-start(bf16[2,128,2048]{2,1,0:T(8,128)(2,1)S(1)} %pad_maximum_fusion.1.refs_0_), channel_id=1, source_target_pairs={{0,4},{1,5},{2,6},{3,7},{4,12},{5,13},{6,14},{7,15},{8,0},{9,1},{1... | collective-permute-start | bytes 3145736 | tf_op jit(solution)/shard_map/ppermute | solution.py:376
  68.7 16.3 %collective-permute-start.12 = (bf16[320,768]{1,0:T(8,128)(2,1)S(1)}, bf16[320,768]{1,0:T(8,128)(2,1)S(1)}, u32[]{:S(2)}, u32[]{:S(2)}) collective-permute-start(bf16[320,768]{1,0:T(8,128)(2,1)S(1)} %gate_up.5.refs_5_.refs_0_), channel_id=1, source_target_pairs={{0,16},{1,17},{2,18},{3,19},{4,20},{5,21},{6,22},{7,23},{8,24},{9,... | collective-permute-start | bytes 1474568 | tf_op jit(solution)/shard_map/ppermute | solution.py:376
  70.3 14.8 %collective-permute-start.16 = (bf16[2,128,2048]{2,1,0:T(8,128)(2,1)S(1)}, bf16[2,128,2048]{2,1,0:T(8,128)(2,1)S(1)}, u32[]{:S(2)}, u32[]{:S(2)}) collective-permute-start(bf16[2,128,2048]{2,1,0:T(8,128)(2,1)S(1)} %pad_maximum_fusion.1.refs_0_), channel_id=1, source_target_pairs={{0,1},{1,0},{2,3},{3,2},{4,5},{5,4},{6,7},{7,6},{8,9},{9,8},{10,11... | collective-permute-start | bytes 3145736 | tf_op jit(solution)/shard_map/ppermute | solution.py:376
  71.6 13.5 %collective-permute-start.17 = (bf16[2,128,2048]{2,1,0:T(8,128)(2,1)S(1)}, bf16[2,128,2048]{2,1,0:T(8,128)(2,1)S(1)}, u32[]{:S(2)}, u32[]{:S(2)}) collective-permute-start(bf16[2,128,2048]{2,1,0:T(8,128)(2,1)S(1)} %collective-permute-done.15.refs_1_), channel_id=1, source_target_pairs={{0,1},{1,0},{2,3},{3,2},{4,5},{5,4},{6,7},{7,6},{8,9},{9,8},{10,11... | collective-permute-start | bytes 3145736 | tf_op jit(solution)/shard_map/ppermute | solution.py:376
  85.0 14.8 %collective-permute-start.13 = (bf16[2,128,2048]{2,1,0:T(8,128)(2,1)S(1)}, bf16[2,128,2048]{2,1,0:T(8,128)(2,1)S(1)}, u32[]{:S(2)}, u32[]{:S(2)}) collective-permute-start(bf16[2,128,2048]{2,1,0:T(8,128)(2,1)S(1)} %collective-permute-done.8.refs_6_.refs_0_), channel_id=1, source_target_pairs={{0,2},{1,17},{2,0},{3,19},{4,6},{5,21},{6,4},{7,23},{8,10},{9,25},... | collective-permute-start | bytes 3145736 | tf_op jit(solution)/shard_map/ppermute | solution.py:376
  106.6 13.6 %collective-permute-start.21 = (bf16[320,768]{1,0:T(8,128)(2,1)S(1)}, bf16[320,768]{1,0:T(8,128)(2,1)S(1)}, u32[]{:S(2)}, u32[]{:S(2)}) collective-permute-start(bf16[320,768]{1,0:T(8,128)(2,1)S(1)} %gate_up.6.refs_3_.refs_0_), channel_id=1, source_target_pairs={{0,16},{1,17},{2,18},{3,19},{4,20},{5,21},{6,22},{7,23},{8,24},{9,... | collective-permute-start | bytes 1474568 | tf_op jit(solution)/shard_map/ppermute | solution.py:376
  108.8 14.0 %collective-permute-start.23 = (bf16[128,2048]{1,0:T(8,128)(2,1)S(1)}, bf16[128,2048]{1,0:T(8,128)(2,1)S(1)}, u32[]{:S(2)}, u32[]{:S(2)}) collective-permute-start(bf16[128,2048]{1,0:T(8,128)(2,1)S(1)} %fusion.10), channel_id=1, source_target_pairs={{0,2},{1,3},{2,0},{3,1},{4,6},{5,7},{6,4},{7,5},{8,10},{9,11},{10,... | collective-permute-start | bytes 1572872 | tf_op jit(solution)/shard_map/ppermute | solution.py:376
  119.8 13.3 %collective-permute-start.19 = (bf16[320,768]{1,0:T(8,128)(2,1)S(1)}, bf16[320,768]{1,0:T(8,128)(2,1)S(1)}, u32[]{:S(2)}, u32[]{:S(2)}) collective-permute-start(bf16[320,768]{1,0:T(8,128)(2,1)S(1)} %gate_up.7.refs_3_.refs_0_), channel_id=1, source_target_pairs={{0,16},{1,17},{2,18},{3,19},{4,20},{5,21},{6,22},{7,23},{8,24},{9,... | collective-permute-start | bytes 1474568 | tf_op jit(solution)/shard_map/ppermute | solution.py:376
  133.1 13.6 %collective-permute-start.20 = (bf16[320,768]{1,0:T(8,128)(2,1)S(1)}, bf16[320,768]{1,0:T(8,128)(2,1)S(1)}, u32[]{:S(2)}, u32[]{:S(2)}) collective-permute-start(bf16[320,768]{1,0:T(8,128)(2,1)S(1)} %gate_up.4.refs_5_.refs_0_), channel_id=1, source_target_pairs={{0,16},{1,17},{2,18},{3,19},{4,20},{5,21},{6,22},{7,23},{8,24},{9,... | collective-permute-start | bytes 1474568 | tf_op jit(solution)/shard_map/ppermute | solution.py:376
  133.7 19.2 %collective-permute-start.25 = (bf16[128,2048]{1,0:T(8,128)(2,1)S(1)}, bf16[128,2048]{1,0:T(8,128)(2,1)S(1)}, u32[]{:S(2)}, u32[]{:S(2)}) collective-permute-start(bf16[128,2048]{1,0:T(8,128)(2,1)S(1)} %fusion.6), channel_id=1, source_target_pairs={{4,0},{5,1},{6,2},{7,3},{12,4},{13,5},{14,6},{15,7},{0,8},{1,9},{2... | collective-permute-start | bytes 1572872 | tf_op jit(solution)/shard_map/ppermute | solution.py:376
  135.9 17.0 %collective-permute-start.27 = (bf16[128,2048]{1,0:T(8,128)(2,1)S(1)}, bf16[128,2048]{1,0:T(8,128)(2,1)S(1)}, u32[]{:S(2)}, u32[]{:S(2)}) collective-permute-start(bf16[128,2048]{1,0:T(8,128)(2,1)S(1)} %fusion.12), channel_id=1, source_target_pairs={{0,2},{1,3},{2,0},{3,1},{4,6},{5,7},{6,4},{7,5},{8,10},{9,11},{10,... | collective-permute-start | bytes 1572872 | tf_op jit(solution)/shard_map/ppermute | solution.py:376
  153.7 14.9 %collective-permute-start.31 = (bf16[128,2048]{1,0:T(8,128)(2,1)S(1)}, bf16[128,2048]{1,0:T(8,128)(2,1)S(1)}, u32[]{:S(2)}, u32[]{:S(2)}) collective-permute-start(bf16[128,2048]{1,0:T(8,128)(2,1)S(1)} %fusion.3), channel_id=1, source_target_pairs={{0,4},{1,5},{2,6},{3,7},{4,12},{5,13},{6,14},{7,15},{8,0},{9,1},{1... | collective-permute-start | bytes 1572872 | tf_op jit(solution)/shard_map/ppermute | solution.py:376
  155.8 14.0 %collective-permute-start.29 = (bf16[128,2048]{1,0:T(8,128)(2,1)S(1)}, bf16[128,2048]{1,0:T(8,128)(2,1)S(1)}, u32[]{:S(2)}, u32[]{:S(2)}) collective-permute-start(bf16[128,2048]{1,0:T(8,128)(2,1)S(1)} %fusion.13), channel_id=1, source_target_pairs={{0,2},{1,3},{2,0},{3,1},{4,6},{5,7},{6,4},{7,5},{8,10},{9,11},{10,... | collective-permute-start | bytes 1572872 | tf_op jit(solution)/shard_map/ppermute | solution.py:376
  170.1 14.1 %collective-permute-start.32 = (bf16[128,2048]{1,0:T(8,128)(2,1)S(1)}, bf16[128,2048]{1,0:T(8,128)(2,1)S(1)}, u32[]{:S(2)}, u32[]{:S(2)}) collective-permute-start(bf16[128,2048]{1,0:T(8,128)(2,1)S(1)} %fusion.5), channel_id=1, source_target_pairs={{0,4},{1,5},{2,6},{3,7},{4,12},{5,13},{6,14},{7,15},{8,0},{9,1},{1... | collective-permute-start | bytes 1572872 | tf_op jit(solution)/shard_map/ppermute | solution.py:376
  171.9 12.5 %collective-permute-start.30 = (bf16[128,2048]{1,0:T(8,128)(2,1)S(1)}, bf16[128,2048]{1,0:T(8,128)(2,1)S(1)}, u32[]{:S(2)}, u32[]{:S(2)}) collective-permute-start(bf16[128,2048]{1,0:T(8,128)(2,1)S(1)} %fusion.11), channel_id=1, source_target_pairs={{0,2},{1,3},{2,0},{3,1},{4,6},{5,7},{6,4},{7,5},{8,10},{9,11},{10,... | collective-permute-start | bytes 1572872 | tf_op jit(solution)/shard_map/ppermute | solution.py:376
  (11 other events, 114.8 us)

commit v12 on v11

--- a/solution.py
+++ b/solution.py
@@ -394,8 +394,9 @@
     crosses = [move(pairs[0], second)]
     near_last = move(after(last, near_later, crosses[0], code), first)
     pairs.append(jnp.stack([last, near_last]))
-    pairs.append(move(pairs[2], onward))
-    crosses.append(move(after(pairs[1], pairs[2]), second))
+    third = move(last, onward)
+    pairs.append(jnp.stack([third, move(near_last, onward)]))
+    crosses.append(move(after(pairs[1], pairs[2], third), second))
 
     def spread(k, *done):
         return [pairs[k], crosses[k], move(pairs[k], sibling), move(after(crosses[k], *done), sibling)]
@@ -427,11 +428,11 @@
     crosses.append(move(after(pairs[3], hidden1[1]), second))
     hidden2 = swap(gate_up(2, spread(2, hidden1[0]), hidden1[0], pairs[3]))
     part1 = down(1, hidden1, hidden2[0], crosses[3])
-    shards3 = spread(3, part1[0])
+    shards3 = spread(3, hidden2[0])
     part1 = give(part1)
     back1 = move(away(part1), over_y)
     hidden3 = swap(gate_up(3, shards3, part1[0]))
-    part2 = give(down(2, hidden2, hidden3[0], back1), hidden3[1])
+    part2 = give(down(2, hidden2, hidden3[0]), hidden3[1], back1)
     hidden0 = swap(mine0, hidden3[1])
     from_next = move(total(part1, after(back1, hidden3[0])), backward)
     back2 = move(away(part2), over_y)

time: 186 us -> 190 us (1.022)
  starting transfers between devices: 27.5 us -> 31.9 us
    ppermute x33 -> x34, starting transfers between devices: 27.5 us -> 31.9 us  [move(): return lax.ppermute(value, axes, moves)]
    ppermute x33 -> x34, waiting for transfers between devices: 82.6 us -> 81.2 us  [move(): return lax.ppermute(value, axes, moves)]
  transfers between devices with their start and end apart: 33 -> 34, of which waited for: 20 -> 20; matrix products, arithmetic and copies ran while one was open for 2% -> 3% of each run, Pallas kernels for 28% -> 27%
where the time goes in v12:
time: 190 us
  waiting for transfers between devices  81.2 us (43%)
  Pallas kernels  57.9 us (30%)
  starting transfers between devices  31.9 us (17%)
  blocking collectives  10.9 us (6%)
  other arithmetic  6.45 us (3%)
    ppermute x34, waiting for transfers between devices, move(): return lax.ppermute(value, axes, moves)  81.2 us
    pallas_call x4, Pallas kernels, pick_call(): pl.pallas_call(functools.partial(pick_kernel, capacity, k), in_specs=[pl....  33.5 us
    ppermute x34, starting transfers between devices, move(): return lax.ppermute(value, axes, moves)  31.9 us
    pallas_call x4, Pallas kernels, sum_call(): pl.pallas_call(functools.partial(sum_kernel, capacity, k), in_specs=[pl.B...  24.5 us
    all_to_all x1, blocking collectives, pair_shards(): lax.all_to_all(named, 'expert', split_axis=0, concat_axis=0, tiled=True)  10.9 us
  transfers between devices with their start and end apart: 34, of which 20 were waited for; matrix products, arithmetic and copies ran while one was open for 3% of the time, Pallas kernels for 27%

profile of v12, /device:TPU:0, one launch (start us, length us, event | category | flops | bytes accessed | tf_op | source)
XLA Modules:
  0.0 190.1 jit_solution(6384168328767757745)
XLA Ops:
  0.0 2.9 %collective-permute-start.1 = (bf16[128,2048]{1,0:T(8,128)(2,1)}, bf16[128,2048]{1,0:T(8,128)(2,1)S(1)}, u32[]{:S(2)}, u32[]{:S(2)}) collective-permute-start(bf16[128,2048]{1,0:T(8,128)(2,1)} %param.6), channel_id=1, source_target_pairs={{0,16},{1,3},{2,18},{3,1},{4,20},{5,7},{6,22},{7,5},{8,24},{9,11},... | collective-permute-start | bytes 1572872 | tf_op jit(solution)/shard_map/ppermute | solution.py:376
  4.5 5.8 %collective-permute-done.1 = bf16[128,2048]{1,0:T(8,128)(2,1)S(1)} collective-permute-done((bf16[128,2048]{1,0:T(8,128)(2,1)}, bf16[128,2048]{1,0:T(8,128)(2,1)S(1)}, u32[]{:S(2)}, u32[]{:S(2)}) %collective-permute-start.1) | collective-permute-done | bytes 524320 | tf_op jit(solution)/shard_map/ppermute | solution.py:376
  13.6 3.9 %collective-permute-done = bf16[128,2048]{1,0:T(8,128)(2,1)S(1)} collective-permute-done((bf16[128,2048]{1,0:T(8,128)(2,1)}, bf16[128,2048]{1,0:T(8,128)(2,1)S(1)}, u32[]{:S(2)}, u32[]{:S(2)}) %collective-permute-start) | collective-permute-done | bytes 524320 | tf_op jit(solution)/shard_map/ppermute | solution.py:376
  21.4 10.9 %all_to_all.11 = s32[16,1,128]{2,1,0:T(1,128)S(1)} all-to-all(s32[16,1,128]{2,1,0:T(1,128)S(1)} %bitcast.76), channel_id=1, replica_groups=mesh['section'=2,'expert'=16] {'expert'}, dimensions={0} | all-to-all | bytes 16384 | tf_op jit(solution)/shard_map/all_to_all | solution.py:392
  32.3 2.2 %collective-permute-start.8 = (bf16[128,2048]{1,0:T(8,128)(2,1)S(1)}, bf16[128,2048]{1,0:T(8,128)(2,1)S(1)}, u32[]{:S(2)}, u32[]{:S(2)}) collective-permute-start(bf16[128,2048]{1,0:T(8,128)(2,1)S(1)} %collective-permute-done.5), channel_id=1, source_target_pairs={{0,16},{1,3},{2,18},{3,1},{4,20},{5,7},{6,22},{7,5},{8,24},{9,11},... | collective-permute-start | bytes 1572872 | tf_op jit(solution)/shard_map/ppermute | solution.py:376
  36.3 5.4 %collective-permute-done.8 = bf16[128,2048]{1,0:T(8,128)(2,1)S(1)} collective-permute-done((bf16[128,2048]{1,0:T(8,128)(2,1)S(1)}, bf16[128,2048]{1,0:T(8,128)(2,1)S(1)}, u32[]{:S(2)}, u32[]{:S(2)}) %collective-permute-start.8) | collective-permute-done | bytes 524320 | tf_op jit(solution)/shard_map/ppermute | solution.py:376
  42.5 6.4 %collective-permute-done.6 = bf16[128,2048]{1,0:T(8,128)(2,1)} collective-permute-done((bf16[128,2048]{1,0:T(8,128)(2,1)S(1)}, bf16[128,2048]{1,0:T(8,128)(2,1)}, u32[]{:S(2)}, u32[]{:S(2)}) %collective-permute-start.6) | collective-permute-done | bytes 524320 | tf_op jit(solution)/shard_map/ppermute | solution.py:376
  51.0 8.9 %gate_up.4.refs_5_.refs_0_ = bf16[320,768]{1,0:T(8,128)(2,1)S(1)} custom-call(s32[4,6]{1,0:T(4,128)S(1)} %dynamic-slice_bitcast_fusion.where_ref, s32[16,128]{1,0:T(8,128)S(1)} %bitcast.55, bf16[2,128,2048]{2,1,0:T(8,128)(2,1)S(1)} %pad_maximum_fusion.refs_0_, bf16[2,128,2048]{2,1,0:T(8,128)(2,1)} %collective-permute-done.2.refs_1_, ...), custom_call_target="tpu_custom_call" | custom-call | flops 4362076160 | bytes 17268736 | tf_op jit(solution)/shard_map/gate_up/pallas_call | solution.py:257
  59.9 3.9 %collective-permute-done.10.refs_1_ = bf16[2,128,2048]{2,1,0:T(8,128)(2,1)} collective-permute-done((bf16[2,128,2048]{2,1,0:T(8,128)(2,1)S(1)}, bf16[2,128,2048]{2,1,0:T(8,128)(2,1)}, u32[]{:S(2)}, u32[]{:S(2)}) %collective-permute-start.10) | collective-permute-done | bytes 1048608 | tf_op jit(solution)/shard_map/ppermute | solution.py:376
  66.7 8.3 %gate_up.5.refs_5_.refs_0_ = bf16[320,768]{1,0:T(8,128)(2,1)S(1)} custom-call(s32[4,6]{1,0:T(4,128)S(1)} %dynamic-slice_bitcast_fusion.where_ref, s32[16,128]{1,0:T(8,128)S(1)} %bitcast.56, bf16[2,128,2048]{2,1,0:T(8,128)(2,1)S(1)} %pad_maximum_fusion.2.refs_0_, bf16[2,128,2048]{2,1,0:T(8,128)(2,1)} %collective-permute-done.10.refs_1_, ...), custom_call_target="tpu_custom_call" | custom-call | flops 4362076160 | bytes 17268736 | tf_op jit(solution)/shard_map/gate_up/pallas_call | solution.py:257
  80.8 7.8 %collective-permute-done.13.refs_1_ = bf16[320,768]{1,0:T(8,128)(2,1)S(1)} collective-permute-done((bf16[320,768]{1,0:T(8,128)(2,1)S(1)}, bf16[320,768]{1,0:T(8,128)(2,1)S(1)}, u32[]{:S(2)}, u32[]{:S(2)}) %collective-permute-start.13) | collective-permute-done | bytes 491552 | tf_op jit(solution)/shard_map/ppermute | solution.py:376
  89.1 8.2 %gate_up.6.refs_3_.refs_0_ = bf16[320,768]{1,0:T(8,128)(2,1)S(1)} custom-call(s32[4,6]{1,0:T(4,128)S(1)} %dynamic-slice_bitcast_fusion.where_ref, s32[16,128]{1,0:T(8,128)S(1)} %bitcast.57, bf16[2,128,2048]{2,1,0:T(8,128)(2,1)S(1)} %pad_maximum_fusion.3.refs_0_, bf16[2,128,2048]{2,1,0:T(8,128)(2,1)S(1)} %collective-permute-done.16.refs_1_, ...), custom_call_target="tpu_custom_call" | custom-call | flops 4362076160 | bytes 17268736 | tf_op jit(solution)/shard_map/gate_up/pallas_call | solution.py:257
  97.3 6.2 %collective-permute-done.14.refs_4_.refs_1_ = bf16[2,128,2048]{2,1,0:T(8,128)(2,1)S(1)} collective-permute-done((bf16[2,128,2048]{2,1,0:T(8,128)(2,1)S(1)}, bf16[2,128,2048]{2,1,0:T(8,128)(2,1)S(1)}, u32[]{:S(2)}, u32[]{:S(2)}) %collective-permute-start.14) | collective-permute-done | bytes 1048608 | tf_op jit(solution)/shard_map/ppermute | solution.py:376
  103.5 6.1 %down.4 = (bf16[2,128,2048]{2,1,0:T(8,128)(2,1)S(1)}, bf16[2,128,2048]{2,1,0:T(8,128)(2,1)S(1)}) custom-call(s32[4,6]{1,0:T(4,128)S(1)} %dynamic-slice_bitcast_fusion.where_ref, s32[16,128]{1,0:T(8,128)S(1)} %bitcast.58, bf16[320,768]{1,0:T(8,128)(2,1)S(1)} %gate_up.5.refs_5_.refs_0_, bf16[320,768]{1,0:T(8,128)(2,1)S(1)} %collective-permute-done.13.refs_1_, ...), custom_call_target="tpu_custom_call" | custom-call | flops 2181038080 | bytes 9371648 | tf_op jit(solution)/shard_map/down/pallas_call | solution.py:287
  115.3 8.1 %gate_up.7.refs_3_.refs_0_ = bf16[320,768]{1,0:T(8,128)(2,1)S(1)} custom-call(s32[4,6]{1,0:T(4,128)S(1)} %dynamic-slice_bitcast_fusion.where_ref, s32[16,128]{1,0:T(8,128)S(1)} %bitcast.59, bf16[2,128,2048]{2,1,0:T(8,128)(2,1)S(1)} %pad_maximum_fusion.1.refs_6_.refs_0_, bf16[2,128,2048]{2,1,0:T(8,128)(2,1)S(1)} %collective-permute-done.14.refs_4_.refs_1_, ...), custom_call_target="tpu_custom_call" | custom-call | flops 4362076160 | bytes 17268736 | tf_op jit(solution)/shard_map/gate_up/pallas_call | solution.py:257
  125.0 6.1 %down.5 = (bf16[2,128,2048]{2,1,0:T(8,128)(2,1)S(1)}, bf16[2,128,2048]{2,1,0:T(8,128)(2,1)S(1)}) custom-call(s32[4,6]{1,0:T(4,128)S(1)} %dynamic-slice_bitcast_fusion.where_ref, s32[16,128]{1,0:T(8,128)S(1)} %bitcast.60, bf16[320,768]{1,0:T(8,128)(2,1)S(1)} %gate_up.6.refs_3_.refs_0_, bf16[320,768]{1,0:T(8,128)(2,1)S(1)} %collective-permute-done.22.refs_1_, ...), custom_call_target="tpu_custom_call" | custom-call | flops 2181038080 | bytes 9371648 | tf_op jit(solution)/shard_map/down/pallas_call | solution.py:287
  131.2 5.6 %collective-permute-done.20.refs_1_ = bf16[320,768]{1,0:T(8,128)(2,1)S(1)} collective-permute-done((bf16[320,768]{1,0:T(8,128)(2,1)S(1)}, bf16[320,768]{1,0:T(8,128)(2,1)S(1)}, u32[]{:S(2)}, u32[]{:S(2)}) %collective-permute-start.20) | collective-permute-done | bytes 491552 | tf_op jit(solution)/shard_map/ppermute | solution.py:376
  141.2 6.1 %down.6 = (bf16[2,128,2048]{2,1,0:T(8,128)(2,1)S(1)}, bf16[2,128,2048]{2,1,0:T(8,128)(2,1)S(1)}) custom-call(s32[4,6]{1,0:T(4,128)S(1)} %dynamic-slice_bitcast_fusion.where_ref, s32[16,128]{1,0:T(8,128)S(1)} %bitcast.61, bf16[320,768]{1,0:T(8,128)(2,1)S(1)} %gate_up.7.refs_3_.refs_0_, bf16[320,768]{1,0:T(8,128)(2,1)S(1)} %collective-permute-done.20.refs_1_, ...), custom_call_target="tpu_custom_call" | custom-call | flops 2181038080 | bytes 9371648 | tf_op jit(solution)/shard_map/down/pallas_call | solution.py:287
  147.4 3.1 %collective-permute-done.21.refs_1_ = bf16[320,768]{1,0:T(8,128)(2,1)S(1)} collective-permute-done((bf16[320,768]{1,0:T(8,128)(2,1)S(1)}, bf16[320,768]{1,0:T(8,128)(2,1)S(1)}, u32[]{:S(2)}, u32[]{:S(2)}) %collective-permute-start.21) | collective-permute-done | bytes 491552 | tf_op jit(solution)/shard_map/ppermute | solution.py:376
  150.4 6.1 %down.7 = (bf16[2,128,2048]{2,1,0:T(8,128)(2,1)S(1)}, bf16[2,128,2048]{2,1,0:T(8,128)(2,1)S(1)}) custom-call(s32[4,6]{1,0:T(4,128)S(1)} %dynamic-slice_bitcast_fusion.where_ref, s32[16,128]{1,0:T(8,128)S(1)} %bitcast.62, bf16[320,768]{1,0:T(8,128)(2,1)S(1)} %gate_up.4.refs_5_.refs_0_, bf16[320,768]{1,0:T(8,128)(2,1)S(1)} %collective-permute-done.21.refs_1_, ...), custom_call_target="tpu_custom_call" | custom-call | flops 2181038080 | bytes 9371648 | tf_op jit(solution)/shard_map/down/pallas_call | solution.py:287
  157.4 2.3 %collective-permute-start.32 = (bf16[128,2048]{1,0:T(8,128)(2,1)S(1)}, bf16[128,2048]{1,0:T(8,128)(2,1)S(1)}, u32[]{:S(2)}, u32[]{:S(2)}) collective-permute-start(bf16[128,2048]{1,0:T(8,128)(2,1)S(1)} %fusion.3), channel_id=1, source_target_pairs={{0,4},{1,5},{2,6},{3,7},{4,12},{5,13},{6,14},{7,15},{8,0},{9,1},{1... | collective-permute-start | bytes 1572872 | tf_op jit(solution)/shard_map/ppermute | solution.py:376
  160.9 11.3 %collective-permute-done.32 = bf16[128,2048]{1,0:T(8,128)(2,1)S(1)} collective-permute-done((bf16[128,2048]{1,0:T(8,128)(2,1)S(1)}, bf16[128,2048]{1,0:T(8,128)(2,1)S(1)}, u32[]{:S(2)}, u32[]{:S(2)}) %collective-permute-start.32) | collective-permute-done | bytes 524320 | tf_op jit(solution)/shard_map/ppermute | solution.py:376
  173.9 2.2 %collective-permute-start.33 = (bf16[128,2048]{1,0:T(8,128)(2,1)S(1)}, bf16[128,2048]{1,0:T(8,128)(2,1)S(1)}, u32[]{:S(2)}, u32[]{:S(2)}) collective-permute-start(bf16[128,2048]{1,0:T(8,128)(2,1)S(1)} %fusion.5), channel_id=1, source_target_pairs={{0,4},{1,5},{2,6},{3,7},{4,12},{5,13},{6,14},{7,15},{8,0},{9,1},{1... | collective-permute-start | bytes 1572872 | tf_op jit(solution)/shard_map/ppermute | solution.py:376
  176.6 11.0 %collective-permute-done.33 = bf16[128,2048]{1,0:T(8,128)(2,1)S(1)} collective-permute-done((bf16[128,2048]{1,0:T(8,128)(2,1)S(1)}, bf16[128,2048]{1,0:T(8,128)(2,1)S(1)}, u32[]{:S(2)}, u32[]{:S(2)}) %collective-permute-start.33) | collective-permute-done | bytes 524320 | tf_op jit(solution)/shard_map/ppermute | solution.py:376
  (78 shorter events, 40.9 us)
Async XLA Ops:
  2.9 14.5 %collective-permute-start = (bf16[128,2048]{1,0:T(8,128)(2,1)}, bf16[128,2048]{1,0:T(8,128)(2,1)S(1)}, u32[]{:S(2)}, u32[]{:S(2)}) collective-permute-start(bf16[128,2048]{1,0:T(8,128)(2,1)} %param.6), channel_id=1, source_target_pairs={{0,4},{1,5},{2,6},{3,7},{4,12},{5,13},{6,14},{7,15},{8,0},{9,1},{1... | collective-permute-start | bytes 1572872 | tf_op jit(solution)/shard_map/ppermute | solution.py:376
  11.4 20.8 %collective-permute-start.2 = (bf16[2,128,2048]{2,1,0:T(8,128)(2,1)S(1)}, bf16[2,128,2048]{2,1,0:T(8,128)(2,1)}, u32[]{:S(2)}, u32[]{:S(2)}) collective-permute-start(bf16[2,128,2048]{2,1,0:T(8,128)(2,1)S(1)} %pad_maximum_fusion.refs_0_), channel_id=1, source_target_pairs={{0,2},{1,17},{2,0},{3,19},{4,6},{5,21},{6,4},{7,23},{8,10},{9,25},... | collective-permute-start | bytes 3145736 | tf_op jit(solution)/shard_map/ppermute | solution.py:376
  17.5 14.8 %collective-permute-start.5 = (bf16[128,2048]{1,0:T(8,128)(2,1)S(1)}, bf16[128,2048]{1,0:T(8,128)(2,1)S(1)}, u32[]{:S(2)}, u32[]{:S(2)}) collective-permute-start(bf16[128,2048]{1,0:T(8,128)(2,1)S(1)} %collective-permute-done), channel_id=1, source_target_pairs={{0,4},{1,5},{2,6},{3,7},{4,12},{5,13},{6,14},{7,15},{8,0},{9,1},{1... | collective-permute-start | bytes 1572872 | tf_op jit(solution)/shard_map/ppermute | solution.py:376
  18.4 13.9 %collective-permute-start.7 = (bf16[128,2048]{1,0:T(8,128)(2,1)S(1)}, bf16[128,2048]{1,0:T(8,128)(2,1)S(1)}, u32[]{:S(2)}, u32[]{:S(2)}) collective-permute-start(bf16[128,2048]{1,0:T(8,128)(2,1)S(1)} %collective-permute-done), channel_id=1, source_target_pairs={{0,16},{1,3},{2,18},{3,1},{4,20},{5,7},{6,22},{7,5},{8,24},{9,11},... | collective-permute-start | bytes 1572872 | tf_op jit(solution)/shard_map/ppermute | solution.py:376
  34.5 14.4 %collective-permute-start.6 = (bf16[128,2048]{1,0:T(8,128)(2,1)S(1)}, bf16[128,2048]{1,0:T(8,128)(2,1)}, u32[]{:S(2)}, u32[]{:S(2)}) collective-permute-start(bf16[128,2048]{1,0:T(8,128)(2,1)S(1)} %collective-permute-done.5), channel_id=1, source_target_pairs={{0,4},{1,5},{2,6},{3,7},{4,12},{5,13},{6,14},{7,15},{8,0},{9,1},{1... | collective-permute-start | bytes 1572872 | tf_op jit(solution)/shard_map/ppermute | solution.py:376
  35.7 15.3 %collective-permute-start.3 = (bf16[2,128,2048]{2,1,0:T(8,128)(2,1)S(1)}, bf16[2,128,2048]{2,1,0:T(8,128)(2,1)}, u32[]{:S(2)}, u32[]{:S(2)}) collective-permute-start(bf16[2,128,2048]{2,1,0:T(8,128)(2,1)S(1)} %pad_maximum_fusion.refs_0_), channel_id=1, source_target_pairs={{0,1},{1,0},{2,3},{3,2},{4,5},{5,4},{6,7},{7,6},{8,9},{9,8},{10,11... | collective-permute-start | bytes 3145736 | tf_op jit(solution)/shard_map/ppermute | solution.py:376
  35.7 15.3 %collective-permute-start.4 = (bf16[2,128,2048]{2,1,0:T(8,128)(2,1)}, bf16[2,128,2048]{2,1,0:T(8,128)(2,1)}, u32[]{:S(2)}, u32[]{:S(2)}) collective-permute-start(bf16[2,128,2048]{2,1,0:T(8,128)(2,1)} %collective-permute-done.2.refs_1_), channel_id=1, source_target_pairs={{0,1},{1,0},{2,3},{3,2},{4,5},{5,4},{6,7},{7,6},{8,9},{9,8},{10,11... | collective-permute-start | bytes 3145736 | tf_op jit(solution)/shard_map/ppermute | solution.py:376
  48.9 14.9 %collective-permute-start.10 = (bf16[2,128,2048]{2,1,0:T(8,128)(2,1)S(1)}, bf16[2,128,2048]{2,1,0:T(8,128)(2,1)}, u32[]{:S(2)}, u32[]{:S(2)}) collective-permute-start(bf16[2,128,2048]{2,1,0:T(8,128)(2,1)S(1)} %pad_maximum_fusion.2.refs_0_), channel_id=1, source_target_pairs={{0,2},{1,17},{2,0},{3,19},{4,6},{5,21},{6,4},{7,23},{8,10},{9,25},... | collective-permute-start | bytes 3145736 | tf_op jit(solution)/shard_map/ppermute | solution.py:376
  50.1 14.9 %collective-permute-start.11 = (bf16[2,128,2048]{2,1,0:T(8,128)(2,1)S(1)}, bf16[2,128,2048]{2,1,0:T(8,128)(2,1)S(1)}, u32[]{:S(2)}, u32[]{:S(2)}) collective-permute-start(bf16[2,128,2048]{2,1,0:T(8,128)(2,1)S(1)} %pad_maximum_fusion.2.refs_0_), channel_id=1, source_target_pairs={{0,1},{1,0},{2,3},{3,2},{4,5},{5,4},{6,7},{7,6},{8,9},{9,8},{10,11... | collective-permute-start | bytes 3145736 | tf_op jit(solution)/shard_map/ppermute | solution.py:376
  63.8 14.8 %collective-permute-start.16 = (bf16[2,128,2048]{2,1,0:T(8,128)(2,1)S(1)}, bf16[2,128,2048]{2,1,0:T(8,128)(2,1)S(1)}, u32[]{:S(2)}, u32[]{:S(2)}) collective-permute-start(bf16[2,128,2048]{2,1,0:T(8,128)(2,1)S(1)} %pad_maximum_fusion.3.refs_0_), channel_id=1, source_target_pairs={{0,2},{1,17},{2,0},{3,19},{4,6},{5,21},{6,4},{7,23},{8,10},{9,25},... | collective-permute-start | bytes 3145736 | tf_op jit(solution)/shard_map/ppermute | solution.py:376
  64.3 15.4 %collective-permute-start.9 = (bf16[128,2048]{1,0:T(8,128)(2,1)S(1)}, bf16[128,2048]{1,0:T(8,128)(2,1)S(1)}, u32[]{:S(2)}, u32[]{:S(2)}) collective-permute-start(bf16[128,2048]{1,0:T(8,128)(2,1)S(1)} %copy-done.1), channel_id=1, source_target_pairs={{0,4},{1,5},{2,6},{3,7},{4,12},{5,13},{6,14},{7,15},{8,0},{9,1},{1... | collective-permute-start | bytes 1572872 | tf_op jit(solution)/shard_map/ppermute | solution.py:376
  75.0 13.7 %collective-permute-start.13 = (bf16[320,768]{1,0:T(8,128)(2,1)S(1)}, bf16[320,768]{1,0:T(8,128)(2,1)S(1)}, u32[]{:S(2)}, u32[]{:S(2)}) collective-permute-start(bf16[320,768]{1,0:T(8,128)(2,1)S(1)} %gate_up.5.refs_5_.refs_0_), channel_id=1, source_target_pairs={{0,16},{1,17},{2,18},{3,19},{4,20},{5,21},{6,22},{7,23},{8,24},{9,... | collective-permute-start | bytes 1474568 | tf_op jit(solution)/shard_map/ppermute | solution.py:376
  76.5 12.6 %collective-permute-start.17 = (bf16[2,128,2048]{2,1,0:T(8,128)(2,1)S(1)}, bf16[2,128,2048]{2,1,0:T(8,128)(2,1)S(1)}, u32[]{:S(2)}, u32[]{:S(2)}) collective-permute-start(bf16[2,128,2048]{2,1,0:T(8,128)(2,1)S(1)} %pad_maximum_fusion.3.refs_0_), channel_id=1, source_target_pairs={{0,1},{1,0},{2,3},{3,2},{4,5},{5,4},{6,7},{7,6},{8,9},{9,8},{10,11... | collective-permute-start | bytes 3145736 | tf_op jit(solution)/shard_map/ppermute | solution.py:376
  88.7 14.8 %collective-permute-start.14 = (bf16[2,128,2048]{2,1,0:T(8,128)(2,1)S(1)}, bf16[2,128,2048]{2,1,0:T(8,128)(2,1)S(1)}, u32[]{:S(2)}, u32[]{:S(2)}) collective-permute-start(bf16[2,128,2048]{2,1,0:T(8,128)(2,1)S(1)} %pad_maximum_fusion.1.refs_6_.refs_0_), channel_id=1, source_target_pairs={{0,2},{1,17},{2,0},{3,19},{4,6},{5,21},{6,4},{7,23},{8,10},{9,25},... | collective-permute-start | bytes 3145736 | tf_op jit(solution)/shard_map/ppermute | solution.py:376
  110.2 14.8 %collective-permute-start.22 = (bf16[320,768]{1,0:T(8,128)(2,1)S(1)}, bf16[320,768]{1,0:T(8,128)(2,1)S(1)}, u32[]{:S(2)}, u32[]{:S(2)}) collective-permute-start(bf16[320,768]{1,0:T(8,128)(2,1)S(1)} %gate_up.6.refs_3_.refs_0_), channel_id=1, source_target_pairs={{0,16},{1,17},{2,18},{3,19},{4,20},{5,21},{6,22},{7,23},{8,24},{9,... | collective-permute-start | bytes 1474568 | tf_op jit(solution)/shard_map/ppermute | solution.py:376
  112.4 24.4 %collective-permute-start.25 = (bf16[128,2048]{1,0:T(8,128)(2,1)S(1)}, bf16[128,2048]{1,0:T(8,128)(2,1)S(1)}, u32[]{:S(2)}, u32[]{:S(2)}) collective-permute-start(bf16[128,2048]{1,0:T(8,128)(2,1)S(1)} %fusion.11), channel_id=1, source_target_pairs={{0,2},{1,3},{2,0},{3,1},{4,6},{5,7},{6,4},{7,5},{8,10},{9,11},{10,... | collective-permute-start | bytes 1572872 | tf_op jit(solution)/shard_map/ppermute | solution.py:376
  123.5 13.3 %collective-permute-start.20 = (bf16[320,768]{1,0:T(8,128)(2,1)S(1)}, bf16[320,768]{1,0:T(8,128)(2,1)S(1)}, u32[]{:S(2)}, u32[]{:S(2)}) collective-permute-start(bf16[320,768]{1,0:T(8,128)(2,1)S(1)} %gate_up.7.refs_3_.refs_0_), channel_id=1, source_target_pairs={{0,16},{1,17},{2,18},{3,19},{4,20},{5,21},{6,22},{7,23},{8,24},{9,... | collective-permute-start | bytes 1474568 | tf_op jit(solution)/shard_map/ppermute | solution.py:376
  136.8 13.6 %collective-permute-start.21 = (bf16[320,768]{1,0:T(8,128)(2,1)S(1)}, bf16[320,768]{1,0:T(8,128)(2,1)S(1)}, u32[]{:S(2)}, u32[]{:S(2)}) collective-permute-start(bf16[320,768]{1,0:T(8,128)(2,1)S(1)} %gate_up.4.refs_5_.refs_0_), channel_id=1, source_target_pairs={{0,16},{1,17},{2,18},{3,19},{4,20},{5,21},{6,22},{7,23},{8,24},{9,... | collective-permute-start | bytes 1474568 | tf_op jit(solution)/shard_map/ppermute | solution.py:376
  138.6 18.0 %collective-permute-start.26 = (bf16[128,2048]{1,0:T(8,128)(2,1)S(1)}, bf16[128,2048]{1,0:T(8,128)(2,1)S(1)}, u32[]{:S(2)}, u32[]{:S(2)}) collective-permute-start(bf16[128,2048]{1,0:T(8,128)(2,1)S(1)} %fusion.6), channel_id=1, source_target_pairs={{4,0},{5,1},{6,2},{7,3},{12,4},{13,5},{14,6},{15,7},{0,8},{1,9},{2... | collective-permute-start | bytes 1572872 | tf_op jit(solution)/shard_map/ppermute | solution.py:376
  140.7 15.9 %collective-permute-start.28 = (bf16[128,2048]{1,0:T(8,128)(2,1)S(1)}, bf16[128,2048]{1,0:T(8,128)(2,1)S(1)}, u32[]{:S(2)}, u32[]{:S(2)}) collective-permute-start(bf16[128,2048]{1,0:T(8,128)(2,1)S(1)} %fusion.12), channel_id=1, source_target_pairs={{0,2},{1,3},{2,0},{3,1},{4,6},{5,7},{6,4},{7,5},{8,10},{9,11},{10,... | collective-permute-start | bytes 1572872 | tf_op jit(solution)/shard_map/ppermute | solution.py:376
  157.4 14.9 %collective-permute-start.32 = (bf16[128,2048]{1,0:T(8,128)(2,1)S(1)}, bf16[128,2048]{1,0:T(8,128)(2,1)S(1)}, u32[]{:S(2)}, u32[]{:S(2)}) collective-permute-start(bf16[128,2048]{1,0:T(8,128)(2,1)S(1)} %fusion.3), channel_id=1, source_target_pairs={{0,4},{1,5},{2,6},{3,7},{4,12},{5,13},{6,14},{7,15},{8,0},{9,1},{1... | collective-permute-start | bytes 1572872 | tf_op jit(solution)/shard_map/ppermute | solution.py:376
  159.8 13.7 %collective-permute-start.30 = (bf16[128,2048]{1,0:T(8,128)(2,1)S(1)}, bf16[128,2048]{1,0:T(8,128)(2,1)S(1)}, u32[]{:S(2)}, u32[]{:S(2)}) collective-permute-start(bf16[128,2048]{1,0:T(8,128)(2,1)S(1)} %fusion.13), channel_id=1, source_target_pairs={{0,2},{1,3},{2,0},{3,1},{4,6},{5,7},{6,4},{7,5},{8,10},{9,11},{10,... | collective-permute-start | bytes 1572872 | tf_op jit(solution)/shard_map/ppermute | solution.py:376
  173.9 13.7 %collective-permute-start.33 = (bf16[128,2048]{1,0:T(8,128)(2,1)S(1)}, bf16[128,2048]{1,0:T(8,128)(2,1)S(1)}, u32[]{:S(2)}, u32[]{:S(2)}) collective-permute-start(bf16[128,2048]{1,0:T(8,128)(2,1)S(1)} %fusion.5), channel_id=1, source_target_pairs={{0,4},{1,5},{2,6},{3,7},{4,12},{5,13},{6,14},{7,15},{8,0},{9,1},{1... | collective-permute-start | bytes 1572872 | tf_op jit(solution)/shard_map/ppermute | solution.py:376
  176.1 12.8 %collective-permute-start.31 = (bf16[128,2048]{1,0:T(8,128)(2,1)S(1)}, bf16[128,2048]{1,0:T(8,128)(2,1)S(1)}, u32[]{:S(2)}, u32[]{:S(2)}) collective-permute-start(bf16[128,2048]{1,0:T(8,128)(2,1)S(1)} %fusion.10), channel_id=1, source_target_pairs={{0,2},{1,3},{2,0},{3,1},{4,6},{5,7},{6,4},{7,5},{8,10},{9,11},{10,... | collective-permute-start | bytes 1572872 | tf_op jit(solution)/shard_map/ppermute | solution.py:376
  (14 other events, 123.0 us)

commit v13 on v11

--- a/solution.py
+++ b/solution.py
@@ -427,11 +427,11 @@
     crosses.append(move(after(pairs[3], hidden1[1]), second))
     hidden2 = swap(gate_up(2, spread(2, hidden1[0]), hidden1[0], pairs[3]))
     part1 = down(1, hidden1, hidden2[0], crosses[3])
-    shards3 = spread(3, part1[0])
-    part1 = give(part1)
-    back1 = move(away(part1), over_y)
+    shards3 = spread(3, hidden2[0])
     hidden3 = swap(gate_up(3, shards3, part1[0]))
-    part2 = give(down(2, hidden2, hidden3[0], back1), hidden3[1])
+    part1 = give(part1, shards3[3])
+    back1 = move(after(away(part1), hidden3[0]), over_y)
+    part2 = give(down(2, hidden2, hidden3[0]), hidden3[1], back1)
     hidden0 = swap(mine0, hidden3[1])
     from_next = move(total(part1, after(back1, hidden3[0])), backward)
     back2 = move(away(part2), over_y)

time: 186 us -> 183 us (0.984)
  waiting for transfers between devices: 82.6 us -> 78.7 us
    ppermute x33, waiting for transfers between devices: 82.6 us -> 78.7 us  [move(): return lax.ppermute(value, axes, moves)]
  transfers between devices with their start and end apart: 33 -> 33, of which waited for: 20 -> 17; matrix products, arithmetic and copies ran while one was open for 2% -> 3% of each run, Pallas kernels for 28% -> 32%
where the time goes in v13:
time: 183 us
  waiting for transfers between devices  78.7 us (43%)
  Pallas kernels  58.2 us (32%)
  starting transfers between devices  28.9 us (16%)
  blocking collectives  10.9 us (6%)
  other arithmetic  5.32 us (3%)
    ppermute x33, waiting for transfers between devices, move(): return lax.ppermute(value, axes, moves)  78.7 us
    pallas_call x4, Pallas kernels, pick_call(): pl.pallas_call(functools.partial(pick_kernel, capacity, k), in_specs=[pl....  33.7 us
    ppermute x33, starting transfers between devices, move(): return lax.ppermute(value, axes, moves)  28.9 us
    pallas_call x4, Pallas kernels, sum_call(): pl.pallas_call(functools.partial(sum_kernel, capacity, k), in_specs=[pl.B...  24.5 us
    all_to_all x1, blocking collectives, pair_shards(): lax.all_to_all(named, 'expert', split_axis=0, concat_axis=0, tiled=True)  10.9 us
  transfers between devices with their start and end apart: 33, of which 17 were waited for; matrix products, arithmetic and copies ran while one was open for 3% of the time, Pallas kernels for 32%

profile of v13, /device:TPU:0, one launch (start us, length us, event | category | flops | bytes accessed | tf_op | source)
XLA Modules:
  0.0 183.1 jit_solution(5561114394776440071)
XLA Ops:
  0.0 2.9 %collective-permute-start.1 = (bf16[128,2048]{1,0:T(8,128)(2,1)}, bf16[128,2048]{1,0:T(8,128)(2,1)S(1)}, u32[]{:S(2)}, u32[]{:S(2)}) collective-permute-start(bf16[128,2048]{1,0:T(8,128)(2,1)} %param.6), channel_id=1, source_target_pairs={{0,16},{1,3},{2,18},{3,1},{4,20},{5,7},{6,22},{7,5},{8,24},{9,11},... | collective-permute-start | bytes 1572872 | tf_op jit(solution)/shard_map/ppermute | solution.py:376
  4.5 5.8 %collective-permute-done.1 = bf16[128,2048]{1,0:T(8,128)(2,1)S(1)} collective-permute-done((bf16[128,2048]{1,0:T(8,128)(2,1)}, bf16[128,2048]{1,0:T(8,128)(2,1)S(1)}, u32[]{:S(2)}, u32[]{:S(2)}) %collective-permute-start.1) | collective-permute-done | bytes 524320 | tf_op jit(solution)/shard_map/ppermute | solution.py:376
  11.4 2.1 %collective-permute-start.2 = (bf16[2,128,2048]{2,1,0:T(8,128)(2,1)S(1)}, bf16[2,128,2048]{2,1,0:T(8,128)(2,1)}, u32[]{:S(2)}, u32[]{:S(2)}) collective-permute-start(bf16[2,128,2048]{2,1,0:T(8,128)(2,1)S(1)} %pad_maximum_fusion.refs_0_), channel_id=1, source_target_pairs={{0,2},{1,17},{2,0},{3,19},{4,6},{5,21},{6,4},{7,23},{8,10},{9,25},... | collective-permute-start | bytes 3145736 | tf_op jit(solution)/shard_map/ppermute | solution.py:376
  13.6 3.9 %collective-permute-done = bf16[128,2048]{1,0:T(8,128)(2,1)S(1)} collective-permute-done((bf16[128,2048]{1,0:T(8,128)(2,1)}, bf16[128,2048]{1,0:T(8,128)(2,1)S(1)}, u32[]{:S(2)}, u32[]{:S(2)}) %collective-permute-start) | collective-permute-done | bytes 524320 | tf_op jit(solution)/shard_map/ppermute | solution.py:376
  21.4 10.9 %all_to_all.11 = s32[16,1,128]{2,1,0:T(1,128)S(1)} all-to-all(s32[16,1,128]{2,1,0:T(1,128)S(1)} %bitcast.73), channel_id=1, replica_groups=mesh['section'=2,'expert'=16] {'expert'}, dimensions={0} | all-to-all | bytes 16384 | tf_op jit(solution)/shard_map/all_to_all | solution.py:392
  32.3 2.2 %collective-permute-start.7 = (bf16[128,2048]{1,0:T(8,128)(2,1)S(1)}, bf16[128,2048]{1,0:T(8,128)(2,1)S(1)}, u32[]{:S(2)}, u32[]{:S(2)}) collective-permute-start(bf16[128,2048]{1,0:T(8,128)(2,1)S(1)} %collective-permute-done.5), channel_id=1, source_target_pairs={{0,16},{1,3},{2,18},{3,1},{4,20},{5,7},{6,22},{7,5},{8,24},{9,11},... | collective-permute-start | bytes 1572872 | tf_op jit(solution)/shard_map/ppermute | solution.py:376
  35.1 6.5 %collective-permute-done.7 = bf16[128,2048]{1,0:T(8,128)(2,1)S(1)} collective-permute-done((bf16[128,2048]{1,0:T(8,128)(2,1)S(1)}, bf16[128,2048]{1,0:T(8,128)(2,1)S(1)}, u32[]{:S(2)}, u32[]{:S(2)}) %collective-permute-start.7) | collective-permute-done | bytes 524320 | tf_op jit(solution)/shard_map/ppermute | solution.py:376
  44.3 8.9 %gate_up.4.refs_5_.refs_0_ = bf16[320,768]{1,0:T(8,128)(2,1)S(1)} custom-call(s32[4,6]{1,0:T(4,128)S(1)} %dynamic-slice_bitcast_fusion.where_ref, s32[16,128]{1,0:T(8,128)S(1)} %bitcast.53, bf16[2,128,2048]{2,1,0:T(8,128)(2,1)S(1)} %pad_maximum_fusion.refs_0_, bf16[2,128,2048]{2,1,0:T(8,128)(2,1)} %collective-permute-done.2.refs_1_, ...), custom_call_target="tpu_custom_call" | custom-call | flops 4362076160 | bytes 17268736 | tf_op jit(solution)/shard_map/gate_up/pallas_call | solution.py:257
  53.2 3.6 %collective-permute-done.9.refs_1_ = bf16[2,128,2048]{2,1,0:T(8,128)(2,1)} collective-permute-done((bf16[2,128,2048]{2,1,0:T(8,128)(2,1)S(1)}, bf16[2,128,2048]{2,1,0:T(8,128)(2,1)}, u32[]{:S(2)}, u32[]{:S(2)}) %collective-permute-start.9) | collective-permute-done | bytes 1048608 | tf_op jit(solution)/shard_map/ppermute | solution.py:376
  60.1 8.6 %gate_up.5.refs_5_.refs_0_ = bf16[320,768]{1,0:T(8,128)(2,1)S(1)} custom-call(s32[4,6]{1,0:T(4,128)S(1)} %dynamic-slice_bitcast_fusion.where_ref, s32[16,128]{1,0:T(8,128)S(1)} %bitcast.54, bf16[2,128,2048]{2,1,0:T(8,128)(2,1)S(1)} %pad_maximum_fusion.2.refs_0_, bf16[2,128,2048]{2,1,0:T(8,128)(2,1)} %collective-permute-done.9.refs_1_, ...), custom_call_target="tpu_custom_call" | custom-call | flops 4362076160 | bytes 17268736 | tf_op jit(solution)/shard_map/gate_up/pallas_call | solution.py:257
  71.6 13.4 %collective-permute-done.8.refs_6_.refs_0_ = bf16[2,128,2048]{2,1,0:T(8,128)(2,1)S(1)} collective-permute-done((bf16[2,128,2048]{2,1,0:T(8,128)(2,1)S(1)}, bf16[2,128,2048]{2,1,0:T(8,128)(2,1)S(1)}, u32[]{:S(2)}, u32[]{:S(2)}) %collective-permute-start.8) | collective-permute-done | bytes 1048608 | tf_op jit(solution)/shard_map/ppermute | solution.py:376
  85.1 8.1 %gate_up.6.refs_3_.refs_0_ = bf16[320,768]{1,0:T(8,128)(2,1)S(1)} custom-call(s32[4,6]{1,0:T(4,128)S(1)} %dynamic-slice_bitcast_fusion.where_ref, s32[16,128]{1,0:T(8,128)S(1)} %bitcast.55, bf16[2,128,2048]{2,1,0:T(8,128)(2,1)S(1)} %pad_maximum_fusion.1.refs_0_, bf16[2,128,2048]{2,1,0:T(8,128)(2,1)S(1)} %collective-permute-done.15.refs_1_, ...), custom_call_target="tpu_custom_call" | custom-call | flops 4362076160 | bytes 17268736 | tf_op jit(solution)/shard_map/gate_up/pallas_call | solution.py:257
  93.2 6.6 %collective-permute-done.13.refs_4_.refs_1_ = bf16[2,128,2048]{2,1,0:T(8,128)(2,1)S(1)} collective-permute-done((bf16[2,128,2048]{2,1,0:T(8,128)(2,1)S(1)}, bf16[2,128,2048]{2,1,0:T(8,128)(2,1)S(1)}, u32[]{:S(2)}, u32[]{:S(2)}) %collective-permute-start.13) | collective-permute-done | bytes 1048608 | tf_op jit(solution)/shard_map/ppermute | solution.py:376
  100.3 6.1 %down.4 = (bf16[2,128,2048]{2,1,0:T(8,128)(2,1)S(1)}, bf16[2,128,2048]{2,1,0:T(8,128)(2,1)S(1)}) custom-call(s32[4,6]{1,0:T(4,128)S(1)} %dynamic-slice_bitcast_fusion.where_ref, s32[16,128]{1,0:T(8,128)S(1)} %bitcast.56, bf16[320,768]{1,0:T(8,128)(2,1)S(1)} %gate_up.5.refs_5_.refs_0_, bf16[320,768]{1,0:T(8,128)(2,1)S(1)} %collective-permute-done.12.refs_1_, ...), custom_call_target="tpu_custom_call" | custom-call | flops 2181038080 | bytes 9371648 | tf_op jit(solution)/shard_map/down/pallas_call | solution.py:287
  106.9 8.1 %gate_up.7.refs_3_.refs_0_ = bf16[320,768]{1,0:T(8,128)(2,1)S(1)} custom-call(s32[4,6]{1,0:T(4,128)S(1)} %dynamic-slice_bitcast_fusion.where_ref, s32[16,128]{1,0:T(8,128)S(1)} %bitcast.57, bf16[2,128,2048]{2,1,0:T(8,128)(2,1)S(1)} %collective-permute-done.8.refs_6_.refs_0_, bf16[2,128,2048]{2,1,0:T(8,128)(2,1)S(1)} %collective-permute-done.13.refs_4_.refs_1_, ...), custom_call_target="tpu_custom_call" | custom-call | flops 4362076160 | bytes 17268736 | tf_op jit(solution)/shard_map/gate_up/pallas_call | solution.py:257
  117.0 3.5 %collective-permute-done.21.refs_1_ = bf16[320,768]{1,0:T(8,128)(2,1)S(1)} collective-permute-done((bf16[320,768]{1,0:T(8,128)(2,1)S(1)}, bf16[320,768]{1,0:T(8,128)(2,1)S(1)}, u32[]{:S(2)}, u32[]{:S(2)}) %collective-permute-start.21) | collective-permute-done | bytes 491552 | tf_op jit(solution)/shard_map/ppermute | solution.py:376
  120.6 6.1 %down.5 = (bf16[2,128,2048]{2,1,0:T(8,128)(2,1)S(1)}, bf16[2,128,2048]{2,1,0:T(8,128)(2,1)S(1)}) custom-call(s32[4,6]{1,0:T(4,128)S(1)} %dynamic-slice_bitcast_fusion.where_ref, s32[16,128]{1,0:T(8,128)S(1)} %bitcast.58, bf16[320,768]{1,0:T(8,128)(2,1)S(1)} %gate_up.6.refs_3_.refs_0_, bf16[320,768]{1,0:T(8,128)(2,1)S(1)} %collective-permute-done.21.refs_1_, ...), custom_call_target="tpu_custom_call" | custom-call | flops 2181038080 | bytes 9371648 | tf_op jit(solution)/shard_map/down/pallas_call | solution.py:287
  126.7 4.0 %collective-permute-done.19.refs_1_ = bf16[320,768]{1,0:T(8,128)(2,1)S(1)} collective-permute-done((bf16[320,768]{1,0:T(8,128)(2,1)S(1)}, bf16[320,768]{1,0:T(8,128)(2,1)S(1)}, u32[]{:S(2)}, u32[]{:S(2)}) %collective-permute-start.19) | collective-permute-done | bytes 491552 | tf_op jit(solution)/shard_map/ppermute | solution.py:376
  131.2 1.9 %collective-permute-start.25 = (bf16[128,2048]{1,0:T(8,128)(2,1)S(1)}, bf16[128,2048]{1,0:T(8,128)(2,1)S(1)}, u32[]{:S(2)}, u32[]{:S(2)}) collective-permute-start(bf16[128,2048]{1,0:T(8,128)(2,1)S(1)} %fusion.6), channel_id=1, source_target_pairs={{4,0},{5,1},{6,2},{7,3},{12,4},{13,5},{14,6},{15,7},{0,8},{1,9},{2... | collective-permute-start | bytes 1572872 | tf_op jit(solution)/shard_map/ppermute | solution.py:376
  134.8 6.1 %down.6 = (bf16[2,128,2048]{2,1,0:T(8,128)(2,1)S(1)}, bf16[2,128,2048]{2,1,0:T(8,128)(2,1)S(1)}) custom-call(s32[4,6]{1,0:T(4,128)S(1)} %dynamic-slice_bitcast_fusion.where_ref, s32[16,128]{1,0:T(8,128)S(1)} %bitcast.59, bf16[320,768]{1,0:T(8,128)(2,1)S(1)} %gate_up.7.refs_3_.refs_0_, bf16[320,768]{1,0:T(8,128)(2,1)S(1)} %collective-permute-done.19.refs_1_, ...), custom_call_target="tpu_custom_call" | custom-call | flops 2181038080 | bytes 9371648 | tf_op jit(solution)/shard_map/down/pallas_call | solution.py:287
  141.0 3.3 %collective-permute-done.20.refs_1_ = bf16[320,768]{1,0:T(8,128)(2,1)S(1)} collective-permute-done((bf16[320,768]{1,0:T(8,128)(2,1)S(1)}, bf16[320,768]{1,0:T(8,128)(2,1)S(1)}, u32[]{:S(2)}, u32[]{:S(2)}) %collective-permute-start.20) | collective-permute-done | bytes 491552 | tf_op jit(solution)/shard_map/ppermute | solution.py:376
  144.3 6.1 %down.7 = (bf16[2,128,2048]{2,1,0:T(8,128)(2,1)S(1)}, bf16[2,128,2048]{2,1,0:T(8,128)(2,1)S(1)}) custom-call(s32[4,6]{1,0:T(4,128)S(1)} %dynamic-slice_bitcast_fusion.where_ref, s32[16,128]{1,0:T(8,128)S(1)} %bitcast.60, bf16[320,768]{1,0:T(8,128)(2,1)S(1)} %gate_up.4.refs_5_.refs_0_, bf16[320,768]{1,0:T(8,128)(2,1)S(1)} %collective-permute-done.20.refs_1_, ...), custom_call_target="tpu_custom_call" | custom-call | flops 2181038080 | bytes 9371648 | tf_op jit(solution)/shard_map/down/pallas_call | solution.py:287
  154.8 11.3 %collective-permute-done.31 = bf16[128,2048]{1,0:T(8,128)(2,1)S(1)} collective-permute-done((bf16[128,2048]{1,0:T(8,128)(2,1)S(1)}, bf16[128,2048]{1,0:T(8,128)(2,1)S(1)}, u32[]{:S(2)}, u32[]{:S(2)}) %collective-permute-start.31) | collective-permute-done | bytes 524320 | tf_op jit(solution)/shard_map/ppermute | solution.py:376
  170.4 11.3 %collective-permute-done.32 = bf16[128,2048]{1,0:T(8,128)(2,1)S(1)} collective-permute-done((bf16[128,2048]{1,0:T(8,128)(2,1)S(1)}, bf16[128,2048]{1,0:T(8,128)(2,1)S(1)}, u32[]{:S(2)}, u32[]{:S(2)}) %collective-permute-start.32) | collective-permute-done | bytes 524320 | tf_op jit(solution)/shard_map/ppermute | solution.py:376
  (71 shorter events, 31.3 us)
Async XLA Ops:
  0.0 10.3 %collective-permute-start.1 = (bf16[128,2048]{1,0:T(8,128)(2,1)}, bf16[128,2048]{1,0:T(8,128)(2,1)S(1)}, u32[]{:S(2)}, u32[]{:S(2)}) collective-permute-start(bf16[128,2048]{1,0:T(8,128)(2,1)} %param.6), channel_id=1, source_target_pairs={{0,16},{1,3},{2,18},{3,1},{4,20},{5,7},{6,22},{7,5},{8,24},{9,11},... | collective-permute-start | bytes 1572872 | tf_op jit(solution)/shard_map/ppermute | solution.py:376
  2.9 14.5 %collective-permute-start = (bf16[128,2048]{1,0:T(8,128)(2,1)}, bf16[128,2048]{1,0:T(8,128)(2,1)S(1)}, u32[]{:S(2)}, u32[]{:S(2)}) collective-permute-start(bf16[128,2048]{1,0:T(8,128)(2,1)} %param.6), channel_id=1, source_target_pairs={{0,4},{1,5},{2,6},{3,7},{4,12},{5,13},{6,14},{7,15},{8,0},{9,1},{1... | collective-permute-start | bytes 1572872 | tf_op jit(solution)/shard_map/ppermute | solution.py:376
  11.4 20.8 %collective-permute-start.2 = (bf16[2,128,2048]{2,1,0:T(8,128)(2,1)S(1)}, bf16[2,128,2048]{2,1,0:T(8,128)(2,1)}, u32[]{:S(2)}, u32[]{:S(2)}) collective-permute-start(bf16[2,128,2048]{2,1,0:T(8,128)(2,1)S(1)} %pad_maximum_fusion.refs_0_), channel_id=1, source_target_pairs={{0,2},{1,17},{2,0},{3,19},{4,6},{5,21},{6,4},{7,23},{8,10},{9,25},... | collective-permute-start | bytes 3145736 | tf_op jit(solution)/shard_map/ppermute | solution.py:376
  17.5 14.8 %collective-permute-start.5 = (bf16[128,2048]{1,0:T(8,128)(2,1)S(1)}, bf16[128,2048]{1,0:T(8,128)(2,1)S(1)}, u32[]{:S(2)}, u32[]{:S(2)}) collective-permute-start(bf16[128,2048]{1,0:T(8,128)(2,1)S(1)} %collective-permute-done), channel_id=1, source_target_pairs={{0,4},{1,5},{2,6},{3,7},{4,12},{5,13},{6,14},{7,15},{8,0},{9,1},{1... | collective-permute-start | bytes 1572872 | tf_op jit(solution)/shard_map/ppermute | solution.py:376
  18.4 13.9 %collective-permute-start.6 = (bf16[128,2048]{1,0:T(8,128)(2,1)S(1)}, bf16[128,2048]{1,0:T(8,128)(2,1)S(1)}, u32[]{:S(2)}, u32[]{:S(2)}) collective-permute-start(bf16[128,2048]{1,0:T(8,128)(2,1)S(1)} %collective-permute-done), channel_id=1, source_target_pairs={{0,16},{1,3},{2,18},{3,1},{4,20},{5,7},{6,22},{7,5},{8,24},{9,11},... | collective-permute-start | bytes 1572872 | tf_op jit(solution)/shard_map/ppermute | solution.py:376
  34.5 9.8 %collective-permute-start.3 = (bf16[2,128,2048]{2,1,0:T(8,128)(2,1)S(1)}, bf16[2,128,2048]{2,1,0:T(8,128)(2,1)}, u32[]{:S(2)}, u32[]{:S(2)}) collective-permute-start(bf16[2,128,2048]{2,1,0:T(8,128)(2,1)S(1)} %pad_maximum_fusion.refs_0_), channel_id=1, source_target_pairs={{0,1},{1,0},{2,3},{3,2},{4,5},{5,4},{6,7},{7,6},{8,9},{9,8},{10,11... | collective-permute-start | bytes 3145736 | tf_op jit(solution)/shard_map/ppermute | solution.py:376
  41.8 15.0 %collective-permute-start.9 = (bf16[2,128,2048]{2,1,0:T(8,128)(2,1)S(1)}, bf16[2,128,2048]{2,1,0:T(8,128)(2,1)}, u32[]{:S(2)}, u32[]{:S(2)}) collective-permute-start(bf16[2,128,2048]{2,1,0:T(8,128)(2,1)S(1)} %pad_maximum_fusion.2.refs_0_), channel_id=1, source_target_pairs={{0,2},{1,17},{2,0},{3,19},{4,6},{5,21},{6,4},{7,23},{8,10},{9,25},... | collective-permute-start | bytes 3145736 | tf_op jit(solution)/shard_map/ppermute | solution.py:376
  44.3 15.8 %collective-permute-start.10 = (bf16[2,128,2048]{2,1,0:T(8,128)(2,1)S(1)}, bf16[2,128,2048]{2,1,0:T(8,128)(2,1)S(1)}, u32[]{:S(2)}, u32[]{:S(2)}) collective-permute-start(bf16[2,128,2048]{2,1,0:T(8,128)(2,1)S(1)} %pad_maximum_fusion.2.refs_0_), channel_id=1, source_target_pairs={{0,1},{1,0},{2,3},{3,2},{4,5},{5,4},{6,7},{7,6},{8,9},{9,8},{10,11... | collective-permute-start | bytes 3145736 | tf_op jit(solution)/shard_map/ppermute | solution.py:376
  56.8 14.8 %collective-permute-start.15 = (bf16[2,128,2048]{2,1,0:T(8,128)(2,1)S(1)}, bf16[2,128,2048]{2,1,0:T(8,128)(2,1)S(1)}, u32[]{:S(2)}, u32[]{:S(2)}) collective-permute-start(bf16[2,128,2048]{2,1,0:T(8,128)(2,1)S(1)} %pad_maximum_fusion.1.refs_0_), channel_id=1, source_target_pairs={{0,2},{1,17},{2,0},{3,19},{4,6},{5,21},{6,4},{7,23},{8,10},{9,25},... | collective-permute-start | bytes 3145736 | tf_op jit(solution)/shard_map/ppermute | solution.py:376
  58.5 26.5 %collective-permute-start.8 = (bf16[2,128,2048]{2,1,0:T(8,128)(2,1)S(1)}, bf16[2,128,2048]{2,1,0:T(8,128)(2,1)S(1)}, u32[]{:S(2)}, u32[]{:S(2)}) collective-permute-start(bf16[2,128,2048]{2,1,0:T(8,128)(2,1)S(1)} %pad_maximum_fusion.1.refs_0_), channel_id=1, source_target_pairs={{0,4},{1,5},{2,6},{3,7},{4,12},{5,13},{6,14},{7,15},{8,0},{9,1},{1... | collective-permute-start | bytes 3145736 | tf_op jit(solution)/shard_map/ppermute | solution.py:376
  68.7 16.3 %collective-permute-start.12 = (bf16[320,768]{1,0:T(8,128)(2,1)S(1)}, bf16[320,768]{1,0:T(8,128)(2,1)S(1)}, u32[]{:S(2)}, u32[]{:S(2)}) collective-permute-start(bf16[320,768]{1,0:T(8,128)(2,1)S(1)} %gate_up.5.refs_5_.refs_0_), channel_id=1, source_target_pairs={{0,16},{1,17},{2,18},{3,19},{4,20},{5,21},{6,22},{7,23},{8,24},{9,... | collective-permute-start | bytes 1474568 | tf_op jit(solution)/shard_map/ppermute | solution.py:376
  70.3 14.8 %collective-permute-start.16 = (bf16[2,128,2048]{2,1,0:T(8,128)(2,1)S(1)}, bf16[2,128,2048]{2,1,0:T(8,128)(2,1)S(1)}, u32[]{:S(2)}, u32[]{:S(2)}) collective-permute-start(bf16[2,128,2048]{2,1,0:T(8,128)(2,1)S(1)} %pad_maximum_fusion.1.refs_0_), channel_id=1, source_target_pairs={{0,1},{1,0},{2,3},{3,2},{4,5},{5,4},{6,7},{7,6},{8,9},{9,8},{10,11... | collective-permute-start | bytes 3145736 | tf_op jit(solution)/shard_map/ppermute | solution.py:376
  71.6 13.5 %collective-permute-start.17 = (bf16[2,128,2048]{2,1,0:T(8,128)(2,1)S(1)}, bf16[2,128,2048]{2,1,0:T(8,128)(2,1)S(1)}, u32[]{:S(2)}, u32[]{:S(2)}) collective-permute-start(bf16[2,128,2048]{2,1,0:T(8,128)(2,1)S(1)} %collective-permute-done.15.refs_1_), channel_id=1, source_target_pairs={{0,1},{1,0},{2,3},{3,2},{4,5},{5,4},{6,7},{7,6},{8,9},{9,8},{10,11... | collective-permute-start | bytes 3145736 | tf_op jit(solution)/shard_map/ppermute | solution.py:376
  85.0 14.8 %collective-permute-start.13 = (bf16[2,128,2048]{2,1,0:T(8,128)(2,1)S(1)}, bf16[2,128,2048]{2,1,0:T(8,128)(2,1)S(1)}, u32[]{:S(2)}, u32[]{:S(2)}) collective-permute-start(bf16[2,128,2048]{2,1,0:T(8,128)(2,1)S(1)} %collective-permute-done.8.refs_6_.refs_0_), channel_id=1, source_target_pairs={{0,2},{1,17},{2,0},{3,19},{4,6},{5,21},{6,4},{7,23},{8,10},{9,25},... | collective-permute-start | bytes 3145736 | tf_op jit(solution)/shard_map/ppermute | solution.py:376
  106.5 14.1 %collective-permute-start.21 = (bf16[320,768]{1,0:T(8,128)(2,1)S(1)}, bf16[320,768]{1,0:T(8,128)(2,1)S(1)}, u32[]{:S(2)}, u32[]{:S(2)}) collective-permute-start(bf16[320,768]{1,0:T(8,128)(2,1)S(1)} %gate_up.6.refs_3_.refs_0_), channel_id=1, source_target_pairs={{0,16},{1,17},{2,18},{3,19},{4,20},{5,21},{6,22},{7,23},{8,24},{9,... | collective-permute-start | bytes 1474568 | tf_op jit(solution)/shard_map/ppermute | solution.py:376
  115.2 15.5 %collective-permute-start.24 = (bf16[128,2048]{1,0:T(8,128)(2,1)S(1)}, bf16[128,2048]{1,0:T(8,128)(2,1)S(1)}, u32[]{:S(2)}, u32[]{:S(2)}) collective-permute-start(bf16[128,2048]{1,0:T(8,128)(2,1)S(1)} %fusion.11), channel_id=1, source_target_pairs={{0,2},{1,3},{2,0},{3,1},{4,6},{5,7},{6,4},{7,5},{8,10},{9,11},{10,... | collective-permute-start | bytes 1572872 | tf_op jit(solution)/shard_map/ppermute | solution.py:376
  116.7 14.0 %collective-permute-start.19 = (bf16[320,768]{1,0:T(8,128)(2,1)S(1)}, bf16[320,768]{1,0:T(8,128)(2,1)S(1)}, u32[]{:S(2)}, u32[]{:S(2)}) collective-permute-start(bf16[320,768]{1,0:T(8,128)(2,1)S(1)} %gate_up.7.refs_3_.refs_0_), channel_id=1, source_target_pairs={{0,16},{1,17},{2,18},{3,19},{4,20},{5,21},{6,22},{7,23},{8,24},{9,... | collective-permute-start | bytes 1474568 | tf_op jit(solution)/shard_map/ppermute | solution.py:376
  130.7 13.6 %collective-permute-start.20 = (bf16[320,768]{1,0:T(8,128)(2,1)S(1)}, bf16[320,768]{1,0:T(8,128)(2,1)S(1)}, u32[]{:S(2)}, u32[]{:S(2)}) collective-permute-start(bf16[320,768]{1,0:T(8,128)(2,1)S(1)} %gate_up.4.refs_5_.refs_0_), channel_id=1, source_target_pairs={{0,16},{1,17},{2,18},{3,19},{4,20},{5,21},{6,22},{7,23},{8,24},{9,... | collective-permute-start | bytes 1474568 | tf_op jit(solution)/shard_map/ppermute | solution.py:376
  131.2 19.2 %collective-permute-start.25 = (bf16[128,2048]{1,0:T(8,128)(2,1)S(1)}, bf16[128,2048]{1,0:T(8,128)(2,1)S(1)}, u32[]{:S(2)}, u32[]{:S(2)}) collective-permute-start(bf16[128,2048]{1,0:T(8,128)(2,1)S(1)} %fusion.6), channel_id=1, source_target_pairs={{4,0},{5,1},{6,2},{7,3},{12,4},{13,5},{14,6},{15,7},{0,8},{1,9},{2... | collective-permute-start | bytes 1572872 | tf_op jit(solution)/shard_map/ppermute | solution.py:376
  133.5 17.0 %collective-permute-start.27 = (bf16[128,2048]{1,0:T(8,128)(2,1)S(1)}, bf16[128,2048]{1,0:T(8,128)(2,1)S(1)}, u32[]{:S(2)}, u32[]{:S(2)}) collective-permute-start(bf16[128,2048]{1,0:T(8,128)(2,1)S(1)} %fusion.12), channel_id=1, source_target_pairs={{0,2},{1,3},{2,0},{3,1},{4,6},{5,7},{6,4},{7,5},{8,10},{9,11},{10,... | collective-permute-start | bytes 1572872 | tf_op jit(solution)/shard_map/ppermute | solution.py:376
  151.3 14.9 %collective-permute-start.31 = (bf16[128,2048]{1,0:T(8,128)(2,1)S(1)}, bf16[128,2048]{1,0:T(8,128)(2,1)S(1)}, u32[]{:S(2)}, u32[]{:S(2)}) collective-permute-start(bf16[128,2048]{1,0:T(8,128)(2,1)S(1)} %fusion.3), channel_id=1, source_target_pairs={{0,4},{1,5},{2,6},{3,7},{4,12},{5,13},{6,14},{7,15},{8,0},{9,1},{1... | collective-permute-start | bytes 1572872 | tf_op jit(solution)/shard_map/ppermute | solution.py:376
  153.3 14.0 %collective-permute-start.29 = (bf16[128,2048]{1,0:T(8,128)(2,1)S(1)}, bf16[128,2048]{1,0:T(8,128)(2,1)S(1)}, u32[]{:S(2)}, u32[]{:S(2)}) collective-permute-start(bf16[128,2048]{1,0:T(8,128)(2,1)S(1)} %fusion.13), channel_id=1, source_target_pairs={{0,2},{1,3},{2,0},{3,1},{4,6},{5,7},{6,4},{7,5},{8,10},{9,11},{10,... | collective-permute-start | bytes 1572872 | tf_op jit(solution)/shard_map/ppermute | solution.py:376
  167.7 14.1 %collective-permute-start.32 = (bf16[128,2048]{1,0:T(8,128)(2,1)S(1)}, bf16[128,2048]{1,0:T(8,128)(2,1)S(1)}, u32[]{:S(2)}, u32[]{:S(2)}) collective-permute-start(bf16[128,2048]{1,0:T(8,128)(2,1)S(1)} %fusion.5), channel_id=1, source_target_pairs={{0,4},{1,5},{2,6},{3,7},{4,12},{5,13},{6,14},{7,15},{8,0},{9,1},{1... | collective-permute-start | bytes 1572872 | tf_op jit(solution)/shard_map/ppermute | solution.py:376
  169.4 12.5 %collective-permute-start.30 = (bf16[128,2048]{1,0:T(8,128)(2,1)S(1)}, bf16[128,2048]{1,0:T(8,128)(2,1)S(1)}, u32[]{:S(2)}, u32[]{:S(2)}) collective-permute-start(bf16[128,2048]{1,0:T(8,128)(2,1)S(1)} %fusion.10), channel_id=1, source_target_pairs={{0,2},{1,3},{2,0},{3,1},{4,6},{5,7},{6,4},{7,5},{8,10},{9,11},{10,... | collective-permute-start | bytes 1572872 | tf_op jit(solution)/shard_map/ppermute | solution.py:376
  (11 other events, 126.2 us)
